TPU v7x, 32 devices: a whole 2x2x4 slice. The times are simulated.
32 devices in a mesh: gx: 2 (over core), gy: 4 (over y, x), gz: 4 (over z).
Axes of the slice: x: 2, y: 2, z: 4, core: 2. Of those that a mesh axis runs over, the one named last changes fastest.
Arguments:
- charges: float32 [64, 128, 512], P('gz', 'gx', 'gy'), may hold values from -6 to 6
- widths: float32 [4, 3], replicated, may hold values from 2.5 to 6
- amplitudes: float32 [4, 3], replicated, may hold values from 0.2 to 1
Outputs:
- potential: float32 [64, 128, 512], P('gz', 'gx', 'gy')
All inputs are finite; a program needn't handle non-finite values.
Results may differ from a plain program's by a relative error of at most 0.0001.
Values sent between devices are 32-bit elements; how exact they have to be, the bound alone decides.
No kernel may reach another device: no remote copies, remote signals or barrier semaphores. Data moves between devices by JAX's collectives and lax.ppermute only.
A program may use at most 64 MiB of HBM per device.

v0:
```python
import functools

import jax
import jax.numpy as jnp
import numpy as np
from jax import lax
from jax.experimental import pallas as pl
from jax.experimental.pallas import tpu as pltpu
from jax.sharding import PartitionSpec as P

R = 8
TERMS = 3
LANES = 128
NEAR = 9.0 / 16.0
FAR = -1.0 / 16.0
F32 = jnp.float32
BF16 = jnp.bfloat16
HIGHEST = lax.Precision.HIGHEST
VMEM_LIMIT = 40 * 1024 * 1024


def up8(n):
    return -(-n // 8) * 8


class Sizes:
    def __init__(self, nz, nx, ny, gz, gx, gy):
        self.nz, self.nx, self.ny = nz, nx, ny
        self.gz, self.gx, self.gy = gz, gx, gy
        self.z1, self.x1, self.y1 = nz // 2, nx // 2, ny // 2
        self.z2, self.x2, self.y2 = nz // 4, nx // 4, ny // 4
        self.cz = [nz * gz >> l for l in range(4)]
        self.cx = [nx * gx >> l for l in range(4)]
        self.cy = [ny * gy >> l for l in range(4)]
        self.planes = self.z1 + 3
        self.zrows = up8(self.planes)
        self.rows1 = up8(self.x1 + 3)
        self.rows2 = up8(self.x2 + 5)
        self.wide1 = self.y1 + 3
        self.wide2 = self.y2 + 5
        self.tiles1 = -(-self.planes * self.wide1 // LANES)
        self.tiles2 = -(-self.cz[2] * self.wide2 // LANES)
        self.strip = R + 3
        self.per_tile = LANES // self.strip
        self.tiles_s = -(-TERMS * self.planes // self.per_tile)
        self.fine_tiles = -(-nz // (LANES // R))
        self.ext = nx + 2 * R


def restrict_circle(n):
    m = np.zeros((n // 2, n))
    for i in range(n // 2):
        for d, w in ((0, 1.0), (1, NEAR), (-1, NEAR), (3, FAR), (-3, FAR)):
            m[i, (2 * i + d) % n] += w
    return m


def prolong_circle(n):
    m = np.zeros((2 * n, n))
    for i in range(n):
        m[2 * i, i] += 1.0
        for d, w in ((0, NEAR), (1, NEAR), (-1, FAR), (2, FAR)):
            m[2 * i + 1, (i + d) % n] += w
    return m


def restrict_open(first_in, n_in, first_out, n_out):
    m = np.zeros((n_out, n_in))
    for i in range(n_out):
        for d, w in ((0, 1.0), (1, NEAR), (-1, NEAR), (3, FAR), (-3, FAR)):
            j = 2 * (first_out + i) + d - first_in
            if 0 <= j < n_in:
                m[i, j] = w
    return m


def padded(m, rows, columns):
    out = np.zeros((rows, columns), np.float32)
    out[: m.shape[0], : m.shape[1]] = m
    return out


def constants(s):
    c = {}
    c["ry1"] = padded(restrict_open(0, s.ny, -1, s.wide1).T, s.ny, LANES)
    c["rx1"] = padded(restrict_open(0, s.nx, -1, s.x1 + 3), up8(s.rows1), s.nx)
    c["ry2"] = padded(restrict_open(-1, s.wide1, -2, s.wide2).T, LANES, LANES)
    c["rx2"] = padded(restrict_open(-1, s.x1 + 3, -2, s.x2 + 5), s.rows2, s.rows1)

    def chain(n):
        p1 = prolong_circle(n[1])
        p2 = p1 @ prolong_circle(n[2])
        return p1, p2, p2 @ prolong_circle(n[3])

    x1, x2, x3 = chain(s.cx)
    c["px1"], c["px2"], c["px3"] = (m.astype(np.float32) for m in (x1, x2, x3))
    place = np.zeros((s.cx[2], s.rows2))
    for r in range(s.x2 + 5):
        place[(r - 2) % s.cx[2], r] += 1.0
    c["rx3"] = (restrict_circle(s.cx[2]) @ place).astype(np.float32)
    y1, y2, y3 = chain(s.cy)
    c["py1"], c["py2"], c["py3"] = (
        np.ascontiguousarray(m[: s.ny].T).astype(np.float32) for m in (y1, y2, y3)
    )
    c["ry3"] = np.ascontiguousarray(restrict_circle(s.cy[2]).T).astype(np.float32)
    z2 = prolong_circle(s.cz[2])
    z3 = z2 @ prolong_circle(s.cz[3])
    own = [(o - 1) % s.cz[1] for o in range(s.planes)]
    c["pz2"] = padded(z2[own], s.zrows, s.cz[2])
    c["pz3"] = padded(z3[own], s.zrows, s.cz[3])
    c["rz3"] = padded(restrict_circle(s.cz[2]), s.cz[3], LANES)
    return c


def halves(x):
    high = x.astype(BF16)
    return high, (x - high.astype(F32)).astype(BF16)


def dot(a, b):
    return jnp.dot(a, b, preferred_element_type=F32)


def exact_dot(a, b):
    return jnp.dot(a, b, preferred_element_type=F32, precision=HIGHEST)


def dot3(a, b_high, b_low):
    high, low = halves(a)
    return dot(high, b_high) + dot(low, b_high) + dot(high, b_low)


def lanes_of(shape):
    return lax.broadcasted_iota(jnp.int32, shape, len(shape) - 1)


def turn(x, by):
    by = by % x.shape[-1]
    return x if by == 0 else pltpu.roll(x, by, x.ndim - 1)


def packed(planes, wide, tiles):
    out = [None] * tiles

    def add(t, x):
        out[t] = x if out[t] is None else out[t] + x

    for k, x in enumerate(planes):
        t, at = divmod(k * wide, LANES)
        moved = turn(x, at)
        if at + wide <= LANES:
            add(t, moved)
        else:
            lane = lanes_of(x.shape)
            add(t, jnp.where(lane >= at, moved, 0.0))
            add(t + 1, jnp.where(lane < at, moved, 0.0))
    return out


def unpacked(tile, k, wide, shift):
    t, at = divmod(k * wide, LANES)
    x = tile(t)
    lane = lanes_of(x.shape)
    if at + wide > LANES:
        x = jnp.where(lane >= at, x, tile(t + 1))
    x = turn(x, shift - at)
    if shift + wide <= LANES:
        return jnp.where((lane >= shift) & (lane < shift + wide), x, 0.0)
    return jnp.where((lane >= shift) | (lane < shift + wide - LANES), x, 0.0)


def share_kernel(s, b_ref, ry1_ref, rx1_ref, m_ref, sl_ref, sr_ref, cl_ref, cr_ref, xr_ref):
    b = [b_ref[z] for z in range(s.nz)]
    planes = []
    for k in range(-1, s.z1 + 2):
        out = None
        for d, w in ((0, 1.0), (1, NEAR), (-1, NEAR), (3, FAR), (-3, FAR)):
            if 0 <= 2 * k + d < s.nz:
                term = b[2 * k + d] if d == 0 else b[2 * k + d] * w
                out = term if out is None else out + term
        planes.append(out)
    high, low = halves(jnp.concatenate(planes, axis=0))
    ry1 = ry1_ref[...].astype(BF16)
    rx1 = rx1_ref[...].astype(BF16)
    along = dot(high, ry1) + dot(low, ry1)
    shares = []
    for k in range(s.planes):
        high, low = halves(along[k * s.nx : (k + 1) * s.nx])
        shares.append(dot(rx1, high) + dot(rx1, low))
    for t, x in enumerate(packed(shares, s.wide1, s.tiles1)):
        m_ref[t] = x
    lane = lanes_of((s.nx, LANES))
    group = LANES // R
    for t in range(s.fine_tiles):
        left = right = None
        for g in range(min(group, s.nz - t * group)):
            x = b[t * group + g]
            first = turn(x, R * ((g + 1) % group))
            last = turn(x, R * g + R - s.ny)
            at_first = (lane >= R * ((g + 1) % group)) & (lane < R * ((g + 1) % group) + R)
            at_last = (lane >= R * g) & (lane < R * g + R)
            left = jnp.where(at_first, first, 0.0 if left is None else left)
            right = jnp.where(at_last, last, 0.0 if right is None else right)
        sl_ref[t] = left
        sr_ref[t] = right
        cl_ref[t, 0:R] = left[0:R]
        cl_ref[t, R : 2 * R] = left[s.nx - R :]
        cr_ref[t, 0:R] = right[0:R]
        cr_ref[t, R : 2 * R] = right[s.nx - R :]
    for z in range(s.nz):
        xr_ref[z, 0:R] = b[z][0:R]
        xr_ref[z, R : 2 * R] = b[z][s.nx - R :]


def matrix_kernel(s, w_ref, a_ref, px1, px2, px3, rx3, py1, py2, py3, ry3, pz2, pz3, rz3,
                  tap_ref, z_ref, y0h_ref, y0l_ref, y1h_ref, y1l_ref, y2h_ref, y2l_ref,
                  xah_ref, xal_ref, xbh_ref, xbl_ref):
    def spread(level, t):
        w = jnp.full((8, LANES), w_ref[level, t], F32)
        return (-0.5 / (w * w))[0:1, 0:1]

    def bell(c, d):
        d = jnp.abs(d)
        return jnp.where(d <= R, jnp.exp(c * d * d), 0.0)

    def scale(c, count=None):
        n = lanes_of((1, LANES)).astype(F32)
        if count is None:
            d, valid = n - R, n <= 2 * R
        else:
            d, valid = jnp.minimum(n, count - n), n < count
        return 1.0 / jnp.sqrt(jnp.sum(jnp.where(valid, jnp.exp(2.0 * c * d * d), 0.0), axis=1, keepdims=True))

    coef = [[spread(l, t) for t in range(TERMS)] for l in range(4)]
    unit = [[scale(coef[l][t]) for t in range(TERMS)] for l in range(3)]

    def rows_of(shape):
        return lax.broadcasted_iota(jnp.int32, shape, 0)

    def circle(n, shape, first_row, first_lane, c, u):
        d = ((rows_of(shape) + first_row) - (lanes_of(shape) + first_lane)) & (n - 1)
        d = d.astype(F32)
        return (bell(c, d) + bell(c, n - d)) * u

    def full_circle(n, shape, c, u):
        d = ((rows_of(shape) - lanes_of(shape)) & (n - 1)).astype(F32)
        d = jnp.minimum(d, n - d)
        return jnp.exp(c * d * d) * u

    def put(high_ref, low_ref, at, x):
        high, low = halves(x)
        high_ref[:, at : at + x.shape[1]] = high
        low_ref[:, at : at + x.shape[1]] = low

    def by_term(shape, wide, values):
        t = lanes_of(shape)
        return jnp.where(t < wide, values[0], jnp.where(t < 2 * wide, values[1], values[2]))

    d = lanes_of((1, LANES)).astype(F32)
    for t in range(TERMS):
        g0 = bell(coef[0][t], d) * unit[0][t]
        g1 = bell(coef[1][t], d) * unit[1][t]
        tap_ref[t : t + 1] = g0
        tap_ref[TERMS + t : TERMS + t + 1] = g0 * a_ref[0, t]
        tap_ref[2 * TERMS + t : 2 * TERMS + t + 1] = g1 * (a_ref[1, t] * 0.25)
    for t in range(TERMS):
        shape = (2 * LANES, s.ny)
        i = rows_of(shape)
        cell = jnp.where(i < s.ny, i, jnp.where(i < s.ny + R, i - s.ny - R, i - R))
        g = bell(coef[0][t], (cell - lanes_of(shape)).astype(F32)) * unit[0][t]
        put(y0h_ref, y0l_ref, t * s.ny, jnp.where(i < s.ny + 2 * R, g, 0.0))
    for t in range(TERMS):
        shape = (LANES, s.cy[1])
        g = circle(s.cy[1], shape, -(R + 1), 0, coef[1][t], unit[1][t])
        g = jnp.where(rows_of(shape) < s.y1 + 3 + 2 * R, g, 0.0)
        put(y1h_ref, y1l_ref, t * s.ny, exact_dot(g, py1[...]))
        g = circle(s.cy[2], (s.cy[2], s.cy[2]), 0, 0, coef[2][t], unit[2][t])
        put(y2h_ref, y2l_ref, t * s.ny, exact_dot(g, py2[...]))
        u = scale(coef[3][t], s.cy[3])
        g = full_circle(s.cy[3], (s.cy[3], s.cy[3]), coef[3][t], u)
        put(y2h_ref, y2l_ref, (TERMS + t) * s.ny, exact_dot(exact_dot(ry3[...], g), py3[...]))
    wide = s.rows1
    shape = (s.cx[1], TERMS * wide)
    lane = lanes_of(shape)
    column = lane - jnp.where(lane < wide, 0, jnp.where(lane < 2 * wide, wide, 2 * wide))
    d = ((rows_of(shape) - column + 1) & (s.cx[1] - 1)).astype(F32)
    c = by_term(shape, wide, coef[1])
    g = (bell(c, d) + bell(c, s.cx[1] - d)) * by_term(shape, wide, unit[1])
    put(xah_ref, xal_ref, 0, exact_dot(px1[...], jnp.where(column < s.x1 + 3, g, 0.0)))
    wide = s.rows2
    shape = (s.cx[2], TERMS * wide)
    lane = lanes_of(shape)
    column = lane - jnp.where(lane < wide, 0, jnp.where(lane < 2 * wide, wide, 2 * wide))
    d = ((rows_of(shape) - column + 2) & (s.cx[2] - 1)).astype(F32)
    c = by_term(shape, wide, coef[2])
    g = (bell(c, d) + bell(c, s.cx[2] - d)) * by_term(shape, wide, unit[2])
    put(xbh_ref, xbl_ref, 0, exact_dot(px2[...], jnp.where(column < s.x2 + 5, g, 0.0)))
    for t in range(TERMS):
        u = scale(coef[3][t], s.cx[3])
        g = full_circle(s.cx[3], (s.cx[3], s.cx[3]), coef[3][t], u)
        put(xbh_ref, xbl_ref, (TERMS + t) * wide, exact_dot(px3[...], exact_dot(g, rx3[...])))
    for t in range(TERMS):
        g = circle(s.cz[2], (s.cz[2], LANES), 0, 0, coef[2][t], unit[2][t])
        g = exact_dot(pz2[...], g) * (a_ref[2, t] * 0.0625)
        z_ref[t * s.zrows : (t + 1) * s.zrows] = g
        u = scale(coef[3][t], s.cz[3])
        g = full_circle(s.cz[3], (s.cz[3], s.cz[3]), coef[3][t], u)
        g = exact_dot(exact_dot(pz3[...], g), rz3[...]) * (a_ref[3, t] * 0.015625)
        z_ref[(TERMS + t) * s.zrows : (TERMS + t + 1) * s.zrows] = g


def near_kernel(s, tap_ref, b_ref, xlo_ref, xhi_ref, sl_ref, sr_ref, c_lo_l, c_lo_r, c_hi_l, c_hi_r,
                y0h_ref, y0l_ref, own_ref, down_ref, up_ref, eh_ref, el_ref, u_ref, v_ref):
    ext = s.ext
    group = LANES // R
    lane = lanes_of((ext, LANES))
    for t in range(s.fine_tiles):
        left = jnp.concatenate([c_lo_l[t, R : 2 * R], sl_ref[t], c_hi_l[t, 0:R]], axis=0)
        right = jnp.concatenate([c_lo_r[t, R : 2 * R], sr_ref[t], c_hi_r[t, 0:R]], axis=0)
        for g in range(min(group, s.nz - t * group)):
            z = t * group + g
            strips = jnp.where((lane >= R * g) & (lane < R * g + R), left, right)
            strips = turn(strips, -R * g)
            main = jnp.concatenate([xlo_ref[z, R : 2 * R], b_ref[z], xhi_ref[z, 0:R]], axis=0)
            for at, x in ((0, main), (LANES, strips)):
                high, low = halves(x)
                eh_ref[z * ext : (z + 1) * ext, at : at + LANES] = high
                el_ref[z * ext : (z + 1) * ext, at : at + LANES] = low
    step = 4 * ext
    y0h, y0l = y0h_ref[...], y0l_ref[...]
    for at in range(0, s.nz * ext, step):
        high, low = eh_ref[at : at + step], el_ref[at : at + step]
        u = dot(high, y0h) + dot(low, y0h) + dot(high, y0l)
        for t in range(TERMS):
            for q in range(4):
                u_ref[t, at // ext + q] = u[q * ext : (q + 1) * ext, t * s.ny : (t + 1) * s.ny]

    def cross(z, _):
        for t in range(TERMS):
            v = u_ref[t, z, R : R + s.nx] * tap_ref[t, 0]
            for d in range(1, R + 1):
                v += (u_ref[t, z, R + d : R + d + s.nx] + u_ref[t, z, R - d : R - d + s.nx]) * tap_ref[t, d]
            v_ref[t, z] = v
        return 0

    lax.fori_loop(0, s.nz, cross, 0)

    def depth(r, _):
        rows = pl.ds(pl.multiple_of(r * 8, 8), 8)
        taps = [[tap_ref[TERMS + t, d] for d in range(R + 1)] for t in range(TERMS)]
        for first in range(-R, s.nz + R, R):
            acc = [None] * R
            for t in range(TERMS):
                for z in range(max(0, first - R), min(s.nz, first + 2 * R)):
                    v = v_ref[t, z, rows]
                    for o in range(R):
                        d = abs(first + o - z)
                        if d <= R:
                            term = v * taps[t][d]
                            acc[o] = term if acc[o] is None else acc[o] + term
            for o in range(R):
                if first < 0:
                    down_ref[o, rows] = acc[o]
                elif first >= s.nz:
                    up_ref[o, rows] = acc[o]
                else:
                    own_ref[first + o, rows] = acc[o]
        return 0

    lax.fori_loop(0, s.nx // 8, depth, 0)


def depth_kernel(s, tap_ref, *refs):
    m_refs = refs[: s.gz]
    ry2_ref, rx2_ref, w_ref, down_ref, up_ref, c2_ref, c_ref = refs[s.gz :]
    n = s.cz[1]
    parts = [[] for _ in range(n)]
    for b in range(s.gz):
        for k in range(s.planes):
            parts[(b * s.z1 + k - 1) % n].append((b, k))
    for z in range(n):
        out = None
        for b, k in parts[z]:
            x = unpacked(lambda t, b=b: m_refs[b][t], k, s.wide1, 0)
            out = x if out is None else out + x
        c_ref[z] = out
    lane = lanes_of((s.rows1, LANES))
    down = [jnp.zeros((s.rows1, LANES), F32)] * s.tiles_s
    up = list(down)
    for o in range(s.planes):
        sums = [c_ref[(o - 1) % n]]
        sums += [c_ref[(o - 1 + d) % n] + c_ref[(o - 1 - d) % n] for d in range(1, R + 1)]
        for t in range(TERMS):
            x = sums[0] * tap_ref[2 * TERMS + t, 0]
            for d in range(1, R + 1):
                x += sums[d] * tap_ref[2 * TERMS + t, d]
            k = t * s.planes + o
            w_ref[k] = x
            tile, slot = divmod(k, s.per_tile)
            at = slot * s.strip
            here = (lane >= at) & (lane < at + s.strip)
            down[tile] = jnp.where(here, turn(x, at), down[tile])
            up[tile] = jnp.where(here, turn(x, at - (s.wide1 - s.strip)), up[tile])
    coarse = []
    for j in range(s.cz[2]):
        at = lambda d: c_ref[(2 * j + d) % n]
        coarse.append(at(0) + NEAR * (at(1) + at(-1)) + FAR * (at(3) + at(-3)))
    high, low = halves(jnp.concatenate(coarse, axis=0))
    ry2 = ry2_ref[...].astype(BF16)
    rx2 = rx2_ref[...].astype(BF16)
    along = dot(high, ry2) + dot(low, ry2)
    shares = []
    for j in range(s.cz[2]):
        high, low = halves(along[j * s.rows1 : (j + 1) * s.rows1])
        shares.append(dot(rx2, high) + dot(rx2, low))
    for t in range(s.tiles_s):
        down_ref[t * s.rows1 : (t + 1) * s.rows1] = down[t]
        up_ref[t * s.rows1 : (t + 1) * s.rows1] = up[t]
    base = s.tiles_s * s.rows1
    for t, x in enumerate(packed(shares, s.wide2, s.tiles2)):
        rows = slice(t * s.rows2, (t + 1) * s.rows2)
        c2_ref[rows] = x
        for ref in (down_ref, up_ref):
            ref[base + t * s.rows2 : base + (t + 1) * s.rows2] = x


def along_kernel(s, z_ref, w_ref, *refs):
    c2_refs = refs[: s.gy]
    (y1h_ref, y1l_ref, y2h_ref, y2l_ref, xah_ref, xal_ref, xbh_ref, xbl_ref,
     *g_refs, yb_ref) = refs[s.gy :]
    base = s.tiles_s * s.rows1
    lane = lanes_of((s.rows1, LANES))
    above, below = c2_refs[1], c2_refs[-1]
    end = s.y1 + R
    along = []
    for t in range(TERMS):
        cells = []
        for o in range(s.planes):
            k = t * s.planes + o
            tile, slot = divmod(k, s.per_tile)
            rows = slice(tile * s.rows1, (tile + 1) * s.rows1)
            at = slot * s.strip
            x = turn(w_ref[k], R)
            x += jnp.where(lane < s.strip, turn(below[rows], -at), 0.0)
            x += jnp.where((lane >= end) & (lane < end + s.strip), turn(above[rows], end - at), 0.0)
            cells.append(x)
        columns = slice(t * s.ny, (t + 1) * s.ny)
        along.append(dot3(jnp.concatenate(cells, axis=0), y1h_ref[:, columns], y1l_ref[:, columns]))
    cells = []
    for j in range(s.cz[2]):
        out = None
        for b in range(s.gy):
            first = 0 if b == 0 or c2_refs[b].shape[0] == s.tiles2 * s.rows2 else base
            tile = lambda t, b=b, f=first: c2_refs[b][f + t * s.rows2 : f + (t + 1) * s.rows2]
            x = unpacked(tile, j, s.wide2, (b * s.y2 - 2) % LANES)
            out = x if out is None else out + x
        cells.append(out)
    yb = dot3(jnp.concatenate(cells, axis=0), y2h_ref[...], y2l_ref[...])
    for j in range(s.cz[2]):
        for q in range(2 * TERMS):
            yb_ref[q, j] = yb[j * s.rows2 : (j + 1) * s.rows2, q * s.ny : (q + 1) * s.ny]
    xah, xal, xbh, xbl = xah_ref[...], xal_ref[...], xbh_ref[...], xbl_ref[...]
    for o in range(s.planes):
        rows = slice(o * s.rows1, (o + 1) * s.rows1)
        near_high, near_low = halves(jnp.concatenate([a[rows] for a in along], axis=0))
        far = []
        for q in range(2 * TERMS):
            x = yb_ref[q, 0] * z_ref[q * s.zrows + o, 0]
            for j in range(1, s.cz[2]):
                x += yb_ref[q, j] * z_ref[q * s.zrows + o, j]
            far.append(x)
        far_high, far_low = halves(jnp.concatenate(far, axis=0))
        g = dot(xah, near_high) + dot(xal, near_high) + dot(xah, near_low)
        g += dot(xbh, far_high) + dot(xbl, far_high) + dot(xbh, far_low)
        for shift, ref in enumerate(g_refs):
            ref[o] = g[shift * s.nx : (shift + 1) * s.nx]


def last_kernel(s, own_ref, low_ref, high_ref, *refs):
    g_refs, out_ref = refs[:-1], refs[-1]
    level = []
    for o in range(s.planes):
        x = g_refs[0][o]
        for ref in g_refs[1:]:
            x += ref[o]
        level.append(x)
    for z in range(s.nz):
        m = z // 2 + 1
        if z % 2 == 0:
            x = level[m]
        else:
            x = NEAR * (level[m] + level[m + 1]) + FAR * (level[m - 1] + level[m + 2])
        x += own_ref[z]
        if z < R:
            x += low_ref[z]
        if z >= s.nz - R:
            x += high_ref[z - (s.nz - R)]
        out_ref[z] = x


def call(kernel, name, operands, out_shapes, scalars=(), scratch=(), flops=0):
    def spec(i):
        return pl.BlockSpec(memory_space=pltpu.SMEM if i in scalars else pltpu.VMEM)

    moved = sum(x.size * x.dtype.itemsize for x in operands)
    moved += sum(int(np.prod(x.shape)) * x.dtype.itemsize for x in out_shapes)
    return pl.pallas_call(
        kernel,
        name=name,
        out_shape=out_shapes,
        in_specs=[spec(i) for i in range(len(operands))],
        out_specs=[pl.BlockSpec(memory_space=pltpu.VMEM)] * len(out_shapes),
        scratch_shapes=list(scratch),
        compiler_params=pltpu.CompilerParams(vmem_limit_bytes=VMEM_LIMIT),
        cost_estimate=pl.CostEstimate(flops=flops, bytes_accessed=moved, transcendentals=0),
    )(*operands)


def arrays(*shapes, dtype=F32):
    return [jax.ShapeDtypeStruct(shape, dtype) for shape in shapes]


def fetch(x, **shifts):
    names = tuple(shifts)
    sizes = [lax.axis_size(n) for n in names]
    pairs = []
    for here in np.ndindex(*sizes):
        there = [(h + shifts[n]) % size for h, n, size in zip(here, names, sizes)]
        pairs.append((int(np.ravel_multi_index(there, sizes)), int(np.ravel_multi_index(here, sizes))))
    return lax.ppermute(x, names if len(names) > 1 else names[0], pairs)


def shards(charges, widths, amplitudes):
    s = Sizes(*charges.shape, lax.axis_size("gz"), lax.axis_size("gx"), lax.axis_size("gy"))
    c = {k: jnp.asarray(v) for k, v in constants(s).items()}
    strips = (s.fine_tiles, s.nx, LANES)
    corners = (s.fine_tiles, 2 * R, LANES)
    share, to_low, to_high, corner_low, corner_high, edge_rows = call(
        functools.partial(share_kernel, s), "share",
        [charges, c["ry1"], c["rx1"]],
        arrays((s.tiles1, s.rows1, LANES), strips, strips, corners, corners, (s.nz, 2 * R, s.ny)),
        flops=10**8,
    )
    shares = [share] + [fetch(share, gz=b) for b in range(1, s.gz)]
    left, right = fetch(to_high, gy=-1), fetch(to_low, gy=1)
    x_shifts = (1,) if s.gx == 2 else (-1, 1)
    rows, lefts, rights = [], [], []
    for dx in x_shifts:
        rows.append(fetch(edge_rows, gx=dx))
        lefts.append(fetch(corner_high, gx=dx, gy=-1))
        rights.append(fetch(corner_low, gx=dx, gy=1))

    two = lambda *shape: arrays(shape, shape, dtype=BF16)
    taps, z_taps, y0h, y0l, y1h, y1l, y2h, y2l, xah, xal, xbh, xbl = call(
        functools.partial(matrix_kernel, s), "matrices",
        [widths, amplitudes] + [c[k] for k in "px1 px2 px3 rx3 py1 py2 py3 ry3 pz2 pz3 rz3".split()],
        arrays((16, LANES), (2 * TERMS * s.zrows, LANES))
        + two(2 * LANES, TERMS * s.ny) + two(LANES, TERMS * s.ny) + two(s.cy[2], 2 * TERMS * s.ny)
        + two(s.cx[0], TERMS * s.rows1) + two(s.cx[0], 2 * TERMS * s.rows2),
        scalars=(0, 1), flops=10**8,
    )
    brick = (s.nz, s.nx, s.ny)
    side = (R, s.nx, s.ny)
    near, near_down, near_up = call(
        functools.partial(near_kernel, s), "near",
        [taps, charges, rows[0], rows[-1], left, right, lefts[0], rights[0], lefts[-1], rights[-1], y0h, y0l],
        arrays(brick, side, side), scalars=(0,),
        scratch=[
            pltpu.VMEM((s.nz * s.ext, 2 * LANES), BF16), pltpu.VMEM((s.nz * s.ext, 2 * LANES), BF16),
            pltpu.VMEM((TERMS, s.nz, s.ext, s.ny), F32), pltpu.VMEM((TERMS,) + brick, F32),
        ],
        flops=3 * 10**9,
    )
    base = s.tiles_s * s.rows1
    size2 = s.tiles2 * s.rows2
    waves, to_low, to_high, coarse = call(
        functools.partial(depth_kernel, s), "depth",
        [taps] + shares + [c["ry2"], c["rx2"]],
        arrays((TERMS * s.planes, s.rows1, LANES), (base + size2, LANES), (base + size2, LANES), (size2, LANES)),
        scalars=(0,), scratch=[pltpu.VMEM((s.cz[1], s.rows1, LANES), F32)], flops=10**8,
    )
    coarses = [coarse]
    for b in range(1, s.gy):
        coarses.append(fetch({1: to_low, s.gy - 1: to_high}.get(b, coarse), gy=b))
    near_low, near_high = fetch(near_up, gz=-1), fetch(near_down, gz=1)
    parts = call(
        functools.partial(along_kernel, s), "along",
        [z_taps, waves] + coarses + [y1h, y1l, y2h, y2l, xah, xal, xbh, xbl],
        arrays(*[(s.planes, s.nx, s.ny)] * s.gx), scalars=(0,),
        scratch=[pltpu.VMEM((2 * TERMS, s.cz[2], s.rows2, s.ny), F32)], flops=10**9,
    )
    parts = [parts[0]] + [fetch(parts[dx], gx=-dx) for dx in range(1, s.gx)]
    (out,) = call(
        functools.partial(last_kernel, s), "last",
        [near, near_low, near_high] + list(parts), arrays(brick), flops=10**7,
    )
    return out


def solution(mesh):
    placed = (P("gz", "gx", "gy"), P(), P())
    return jax.shard_map(
        shards, mesh=mesh, in_specs=placed, out_specs=P("gz", "gx", "gy"), check_vma=False
    )
```

profile of v0, /device:TPU:0, one launch (start us, length us, event | category | flops | bytes accessed | tf_op | source)
XLA Modules:
  0.0 59.0 jit_solution(10160897196467204924)
XLA Ops:
  0.0 0.7 %copy-done.10 = f32[40,64]{1,0:T(8,128)S(1)} copy-done((f32[40,64]{1,0:T(8,128)S(1)}, f32[40,64]{1,0:T(8,128)}, u32[]{:S(2)}) %copy-start.10) | copy-done | bytes 10264
  0.7 1.0 %copy-done = f32[16,64,128]{2,1,0:T(8,128)S(1)} copy-done((f32[16,64,128]{2,1,0:T(8,128)S(1)}, f32[16,64,128]{2,1,0:T(8,128)}, u32[]{:S(2)}) %copy-start) | copy-done | bytes 524312
  1.8 0.8 %copy-done.5 = f32[128,128]{1,0:T(8,128)S(1)} copy-done((f32[128,128]{1,0:T(8,128)S(1)}, f32[128,128]{1,0:T(8,128)}, u32[]{:S(2)}) %copy-start.5) | copy-done | bytes 65560
  2.6 0.0 copy-start.8
  2.6 0.0 copy-start.9
  2.6 0.0 copy-start.12
  2.7 0.0 copy-start.13
  2.7 0.0 copy-start.14
  2.7 0.0 copy-start.15
  2.7 0.0 copy-start.16
  2.7 0.0 copy-start.17
  2.7 0.7 %share.1 = (f32[6,40,128]{2,1,0:T(8,128)S(1)}, f32[1,64,128]{2,1,0:T(8,128)S(1)}, f32[1,64,128]{2,1,0:T(8,128)S(1)}, f32[1,16,128]{2,1,0:T(8,128)S(1)}, f32[1,16...) custom-call(f32[16,64,128]{2,1,0:T(8,128)S(1)} %copy-done, f32[128,128]{1,0:T(8,128)S(1)} %copy-done.5, f32[40,64]{1,0:T(8,128)S(1)} %copy-done.10), custom_call_target="tpu_custom_call" | custom-call | flops 100000000 | bytes 935936 | tf_op jit(solution)/shard_map/share/pallas_call | solution.py:507
  3.4 0.0 copy-start.4
  3.4 0.0 copy-start.11
  3.4 5.1 %collective-permute-start.7 = (f32[6,40,128]{2,1,0:T(8,128)S(1)}, f32[6,40,128]{2,1,0:T(8,128)S(1)}, u32[]{:S(2)}, u32[]{:S(2)}) collective-permute-start(f32[6,40,128]{2,1,0:T(8,128)S(1)} %get-tuple-element.44.refs_0_), channel_id=1, source_target_pairs={{1,0},{2,1},{3,2},{0,3},{5,4},{6,5},{7,6},{4,7},{9,8},{10,9},{11,1... | collective-permute-start | bytes 368648 | tf_op jit(solution)/shard_map/ppermute | solution.py:530
  8.5 0.0 collective-permute-start.8
  8.5 1.0 %collective-permute-start.9 = (f32[6,40,128]{2,1,0:T(8,128)S(1)}, f32[6,40,128]{2,1,0:T(8,128)S(1)}, u32[]{:S(2)}, u32[]{:S(2)}) collective-permute-start(f32[6,40,128]{2,1,0:T(8,128)S(1)} %get-tuple-element.44.refs_0_), channel_id=1, source_target_pairs={{3,0},{0,1},{1,2},{2,3},{7,4},{4,5},{5,6},{6,7},{11,8},{8,9},{9,10... | collective-permute-start | bytes 368648 | tf_op jit(solution)/shard_map/ppermute | solution.py:530
  9.5 0.0 copy-done.6
  9.6 3.0 %matrices.1 = (f32[16,128]{1,0:T(8,128)S(1)}, f32[96,128]{1,0:T(8,128)S(1)}, bf16[256,384]{1,0:T(8,128)(2,1)S(1)}, bf16[256,384]{1,0:T(8,128)(2,1)S(1)}, bf16[12...) custom-call(f32[4,3]{1,0:T(4,128)S(1)} %copy-done.16, ...), custom_call_target="tpu_custom_call" | custom-call | flops 100000000 | bytes 1502304 | tf_op jit(solution)/shard_map/matrices/pallas_call | solution.py:507
  12.7 0.0 collective-permute-done.7.refs_1_
  12.7 6.4 %collective-permute-done.8.refs_2_ = f32[6,40,128]{2,1,0:T(8,128)S(1)} collective-permute-done((f32[6,40,128]{2,1,0:T(8,128)S(1)}, f32[6,40,128]{2,1,0:T(8,128)S(1)}, u32[]{:S(2)}, u32[]{:S(2)}) %collective-permute-start.8) | collective-permute-done | bytes 122912 | tf_op jit(solution)/shard_map/ppermute | solution.py:530
  19.1 0.0 collective-permute-done.9.refs_3_
  19.1 1.6 %depth.1 = (f32[33,40,128]{2,1,0:T(8,128)S(1)}, f32[240,128]{1,0:T(8,128)S(1)}, f32[240,128]{1,0:T(8,128)S(1)}, f32[120,128]{1,0:T(8,128)S(1)}) custom-call(f32[16,128]{1,0:T(8,128)S(1)} %get-tuple-element.32.tap_ref, f32[6,40,128]{2,1,0:T(8,128)S(1)} %get-tuple-element.44.refs_0_, f32[6,40,128]{2,1,0:T(8,128)S(1)} %collective-permute-done.7.refs_1_, ...), custom_call_target="tpu_custom_call" | custom-call | flops 100000000 | bytes 1552128 | tf_op jit(solution)/shard_map/depth/pallas_call | solution.py:507
  20.8 2.5 %collective-permute-start.10 = (f32[240,128]{1,0:T(8,128)S(1)}, f32[240,128]{1,0:T(8,128)S(1)}, u32[]{:S(2)}, u32[]{:S(2)}) collective-permute-start(f32[240,128]{1,0:T(8,128)S(1)} %get-tuple-element.47), channel_id=1, source_target_pairs={{4,0},{8,4},{12,8},{0,12},{5,1},{9,5},{13,9},{1,13},{6,2},{10,6},{... | collective-permute-start | bytes 368648 | tf_op jit(solution)/shard_map/ppermute | solution.py:530
  23.3 0.0 collective-permute-start.12
  23.3 1.1 %collective-permute-start.11 = (f32[120,128]{1,0:T(8,128)S(1)}, f32[120,128]{1,0:T(8,128)S(1)}, u32[]{:S(2)}, u32[]{:S(2)}) collective-permute-start(f32[120,128]{1,0:T(8,128)S(1)} %get-tuple-element.46.refs_0_), channel_id=1, source_target_pairs={{8,0},{12,4},{0,8},{4,12},{9,1},{13,5},{1,9},{5,13},{10,2},{14,6},... | collective-permute-start | bytes 184328 | tf_op jit(solution)/shard_map/ppermute | solution.py:530
  24.4 0.0 collective-permute-start
  24.4 2.4 %collective-permute-start.1 = (f32[1,64,128]{2,1,0:T(8,128)S(1)}, f32[1,64,128]{2,1,0:T(8,128)S(1)}, u32[]{:S(2)}, u32[]{:S(2)}) collective-permute-start(f32[1,64,128]{2,1,0:T(8,128)S(1)} %get-tuple-element.34), channel_id=1, source_target_pairs={{12,0},{0,4},{4,8},{8,12},{13,1},{1,5},{5,9},{9,13},{14,2},{2,6},{... | collective-permute-start | bytes 98312 | tf_op jit(solution)/shard_map/ppermute | solution.py:530
  26.8 3.5 %collective-permute-done.11.refs_2_ = f32[120,128]{1,0:T(8,128)S(1)} collective-permute-done((f32[120,128]{1,0:T(8,128)S(1)}, f32[120,128]{1,0:T(8,128)S(1)}, u32[]{:S(2)}, u32[]{:S(2)}) %collective-permute-start.11) | collective-permute-done | bytes 61472 | tf_op jit(solution)/shard_map/ppermute | solution.py:530
  30.2 0.5 collective-permute-start.2
  30.7 0.0 collective-permute-done.10.refs_1_
  30.7 0.0 collective-permute-start.3
  30.7 0.0 collective-permute-done.12.refs_3_
  30.7 2.6 %collective-permute-start.4 = (f32[1,16,128]{2,1,0:T(8,128)S(1)}, f32[1,16,128]{2,1,0:T(8,128)S(1)}, u32[]{:S(2)}, u32[]{:S(2)}) collective-permute-start(f32[1,16,128]{2,1,0:T(8,128)S(1)} %get-tuple-element.37), channel_id=1, source_target_pairs={{20,0},{24,4},{28,8},{16,12},{4,16},{8,20},{12,24},{0,28},{21,1},{... | collective-permute-start | bytes 24584 | tf_op jit(solution)/shard_map/ppermute | solution.py:530
  33.4 3.9 %along.1 = (f32[11,64,128]{2,1,0:T(8,128)S(1)}, f32[11,64,128]{2,1,0:T(8,128)S(1)}) custom-call(f32[96,128]{1,0:T(8,128)S(1)} %get-tuple-element.43.z_ref, f32[33,40,128]{2,1,0:T(8,128)S(1)} %get-tuple-element.45.w_ref, f32[120,128]{1,0:T(8,128)S(1)} %get-tuple-element.46.refs_0_, f32[240,128]{1,0:T(8,128)S(1)} %collective-permute-done.10.refs_1_, ...), custom_call_target="tpu_custom_call" | custom-call | flops 1000000000 | bytes 2539520 | tf_op jit(solution)/shard_map/along/pallas_call | solution.py:507
  37.3 0.0 collective-permute-done.3.c_lo_l.c_hi_l
  37.3 0.1 collective-permute-start.13
  37.4 0.0 collective-permute-done.4.c_lo_r.c_hi_r
  37.4 0.0 collective-permute-done.1.sl_ref
  37.4 0.0 collective-permute-done.2.sr_ref
  37.4 0.0 collective-permute-done.xlo_ref.xhi_ref
  37.4 5.3 %near.1 = (f32[16,64,128]{2,1,0:T(8,128)S(1)}, f32[8,64,128]{2,1,0:T(8,128)S(1)}, f32[8,64,128]{2,1,0:T(8,128)S(1)}) custom-call(f32[16,128]{1,0:T(8,128)S(1)} %get-tuple-element.32.tap_ref, f32[16,64,128]{2,1,0:T(8,128)S(1)} %copy-done.1, f32[16,16,128]{2,1,0:T(8,128)S(1)} %collective-permute-done.xlo_ref.xhi_ref, ...), custom_call_target="tpu_custom_call" | custom-call | flops 3000000000 | bytes 2334720 | tf_op jit(solution)/shard_map/near/pallas_call | solution.py:507
  42.7 0.5 collective-permute-start.5
  43.3 3.3 %collective-permute-start.6 = (f32[8,64,128]{2,1,0:T(8,128)S(1)}, f32[8,64,128]{2,1,0:T(8,128)S(1)}, u32[]{:S(2)}, u32[]{:S(2)}) collective-permute-start(f32[8,64,128]{2,1,0:T(8,128)S(1)} %get-tuple-element.42), channel_id=1, source_target_pairs={{1,0},{2,1},{3,2},{0,3},{5,4},{6,5},{7,6},{4,7},{9,8},{10,9},{11,1... | collective-permute-start | bytes 786440 | tf_op jit(solution)/shard_map/ppermute | solution.py:530
  46.6 7.1 %collective-permute-done.5.low_ref = f32[8,64,128]{2,1,0:T(8,128)S(1)} collective-permute-done((f32[8,64,128]{2,1,0:T(8,128)S(1)}, f32[8,64,128]{2,1,0:T(8,128)S(1)}, u32[]{:S(2)}, u32[]{:S(2)}) %collective-permute-start.5) | collective-permute-done | bytes 262176 | tf_op jit(solution)/shard_map/ppermute | solution.py:530
  53.7 4.3 %collective-permute-done.6.high_ref = f32[8,64,128]{2,1,0:T(8,128)S(1)} collective-permute-done((f32[8,64,128]{2,1,0:T(8,128)S(1)}, f32[8,64,128]{2,1,0:T(8,128)S(1)}, u32[]{:S(2)}, u32[]{:S(2)}) %collective-permute-start.6) | collective-permute-done | bytes 262176 | tf_op jit(solution)/shard_map/ppermute | solution.py:530
  58.0 0.0 collective-permute-done.13.refs_1_
  58.0 0.9 %last.1 = f32[16,64,128]{2,1,0:T(8,128)} custom-call(f32[16,64,128]{2,1,0:T(8,128)S(1)} %get-tuple-element.40.own_ref, f32[8,64,128]{2,1,0:T(8,128)S(1)} %collective-permute-done.5.low_ref, f32[8,64,128]{2,1,0:T(8,128)S(1)} %collective-permute-done.6.high_ref, f32[11,64,128]{2,1,0:T(8,128)S(1)} %get-tuple-element.57.refs_0_, ...), custom_call_target="tpu_custom_call" | custom-call | flops 10000000 | bytes 2293760 | tf_op jit(solution)/shard_map/last/pallas_call | solution.py:507
  (22 shorter events, 0.0 us)
Async XLA Ops:
  0.0 0.7 %copy-start.10 = (f32[40,64]{1,0:T(8,128)S(1)}, f32[40,64]{1,0:T(8,128)}, u32[]{:S(2)}) copy-start(f32[40,64]{1,0:T(8,128)} %constant.29.clone.rx1_ref) | copy-start | bytes 30724
  0.7 1.0 %copy-start = (f32[16,64,128]{2,1,0:T(8,128)S(1)}, f32[16,64,128]{2,1,0:T(8,128)}, u32[]{:S(2)}) copy-start(f32[16,64,128]{2,1,0:T(8,128)} %b_ref.3) | copy-start | bytes 1572868
  1.8 0.8 %copy-start.5 = (f32[128,128]{1,0:T(8,128)S(1)}, f32[128,128]{1,0:T(8,128)}, u32[]{:S(2)}) copy-start(f32[128,128]{1,0:T(8,128)} %constant.28.clone.ry1_ref) | copy-start | bytes 196612
  2.6 6.9 %copy-start.2 = (f32[128,64]{1,0:T(8,128)S(1)}, f32[128,64]{1,0:T(8,128)}, u32[]{:S(2)}) copy-start(f32[128,64]{1,0:T(8,128)} %constant.32.clone.px1.ry3) | copy-start | bytes 98308
  2.6 6.9 %copy-start.3 = (f32[256,128]{1,0:T(8,128)S(1)}, f32[256,128]{1,0:T(8,128)}, u32[]{:S(2)}) copy-start(f32[256,128]{1,0:T(8,128)} %constant.36.clone.py1) | copy-start | bytes 393220
  2.6 6.9 %copy-start.6 = (f32[128,32]{1,0:T(8,128)S(1)}, f32[128,32]{1,0:T(8,128)}, u32[]{:S(2)}) copy-start(f32[128,32]{1,0:T(8,128)} %constant.33.clone.px2) | copy-start | bytes 49156
  2.6 6.9 %copy-start.7 = (f32[128,16]{1,0:T(8,128)S(1)}, f32[128,16]{1,0:T(8,128)}, u32[]{:S(2)}) copy-start(f32[128,16]{1,0:T(8,128)} %constant.34.clone.px3) | copy-start | bytes 24580
  2.6 6.9 %copy-start.8 = (f32[128,128]{1,0:T(8,128)S(1)}, f32[128,128]{1,0:T(8,128)}, u32[]{:S(2)}) copy-start(f32[128,128]{1,0:T(8,128)} %constant.37.clone.py2) | copy-start | bytes 196612
  2.6 6.9 %copy-start.9 = (f32[64,128]{1,0:T(8,128)S(1)}, f32[64,128]{1,0:T(8,128)}, u32[]{:S(2)}) copy-start(f32[64,128]{1,0:T(8,128)} %constant.38.clone.py3) | copy-start | bytes 98308
  2.6 6.9 %copy-start.12 = (f32[16,24]{1,0:T(8,128)S(1)}, f32[16,24]{1,0:T(8,128)}, u32[]{:S(2)}) copy-start(f32[16,24]{1,0:T(8,128)} %constant.35.clone.rx3) | copy-start | bytes 4612
  2.7 6.9 %copy-start.13 = (f32[16,16]{1,0:T(8,128)S(1)}, f32[16,16]{1,0:T(8,128)}, u32[]{:S(2)}) copy-start(f32[16,16]{1,0:T(8,128)} %constant.39.clone.pz2) | copy-start | bytes 3076
  2.7 6.9 %copy-start.14 = (f32[16,8]{1,0:T(8,128)S(1)}, f32[16,8]{1,0:T(8,128)}, u32[]{:S(2)}) copy-start(f32[16,8]{1,0:T(8,128)} %constant.40.clone.pz3) | copy-start | bytes 1540
  2.7 6.9 %copy-start.15 = (f32[8,128]{1,0:T(8,128)S(1)}, f32[8,128]{1,0:T(8,128)}, u32[]{:S(2)}) copy-start(f32[8,128]{1,0:T(8,128)} %constant.41.clone.rz3) | copy-start | bytes 12292
  2.7 6.9 %copy-start.16 = (f32[4,3]{1,0:T(4,128)S(1)}, f32[4,3]{1,0:T(4,128)}, u32[]{:S(2)}) copy-start(f32[4,3]{1,0:T(4,128)} %w_ref.1) | copy-start | bytes 148
  2.7 6.9 %copy-start.17 = (f32[4,3]{1,0:T(4,128)S(1)}, f32[4,3]{1,0:T(4,128)}, u32[]{:S(2)}) copy-start(f32[4,3]{1,0:T(4,128)} %a_ref.1) | copy-start | bytes 148
  3.4 15.7 %copy-start.4 = (f32[128,128]{1,0:T(8,128)S(1)}, f32[128,128]{1,0:T(8,128)}, u32[]{:S(2)}) copy-start(f32[128,128]{1,0:T(8,128)} %constant.30.clone.refs_4_) | copy-start | bytes 196612
  3.4 15.7 %copy-start.11 = (f32[24,40]{1,0:T(8,128)S(1)}, f32[24,40]{1,0:T(8,128)}, u32[]{:S(2)}) copy-start(f32[24,40]{1,0:T(8,128)} %constant.31.clone.refs_5_) | copy-start | bytes 11524
  3.4 9.3 %collective-permute-start.7 = (f32[6,40,128]{2,1,0:T(8,128)S(1)}, f32[6,40,128]{2,1,0:T(8,128)S(1)}, u32[]{:S(2)}, u32[]{:S(2)}) collective-permute-start(f32[6,40,128]{2,1,0:T(8,128)S(1)} %get-tuple-element.44.refs_0_), channel_id=1, source_target_pairs={{1,0},{2,1},{3,2},{0,3},{5,4},{6,5},{7,6},{4,7},{9,8},{10,9},{11,1... | collective-permute-start | bytes 368648 | tf_op jit(solution)/shard_map/ppermute | solution.py:530
  8.5 10.6 %collective-permute-start.8 = (f32[6,40,128]{2,1,0:T(8,128)S(1)}, f32[6,40,128]{2,1,0:T(8,128)S(1)}, u32[]{:S(2)}, u32[]{:S(2)}) collective-permute-start(f32[6,40,128]{2,1,0:T(8,128)S(1)} %get-tuple-element.44.refs_0_), channel_id=1, source_target_pairs={{2,0},{3,1},{0,2},{1,3},{6,4},{7,5},{4,6},{5,7},{10,8},{11,9},{8,1... | collective-permute-start | bytes 368648 | tf_op jit(solution)/shard_map/ppermute | solution.py:530
  8.5 10.6 %collective-permute-start.9 = (f32[6,40,128]{2,1,0:T(8,128)S(1)}, f32[6,40,128]{2,1,0:T(8,128)S(1)}, u32[]{:S(2)}, u32[]{:S(2)}) collective-permute-start(f32[6,40,128]{2,1,0:T(8,128)S(1)} %get-tuple-element.44.refs_0_), channel_id=1, source_target_pairs={{3,0},{0,1},{1,2},{2,3},{7,4},{4,5},{5,6},{6,7},{11,8},{8,9},{9,10... | collective-permute-start | bytes 368648 | tf_op jit(solution)/shard_map/ppermute | solution.py:530
  20.8 10.0 %collective-permute-start.10 = (f32[240,128]{1,0:T(8,128)S(1)}, f32[240,128]{1,0:T(8,128)S(1)}, u32[]{:S(2)}, u32[]{:S(2)}) collective-permute-start(f32[240,128]{1,0:T(8,128)S(1)} %get-tuple-element.47), channel_id=1, source_target_pairs={{4,0},{8,4},{12,8},{0,12},{5,1},{9,5},{13,9},{1,13},{6,2},{10,6},{... | collective-permute-start | bytes 368648 | tf_op jit(solution)/shard_map/ppermute | solution.py:530
  23.3 7.5 %collective-permute-start.12 = (f32[240,128]{1,0:T(8,128)S(1)}, f32[240,128]{1,0:T(8,128)S(1)}, u32[]{:S(2)}, u32[]{:S(2)}) collective-permute-start(f32[240,128]{1,0:T(8,128)S(1)} %get-tuple-element.48), channel_id=1, source_target_pairs={{12,0},{0,4},{4,8},{8,12},{13,1},{1,5},{5,9},{9,13},{14,2},{2,6},{... | collective-permute-start | bytes 368648 | tf_op jit(solution)/shard_map/ppermute | solution.py:530
  23.3 6.9 %collective-permute-start.11 = (f32[120,128]{1,0:T(8,128)S(1)}, f32[120,128]{1,0:T(8,128)S(1)}, u32[]{:S(2)}, u32[]{:S(2)}) collective-permute-start(f32[120,128]{1,0:T(8,128)S(1)} %get-tuple-element.46.refs_0_), channel_id=1, source_target_pairs={{8,0},{12,4},{0,8},{4,12},{9,1},{13,5},{1,9},{5,13},{10,2},{14,6},... | collective-permute-start | bytes 184328 | tf_op jit(solution)/shard_map/ppermute | solution.py:530
  24.4 13.0 %collective-permute-start = (f32[16,16,128]{2,1,0:T(8,128)S(1)}, f32[16,16,128]{2,1,0:T(8,128)S(1)}, u32[]{:S(2)}, u32[]{:S(2)}) collective-permute-start(f32[16,16,128]{2,1,0:T(8,128)S(1)} %get-tuple-element.33), channel_id=1, source_target_pairs={{16,0},{0,16},{17,1},{1,17},{18,2},{2,18},{19,3},{3,19},{20,4},{4,... | collective-permute-start | bytes 393224 | tf_op jit(solution)/shard_map/ppermute | solution.py:530
  24.4 13.0 %collective-permute-start.1 = (f32[1,64,128]{2,1,0:T(8,128)S(1)}, f32[1,64,128]{2,1,0:T(8,128)S(1)}, u32[]{:S(2)}, u32[]{:S(2)}) collective-permute-start(f32[1,64,128]{2,1,0:T(8,128)S(1)} %get-tuple-element.34), channel_id=1, source_target_pairs={{12,0},{0,4},{4,8},{8,12},{13,1},{1,5},{5,9},{9,13},{14,2},{2,6},{... | collective-permute-start | bytes 98312 | tf_op jit(solution)/shard_map/ppermute | solution.py:530
  30.2 7.2 %collective-permute-start.2 = (f32[1,64,128]{2,1,0:T(8,128)S(1)}, f32[1,64,128]{2,1,0:T(8,128)S(1)}, u32[]{:S(2)}, u32[]{:S(2)}) collective-permute-start(f32[1,64,128]{2,1,0:T(8,128)S(1)} %get-tuple-element.35), channel_id=1, source_target_pairs={{4,0},{8,4},{12,8},{0,12},{5,1},{9,5},{13,9},{1,13},{6,2},{10,6},{... | collective-permute-start | bytes 98312 | tf_op jit(solution)/shard_map/ppermute | solution.py:530
  30.7 6.6 %collective-permute-start.3 = (f32[1,16,128]{2,1,0:T(8,128)S(1)}, f32[1,16,128]{2,1,0:T(8,128)S(1)}, u32[]{:S(2)}, u32[]{:S(2)}) collective-permute-start(f32[1,16,128]{2,1,0:T(8,128)S(1)} %get-tuple-element.36), channel_id=1, source_target_pairs={{28,0},{16,4},{20,8},{24,12},{12,16},{0,20},{4,24},{8,28},{29,1},{... | collective-permute-start | bytes 24584 | tf_op jit(solution)/shard_map/ppermute | solution.py:530
  30.7 6.6 %collective-permute-start.4 = (f32[1,16,128]{2,1,0:T(8,128)S(1)}, f32[1,16,128]{2,1,0:T(8,128)S(1)}, u32[]{:S(2)}, u32[]{:S(2)}) collective-permute-start(f32[1,16,128]{2,1,0:T(8,128)S(1)} %get-tuple-element.37), channel_id=1, source_target_pairs={{20,0},{24,4},{28,8},{16,12},{4,16},{8,20},{12,24},{0,28},{21,1},{... | collective-permute-start | bytes 24584 | tf_op jit(solution)/shard_map/ppermute | solution.py:530
  33.4 4.0 %copy-start.1 = (f32[16,64,128]{2,1,0:T(8,128)S(1)}, f32[16,64,128]{2,1,0:T(8,128)}, u32[]{:S(2)}) copy-start(f32[16,64,128]{2,1,0:T(8,128)} %b_ref.3) | copy-start | bytes 1572868
  37.3 20.7 %collective-permute-start.13 = (f32[11,64,128]{2,1,0:T(8,128)S(1)}, f32[11,64,128]{2,1,0:T(8,128)S(1)}, u32[]{:S(2)}, u32[]{:S(2)}) collective-permute-start(f32[11,64,128]{2,1,0:T(8,128)S(1)} %get-tuple-element.58), channel_id=1, source_target_pairs={{16,0},{0,16},{17,1},{1,17},{18,2},{2,18},{19,3},{3,19},{20,4},{4,... | collective-permute-start | bytes 1081352 | tf_op jit(solution)/shard_map/ppermute | solution.py:530
  42.7 11.0 %collective-permute-start.5 = (f32[8,64,128]{2,1,0:T(8,128)S(1)}, f32[8,64,128]{2,1,0:T(8,128)S(1)}, u32[]{:S(2)}, u32[]{:S(2)}) collective-permute-start(f32[8,64,128]{2,1,0:T(8,128)S(1)} %get-tuple-element.41), channel_id=1, source_target_pairs={{3,0},{0,1},{1,2},{2,3},{7,4},{4,5},{5,6},{6,7},{11,8},{8,9},{9,10... | collective-permute-start | bytes 786440 | tf_op jit(solution)/shard_map/ppermute | solution.py:530
  43.3 14.8 %collective-permute-start.6 = (f32[8,64,128]{2,1,0:T(8,128)S(1)}, f32[8,64,128]{2,1,0:T(8,128)S(1)}, u32[]{:S(2)}, u32[]{:S(2)}) collective-permute-start(f32[8,64,128]{2,1,0:T(8,128)S(1)} %get-tuple-element.42), channel_id=1, source_target_pairs={{1,0},{2,1},{3,2},{0,3},{5,4},{6,5},{7,6},{4,7},{9,8},{10,9},{11,1... | collective-permute-start | bytes 786440 | tf_op jit(solution)/shard_map/ppermute | solution.py:530
where the time goes:
time: 59.2 us; the launch traced here: 59 us
  waiting for transfers between devices  21.3 us (36%)
  starting transfers between devices  19.2 us (32%)
  Pallas kernels  15.5 us (26%)
  local copies, waits for them, and re-layouts  2.69 us (5%)
    ppermute x14, waiting for transfers between devices, fetch(): return lax.ppermute(x, names if len(names) > 1 else names[0], pairs)  21.3 us
    ppermute x14, starting transfers between devices, fetch(): return lax.ppermute(x, names if len(names) > 1 else names[0], pairs)  19.2 us
    pallas_call x6, Pallas kernels, call(): pl.pallas_call(kernel, name=name, out_shape=out_shapes, in_specs=[spec(i)...  15.5 us
    unnamed x36, local copies, waits for them, and re-layouts  2.69 us
  transfers between devices with their start and end apart: 14, of which 4 were waited for; matrix products, arithmetic and copies ran while one was open for 0% of the time, Pallas kernels for 21%

commit v1 on v0

--- a/solution.py
+++ b/solution.py
@@ -82,8 +82,6 @@
 
 def constants(s):
     c = {}
-    c["ry1"] = padded(restrict_open(0, s.ny, -1, s.wide1).T, s.ny, LANES)
-    c["rx1"] = padded(restrict_open(0, s.nx, -1, s.x1 + 3), up8(s.rows1), s.nx)
     c["ry2"] = padded(restrict_open(-1, s.wide1, -2, s.wide2).T, LANES, LANES)
     c["rx2"] = padded(restrict_open(-1, s.x1 + 3, -2, s.x2 + 5), s.rows2, s.rows1)
 
@@ -169,7 +167,15 @@
     return jnp.where((lane >= shift) | (lane < shift + wide - LANES), x, 0.0)
 
 
-def share_kernel(s, b_ref, ry1_ref, rx1_ref, m_ref, sl_ref, sr_ref, cl_ref, cr_ref, xr_ref):
+def open_restriction(shape, in_dim, first_out, n_out):
+    i = lax.broadcasted_iota(jnp.int32, shape, in_dim)
+    o = lax.broadcasted_iota(jnp.int32, shape, 1 - in_dim)
+    d = jnp.abs(i - 2 * (o + first_out))
+    w = jnp.where(d == 0, 1.0, jnp.where(d == 1, NEAR, jnp.where(d == 3, FAR, 0.0)))
+    return jnp.where(o < n_out, w, 0.0).astype(BF16)
+
+
+def share_kernel(s, b_ref, m_ref, xr_ref):
     b = [b_ref[z] for z in range(s.nz)]
     planes = []
     for k in range(-1, s.z1 + 2):
@@ -180,8 +186,8 @@
                 out = term if out is None else out + term
         planes.append(out)
     high, low = halves(jnp.concatenate(planes, axis=0))
-    ry1 = ry1_ref[...].astype(BF16)
-    rx1 = rx1_ref[...].astype(BF16)
+    ry1 = open_restriction((s.ny, LANES), 0, -1, s.wide1)
+    rx1 = open_restriction((s.rows1, s.nx), 1, -1, s.x1 + 3)
     along = dot(high, ry1) + dot(low, ry1)
     shares = []
     for k in range(s.planes):
@@ -189,73 +195,62 @@
         shares.append(dot(rx1, high) + dot(rx1, low))
     for t, x in enumerate(packed(shares, s.wide1, s.tiles1)):
         m_ref[t] = x
-    lane = lanes_of((s.nx, LANES))
-    group = LANES // R
-    for t in range(s.fine_tiles):
-        left = right = None
-        for g in range(min(group, s.nz - t * group)):
-            x = b[t * group + g]
-            first = turn(x, R * ((g + 1) % group))
-            last = turn(x, R * g + R - s.ny)
-            at_first = (lane >= R * ((g + 1) % group)) & (lane < R * ((g + 1) % group) + R)
-            at_last = (lane >= R * g) & (lane < R * g + R)
-            left = jnp.where(at_first, first, 0.0 if left is None else left)
-            right = jnp.where(at_last, last, 0.0 if right is None else right)
-        sl_ref[t] = left
-        sr_ref[t] = right
-        cl_ref[t, 0:R] = left[0:R]
-        cl_ref[t, R : 2 * R] = left[s.nx - R :]
-        cr_ref[t, 0:R] = right[0:R]
-        cr_ref[t, R : 2 * R] = right[s.nx - R :]
     for z in range(s.nz):
         xr_ref[z, 0:R] = b[z][0:R]
         xr_ref[z, R : 2 * R] = b[z][s.nx - R :]
 
 
-def matrix_kernel(s, w_ref, a_ref, px1, px2, px3, rx3, py1, py2, py3, ry3, pz2, pz3, rz3,
-                  tap_ref, z_ref, y0h_ref, y0l_ref, y1h_ref, y1l_ref, y2h_ref, y2l_ref,
-                  xah_ref, xal_ref, xbh_ref, xbl_ref):
-    def spread(level, t):
-        w = jnp.full((8, LANES), w_ref[level, t], F32)
-        return (-0.5 / (w * w))[0:1, 0:1]
-
-    def bell(c, d):
-        d = jnp.abs(d)
-        return jnp.where(d <= R, jnp.exp(c * d * d), 0.0)
-
-    def scale(c, count=None):
-        n = lanes_of((1, LANES)).astype(F32)
-        if count is None:
-            d, valid = n - R, n <= 2 * R
-        else:
-            d, valid = jnp.minimum(n, count - n), n < count
-        return 1.0 / jnp.sqrt(jnp.sum(jnp.where(valid, jnp.exp(2.0 * c * d * d), 0.0), axis=1, keepdims=True))
-
-    coef = [[spread(l, t) for t in range(TERMS)] for l in range(4)]
-    unit = [[scale(coef[l][t]) for t in range(TERMS)] for l in range(3)]
-
-    def rows_of(shape):
-        return lax.broadcasted_iota(jnp.int32, shape, 0)
-
-    def circle(n, shape, first_row, first_lane, c, u):
-        d = ((rows_of(shape) + first_row) - (lanes_of(shape) + first_lane)) & (n - 1)
-        d = d.astype(F32)
-        return (bell(c, d) + bell(c, n - d)) * u
-
-    def full_circle(n, shape, c, u):
-        d = ((rows_of(shape) - lanes_of(shape)) & (n - 1)).astype(F32)
-        d = jnp.minimum(d, n - d)
-        return jnp.exp(c * d * d) * u
-
-    def put(high_ref, low_ref, at, x):
-        high, low = halves(x)
-        high_ref[:, at : at + x.shape[1]] = high
-        low_ref[:, at : at + x.shape[1]] = low
-
-    def by_term(shape, wide, values):
-        t = lanes_of(shape)
-        return jnp.where(t < wide, values[0], jnp.where(t < 2 * wide, values[1], values[2]))
-
+def extended(b_ref, lo_ref, hi_ref, z):
+    return jnp.concatenate([lo_ref[z, R : 2 * R], b_ref[z], hi_ref[z, 0:R]], axis=0)
+
+
+def strip_kernel(s, b_ref, lo_ref, hi_ref, first_ref, last_ref):
+    lane = lanes_of((s.ext, LANES))
+    group = LANES // R
+    for t in range(s.fine_tiles):
+        first = last = jnp.zeros((s.ext, LANES), F32)
+        for g in range(min(group, s.nz - t * group)):
+            x = extended(b_ref, lo_ref, hi_ref, t * group + g)
+            at = R * ((g + 1) % group)
+            first = jnp.where((lane >= at) & (lane < at + R), turn(x, at), first)
+            at = R * g
+            last = jnp.where((lane >= at) & (lane < at + R), turn(x, at + R - s.ny), last)
+        first_ref[t] = first
+        last_ref[t] = last
+
+
+def rows_of(shape):
+    return lax.broadcasted_iota(jnp.int32, shape, 0)
+
+
+def spread(w_ref, level, t):
+    w = jnp.full((8, LANES), w_ref[level, t], F32)
+    return (-0.5 / (w * w))[0:1, 0:1]
+
+
+def bell(c, d):
+    d = jnp.abs(d)
+    return jnp.where(d <= R, jnp.exp(c * d * d), 0.0)
+
+
+def scale(c, count=None):
+    n = lanes_of((1, LANES)).astype(F32)
+    if count is None:
+        d, valid = n - R, n <= 2 * R
+    else:
+        d, valid = jnp.minimum(n, count - n), n < count
+    return 1.0 / jnp.sqrt(jnp.sum(jnp.where(valid, jnp.exp(2.0 * c * d * d), 0.0), axis=1, keepdims=True))
+
+
+def put(high_ref, low_ref, at, x):
+    high, low = halves(x)
+    high_ref[:, at : at + x.shape[1]] = high
+    low_ref[:, at : at + x.shape[1]] = low
+
+
+def tap_kernel(s, w_ref, a_ref, tap_ref, y0h_ref, y0l_ref):
+    coef = [[spread(w_ref, l, t) for t in range(TERMS)] for l in range(2)]
+    unit = [[scale(coef[l][t]) for t in range(TERMS)] for l in range(2)]
     d = lanes_of((1, LANES)).astype(F32)
     for t in range(TERMS):
         g0 = bell(coef[0][t], d) * unit[0][t]
@@ -269,6 +264,27 @@
         cell = jnp.where(i < s.ny, i, jnp.where(i < s.ny + R, i - s.ny - R, i - R))
         g = bell(coef[0][t], (cell - lanes_of(shape)).astype(F32)) * unit[0][t]
         put(y0h_ref, y0l_ref, t * s.ny, jnp.where(i < s.ny + 2 * R, g, 0.0))
+
+
+def matrix_kernel(s, w_ref, a_ref, px1, px2, px3, rx3, py1, py2, py3, ry3, pz2, pz3, rz3, _,
+                  z_ref, y1h_ref, y1l_ref, y2h_ref, y2l_ref, xh_ref, xl_ref):
+    coef = [[spread(w_ref, l, t) for t in range(TERMS)] for l in range(4)]
+    unit = [[scale(coef[l][t]) for t in range(TERMS)] for l in range(3)]
+
+    def circle(n, shape, first_row, first_lane, c, u):
+        d = ((rows_of(shape) + first_row) - (lanes_of(shape) + first_lane)) & (n - 1)
+        d = d.astype(F32)
+        return (bell(c, d) + bell(c, n - d)) * u
+
+    def full_circle(n, shape, c, u):
+        d = ((rows_of(shape) - lanes_of(shape)) & (n - 1)).astype(F32)
+        d = jnp.minimum(d, n - d)
+        return jnp.exp(c * d * d) * u
+
+    def by_term(shape, wide, values):
+        t = lanes_of(shape)
+        return jnp.where(t < wide, values[0], jnp.where(t < 2 * wide, values[1], values[2]))
+
     for t in range(TERMS):
         shape = (LANES, s.cy[1])
         g = circle(s.cy[1], shape, -(R + 1), 0, coef[1][t], unit[1][t])
@@ -286,7 +302,7 @@
     d = ((rows_of(shape) - column + 1) & (s.cx[1] - 1)).astype(F32)
     c = by_term(shape, wide, coef[1])
     g = (bell(c, d) + bell(c, s.cx[1] - d)) * by_term(shape, wide, unit[1])
-    put(xah_ref, xal_ref, 0, exact_dot(px1[...], jnp.where(column < s.x1 + 3, g, 0.0)))
+    put(xh_ref, xl_ref, 0, exact_dot(px1[...], jnp.where(column < s.x1 + 3, g, 0.0)))
     wide = s.rows2
     shape = (s.cx[2], TERMS * wide)
     lane = lanes_of(shape)
@@ -294,11 +310,11 @@
     d = ((rows_of(shape) - column + 2) & (s.cx[2] - 1)).astype(F32)
     c = by_term(shape, wide, coef[2])
     g = (bell(c, d) + bell(c, s.cx[2] - d)) * by_term(shape, wide, unit[2])
-    put(xbh_ref, xbl_ref, 0, exact_dot(px2[...], jnp.where(column < s.x2 + 5, g, 0.0)))
+    put(xh_ref, xl_ref, TERMS * s.rows1, exact_dot(px2[...], jnp.where(column < s.x2 + 5, g, 0.0)))
     for t in range(TERMS):
         u = scale(coef[3][t], s.cx[3])
         g = full_circle(s.cx[3], (s.cx[3], s.cx[3]), coef[3][t], u)
-        put(xbh_ref, xbl_ref, (TERMS + t) * wide, exact_dot(px3[...], exact_dot(g, rx3[...])))
+        put(xh_ref, xl_ref, TERMS * s.rows1 + (TERMS + t) * wide, exact_dot(px3[...], exact_dot(g, rx3[...])))
     for t in range(TERMS):
         g = circle(s.cz[2], (s.cz[2], LANES), 0, 0, coef[2][t], unit[2][t])
         g = exact_dot(pz2[...], g) * (a_ref[2, t] * 0.0625)
@@ -309,23 +325,18 @@
         z_ref[(TERMS + t) * s.zrows : (TERMS + t + 1) * s.zrows] = g
 
 
-def near_kernel(s, tap_ref, b_ref, xlo_ref, xhi_ref, sl_ref, sr_ref, c_lo_l, c_lo_r, c_hi_l, c_hi_r,
-                y0h_ref, y0l_ref, own_ref, down_ref, up_ref, eh_ref, el_ref, u_ref, v_ref):
+def near_kernel(s, tap_ref, b_ref, lo_ref, hi_ref, left_ref, right_ref, y0h_ref, y0l_ref,
+                own_ref, down_ref, up_ref, eh_ref, el_ref, u_ref, v_ref):
     ext = s.ext
     group = LANES // R
     lane = lanes_of((ext, LANES))
-    for t in range(s.fine_tiles):
-        left = jnp.concatenate([c_lo_l[t, R : 2 * R], sl_ref[t], c_hi_l[t, 0:R]], axis=0)
-        right = jnp.concatenate([c_lo_r[t, R : 2 * R], sr_ref[t], c_hi_r[t, 0:R]], axis=0)
-        for g in range(min(group, s.nz - t * group)):
-            z = t * group + g
-            strips = jnp.where((lane >= R * g) & (lane < R * g + R), left, right)
-            strips = turn(strips, -R * g)
-            main = jnp.concatenate([xlo_ref[z, R : 2 * R], b_ref[z], xhi_ref[z, 0:R]], axis=0)
-            for at, x in ((0, main), (LANES, strips)):
-                high, low = halves(x)
-                eh_ref[z * ext : (z + 1) * ext, at : at + LANES] = high
-                el_ref[z * ext : (z + 1) * ext, at : at + LANES] = low
+    for z in range(s.nz):
+        t, g = divmod(z, group)
+        strips = jnp.where((lane >= R * g) & (lane < R * g + R), left_ref[t], right_ref[t])
+        for at, x in ((0, extended(b_ref, lo_ref, hi_ref, z)), (LANES, turn(strips, -R * g))):
+            high, low = halves(x)
+            eh_ref[z * ext : (z + 1) * ext, at : at + LANES] = high
+            el_ref[z * ext : (z + 1) * ext, at : at + LANES] = low
     step = 4 * ext
     y0h, y0l = y0h_ref[...], y0l_ref[...]
     for at in range(0, s.nz * ext, step):
@@ -372,7 +383,7 @@
 
 def depth_kernel(s, tap_ref, *refs):
     m_refs = refs[: s.gz]
-    ry2_ref, rx2_ref, w_ref, down_ref, up_ref, c2_ref, c_ref = refs[s.gz :]
+    ry2_ref, rx2_ref, _, w_ref, down_ref, up_ref, c2_ref, c_ref = refs[s.gz :]
     n = s.cz[1]
     parts = [[] for _ in range(n)]
     for b in range(s.gz):
@@ -426,13 +437,11 @@
 
 def along_kernel(s, z_ref, w_ref, *refs):
     c2_refs = refs[: s.gy]
-    (y1h_ref, y1l_ref, y2h_ref, y2l_ref, xah_ref, xal_ref, xbh_ref, xbl_ref,
-     *g_refs, yb_ref) = refs[s.gy :]
+    y1h_ref, y1l_ref, y2h_ref, y2l_ref, d_ref, yb_ref = refs[s.gy :]
     base = s.tiles_s * s.rows1
     lane = lanes_of((s.rows1, LANES))
     above, below = c2_refs[1], c2_refs[-1]
     end = s.y1 + R
-    along = []
     for t in range(TERMS):
         cells = []
         for o in range(s.planes):
@@ -445,7 +454,9 @@
             x += jnp.where((lane >= end) & (lane < end + s.strip), turn(above[rows], end - at), 0.0)
             cells.append(x)
         columns = slice(t * s.ny, (t + 1) * s.ny)
-        along.append(dot3(jnp.concatenate(cells, axis=0), y1h_ref[:, columns], y1l_ref[:, columns]))
+        out = dot3(jnp.concatenate(cells, axis=0), y1h_ref[:, columns], y1l_ref[:, columns])
+        for o in range(s.planes):
+            d_ref[t * s.rows1 : (t + 1) * s.rows1, o * s.ny : (o + 1) * s.ny] = out[o * s.rows1 : (o + 1) * s.rows1]
     cells = []
     for j in range(s.cz[2]):
         out = None
@@ -459,38 +470,38 @@
     for j in range(s.cz[2]):
         for q in range(2 * TERMS):
             yb_ref[q, j] = yb[j * s.rows2 : (j + 1) * s.rows2, q * s.ny : (q + 1) * s.ny]
-    xah, xal, xbh, xbl = xah_ref[...], xal_ref[...], xbh_ref[...], xbl_ref[...]
     for o in range(s.planes):
-        rows = slice(o * s.rows1, (o + 1) * s.rows1)
-        near_high, near_low = halves(jnp.concatenate([a[rows] for a in along], axis=0))
-        far = []
         for q in range(2 * TERMS):
             x = yb_ref[q, 0] * z_ref[q * s.zrows + o, 0]
             for j in range(1, s.cz[2]):
                 x += yb_ref[q, j] * z_ref[q * s.zrows + o, j]
-            far.append(x)
-        far_high, far_low = halves(jnp.concatenate(far, axis=0))
-        g = dot(xah, near_high) + dot(xal, near_high) + dot(xah, near_low)
-        g += dot(xbh, far_high) + dot(xbl, far_high) + dot(xbh, far_low)
-        for shift, ref in enumerate(g_refs):
-            ref[o] = g[shift * s.nx : (shift + 1) * s.nx]
-
-
-def last_kernel(s, own_ref, low_ref, high_ref, *refs):
-    g_refs, out_ref = refs[:-1], refs[-1]
-    level = []
-    for o in range(s.planes):
-        x = g_refs[0][o]
-        for ref in g_refs[1:]:
-            x += ref[o]
-        level.append(x)
+            at = TERMS * s.rows1 + q * s.rows2
+            d_ref[at : at + s.rows2, o * s.ny : (o + 1) * s.ny] = x
+
+
+def across(s, d_ref, xh_ref, xl_ref, shift):
+    rows = slice(shift * s.nx, (shift + 1) * s.nx)
+    high, low = halves(d_ref[...])
+    return dot(xh_ref[rows], high) + dot(xl_ref[rows], high) + dot(xh_ref[rows], low)
+
+
+def away_kernel(s, d_ref, xh_ref, xl_ref, *g_refs):
+    for shift, ref in enumerate(g_refs):
+        ref[...] = across(s, d_ref, xh_ref, xl_ref, shift + 1)
+
+
+def prolonged(s, level, z):
+    m = z // 2 + 1
+    if z % 2 == 0:
+        return level[m]
+    return NEAR * (level[m] + level[m + 1]) + FAR * (level[m - 1] + level[m + 2])
+
+
+def home_kernel(s, d_ref, xh_ref, xl_ref, own_ref, low_ref, high_ref, out_ref):
+    g = across(s, d_ref, xh_ref, xl_ref, 0)
+    level = [g[:, o * s.ny : (o + 1) * s.ny] for o in range(s.planes)]
     for z in range(s.nz):
-        m = z // 2 + 1
-        if z % 2 == 0:
-            x = level[m]
-        else:
-            x = NEAR * (level[m] + level[m + 1]) + FAR * (level[m - 1] + level[m + 2])
-        x += own_ref[z]
+        x = prolonged(s, level, z) + own_ref[z]
         if z < R:
             x += low_ref[z]
         if z >= s.nz - R:
@@ -498,8 +509,25 @@
         out_ref[z] = x
 
 
-def call(kernel, name, operands, out_shapes, scalars=(), scratch=(), flops=0):
+def last_kernel(s, home_ref, *refs):
+    g_refs, out_ref = refs[:-1], refs[-1]
+    level = []
+    for o in range(s.planes):
+        columns = slice(o * s.ny, (o + 1) * s.ny)
+        x = g_refs[0][:, columns]
+        for ref in g_refs[1:]:
+            x += ref[:, columns]
+        level.append(x)
+    for z in range(s.nz):
+        out_ref[z] = home_ref[z] + prolonged(s, level, z)
+
+
+def call(kernel, name, operands, out_shapes, scalars=(), after=(), scratch=(), flops=0):
+    operands = list(operands) + list(after)
+
     def spec(i):
+        if i >= len(operands) - len(after):
+            return pl.BlockSpec(memory_space=pl.ANY)
         return pl.BlockSpec(memory_space=pltpu.SMEM if i in scalars else pltpu.VMEM)
 
     moved = sum(x.size * x.dtype.itemsize for x in operands)
@@ -530,69 +558,81 @@
     return lax.ppermute(x, names if len(names) > 1 else names[0], pairs)
 
 
+def two(*shape):
+    return arrays(shape, shape, dtype=BF16)
+
+
 def shards(charges, widths, amplitudes):
     s = Sizes(*charges.shape, lax.axis_size("gz"), lax.axis_size("gx"), lax.axis_size("gy"))
     c = {k: jnp.asarray(v) for k, v in constants(s).items()}
-    strips = (s.fine_tiles, s.nx, LANES)
-    corners = (s.fine_tiles, 2 * R, LANES)
-    share, to_low, to_high, corner_low, corner_high, edge_rows = call(
-        functools.partial(share_kernel, s), "share",
-        [charges, c["ry1"], c["rx1"]],
-        arrays((s.tiles1, s.rows1, LANES), strips, strips, corners, corners, (s.nz, 2 * R, s.ny)),
-        flops=10**8,
-    )
-    shares = [share] + [fetch(share, gz=b) for b in range(1, s.gz)]
-    left, right = fetch(to_high, gy=-1), fetch(to_low, gy=1)
-    x_shifts = (1,) if s.gx == 2 else (-1, 1)
-    rows, lefts, rights = [], [], []
-    for dx in x_shifts:
-        rows.append(fetch(edge_rows, gx=dx))
-        lefts.append(fetch(corner_high, gx=dx, gy=-1))
-        rights.append(fetch(corner_low, gx=dx, gy=1))
-
-    two = lambda *shape: arrays(shape, shape, dtype=BF16)
-    taps, z_taps, y0h, y0l, y1h, y1l, y2h, y2l, xah, xal, xbh, xbl = call(
-        functools.partial(matrix_kernel, s), "matrices",
-        [widths, amplitudes] + [c[k] for k in "px1 px2 px3 rx3 py1 py2 py3 ry3 pz2 pz3 rz3".split()],
-        arrays((16, LANES), (2 * TERMS * s.zrows, LANES))
-        + two(2 * LANES, TERMS * s.ny) + two(LANES, TERMS * s.ny) + two(s.cy[2], 2 * TERMS * s.ny)
-        + two(s.cx[0], TERMS * s.rows1) + two(s.cx[0], 2 * TERMS * s.rows2),
-        scalars=(0, 1), flops=10**8,
-    )
     brick = (s.nz, s.nx, s.ny)
     side = (R, s.nx, s.ny)
+    share, edge_rows = call(
+        functools.partial(share_kernel, s), "share", [charges],
+        arrays((s.tiles1, s.rows1, LANES), (s.nz, 2 * R, s.ny)), flops=8 * 10**8,
+    )
+    high_rows = fetch(edge_rows, gx=1)
+    low_rows = high_rows if s.gx == 2 else fetch(edge_rows, gx=-1)
+    shares = [share] + [fetch(share, gz=b) for b in range(1, s.gz)]
+    strips = (s.fine_tiles, s.ext, LANES)
+    first_cells, last_cells = call(
+        functools.partial(strip_kernel, s), "strips", [charges, low_rows, high_rows],
+        arrays(strips, strips), flops=4 * 10**8,
+    )
+    left, right = fetch(last_cells, gy=-1), fetch(first_cells, gy=1)
+    taps, y0h, y0l = call(
+        functools.partial(tap_kernel, s), "taps", [widths, amplitudes],
+        arrays((16, LANES)) + two(2 * LANES, TERMS * s.ny), scalars=(0, 1), flops=6 * 10**8,
+    )
     near, near_down, near_up = call(
         functools.partial(near_kernel, s), "near",
-        [taps, charges, rows[0], rows[-1], left, right, lefts[0], rights[0], lefts[-1], rights[-1], y0h, y0l],
+        [taps, charges, low_rows, high_rows, left, right, y0h, y0l],
         arrays(brick, side, side), scalars=(0,),
         scratch=[
             pltpu.VMEM((s.nz * s.ext, 2 * LANES), BF16), pltpu.VMEM((s.nz * s.ext, 2 * LANES), BF16),
             pltpu.VMEM((TERMS, s.nz, s.ext, s.ny), F32), pltpu.VMEM((TERMS,) + brick, F32),
         ],
-        flops=3 * 10**9,
+        flops=6 * 10**9,
     )
     base = s.tiles_s * s.rows1
     size2 = s.tiles2 * s.rows2
+    depth = TERMS * (s.rows1 + 2 * s.rows2)
     waves, to_low, to_high, coarse = call(
         functools.partial(depth_kernel, s), "depth",
         [taps] + shares + [c["ry2"], c["rx2"]],
         arrays((TERMS * s.planes, s.rows1, LANES), (base + size2, LANES), (base + size2, LANES), (size2, LANES)),
-        scalars=(0,), scratch=[pltpu.VMEM((s.cz[1], s.rows1, LANES), F32)], flops=10**8,
+        scalars=(0,), after=[near], scratch=[pltpu.VMEM((s.cz[1], s.rows1, LANES), F32)], flops=2 * 10**9,
+    )
+    named = ("px1", "px2", "px3", "rx3", "py1", "py2", "py3", "ry3", "pz2", "pz3", "rz3")
+    z_taps, y1h, y1l, y2h, y2l, xh, xl = call(
+        functools.partial(matrix_kernel, s), "matrices",
+        [widths, amplitudes] + [c[k] for k in named],
+        arrays((2 * TERMS * s.zrows, LANES))
+        + two(LANES, TERMS * s.ny) + two(s.cy[2], 2 * TERMS * s.ny)
+        + two(s.cx[0], depth),
+        scalars=(0, 1), after=[coarse], flops=3 * 10**9,
     )
     coarses = [coarse]
     for b in range(1, s.gy):
         coarses.append(fetch({1: to_low, s.gy - 1: to_high}.get(b, coarse), gy=b))
     near_low, near_high = fetch(near_up, gz=-1), fetch(near_down, gz=1)
+    (terms,) = call(
+        functools.partial(along_kernel, s), "along",
+        [z_taps, waves] + coarses + [y1h, y1l, y2h, y2l],
+        arrays((depth, s.planes * s.ny)), scalars=(0,),
+        scratch=[pltpu.VMEM((2 * TERMS, s.cz[2], s.rows2, s.ny), F32)], flops=3 * 10**9,
+    )
     parts = call(
-        functools.partial(along_kernel, s), "along",
-        [z_taps, waves] + coarses + [y1h, y1l, y2h, y2l, xah, xal, xbh, xbl],
-        arrays(*[(s.planes, s.nx, s.ny)] * s.gx), scalars=(0,),
-        scratch=[pltpu.VMEM((2 * TERMS, s.cz[2], s.rows2, s.ny), F32)], flops=10**9,
-    )
-    parts = [parts[0]] + [fetch(parts[dx], gx=-dx) for dx in range(1, s.gx)]
+        functools.partial(away_kernel, s), "away", [terms, xh, xl],
+        arrays(*[(s.nx, s.planes * s.ny)] * (s.gx - 1)), flops=10**9,
+    )
+    parts = [fetch(x, gx=-dx) for dx, x in enumerate(parts, 1)]
+    (home,) = call(
+        functools.partial(home_kernel, s), "home",
+        [terms, xh, xl, near, near_low, near_high], arrays(brick), flops=2 * 10**9,
+    )
     (out,) = call(
-        functools.partial(last_kernel, s), "last",
-        [near, near_low, near_high] + list(parts), arrays(brick), flops=10**7,
+        functools.partial(last_kernel, s), "last", [home] + parts, arrays(brick), flops=10**9,
     )
     return out
 

time: 59.2 us -> 42.3 us (0.71)
  waiting for transfers between devices: 21.3 us -> 5.47 us
  Pallas kernels: 15.5 us -> 17.4 us
  local copies, waits for them, and re-layouts: 2.69 us -> 1.13 us
  starting transfers between devices: 19.2 us -> 17.9 us
    ppermute x14 -> x12, waiting for transfers between devices: 21.3 us -> 5.47 us  [fetch(): return lax.ppermute(x, names if len(names) > 1 else names[0], pairs)]
    pallas_call x6 -> x10, Pallas kernels: 15.5 us -> 17.4 us  [call(): pl.pallas_call(kernel, name=name, out_shape=out_shapes, in_specs=[spec(i)...]
    unnamed x36 -> x32, local copies, waits for them, and re-layouts: 2.69 us -> 1.13 us
    ppermute x14 -> x12, starting transfers between devices: 19.2 us -> 17.9 us  [fetch(): return lax.ppermute(x, names if len(names) > 1 else names[0], pairs)]
  transfers between devices with their start and end apart: 14 -> 12, of which waited for: 4 -> 4; matrix products, arithmetic and copies ran while one was open for 0% -> 0% of each run, Pallas kernels for 21% -> 37%
where the time goes in v1:
time: 42.3 us; the launch traced here: 42.2 us
  starting transfers between devices  17.9 us (42%)
  Pallas kernels  17.4 us (41%)
  waiting for transfers between devices  5.47 us (13%)
  local copies, waits for them, and re-layouts  1.13 us (3%)
    ppermute x12, starting transfers between devices, fetch(): return lax.ppermute(x, names if len(names) > 1 else names[0], pairs)  17.9 us
    pallas_call x10, Pallas kernels, call(): pl.pallas_call(kernel, name=name, out_shape=out_shapes, in_specs=[spec(i)...  17.4 us
    ppermute x12, waiting for transfers between devices, fetch(): return lax.ppermute(x, names if len(names) > 1 else names[0], pairs)  5.47 us
    unnamed x32, local copies, waits for them, and re-layouts  1.13 us
  transfers between devices with their start and end apart: 12, of which 4 were waited for; matrix products, arithmetic and copies ran while one was open for 0% of the time, Pallas kernels for 37%

profile of v1, /device:TPU:0, one launch (start us, length us, event | category | flops | bytes accessed | tf_op | source)
XLA Modules:
  0.0 42.2 jit_solution(9491643571069896911)
XLA Ops:
  0.0 1.0 %copy-done = f32[16,64,128]{2,1,0:T(8,128)S(1)} copy-done((f32[16,64,128]{2,1,0:T(8,128)S(1)}, f32[16,64,128]{2,1,0:T(8,128)}, u32[]{:S(2)}) %copy-start) | copy-done | bytes 524312
  1.0 0.7 %share.1 = (f32[6,40,128]{2,1,0:T(8,128)S(1)}, f32[16,16,128]{2,1,0:T(8,128)S(1)}) custom-call(f32[16,64,128]{2,1,0:T(8,128)S(1)} %copy-done), custom_call_target="tpu_custom_call" | custom-call | flops 800000000 | bytes 778240 | tf_op jit(solution)/shard_map/share/pallas_call | solution.py:535
  1.7 0.5 %collective-permute-start.3 = (f32[16,16,128]{2,1,0:T(8,128)S(1)}, f32[16,16,128]{2,1,0:T(8,128)S(1)}, u32[]{:S(2)}, u32[]{:S(2)}) collective-permute-start(f32[16,16,128]{2,1,0:T(8,128)S(1)} %get-tuple-element.28), channel_id=1, source_target_pairs={{16,0},{0,16},{17,1},{1,17},{18,2},{2,18},{19,3},{3,19},{20,4},{4,... | collective-permute-start | bytes 393224 | tf_op jit(solution)/shard_map/ppermute | solution.py:558
  2.3 2.6 %collective-permute-start.2 = (f32[6,40,128]{2,1,0:T(8,128)S(1)}, f32[6,40,128]{2,1,0:T(8,128)S(1)}, u32[]{:S(2)}, u32[]{:S(2)}) collective-permute-start(f32[6,40,128]{2,1,0:T(8,128)S(1)} %get-tuple-element.27.refs_0_), channel_id=1, source_target_pairs={{3,0},{0,1},{1,2},{2,3},{7,4},{4,5},{5,6},{6,7},{11,8},{8,9},{9,10... | collective-permute-start | bytes 368648 | tf_op jit(solution)/shard_map/ppermute | solution.py:558
  4.9 2.6 %collective-permute-start.1 = (f32[6,40,128]{2,1,0:T(8,128)S(1)}, f32[6,40,128]{2,1,0:T(8,128)S(1)}, u32[]{:S(2)}, u32[]{:S(2)}) collective-permute-start(f32[6,40,128]{2,1,0:T(8,128)S(1)} %get-tuple-element.27.refs_0_), channel_id=1, source_target_pairs={{2,0},{3,1},{0,2},{1,3},{6,4},{7,5},{4,6},{5,7},{10,8},{11,9},{8,1... | collective-permute-start | bytes 368648 | tf_op jit(solution)/shard_map/ppermute | solution.py:558
  7.5 1.3 %collective-permute-start = (f32[6,40,128]{2,1,0:T(8,128)S(1)}, f32[6,40,128]{2,1,0:T(8,128)S(1)}, u32[]{:S(2)}, u32[]{:S(2)}) collective-permute-start(f32[6,40,128]{2,1,0:T(8,128)S(1)} %get-tuple-element.27.refs_0_), channel_id=1, source_target_pairs={{1,0},{2,1},{3,2},{0,3},{5,4},{6,5},{7,6},{4,7},{9,8},{10,9},{11,1... | collective-permute-start | bytes 368648 | tf_op jit(solution)/shard_map/ppermute | solution.py:558
  8.9 0.0 collective-permute-done.3.lo_ref.hi_ref
  8.9 0.2 strips.1
  9.1 1.5 %collective-permute-start.4 = (f32[1,80,128]{2,1,0:T(8,128)S(1)}, f32[1,80,128]{2,1,0:T(8,128)S(1)}, u32[]{:S(2)}, u32[]{:S(2)}) collective-permute-start(f32[1,80,128]{2,1,0:T(8,128)S(1)} %get-tuple-element.29), channel_id=1, source_target_pairs={{12,0},{0,4},{4,8},{8,12},{13,1},{1,5},{5,9},{9,13},{14,2},{2,6},{... | collective-permute-start | bytes 122888 | tf_op jit(solution)/shard_map/ppermute | solution.py:558
  10.6 1.4 %collective-permute-start.5 = (f32[1,80,128]{2,1,0:T(8,128)S(1)}, f32[1,80,128]{2,1,0:T(8,128)S(1)}, u32[]{:S(2)}, u32[]{:S(2)}) collective-permute-start(f32[1,80,128]{2,1,0:T(8,128)S(1)} %get-tuple-element.30), channel_id=1, source_target_pairs={{4,0},{8,4},{12,8},{0,12},{5,1},{9,5},{13,9},{1,13},{6,2},{10,6},{... | collective-permute-start | bytes 122888 | tf_op jit(solution)/shard_map/ppermute | solution.py:558
  12.1 0.0 copy-done.2
  12.1 0.8 %taps.1 = (f32[16,128]{1,0:T(8,128)S(1)}, bf16[256,384]{1,0:T(8,128)(2,1)S(1)}, bf16[256,384]{1,0:T(8,128)(2,1)S(1)}) custom-call(f32[4,3]{1,0:T(4,128)S(1)} %copy-done.2, f32[4,3]{1,0:T(4,128)S(1)} %copy-done.3), custom_call_target="tpu_custom_call" | custom-call | flops 600000000 | bytes 401504 | tf_op jit(solution)/shard_map/taps/pallas_call | solution.py:535
  12.8 1.6 %collective-permute-done.4.left_ref = f32[1,80,128]{2,1,0:T(8,128)S(1)} collective-permute-done((f32[1,80,128]{2,1,0:T(8,128)S(1)}, f32[1,80,128]{2,1,0:T(8,128)S(1)}, u32[]{:S(2)}, u32[]{:S(2)}) %collective-permute-start.4) | collective-permute-done | bytes 40992 | tf_op jit(solution)/shard_map/ppermute | solution.py:558
  14.4 0.2 collective-permute-done.5.right_ref
  14.6 5.3 %near.1 = (f32[16,64,128]{2,1,0:T(8,128)S(1)}, f32[8,64,128]{2,1,0:T(8,128)S(1)}, f32[8,64,128]{2,1,0:T(8,128)S(1)}) custom-call(f32[16,128]{1,0:T(8,128)S(1)} %get-tuple-element.26.tap_ref, f32[16,64,128]{2,1,0:T(8,128)S(1)} %copy-done.1, f32[16,16,128]{2,1,0:T(8,128)S(1)} %collective-permute-done.3.lo_ref.hi_ref, ...), custom_call_target="tpu_custom_call" | custom-call | flops 6000000000 | bytes 2318336 | tf_op jit(solution)/shard_map/near/pallas_call | solution.py:535
  19.9 0.7 %collective-permute-start.9 = (f32[8,64,128]{2,1,0:T(8,128)S(1)}, f32[8,64,128]{2,1,0:T(8,128)S(1)}, u32[]{:S(2)}, u32[]{:S(2)}) collective-permute-start(f32[8,64,128]{2,1,0:T(8,128)S(1)} %get-tuple-element.45), channel_id=1, source_target_pairs={{3,0},{0,1},{1,2},{2,3},{7,4},{4,5},{5,6},{6,7},{11,8},{8,9},{9,10... | collective-permute-start | bytes 786440 | tf_op jit(solution)/shard_map/ppermute | solution.py:558
  20.7 3.2 %collective-permute-start.10 = (f32[8,64,128]{2,1,0:T(8,128)S(1)}, f32[8,64,128]{2,1,0:T(8,128)S(1)}, u32[]{:S(2)}, u32[]{:S(2)}) collective-permute-start(f32[8,64,128]{2,1,0:T(8,128)S(1)} %get-tuple-element.46), channel_id=1, source_target_pairs={{1,0},{2,1},{3,2},{0,3},{5,4},{6,5},{7,6},{4,7},{9,8},{10,9},{11,1... | collective-permute-start | bytes 786440 | tf_op jit(solution)/shard_map/ppermute | solution.py:558
  23.8 0.0 collective-permute-done.2.refs_3_
  23.8 0.0 collective-permute-done.1.refs_2_
  23.8 0.0 collective-permute-done.refs_1_
  23.8 0.0 copy-done.9
  23.8 0.0 copy-done.11
  23.8 0.0 copy-start.4
  23.9 0.0 copy-start.5
  23.9 0.0 copy-start.6
  23.9 0.0 copy-start.7
  23.9 0.0 copy-start.8
  23.9 0.0 copy-start.10
  23.9 0.0 copy-start.12
  23.9 0.0 copy-start.13
  23.9 0.0 copy-start.14
  24.0 0.0 copy-start.15
  24.0 1.6 %depth.1 = (f32[33,40,128]{2,1,0:T(8,128)S(1)}, f32[240,128]{1,0:T(8,128)S(1)}, f32[240,128]{1,0:T(8,128)S(1)}, f32[120,128]{1,0:T(8,128)S(1)}) custom-call(f32[16,128]{1,0:T(8,128)S(1)} %get-tuple-element.26.tap_ref, f32[6,40,128]{2,1,0:T(8,128)S(1)} %get-tuple-element.27.refs_0_, f32[6,40,128]{2,1,0:T(8,128)S(1)} %collective-permute-done.refs_1_, ...), custom_call_target="tpu_custom_call" | custom-call | flops 2000000000 | bytes 2076416 | tf_op jit(solution)/shard_map/depth/pallas_call | solution.py:535
  25.6 1.6 %collective-permute-start.7 = (f32[120,128]{1,0:T(8,128)S(1)}, f32[120,128]{1,0:T(8,128)S(1)}, u32[]{:S(2)}, u32[]{:S(2)}) collective-permute-start(f32[120,128]{1,0:T(8,128)S(1)} %get-tuple-element.34._.refs_0_), channel_id=1, source_target_pairs={{8,0},{12,4},{0,8},{4,12},{9,1},{13,5},{1,9},{5,13},{10,2},{14,6},... | collective-permute-start | bytes 184328 | tf_op jit(solution)/shard_map/ppermute | solution.py:558
  27.2 2.3 %collective-permute-start.6 = (f32[240,128]{1,0:T(8,128)S(1)}, f32[240,128]{1,0:T(8,128)S(1)}, u32[]{:S(2)}, u32[]{:S(2)}) collective-permute-start(f32[240,128]{1,0:T(8,128)S(1)} %get-tuple-element.37), channel_id=1, source_target_pairs={{4,0},{8,4},{12,8},{0,12},{5,1},{9,5},{13,9},{1,13},{6,2},{10,6},{... | collective-permute-start | bytes 368648 | tf_op jit(solution)/shard_map/ppermute | solution.py:558
  29.5 0.0 collective-permute-start.8
  29.6 3.0 %matrices.1 = (f32[96,128]{1,0:T(8,128)S(1)}, bf16[128,384]{1,0:T(8,128)(2,1)S(1)}, bf16[128,384]{1,0:T(8,128)(2,1)S(1)}, bf16[128,768]{1,0:T(8,128)(2,1)S(1)}, ...) custom-call(f32[4,3]{1,0:T(4,128)S(1)} %copy-done.2, ...), custom_call_target="tpu_custom_call" | custom-call | flops 3000000000 | bytes 1162336 | tf_op jit(solution)/shard_map/matrices/pallas_call | solution.py:535
  32.6 0.0 collective-permute-done.7.refs_2_
  32.6 0.0 collective-permute-done.6.refs_1_
  32.6 2.7 %collective-permute-done.8.refs_3_ = f32[240,128]{1,0:T(8,128)S(1)} collective-permute-done((f32[240,128]{1,0:T(8,128)S(1)}, f32[240,128]{1,0:T(8,128)S(1)}, u32[]{:S(2)}, u32[]{:S(2)}) %collective-permute-start.8) | collective-permute-done | bytes 122912 | tf_op jit(solution)/shard_map/ppermute | solution.py:558
  35.3 3.6 %along.1.d_ref = f32[264,1408]{1,0:T(8,128)S(1)} custom-call(f32[96,128]{1,0:T(8,128)S(1)} %get-tuple-element.35.z_ref, f32[33,40,128]{2,1,0:T(8,128)S(1)} %get-tuple-element.36.w_ref, f32[120,128]{1,0:T(8,128)S(1)} %get-tuple-element.34._.refs_0_, f32[240,128]{1,0:T(8,128)S(1)} %collective-permute-done.6.refs_1_, ...), custom_call_target="tpu_custom_call" | custom-call | flops 3000000000 | bytes 3170304 | tf_op jit(solution)/shard_map/along/pallas_call | solution.py:535
  38.9 0.6 %away.1 = f32[64,1408]{1,0:T(8,128)S(1)} custom-call(f32[264,1408]{1,0:T(8,128)S(1)} %along.1.d_ref, bf16[128,264]{1,0:T(8,128)(2,1)S(1)} %get-tuple-element.43.xh_ref, bf16[128,264]{1,0:T(8,128)(2,1)S(1)} %get-tuple-element.44.xl_ref), custom_call_target="tpu_custom_call" | custom-call | flops 1000000000 | bytes 1982464 | tf_op jit(solution)/shard_map/away/pallas_call | solution.py:535
  39.6 0.1 collective-permute-start.11
  39.6 0.0 collective-permute-done.9.low_ref
  39.6 0.0 collective-permute-done.10.high_ref
  39.7 0.7 %home.1.home_ref = f32[16,64,128]{2,1,0:T(8,128)S(1)} custom-call(f32[264,1408]{1,0:T(8,128)S(1)} %along.1.d_ref, bf16[128,264]{1,0:T(8,128)(2,1)S(1)} %get-tuple-element.43.xh_ref, bf16[128,264]{1,0:T(8,128)(2,1)S(1)} %get-tuple-element.44.xl_ref, f32[16,64,128]{2,1,0:T(8,128)S(1)} %get-tuple-element.33.refs_6_.own_ref, ...), custom_call_target="tpu_custom_call" | custom-call | flops 2000000000 | bytes 3194880 | tf_op jit(solution)/shard_map/home/pallas_call | solution.py:535
  40.3 1.0 %collective-permute-done.11.refs_0_ = f32[64,1408]{1,0:T(8,128)S(1)} collective-permute-done((f32[64,1408]{1,0:T(8,128)S(1)}, f32[64,1408]{1,0:T(8,128)S(1)}, u32[]{:S(2)}, u32[]{:S(2)}) %collective-permute-start.11) | collective-permute-done | bytes 360480 | tf_op jit(solution)/shard_map/ppermute | solution.py:558
  41.3 0.9 %last.1 = f32[16,64,128]{2,1,0:T(8,128)} custom-call(f32[16,64,128]{2,1,0:T(8,128)S(1)} %home.1.home_ref, f32[64,1408]{1,0:T(8,128)S(1)} %collective-permute-done.11.refs_0_), custom_call_target="tpu_custom_call" | custom-call | flops 1000000000 | bytes 1409024 | tf_op jit(solution)/shard_map/last/pallas_call | solution.py:535
  (18 shorter events, 0.0 us)
Async XLA Ops:
  0.0 1.0 %copy-start = (f32[16,64,128]{2,1,0:T(8,128)S(1)}, f32[16,64,128]{2,1,0:T(8,128)}, u32[]{:S(2)}) copy-start(f32[16,64,128]{2,1,0:T(8,128)} %b_ref.5) | copy-start | bytes 1572868
  1.0 11.0 %copy-start.2 = (f32[4,3]{1,0:T(4,128)S(1)}, f32[4,3]{1,0:T(4,128)}, u32[]{:S(2)}) copy-start(f32[4,3]{1,0:T(4,128)} %w_ref.3) | copy-start | bytes 148
  1.0 11.0 %copy-start.3 = (f32[4,3]{1,0:T(4,128)S(1)}, f32[4,3]{1,0:T(4,128)}, u32[]{:S(2)}) copy-start(f32[4,3]{1,0:T(4,128)} %a_ref.3) | copy-start | bytes 148
  1.7 7.1 %collective-permute-start.3 = (f32[16,16,128]{2,1,0:T(8,128)S(1)}, f32[16,16,128]{2,1,0:T(8,128)S(1)}, u32[]{:S(2)}, u32[]{:S(2)}) collective-permute-start(f32[16,16,128]{2,1,0:T(8,128)S(1)} %get-tuple-element.28), channel_id=1, source_target_pairs={{16,0},{0,16},{17,1},{1,17},{18,2},{2,18},{19,3},{3,19},{20,4},{4,... | collective-permute-start | bytes 393224 | tf_op jit(solution)/shard_map/ppermute | solution.py:558
  2.3 12.4 %copy-start.1 = (f32[16,64,128]{2,1,0:T(8,128)S(1)}, f32[16,64,128]{2,1,0:T(8,128)}, u32[]{:S(2)}) copy-start(f32[16,64,128]{2,1,0:T(8,128)} %b_ref.5) | copy-start | bytes 1572868
  2.3 21.5 %collective-permute-start.2 = (f32[6,40,128]{2,1,0:T(8,128)S(1)}, f32[6,40,128]{2,1,0:T(8,128)S(1)}, u32[]{:S(2)}, u32[]{:S(2)}) collective-permute-start(f32[6,40,128]{2,1,0:T(8,128)S(1)} %get-tuple-element.27.refs_0_), channel_id=1, source_target_pairs={{3,0},{0,1},{1,2},{2,3},{7,4},{4,5},{5,6},{6,7},{11,8},{8,9},{9,10... | collective-permute-start | bytes 368648 | tf_op jit(solution)/shard_map/ppermute | solution.py:558
  4.9 18.9 %collective-permute-start.1 = (f32[6,40,128]{2,1,0:T(8,128)S(1)}, f32[6,40,128]{2,1,0:T(8,128)S(1)}, u32[]{:S(2)}, u32[]{:S(2)}) collective-permute-start(f32[6,40,128]{2,1,0:T(8,128)S(1)} %get-tuple-element.27.refs_0_), channel_id=1, source_target_pairs={{2,0},{3,1},{0,2},{1,3},{6,4},{7,5},{4,6},{5,7},{10,8},{11,9},{8,1... | collective-permute-start | bytes 368648 | tf_op jit(solution)/shard_map/ppermute | solution.py:558
  7.5 16.3 %collective-permute-start = (f32[6,40,128]{2,1,0:T(8,128)S(1)}, f32[6,40,128]{2,1,0:T(8,128)S(1)}, u32[]{:S(2)}, u32[]{:S(2)}) collective-permute-start(f32[6,40,128]{2,1,0:T(8,128)S(1)} %get-tuple-element.27.refs_0_), channel_id=1, source_target_pairs={{1,0},{2,1},{3,2},{0,3},{5,4},{6,5},{7,6},{4,7},{9,8},{10,9},{11,1... | collective-permute-start | bytes 368648 | tf_op jit(solution)/shard_map/ppermute | solution.py:558
  9.1 5.3 %collective-permute-start.4 = (f32[1,80,128]{2,1,0:T(8,128)S(1)}, f32[1,80,128]{2,1,0:T(8,128)S(1)}, u32[]{:S(2)}, u32[]{:S(2)}) collective-permute-start(f32[1,80,128]{2,1,0:T(8,128)S(1)} %get-tuple-element.29), channel_id=1, source_target_pairs={{12,0},{0,4},{4,8},{8,12},{13,1},{1,5},{5,9},{9,13},{14,2},{2,6},{... | collective-permute-start | bytes 122888 | tf_op jit(solution)/shard_map/ppermute | solution.py:558
  10.6 4.0 %collective-permute-start.5 = (f32[1,80,128]{2,1,0:T(8,128)S(1)}, f32[1,80,128]{2,1,0:T(8,128)S(1)}, u32[]{:S(2)}, u32[]{:S(2)}) collective-permute-start(f32[1,80,128]{2,1,0:T(8,128)S(1)} %get-tuple-element.30), channel_id=1, source_target_pairs={{4,0},{8,4},{12,8},{0,12},{5,1},{9,5},{13,9},{1,13},{6,2},{10,6},{... | collective-permute-start | bytes 122888 | tf_op jit(solution)/shard_map/ppermute | solution.py:558
  14.6 9.2 %copy-start.9 = (f32[128,128]{1,0:T(8,128)S(1)}, f32[128,128]{1,0:T(8,128)}, u32[]{:S(2)}) copy-start(f32[128,128]{1,0:T(8,128)} %constant.24.clone.refs_4_) | copy-start | bytes 196612
  14.6 9.2 %copy-start.11 = (f32[24,40]{1,0:T(8,128)S(1)}, f32[24,40]{1,0:T(8,128)}, u32[]{:S(2)}) copy-start(f32[24,40]{1,0:T(8,128)} %constant.25.clone.refs_5_) | copy-start | bytes 11524
  19.9 19.7 %collective-permute-start.9 = (f32[8,64,128]{2,1,0:T(8,128)S(1)}, f32[8,64,128]{2,1,0:T(8,128)S(1)}, u32[]{:S(2)}, u32[]{:S(2)}) collective-permute-start(f32[8,64,128]{2,1,0:T(8,128)S(1)} %get-tuple-element.45), channel_id=1, source_target_pairs={{3,0},{0,1},{1,2},{2,3},{7,4},{4,5},{5,6},{6,7},{11,8},{8,9},{9,10... | collective-permute-start | bytes 786440 | tf_op jit(solution)/shard_map/ppermute | solution.py:558
  20.7 19.0 %collective-permute-start.10 = (f32[8,64,128]{2,1,0:T(8,128)S(1)}, f32[8,64,128]{2,1,0:T(8,128)S(1)}, u32[]{:S(2)}, u32[]{:S(2)}) collective-permute-start(f32[8,64,128]{2,1,0:T(8,128)S(1)} %get-tuple-element.46), channel_id=1, source_target_pairs={{1,0},{2,1},{3,2},{0,3},{5,4},{6,5},{7,6},{4,7},{9,8},{10,9},{11,1... | collective-permute-start | bytes 786440 | tf_op jit(solution)/shard_map/ppermute | solution.py:558
  23.8 5.7 %copy-start.4 = (f32[256,128]{1,0:T(8,128)S(1)}, f32[256,128]{1,0:T(8,128)}, u32[]{:S(2)}) copy-start(f32[256,128]{1,0:T(8,128)} %constant.30.clone.py1) | copy-start | bytes 393220
  23.9 5.7 %copy-start.5 = (f32[128,128]{1,0:T(8,128)S(1)}, f32[128,128]{1,0:T(8,128)}, u32[]{:S(2)}) copy-start(f32[128,128]{1,0:T(8,128)} %constant.31.clone.py2) | copy-start | bytes 196612
  23.9 5.7 %copy-start.6 = (f32[128,16]{1,0:T(8,128)S(1)}, f32[128,16]{1,0:T(8,128)}, u32[]{:S(2)}) copy-start(f32[128,16]{1,0:T(8,128)} %constant.28.clone.px3) | copy-start | bytes 24580
  23.9 5.7 %copy-start.7 = (f32[128,32]{1,0:T(8,128)S(1)}, f32[128,32]{1,0:T(8,128)}, u32[]{:S(2)}) copy-start(f32[128,32]{1,0:T(8,128)} %constant.27.clone.px2) | copy-start | bytes 49156
  23.9 5.6 %copy-start.8 = (f32[128,64]{1,0:T(8,128)S(1)}, f32[128,64]{1,0:T(8,128)}, u32[]{:S(2)}) copy-start(f32[128,64]{1,0:T(8,128)} %constant.26.clone.px1.ry3) | copy-start | bytes 98308
  23.9 5.6 %copy-start.10 = (f32[64,128]{1,0:T(8,128)S(1)}, f32[64,128]{1,0:T(8,128)}, u32[]{:S(2)}) copy-start(f32[64,128]{1,0:T(8,128)} %constant.32.clone.py3) | copy-start | bytes 98308
  23.9 5.6 %copy-start.12 = (f32[16,8]{1,0:T(8,128)S(1)}, f32[16,8]{1,0:T(8,128)}, u32[]{:S(2)}) copy-start(f32[16,8]{1,0:T(8,128)} %constant.34.clone.pz3) | copy-start | bytes 1540
  23.9 5.6 %copy-start.13 = (f32[16,16]{1,0:T(8,128)S(1)}, f32[16,16]{1,0:T(8,128)}, u32[]{:S(2)}) copy-start(f32[16,16]{1,0:T(8,128)} %constant.33.clone.pz2) | copy-start | bytes 3076
  23.9 5.6 %copy-start.14 = (f32[16,24]{1,0:T(8,128)S(1)}, f32[16,24]{1,0:T(8,128)}, u32[]{:S(2)}) copy-start(f32[16,24]{1,0:T(8,128)} %constant.29.clone.rx3) | copy-start | bytes 4612
  24.0 5.6 %copy-start.15 = (f32[8,128]{1,0:T(8,128)S(1)}, f32[8,128]{1,0:T(8,128)}, u32[]{:S(2)}) copy-start(f32[8,128]{1,0:T(8,128)} %constant.35.clone.rz3) | copy-start | bytes 12292
  25.6 7.0 %collective-permute-start.7 = (f32[120,128]{1,0:T(8,128)S(1)}, f32[120,128]{1,0:T(8,128)S(1)}, u32[]{:S(2)}, u32[]{:S(2)}) collective-permute-start(f32[120,128]{1,0:T(8,128)S(1)} %get-tuple-element.34._.refs_0_), channel_id=1, source_target_pairs={{8,0},{12,4},{0,8},{4,12},{9,1},{13,5},{1,9},{5,13},{10,2},{14,6},... | collective-permute-start | bytes 184328 | tf_op jit(solution)/shard_map/ppermute | solution.py:558
  27.2 5.4 %collective-permute-start.6 = (f32[240,128]{1,0:T(8,128)S(1)}, f32[240,128]{1,0:T(8,128)S(1)}, u32[]{:S(2)}, u32[]{:S(2)}) collective-permute-start(f32[240,128]{1,0:T(8,128)S(1)} %get-tuple-element.37), channel_id=1, source_target_pairs={{4,0},{8,4},{12,8},{0,12},{5,1},{9,5},{13,9},{1,13},{6,2},{10,6},{... | collective-permute-start | bytes 368648 | tf_op jit(solution)/shard_map/ppermute | solution.py:558
  29.5 5.8 %collective-permute-start.8 = (f32[240,128]{1,0:T(8,128)S(1)}, f32[240,128]{1,0:T(8,128)S(1)}, u32[]{:S(2)}, u32[]{:S(2)}) collective-permute-start(f32[240,128]{1,0:T(8,128)S(1)} %get-tuple-element.38), channel_id=1, source_target_pairs={{12,0},{0,4},{4,8},{8,12},{13,1},{1,5},{5,9},{9,13},{14,2},{2,6},{... | collective-permute-start | bytes 368648 | tf_op jit(solution)/shard_map/ppermute | solution.py:558
  39.6 1.7 %collective-permute-start.11 = (f32[64,1408]{1,0:T(8,128)S(1)}, f32[64,1408]{1,0:T(8,128)S(1)}, u32[]{:S(2)}, u32[]{:S(2)}) collective-permute-start(f32[64,1408]{1,0:T(8,128)S(1)} %away.1), channel_id=1, source_target_pairs={{16,0},{0,16},{17,1},{1,17},{18,2},{2,18},{19,3},{3,19},{20,4},{4,... | collective-permute-start | bytes 1081352 | tf_op jit(solution)/shard_map/ppermute | solution.py:558

commit v2 on v1

--- a/solution.py
+++ b/solution.py
@@ -34,8 +34,8 @@
         self.cy = [ny * gy >> l for l in range(4)]
         self.planes = self.z1 + 3
         self.zrows = up8(self.planes)
-        self.rows1 = up8(self.x1 + 3)
-        self.rows2 = up8(self.x2 + 5)
+        self.rows1 = self.x1
+        self.rows2 = up8(self.x2 + 3)
         self.wide1 = self.y1 + 3
         self.wide2 = self.y2 + 5
         self.tiles1 = -(-self.planes * self.wide1 // LANES)
@@ -83,7 +83,7 @@
 def constants(s):
     c = {}
     c["ry2"] = padded(restrict_open(-1, s.wide1, -2, s.wide2).T, LANES, LANES)
-    c["rx2"] = padded(restrict_open(-1, s.x1 + 3, -2, s.x2 + 5), s.rows2, s.rows1)
+    c["rx2"] = padded(restrict_open(0, s.x1, -1, s.x2 + 3), s.rows2, s.rows1)
 
     def chain(n):
         p1 = prolong_circle(n[1])
@@ -93,8 +93,8 @@
     x1, x2, x3 = chain(s.cx)
     c["px1"], c["px2"], c["px3"] = (m.astype(np.float32) for m in (x1, x2, x3))
     place = np.zeros((s.cx[2], s.rows2))
-    for r in range(s.x2 + 5):
-        place[(r - 2) % s.cx[2], r] += 1.0
+    for r in range(s.x2 + 3):
+        place[(r - 1) % s.cx[2], r] += 1.0
     c["rx3"] = (restrict_circle(s.cx[2]) @ place).astype(np.float32)
     y1, y2, y3 = chain(s.cy)
     c["py1"], c["py2"], c["py3"] = (
@@ -167,16 +167,20 @@
     return jnp.where((lane >= shift) | (lane < shift + wide - LANES), x, 0.0)
 
 
-def open_restriction(shape, in_dim, first_out, n_out):
-    i = lax.broadcasted_iota(jnp.int32, shape, in_dim)
+def open_restriction(shape, in_dim, first_in, first_out, n_out):
+    i = lax.broadcasted_iota(jnp.int32, shape, in_dim) + first_in
     o = lax.broadcasted_iota(jnp.int32, shape, 1 - in_dim)
     d = jnp.abs(i - 2 * (o + first_out))
     w = jnp.where(d == 0, 1.0, jnp.where(d == 1, NEAR, jnp.where(d == 3, FAR, 0.0)))
     return jnp.where(o < n_out, w, 0.0).astype(BF16)
 
 
-def share_kernel(s, b_ref, m_ref, xr_ref):
-    b = [b_ref[z] for z in range(s.nz)]
+def extended(s, b_ref, lo_ref, hi_ref, z):
+    return jnp.concatenate([lo_ref[z, s.nx - R :], b_ref[z], hi_ref[z, 0:R]], axis=0)
+
+
+def share_kernel(s, b_ref, lo_ref, hi_ref, _, m_ref, first_ref, last_ref):
+    b = [extended(s, b_ref, lo_ref, hi_ref, z) for z in range(s.nz)]
     planes = []
     for k in range(-1, s.z1 + 2):
         out = None
@@ -186,31 +190,21 @@
                 out = term if out is None else out + term
         planes.append(out)
     high, low = halves(jnp.concatenate(planes, axis=0))
-    ry1 = open_restriction((s.ny, LANES), 0, -1, s.wide1)
-    rx1 = open_restriction((s.rows1, s.nx), 1, -1, s.x1 + 3)
+    ry1 = open_restriction((s.ny, LANES), 0, 0, -1, s.wide1)
+    rx1 = open_restriction((s.rows1, s.ext), 1, -R, 0, s.x1)
     along = dot(high, ry1) + dot(low, ry1)
     shares = []
     for k in range(s.planes):
-        high, low = halves(along[k * s.nx : (k + 1) * s.nx])
+        high, low = halves(along[k * s.ext : (k + 1) * s.ext])
         shares.append(dot(rx1, high) + dot(rx1, low))
     for t, x in enumerate(packed(shares, s.wide1, s.tiles1)):
         m_ref[t] = x
-    for z in range(s.nz):
-        xr_ref[z, 0:R] = b[z][0:R]
-        xr_ref[z, R : 2 * R] = b[z][s.nx - R :]
-
-
-def extended(b_ref, lo_ref, hi_ref, z):
-    return jnp.concatenate([lo_ref[z, R : 2 * R], b_ref[z], hi_ref[z, 0:R]], axis=0)
-
-
-def strip_kernel(s, b_ref, lo_ref, hi_ref, first_ref, last_ref):
     lane = lanes_of((s.ext, LANES))
     group = LANES // R
     for t in range(s.fine_tiles):
         first = last = jnp.zeros((s.ext, LANES), F32)
         for g in range(min(group, s.nz - t * group)):
-            x = extended(b_ref, lo_ref, hi_ref, t * group + g)
+            x = b[t * group + g]
             at = R * ((g + 1) % group)
             first = jnp.where((lane >= at) & (lane < at + R), turn(x, at), first)
             at = R * g
@@ -299,18 +293,18 @@
     shape = (s.cx[1], TERMS * wide)
     lane = lanes_of(shape)
     column = lane - jnp.where(lane < wide, 0, jnp.where(lane < 2 * wide, wide, 2 * wide))
-    d = ((rows_of(shape) - column + 1) & (s.cx[1] - 1)).astype(F32)
+    d = ((rows_of(shape) - column) & (s.cx[1] - 1)).astype(F32)
     c = by_term(shape, wide, coef[1])
     g = (bell(c, d) + bell(c, s.cx[1] - d)) * by_term(shape, wide, unit[1])
-    put(xh_ref, xl_ref, 0, exact_dot(px1[...], jnp.where(column < s.x1 + 3, g, 0.0)))
+    put(xh_ref, xl_ref, 0, exact_dot(px1[...], g))
     wide = s.rows2
     shape = (s.cx[2], TERMS * wide)
     lane = lanes_of(shape)
     column = lane - jnp.where(lane < wide, 0, jnp.where(lane < 2 * wide, wide, 2 * wide))
-    d = ((rows_of(shape) - column + 2) & (s.cx[2] - 1)).astype(F32)
+    d = ((rows_of(shape) - column + 1) & (s.cx[2] - 1)).astype(F32)
     c = by_term(shape, wide, coef[2])
     g = (bell(c, d) + bell(c, s.cx[2] - d)) * by_term(shape, wide, unit[2])
-    put(xh_ref, xl_ref, TERMS * s.rows1, exact_dot(px2[...], jnp.where(column < s.x2 + 5, g, 0.0)))
+    put(xh_ref, xl_ref, TERMS * s.rows1, exact_dot(px2[...], jnp.where(column < s.x2 + 3, g, 0.0)))
     for t in range(TERMS):
         u = scale(coef[3][t], s.cx[3])
         g = full_circle(s.cx[3], (s.cx[3], s.cx[3]), coef[3][t], u)
@@ -333,7 +327,7 @@
     for z in range(s.nz):
         t, g = divmod(z, group)
         strips = jnp.where((lane >= R * g) & (lane < R * g + R), left_ref[t], right_ref[t])
-        for at, x in ((0, extended(b_ref, lo_ref, hi_ref, z)), (LANES, turn(strips, -R * g))):
+        for at, x in ((0, extended(s, b_ref, lo_ref, hi_ref, z)), (LANES, turn(strips, -R * g))):
             high, low = halves(x)
             eh_ref[z * ext : (z + 1) * ext, at : at + LANES] = high
             el_ref[z * ext : (z + 1) * ext, at : at + LANES] = low
@@ -567,23 +561,19 @@
     c = {k: jnp.asarray(v) for k, v in constants(s).items()}
     brick = (s.nz, s.nx, s.ny)
     side = (R, s.nx, s.ny)
-    share, edge_rows = call(
-        functools.partial(share_kernel, s), "share", [charges],
-        arrays((s.tiles1, s.rows1, LANES), (s.nz, 2 * R, s.ny)), flops=8 * 10**8,
-    )
-    high_rows = fetch(edge_rows, gx=1)
-    low_rows = high_rows if s.gx == 2 else fetch(edge_rows, gx=-1)
-    shares = [share] + [fetch(share, gz=b) for b in range(1, s.gz)]
-    strips = (s.fine_tiles, s.ext, LANES)
-    first_cells, last_cells = call(
-        functools.partial(strip_kernel, s), "strips", [charges, low_rows, high_rows],
-        arrays(strips, strips), flops=4 * 10**8,
-    )
-    left, right = fetch(last_cells, gy=-1), fetch(first_cells, gy=1)
     taps, y0h, y0l = call(
         functools.partial(tap_kernel, s), "taps", [widths, amplitudes],
         arrays((16, LANES)) + two(2 * LANES, TERMS * s.ny), scalars=(0, 1), flops=6 * 10**8,
     )
+    high_rows = fetch(charges, gx=1)
+    low_rows = high_rows if s.gx == 2 else fetch(charges, gx=-1)
+    strips = (s.fine_tiles, s.ext, LANES)
+    share, first_cells, last_cells = call(
+        functools.partial(share_kernel, s), "share", [charges, low_rows, high_rows],
+        arrays((s.tiles1, s.rows1, LANES), strips, strips), after=[y0h], flops=10**9,
+    )
+    shares = [share] + [fetch(share, gz=b) for b in range(1, s.gz)]
+    left, right = fetch(last_cells, gy=-1), fetch(first_cells, gy=1)
     near, near_down, near_up = call(
         functools.partial(near_kernel, s), "near",
         [taps, charges, low_rows, high_rows, left, right, y0h, y0l],

time: 42.3 us -> 38.3 us (0.905)
  waiting for transfers between devices: 5.47 us -> 2.14 us
  Pallas kernels: 17.4 us -> 16.6 us
    ppermute x12, waiting for transfers between devices: 5.47 us -> 2.14 us  [fetch(): return lax.ppermute(x, names if len(names) > 1 else names[0], pairs)]
    pallas_call x10 -> x9, Pallas kernels: 17.4 us -> 16.6 us  [call(): pl.pallas_call(kernel, name=name, out_shape=out_shapes, in_specs=[spec(i)...]
    unnamed x32 -> x34, local copies, waits for them, and re-layouts: 1.13 us -> 1.46 us
  transfers between devices with their start and end apart: 12 -> 12, of which waited for: 4 -> 2; matrix products, arithmetic and copies ran while one was open for 0% -> 0% of each run, Pallas kernels for 37% -> 40%
where the time goes in v2:
time: 38.3 us; the launch traced here: 38.1 us
  starting transfers between devices  17.6 us (46%)
  Pallas kernels  16.6 us (43%)
  waiting for transfers between devices  2.14 us (6%)
  local copies, waits for them, and re-layouts  1.46 us (4%)
    ppermute x12, starting transfers between devices, fetch(): return lax.ppermute(x, names if len(names) > 1 else names[0], pairs)  17.6 us
    pallas_call x9, Pallas kernels, call(): pl.pallas_call(kernel, name=name, out_shape=out_shapes, in_specs=[spec(i)...  16.6 us
    ppermute x12, waiting for transfers between devices, fetch(): return lax.ppermute(x, names if len(names) > 1 else names[0], pairs)  2.14 us
    unnamed x34, local copies, waits for them, and re-layouts  1.46 us
  transfers between devices with their start and end apart: 12, of which 2 were waited for; matrix products, arithmetic and copies ran while one was open for 0% of the time, Pallas kernels for 40%

profile of v2, /device:TPU:0, one launch (start us, length us, event | category | flops | bytes accessed | tf_op | source)
XLA Modules:
  0.0 38.1 jit_solution(9530268711001863036)
XLA Ops:
  0.0 0.5 %collective-permute-start = (f32[16,64,128]{2,1,0:T(8,128)}, f32[16,64,128]{2,1,0:T(8,128)S(1)}, u32[]{:S(2)}, u32[]{:S(2)}) collective-permute-start(f32[16,64,128]{2,1,0:T(8,128)} %b_ref.3), channel_id=1, source_target_pairs={{16,0},{0,16},{17,1},{1,17},{18,2},{2,18},{19,3},{3,19},{20,4},{4,... | collective-permute-start | bytes 1572872 | tf_op jit(solution)/shard_map/ppermute | solution.py:552
  0.5 0.7 %copy-done.1 = f32[4,3]{1,0:T(4,128)S(1)} copy-done((f32[4,3]{1,0:T(4,128)S(1)}, f32[4,3]{1,0:T(4,128)}, u32[]{:S(2)}) %copy-start.1) | copy-done | bytes 72
  1.1 0.7 %copy-done.3 = f32[4,3]{1,0:T(4,128)S(1)} copy-done((f32[4,3]{1,0:T(4,128)S(1)}, f32[4,3]{1,0:T(4,128)}, u32[]{:S(2)}) %copy-start.3) | copy-done | bytes 72
  1.8 0.8 %taps.1 = (f32[16,128]{1,0:T(8,128)S(1)}, bf16[256,384]{1,0:T(8,128)(2,1)S(1)}, bf16[256,384]{1,0:T(8,128)(2,1)S(1)}) custom-call(f32[4,3]{1,0:T(4,128)S(1)} %copy-done.1, f32[4,3]{1,0:T(4,128)S(1)} %copy-done.3), custom_call_target="tpu_custom_call" | custom-call | flops 600000000 | bytes 401504 | tf_op jit(solution)/shard_map/taps/pallas_call | solution.py:529
  2.6 0.0 collective-permute-done.lo_ref.hi_ref
  2.6 0.7 %share.1 = (f32[6,32,128]{2,1,0:T(8,128)S(1)}, f32[1,80,128]{2,1,0:T(8,128)S(1)}, f32[1,80,128]{2,1,0:T(8,128)S(1)}) custom-call(f32[16,64,128]{2,1,0:T(8,128)S(1)} %copy-done, f32[16,64,128]{2,1,0:T(8,128)S(1)} %collective-permute-done.lo_ref.hi_ref, f32[16,64,128]{2,1,0:T(8,128)S(1)} %collective-permute-done.lo_ref.hi_ref, ...), custom_call_target="tpu_custom_call" | custom-call | flops 1000000000 | bytes 1949696 | tf_op jit(solution)/shard_map/share/pallas_call | solution.py:529
  3.3 2.6 %collective-permute-start.4 = (f32[1,80,128]{2,1,0:T(8,128)S(1)}, f32[1,80,128]{2,1,0:T(8,128)S(1)}, u32[]{:S(2)}, u32[]{:S(2)}) collective-permute-start(f32[1,80,128]{2,1,0:T(8,128)S(1)} %get-tuple-element.28), channel_id=1, source_target_pairs={{12,0},{0,4},{4,8},{8,12},{13,1},{1,5},{5,9},{9,13},{14,2},{2,6},{... | collective-permute-start | bytes 122888 | tf_op jit(solution)/shard_map/ppermute | solution.py:552
  5.9 1.0 %collective-permute-start.5 = (f32[1,80,128]{2,1,0:T(8,128)S(1)}, f32[1,80,128]{2,1,0:T(8,128)S(1)}, u32[]{:S(2)}, u32[]{:S(2)}) collective-permute-start(f32[1,80,128]{2,1,0:T(8,128)S(1)} %get-tuple-element.29), channel_id=1, source_target_pairs={{4,0},{8,4},{12,8},{0,12},{5,1},{9,5},{13,9},{1,13},{6,2},{10,6},{... | collective-permute-start | bytes 122888 | tf_op jit(solution)/shard_map/ppermute | solution.py:552
  6.9 2.0 %collective-permute-start.3 = (f32[6,32,128]{2,1,0:T(8,128)S(1)}, f32[6,32,128]{2,1,0:T(8,128)S(1)}, u32[]{:S(2)}, u32[]{:S(2)}) collective-permute-start(f32[6,32,128]{2,1,0:T(8,128)S(1)} %get-tuple-element.27.refs_0_), channel_id=1, source_target_pairs={{3,0},{0,1},{1,2},{2,3},{7,4},{4,5},{5,6},{6,7},{11,8},{8,9},{9,10... | collective-permute-start | bytes 294920 | tf_op jit(solution)/shard_map/ppermute | solution.py:552
  8.9 2.6 %collective-permute-start.2 = (f32[6,32,128]{2,1,0:T(8,128)S(1)}, f32[6,32,128]{2,1,0:T(8,128)S(1)}, u32[]{:S(2)}, u32[]{:S(2)}) collective-permute-start(f32[6,32,128]{2,1,0:T(8,128)S(1)} %get-tuple-element.27.refs_0_), channel_id=1, source_target_pairs={{2,0},{3,1},{0,2},{1,3},{6,4},{7,5},{4,6},{5,7},{10,8},{11,9},{8,1... | collective-permute-start | bytes 294920 | tf_op jit(solution)/shard_map/ppermute | solution.py:552
  11.5 1.3 %collective-permute-start.1 = (f32[6,32,128]{2,1,0:T(8,128)S(1)}, f32[6,32,128]{2,1,0:T(8,128)S(1)}, u32[]{:S(2)}, u32[]{:S(2)}) collective-permute-start(f32[6,32,128]{2,1,0:T(8,128)S(1)} %get-tuple-element.27.refs_0_), channel_id=1, source_target_pairs={{1,0},{2,1},{3,2},{0,3},{5,4},{6,5},{7,6},{4,7},{9,8},{10,9},{11,1... | collective-permute-start | bytes 294920 | tf_op jit(solution)/shard_map/ppermute | solution.py:552
  12.8 0.0 collective-permute-done.4.left_ref
  12.9 0.0 collective-permute-done.5.right_ref
  12.9 0.0 copy-start.12
  12.9 5.3 %near.1 = (f32[16,64,128]{2,1,0:T(8,128)S(1)}, f32[8,64,128]{2,1,0:T(8,128)S(1)}, f32[8,64,128]{2,1,0:T(8,128)S(1)}) custom-call(f32[16,128]{1,0:T(8,128)S(1)} %get-tuple-element.25.tap_ref, f32[16,64,128]{2,1,0:T(8,128)S(1)} %copy-done, f32[16,64,128]{2,1,0:T(8,128)S(1)} %collective-permute-done.lo_ref.hi_ref, ...), custom_call_target="tpu_custom_call" | custom-call | flops 6000000000 | bytes 3104768 | tf_op jit(solution)/shard_map/near/pallas_call | solution.py:529
  18.2 0.7 %collective-permute-start.9 = (f32[8,64,128]{2,1,0:T(8,128)S(1)}, f32[8,64,128]{2,1,0:T(8,128)S(1)}, u32[]{:S(2)}, u32[]{:S(2)}) collective-permute-start(f32[8,64,128]{2,1,0:T(8,128)S(1)} %get-tuple-element.43), channel_id=1, source_target_pairs={{3,0},{0,1},{1,2},{2,3},{7,4},{4,5},{5,6},{6,7},{11,8},{8,9},{9,10... | collective-permute-start | bytes 786440 | tf_op jit(solution)/shard_map/ppermute | solution.py:552
  18.9 3.1 %collective-permute-start.10 = (f32[8,64,128]{2,1,0:T(8,128)S(1)}, f32[8,64,128]{2,1,0:T(8,128)S(1)}, u32[]{:S(2)}, u32[]{:S(2)}) collective-permute-start(f32[8,64,128]{2,1,0:T(8,128)S(1)} %get-tuple-element.44), channel_id=1, source_target_pairs={{1,0},{2,1},{3,2},{0,3},{5,4},{6,5},{7,6},{4,7},{9,8},{10,9},{11,1... | collective-permute-start | bytes 786440 | tf_op jit(solution)/shard_map/ppermute | solution.py:552
  22.1 0.0 collective-permute-done.3.refs_3_
  22.1 0.0 collective-permute-done.2.refs_2_
  22.1 0.0 collective-permute-done.1.refs_1_
  22.1 0.0 copy-start.2
  22.1 0.0 copy-start.4
  22.1 0.0 copy-start.5
  22.1 0.0 copy-start.6
  22.1 0.0 copy-start.7
  22.1 0.0 copy-start.8
  22.2 0.0 copy-start.9
  22.2 0.0 copy-start.11
  22.2 0.0 copy-start.13
  22.2 0.0 copy-start.14
  22.2 0.0 copy-start.15
  22.2 0.0 copy-start.16
  22.2 1.5 %depth.1 = (f32[33,32,128]{2,1,0:T(8,128)S(1)}, f32[216,128]{1,0:T(8,128)S(1)}, f32[216,128]{1,0:T(8,128)S(1)}, f32[120,128]{1,0:T(8,128)S(1)}) custom-call(f32[16,128]{1,0:T(8,128)S(1)} %get-tuple-element.25.tap_ref, f32[6,32,128]{2,1,0:T(8,128)S(1)} %get-tuple-element.27.refs_0_, f32[6,32,128]{2,1,0:T(8,128)S(1)} %collective-permute-done.1.refs_1_, ...), custom_call_target="tpu_custom_call" | custom-call | flops 2000000000 | bytes 1817600 | tf_op jit(solution)/shard_map/depth/pallas_call | solution.py:529
  23.7 1.6 %collective-permute-start.7 = (f32[120,128]{1,0:T(8,128)S(1)}, f32[120,128]{1,0:T(8,128)S(1)}, u32[]{:S(2)}, u32[]{:S(2)}) collective-permute-start(f32[120,128]{1,0:T(8,128)S(1)} %get-tuple-element.32._.refs_0_), channel_id=1, source_target_pairs={{8,0},{12,4},{0,8},{4,12},{9,1},{13,5},{1,9},{5,13},{10,2},{14,6},... | collective-permute-start | bytes 184328 | tf_op jit(solution)/shard_map/ppermute | solution.py:552
  25.3 0.5 %collective-permute-start.6 = (f32[216,128]{1,0:T(8,128)S(1)}, f32[216,128]{1,0:T(8,128)S(1)}, u32[]{:S(2)}, u32[]{:S(2)}) collective-permute-start(f32[216,128]{1,0:T(8,128)S(1)} %get-tuple-element.35), channel_id=1, source_target_pairs={{4,0},{8,4},{12,8},{0,12},{5,1},{9,5},{13,9},{1,13},{6,2},{10,6},{... | collective-permute-start | bytes 331784 | tf_op jit(solution)/shard_map/ppermute | solution.py:552
  25.8 1.5 %collective-permute-start.8 = (f32[216,128]{1,0:T(8,128)S(1)}, f32[216,128]{1,0:T(8,128)S(1)}, u32[]{:S(2)}, u32[]{:S(2)}) collective-permute-start(f32[216,128]{1,0:T(8,128)S(1)} %get-tuple-element.36), channel_id=1, source_target_pairs={{12,0},{0,4},{4,8},{8,12},{13,1},{1,5},{5,9},{9,13},{14,2},{2,6},{... | collective-permute-start | bytes 331784 | tf_op jit(solution)/shard_map/ppermute | solution.py:552
  27.4 3.0 %matrices.1 = (f32[96,128]{1,0:T(8,128)S(1)}, bf16[128,384]{1,0:T(8,128)(2,1)S(1)}, bf16[128,384]{1,0:T(8,128)(2,1)S(1)}, bf16[128,768]{1,0:T(8,128)(2,1)S(1)}, ...) custom-call(f32[4,3]{1,0:T(4,128)S(1)} %copy-done.2, ...), custom_call_target="tpu_custom_call" | custom-call | flops 3000000000 | bytes 1150048 | tf_op jit(solution)/shard_map/matrices/pallas_call | solution.py:529
  30.4 0.0 collective-permute-done.7.refs_2_
  30.4 0.0 collective-permute-done.6.refs_1_
  30.4 1.0 %collective-permute-done.8.refs_3_ = f32[216,128]{1,0:T(8,128)S(1)} collective-permute-done((f32[216,128]{1,0:T(8,128)S(1)}, f32[216,128]{1,0:T(8,128)S(1)}, u32[]{:S(2)}, u32[]{:S(2)}) %collective-permute-start.8) | collective-permute-done | bytes 110624 | tf_op jit(solution)/shard_map/ppermute | solution.py:552
  31.4 3.5 %along.1.d_ref = f32[240,1408]{1,0:T(8,128)S(1)} custom-call(f32[96,128]{1,0:T(8,128)S(1)} %get-tuple-element.33.z_ref, f32[33,32,128]{2,1,0:T(8,128)S(1)} %get-tuple-element.34.w_ref, f32[120,128]{1,0:T(8,128)S(1)} %get-tuple-element.32._.refs_0_, f32[216,128]{1,0:T(8,128)S(1)} %collective-permute-done.6.refs_1_, ...), custom_call_target="tpu_custom_call" | custom-call | flops 3000000000 | bytes 2875392 | tf_op jit(solution)/shard_map/along/pallas_call | solution.py:529
  34.9 0.5 %away.1 = f32[64,1408]{1,0:T(8,128)S(1)} custom-call(f32[240,1408]{1,0:T(8,128)S(1)} %along.1.d_ref, bf16[128,240]{1,0:T(8,128)(2,1)S(1)} %get-tuple-element.41.xh_ref, bf16[128,240]{1,0:T(8,128)(2,1)S(1)} %get-tuple-element.42.xl_ref), custom_call_target="tpu_custom_call" | custom-call | flops 1000000000 | bytes 1835008 | tf_op jit(solution)/shard_map/away/pallas_call | solution.py:529
  35.5 0.1 collective-permute-start.11
  35.5 0.0 collective-permute-done.9.low_ref
  35.6 0.0 collective-permute-done.10.high_ref
  35.6 0.6 %home.1.home_ref = f32[16,64,128]{2,1,0:T(8,128)S(1)} custom-call(f32[240,1408]{1,0:T(8,128)S(1)} %along.1.d_ref, bf16[128,240]{1,0:T(8,128)(2,1)S(1)} %get-tuple-element.41.xh_ref, bf16[128,240]{1,0:T(8,128)(2,1)S(1)} %get-tuple-element.42.xl_ref, f32[16,64,128]{2,1,0:T(8,128)S(1)} %get-tuple-element.31.refs_6_.own_ref, ...), custom_call_target="tpu_custom_call" | custom-call | flops 2000000000 | bytes 3047424 | tf_op jit(solution)/shard_map/home/pallas_call | solution.py:529
  36.1 1.1 %collective-permute-done.11.refs_0_ = f32[64,1408]{1,0:T(8,128)S(1)} collective-permute-done((f32[64,1408]{1,0:T(8,128)S(1)}, f32[64,1408]{1,0:T(8,128)S(1)}, u32[]{:S(2)}, u32[]{:S(2)}) %collective-permute-start.11) | collective-permute-done | bytes 360480 | tf_op jit(solution)/shard_map/ppermute | solution.py:552
  37.2 0.9 %last.1 = f32[16,64,128]{2,1,0:T(8,128)} custom-call(f32[16,64,128]{2,1,0:T(8,128)S(1)} %home.1.home_ref, f32[64,1408]{1,0:T(8,128)S(1)} %collective-permute-done.11.refs_0_), custom_call_target="tpu_custom_call" | custom-call | flops 1000000000 | bytes 1409024 | tf_op jit(solution)/shard_map/last/pallas_call | solution.py:529
  (19 shorter events, 0.0 us)
Async XLA Ops:
  0.0 2.6 %copy-start = (f32[16,64,128]{2,1,0:T(8,128)S(1)}, f32[16,64,128]{2,1,0:T(8,128)}, u32[]{:S(2)}) copy-start(f32[16,64,128]{2,1,0:T(8,128)} %b_ref.3) | copy-start | bytes 1572868
  0.0 2.6 %collective-permute-start = (f32[16,64,128]{2,1,0:T(8,128)}, f32[16,64,128]{2,1,0:T(8,128)S(1)}, u32[]{:S(2)}, u32[]{:S(2)}) collective-permute-start(f32[16,64,128]{2,1,0:T(8,128)} %b_ref.3), channel_id=1, source_target_pairs={{16,0},{0,16},{17,1},{1,17},{18,2},{2,18},{19,3},{3,19},{20,4},{4,... | collective-permute-start | bytes 1572872 | tf_op jit(solution)/shard_map/ppermute | solution.py:552
  0.5 0.7 %copy-start.1 = (f32[4,3]{1,0:T(4,128)S(1)}, f32[4,3]{1,0:T(4,128)}, u32[]{:S(2)}) copy-start(f32[4,3]{1,0:T(4,128)} %w_ref.3) | copy-start | bytes 148
  1.1 0.7 %copy-start.3 = (f32[4,3]{1,0:T(4,128)S(1)}, f32[4,3]{1,0:T(4,128)}, u32[]{:S(2)}) copy-start(f32[4,3]{1,0:T(4,128)} %a_ref.3) | copy-start | bytes 148
  3.3 9.6 %collective-permute-start.4 = (f32[1,80,128]{2,1,0:T(8,128)S(1)}, f32[1,80,128]{2,1,0:T(8,128)S(1)}, u32[]{:S(2)}, u32[]{:S(2)}) collective-permute-start(f32[1,80,128]{2,1,0:T(8,128)S(1)} %get-tuple-element.28), channel_id=1, source_target_pairs={{12,0},{0,4},{4,8},{8,12},{13,1},{1,5},{5,9},{9,13},{14,2},{2,6},{... | collective-permute-start | bytes 122888 | tf_op jit(solution)/shard_map/ppermute | solution.py:552
  5.9 7.0 %collective-permute-start.5 = (f32[1,80,128]{2,1,0:T(8,128)S(1)}, f32[1,80,128]{2,1,0:T(8,128)S(1)}, u32[]{:S(2)}, u32[]{:S(2)}) collective-permute-start(f32[1,80,128]{2,1,0:T(8,128)S(1)} %get-tuple-element.29), channel_id=1, source_target_pairs={{4,0},{8,4},{12,8},{0,12},{5,1},{9,5},{13,9},{1,13},{6,2},{10,6},{... | collective-permute-start | bytes 122888 | tf_op jit(solution)/shard_map/ppermute | solution.py:552
  6.9 15.1 %collective-permute-start.3 = (f32[6,32,128]{2,1,0:T(8,128)S(1)}, f32[6,32,128]{2,1,0:T(8,128)S(1)}, u32[]{:S(2)}, u32[]{:S(2)}) collective-permute-start(f32[6,32,128]{2,1,0:T(8,128)S(1)} %get-tuple-element.27.refs_0_), channel_id=1, source_target_pairs={{3,0},{0,1},{1,2},{2,3},{7,4},{4,5},{5,6},{6,7},{11,8},{8,9},{9,10... | collective-permute-start | bytes 294920 | tf_op jit(solution)/shard_map/ppermute | solution.py:552
  8.9 13.1 %collective-permute-start.2 = (f32[6,32,128]{2,1,0:T(8,128)S(1)}, f32[6,32,128]{2,1,0:T(8,128)S(1)}, u32[]{:S(2)}, u32[]{:S(2)}) collective-permute-start(f32[6,32,128]{2,1,0:T(8,128)S(1)} %get-tuple-element.27.refs_0_), channel_id=1, source_target_pairs={{2,0},{3,1},{0,2},{1,3},{6,4},{7,5},{4,6},{5,7},{10,8},{11,9},{8,1... | collective-permute-start | bytes 294920 | tf_op jit(solution)/shard_map/ppermute | solution.py:552
  11.5 10.6 %collective-permute-start.1 = (f32[6,32,128]{2,1,0:T(8,128)S(1)}, f32[6,32,128]{2,1,0:T(8,128)S(1)}, u32[]{:S(2)}, u32[]{:S(2)}) collective-permute-start(f32[6,32,128]{2,1,0:T(8,128)S(1)} %get-tuple-element.27.refs_0_), channel_id=1, source_target_pairs={{1,0},{2,1},{3,2},{0,3},{5,4},{6,5},{7,6},{4,7},{9,8},{10,9},{11,1... | collective-permute-start | bytes 294920 | tf_op jit(solution)/shard_map/ppermute | solution.py:552
  12.9 9.2 %copy-start.10 = (f32[128,128]{1,0:T(8,128)S(1)}, f32[128,128]{1,0:T(8,128)}, u32[]{:S(2)}) copy-start(f32[128,128]{1,0:T(8,128)} %constant.24.clone.refs_4_) | copy-start | bytes 196612
  12.9 9.2 %copy-start.12 = (f32[24,32]{1,0:T(8,128)S(1)}, f32[24,32]{1,0:T(8,128)}, u32[]{:S(2)}) copy-start(f32[24,32]{1,0:T(8,128)} %constant.25.clone.refs_5_) | copy-start | bytes 9220
  18.2 17.4 %collective-permute-start.9 = (f32[8,64,128]{2,1,0:T(8,128)S(1)}, f32[8,64,128]{2,1,0:T(8,128)S(1)}, u32[]{:S(2)}, u32[]{:S(2)}) collective-permute-start(f32[8,64,128]{2,1,0:T(8,128)S(1)} %get-tuple-element.43), channel_id=1, source_target_pairs={{3,0},{0,1},{1,2},{2,3},{7,4},{4,5},{5,6},{6,7},{11,8},{8,9},{9,10... | collective-permute-start | bytes 786440 | tf_op jit(solution)/shard_map/ppermute | solution.py:552
  18.9 16.7 %collective-permute-start.10 = (f32[8,64,128]{2,1,0:T(8,128)S(1)}, f32[8,64,128]{2,1,0:T(8,128)S(1)}, u32[]{:S(2)}, u32[]{:S(2)}) collective-permute-start(f32[8,64,128]{2,1,0:T(8,128)S(1)} %get-tuple-element.44), channel_id=1, source_target_pairs={{1,0},{2,1},{3,2},{0,3},{5,4},{6,5},{7,6},{4,7},{9,8},{10,9},{11,1... | collective-permute-start | bytes 786440 | tf_op jit(solution)/shard_map/ppermute | solution.py:552
  22.1 5.2 %copy-start.2 = (f32[4,3]{1,0:T(4,128)S(1)}, f32[4,3]{1,0:T(4,128)}, u32[]{:S(2)}) copy-start(f32[4,3]{1,0:T(4,128)} %w_ref.3) | copy-start | bytes 148
  22.1 5.2 %copy-start.4 = (f32[4,3]{1,0:T(4,128)S(1)}, f32[4,3]{1,0:T(4,128)}, u32[]{:S(2)}) copy-start(f32[4,3]{1,0:T(4,128)} %a_ref.3) | copy-start | bytes 148
  22.1 5.2 %copy-start.5 = (f32[256,128]{1,0:T(8,128)S(1)}, f32[256,128]{1,0:T(8,128)}, u32[]{:S(2)}) copy-start(f32[256,128]{1,0:T(8,128)} %constant.30.clone.py1) | copy-start | bytes 393220
  22.1 5.2 %copy-start.6 = (f32[128,128]{1,0:T(8,128)S(1)}, f32[128,128]{1,0:T(8,128)}, u32[]{:S(2)}) copy-start(f32[128,128]{1,0:T(8,128)} %constant.31.clone.py2) | copy-start | bytes 196612
  22.1 5.2 %copy-start.7 = (f32[128,16]{1,0:T(8,128)S(1)}, f32[128,16]{1,0:T(8,128)}, u32[]{:S(2)}) copy-start(f32[128,16]{1,0:T(8,128)} %constant.28.clone.px3) | copy-start | bytes 24580
  22.1 5.2 %copy-start.8 = (f32[128,32]{1,0:T(8,128)S(1)}, f32[128,32]{1,0:T(8,128)}, u32[]{:S(2)}) copy-start(f32[128,32]{1,0:T(8,128)} %constant.27.clone.px2) | copy-start | bytes 49156
  22.2 5.2 %copy-start.9 = (f32[128,64]{1,0:T(8,128)S(1)}, f32[128,64]{1,0:T(8,128)}, u32[]{:S(2)}) copy-start(f32[128,64]{1,0:T(8,128)} %constant.26.clone.px1.ry3) | copy-start | bytes 98308
  22.2 5.2 %copy-start.11 = (f32[64,128]{1,0:T(8,128)S(1)}, f32[64,128]{1,0:T(8,128)}, u32[]{:S(2)}) copy-start(f32[64,128]{1,0:T(8,128)} %constant.32.clone.py3) | copy-start | bytes 98308
  22.2 5.2 %copy-start.13 = (f32[16,8]{1,0:T(8,128)S(1)}, f32[16,8]{1,0:T(8,128)}, u32[]{:S(2)}) copy-start(f32[16,8]{1,0:T(8,128)} %constant.34.clone.pz3) | copy-start | bytes 1540
  22.2 5.2 %copy-start.14 = (f32[16,16]{1,0:T(8,128)S(1)}, f32[16,16]{1,0:T(8,128)}, u32[]{:S(2)}) copy-start(f32[16,16]{1,0:T(8,128)} %constant.33.clone.pz2) | copy-start | bytes 3076
  22.2 5.2 %copy-start.15 = (f32[16,24]{1,0:T(8,128)S(1)}, f32[16,24]{1,0:T(8,128)}, u32[]{:S(2)}) copy-start(f32[16,24]{1,0:T(8,128)} %constant.29.clone.rx3) | copy-start | bytes 4612
  22.2 5.2 %copy-start.16 = (f32[8,128]{1,0:T(8,128)S(1)}, f32[8,128]{1,0:T(8,128)}, u32[]{:S(2)}) copy-start(f32[8,128]{1,0:T(8,128)} %constant.35.clone.rz3) | copy-start | bytes 12292
  23.7 6.7 %collective-permute-start.7 = (f32[120,128]{1,0:T(8,128)S(1)}, f32[120,128]{1,0:T(8,128)S(1)}, u32[]{:S(2)}, u32[]{:S(2)}) collective-permute-start(f32[120,128]{1,0:T(8,128)S(1)} %get-tuple-element.32._.refs_0_), channel_id=1, source_target_pairs={{8,0},{12,4},{0,8},{4,12},{9,1},{13,5},{1,9},{5,13},{10,2},{14,6},... | collective-permute-start | bytes 184328 | tf_op jit(solution)/shard_map/ppermute | solution.py:552
  25.3 5.1 %collective-permute-start.6 = (f32[216,128]{1,0:T(8,128)S(1)}, f32[216,128]{1,0:T(8,128)S(1)}, u32[]{:S(2)}, u32[]{:S(2)}) collective-permute-start(f32[216,128]{1,0:T(8,128)S(1)} %get-tuple-element.35), channel_id=1, source_target_pairs={{4,0},{8,4},{12,8},{0,12},{5,1},{9,5},{13,9},{1,13},{6,2},{10,6},{... | collective-permute-start | bytes 331784 | tf_op jit(solution)/shard_map/ppermute | solution.py:552
  25.8 5.6 %collective-permute-start.8 = (f32[216,128]{1,0:T(8,128)S(1)}, f32[216,128]{1,0:T(8,128)S(1)}, u32[]{:S(2)}, u32[]{:S(2)}) collective-permute-start(f32[216,128]{1,0:T(8,128)S(1)} %get-tuple-element.36), channel_id=1, source_target_pairs={{12,0},{0,4},{4,8},{8,12},{13,1},{1,5},{5,9},{9,13},{14,2},{2,6},{... | collective-permute-start | bytes 331784 | tf_op jit(solution)/shard_map/ppermute | solution.py:552
  35.5 1.7 %collective-permute-start.11 = (f32[64,1408]{1,0:T(8,128)S(1)}, f32[64,1408]{1,0:T(8,128)S(1)}, u32[]{:S(2)}, u32[]{:S(2)}) collective-permute-start(f32[64,1408]{1,0:T(8,128)S(1)} %away.1), channel_id=1, source_target_pairs={{16,0},{0,16},{17,1},{1,17},{18,2},{2,18},{19,3},{3,19},{20,4},{4,... | collective-permute-start | bytes 1081352 | tf_op jit(solution)/shard_map/ppermute | solution.py:552

commit v3 on v2

--- a/solution.py
+++ b/solution.py
@@ -377,7 +377,7 @@
 
 def depth_kernel(s, tap_ref, *refs):
     m_refs = refs[: s.gz]
-    ry2_ref, rx2_ref, _, w_ref, down_ref, up_ref, c2_ref, c_ref = refs[s.gz :]
+    ry2_ref, rx2_ref, _, w_ref, send_ref, c_ref = refs[s.gz :]
     n = s.cz[1]
     parts = [[] for _ in range(n)]
     for b in range(s.gz):
@@ -418,23 +418,23 @@
     for j in range(s.cz[2]):
         high, low = halves(along[j * s.rows1 : (j + 1) * s.rows1])
         shares.append(dot(rx2, high) + dot(rx2, low))
-    for t in range(s.tiles_s):
-        down_ref[t * s.rows1 : (t + 1) * s.rows1] = down[t]
-        up_ref[t * s.rows1 : (t + 1) * s.rows1] = up[t]
+    me = lax.axis_index("gy")
     base = s.tiles_s * s.rows1
-    for t, x in enumerate(packed(shares, s.wide2, s.tiles2)):
-        rows = slice(t * s.rows2, (t + 1) * s.rows2)
-        c2_ref[rows] = x
-        for ref in (down_ref, up_ref):
-            ref[base + t * s.rows2 : base + (t + 1) * s.rows2] = x
-
-
-def along_kernel(s, z_ref, w_ref, *refs):
-    c2_refs = refs[: s.gy]
-    y1h_ref, y1l_ref, y2h_ref, y2l_ref, d_ref, yb_ref = refs[s.gy :]
+    coarse = packed(shares, s.wide2, s.tiles2)
+    for shift in range(s.gy):
+        slot = lax.rem(me + shift, s.gy)
+        strips = {1: up, s.gy - 1: down}.get(shift)
+        for t in range(s.tiles_s if strips else 0):
+            send_ref[slot, t * s.rows1 : (t + 1) * s.rows1] = strips[t]
+        for t, x in enumerate(coarse):
+            send_ref[slot, base + t * s.rows2 : base + (t + 1) * s.rows2] = x
+
+
+def along_kernel(s, z_ref, w_ref, got_ref, y1h_ref, y1l_ref, y2h_ref, y2l_ref, d_ref, yb_ref):
+    me = lax.axis_index("gy")
+    slots = [lax.rem(me + shift, s.gy) for shift in range(s.gy)]
     base = s.tiles_s * s.rows1
     lane = lanes_of((s.rows1, LANES))
-    above, below = c2_refs[1], c2_refs[-1]
     end = s.y1 + R
     for t in range(TERMS):
         cells = []
@@ -444,8 +444,8 @@
             rows = slice(tile * s.rows1, (tile + 1) * s.rows1)
             at = slot * s.strip
             x = turn(w_ref[k], R)
-            x += jnp.where(lane < s.strip, turn(below[rows], -at), 0.0)
-            x += jnp.where((lane >= end) & (lane < end + s.strip), turn(above[rows], end - at), 0.0)
+            x += jnp.where(lane < s.strip, turn(got_ref[slots[-1], rows], -at), 0.0)
+            x += jnp.where((lane >= end) & (lane < end + s.strip), turn(got_ref[slots[1], rows], end - at), 0.0)
             cells.append(x)
         columns = slice(t * s.ny, (t + 1) * s.ny)
         out = dot3(jnp.concatenate(cells, axis=0), y1h_ref[:, columns], y1l_ref[:, columns])
@@ -455,8 +455,7 @@
     for j in range(s.cz[2]):
         out = None
         for b in range(s.gy):
-            first = 0 if b == 0 or c2_refs[b].shape[0] == s.tiles2 * s.rows2 else base
-            tile = lambda t, b=b, f=first: c2_refs[b][f + t * s.rows2 : f + (t + 1) * s.rows2]
+            tile = lambda t, b=b: got_ref[slots[b], base + t * s.rows2 : base + (t + 1) * s.rows2]
             x = unpacked(tile, j, s.wide2, (b * s.y2 - 2) % LANES)
             out = x if out is None else out + x
         cells.append(out)
@@ -587,10 +586,10 @@
     base = s.tiles_s * s.rows1
     size2 = s.tiles2 * s.rows2
     depth = TERMS * (s.rows1 + 2 * s.rows2)
-    waves, to_low, to_high, coarse = call(
+    waves, send = call(
         functools.partial(depth_kernel, s), "depth",
         [taps] + shares + [c["ry2"], c["rx2"]],
-        arrays((TERMS * s.planes, s.rows1, LANES), (base + size2, LANES), (base + size2, LANES), (size2, LANES)),
+        arrays((TERMS * s.planes, s.rows1, LANES), (s.gy, base + size2, LANES)),
         scalars=(0,), after=[near], scratch=[pltpu.VMEM((s.cz[1], s.rows1, LANES), F32)], flops=2 * 10**9,
     )
     named = ("px1", "px2", "px3", "rx3", "py1", "py2", "py3", "ry3", "pz2", "pz3", "rz3")
@@ -600,15 +599,13 @@
         arrays((2 * TERMS * s.zrows, LANES))
         + two(LANES, TERMS * s.ny) + two(s.cy[2], 2 * TERMS * s.ny)
         + two(s.cx[0], depth),
-        scalars=(0, 1), after=[coarse], flops=3 * 10**9,
-    )
-    coarses = [coarse]
-    for b in range(1, s.gy):
-        coarses.append(fetch({1: to_low, s.gy - 1: to_high}.get(b, coarse), gy=b))
+        scalars=(0, 1), after=[waves], flops=3 * 10**9,
+    )
+    got = lax.all_to_all(send, "gy", 0, 0)
     near_low, near_high = fetch(near_up, gz=-1), fetch(near_down, gz=1)
     (terms,) = call(
         functools.partial(along_kernel, s), "along",
-        [z_taps, waves] + coarses + [y1h, y1l, y2h, y2l],
+        [z_taps, waves, got, y1h, y1l, y2h, y2l],
         arrays((depth, s.planes * s.ny)), scalars=(0,),
         scratch=[pltpu.VMEM((2 * TERMS, s.cz[2], s.rows2, s.ny), F32)], flops=3 * 10**9,
     )

time: 38.3 us -> 42.4 us (1.11)
  local copies, waits for them, and re-layouts: 1.46 us -> 5.93 us
  waiting for transfers between devices: 2.14 us -> 1.09 us
  Pallas kernels: 16.6 us -> 17.4 us
    unnamed x34 -> x46, local copies, waits for them, and re-layouts: 1.46 us -> 5.93 us
    ppermute x12 -> x9, starting transfers between devices: 17.6 us -> 13.9 us  [fetch(): return lax.ppermute(x, names if len(names) > 1 else names[0], pairs)]
    all_to_all x0 -> x1, starting transfers between devices: none -> 3.46 us  [shards(): got = lax.all_to_all(send, 'gy', 0, 0)]
    ppermute x12 -> x9, waiting for transfers between devices: 2.14 us -> 1.09 us  [fetch(): return lax.ppermute(x, names if len(names) > 1 else names[0], pairs)]
    pallas_call x9, Pallas kernels: 16.6 us -> 17.4 us  [call(): pl.pallas_call(kernel, name=name, out_shape=out_shapes, in_specs=[spec(i)...]
  transfers between devices with their start and end apart: 12 -> 10, of which waited for: 2 -> 1; matrix products, arithmetic and copies ran while one was open for 0% -> 0% of each run, Pallas kernels for 40% -> 32%
where the time goes in v3:
time: 42.4 us; the launch traced here: 42.1 us
  starting transfers between devices  17.4 us (41%)
  Pallas kernels  17.4 us (41%)
  local copies, waits for them, and re-layouts  5.93 us (14%)
  waiting for transfers between devices  1.09 us (3%)
    pallas_call x9, Pallas kernels, call(): pl.pallas_call(kernel, name=name, out_shape=out_shapes, in_specs=[spec(i)...  17.4 us
    ppermute x9, starting transfers between devices, fetch(): return lax.ppermute(x, names if len(names) > 1 else names[0], pairs)  13.9 us
    unnamed x46, local copies, waits for them, and re-layouts  5.93 us
    all_to_all x1, starting transfers between devices, shards(): got = lax.all_to_all(send, 'gy', 0, 0)  3.46 us
    ppermute x9, waiting for transfers between devices, fetch(): return lax.ppermute(x, names if len(names) > 1 else names[0], pairs)  1.09 us
  transfers between devices with their start and end apart: 10, of which 1 were waited for; matrix products, arithmetic and copies ran while one was open for 0% of the time, Pallas kernels for 32%

profile of v3, /device:TPU:0, one launch (start us, length us, event | category | flops | bytes accessed | tf_op | source)
XLA Modules:
  0.0 42.1 jit_solution(17333048799790439029)
XLA Ops:
  0.0 0.5 %collective-permute-start = (f32[16,64,128]{2,1,0:T(8,128)}, f32[16,64,128]{2,1,0:T(8,128)S(1)}, u32[]{:S(2)}, u32[]{:S(2)}) collective-permute-start(f32[16,64,128]{2,1,0:T(8,128)} %b_ref.3), channel_id=1, source_target_pairs={{16,0},{0,16},{17,1},{1,17},{18,2},{2,18},{19,3},{3,19},{20,4},{4,... | collective-permute-start | bytes 1572872 | tf_op jit(solution)/shard_map/ppermute | solution.py:551
  0.5 0.7 %copy-done.1 = f32[4,3]{1,0:T(4,128)S(1)} copy-done((f32[4,3]{1,0:T(4,128)S(1)}, f32[4,3]{1,0:T(4,128)}, u32[]{:S(2)}) %copy-start.1) | copy-done | bytes 72
  1.1 0.7 %copy-done.3 = f32[4,3]{1,0:T(4,128)S(1)} copy-done((f32[4,3]{1,0:T(4,128)S(1)}, f32[4,3]{1,0:T(4,128)}, u32[]{:S(2)}) %copy-start.3) | copy-done | bytes 72
  1.8 0.8 %taps.1 = (f32[16,128]{1,0:T(8,128)S(1)}, bf16[256,384]{1,0:T(8,128)(2,1)S(1)}, bf16[256,384]{1,0:T(8,128)(2,1)S(1)}) custom-call(f32[4,3]{1,0:T(4,128)S(1)} %copy-done.1, f32[4,3]{1,0:T(4,128)S(1)} %copy-done.3), custom_call_target="tpu_custom_call" | custom-call | flops 600000000 | bytes 401504 | tf_op jit(solution)/shard_map/taps/pallas_call | solution.py:528
  2.6 0.0 collective-permute-done.lo_ref.hi_ref
  2.6 0.7 %share.1 = (f32[6,32,128]{2,1,0:T(8,128)S(1)}, f32[1,80,128]{2,1,0:T(8,128)S(1)}, f32[1,80,128]{2,1,0:T(8,128)S(1)}) custom-call(f32[16,64,128]{2,1,0:T(8,128)S(1)} %copy-done, f32[16,64,128]{2,1,0:T(8,128)S(1)} %collective-permute-done.lo_ref.hi_ref, f32[16,64,128]{2,1,0:T(8,128)S(1)} %collective-permute-done.lo_ref.hi_ref, ...), custom_call_target="tpu_custom_call" | custom-call | flops 1000000000 | bytes 1949696 | tf_op jit(solution)/shard_map/share/pallas_call | solution.py:528
  3.3 2.6 %collective-permute-start.4 = (f32[1,80,128]{2,1,0:T(8,128)S(1)}, f32[1,80,128]{2,1,0:T(8,128)S(1)}, u32[]{:S(2)}, u32[]{:S(2)}) collective-permute-start(f32[1,80,128]{2,1,0:T(8,128)S(1)} %get-tuple-element.26), channel_id=1, source_target_pairs={{12,0},{0,4},{4,8},{8,12},{13,1},{1,5},{5,9},{9,13},{14,2},{2,6},{... | collective-permute-start | bytes 122888 | tf_op jit(solution)/shard_map/ppermute | solution.py:551
  5.9 1.0 %collective-permute-start.5 = (f32[1,80,128]{2,1,0:T(8,128)S(1)}, f32[1,80,128]{2,1,0:T(8,128)S(1)}, u32[]{:S(2)}, u32[]{:S(2)}) collective-permute-start(f32[1,80,128]{2,1,0:T(8,128)S(1)} %get-tuple-element.27), channel_id=1, source_target_pairs={{4,0},{8,4},{12,8},{0,12},{5,1},{9,5},{13,9},{1,13},{6,2},{10,6},{... | collective-permute-start | bytes 122888 | tf_op jit(solution)/shard_map/ppermute | solution.py:551
  6.9 2.0 %collective-permute-start.3 = (f32[6,32,128]{2,1,0:T(8,128)S(1)}, f32[6,32,128]{2,1,0:T(8,128)S(1)}, u32[]{:S(2)}, u32[]{:S(2)}) collective-permute-start(f32[6,32,128]{2,1,0:T(8,128)S(1)} %get-tuple-element.25.refs_0_), channel_id=1, source_target_pairs={{3,0},{0,1},{1,2},{2,3},{7,4},{4,5},{5,6},{6,7},{11,8},{8,9},{9,10... | collective-permute-start | bytes 294920 | tf_op jit(solution)/shard_map/ppermute | solution.py:551
  8.9 2.6 %collective-permute-start.2 = (f32[6,32,128]{2,1,0:T(8,128)S(1)}, f32[6,32,128]{2,1,0:T(8,128)S(1)}, u32[]{:S(2)}, u32[]{:S(2)}) collective-permute-start(f32[6,32,128]{2,1,0:T(8,128)S(1)} %get-tuple-element.25.refs_0_), channel_id=1, source_target_pairs={{2,0},{3,1},{0,2},{1,3},{6,4},{7,5},{4,6},{5,7},{10,8},{11,9},{8,1... | collective-permute-start | bytes 294920 | tf_op jit(solution)/shard_map/ppermute | solution.py:551
  11.5 1.3 %collective-permute-start.1 = (f32[6,32,128]{2,1,0:T(8,128)S(1)}, f32[6,32,128]{2,1,0:T(8,128)S(1)}, u32[]{:S(2)}, u32[]{:S(2)}) collective-permute-start(f32[6,32,128]{2,1,0:T(8,128)S(1)} %get-tuple-element.25.refs_0_), channel_id=1, source_target_pairs={{1,0},{2,1},{3,2},{0,3},{5,4},{6,5},{7,6},{4,7},{9,8},{10,9},{11,1... | collective-permute-start | bytes 294920 | tf_op jit(solution)/shard_map/ppermute | solution.py:551
  12.8 0.0 collective-permute-done.4.left_ref
  12.9 0.0 collective-permute-done.5.right_ref
  12.9 0.0 copy-start.12
  12.9 5.3 %near.1 = (f32[16,64,128]{2,1,0:T(8,128)S(1)}, f32[8,64,128]{2,1,0:T(8,128)S(1)}, f32[8,64,128]{2,1,0:T(8,128)S(1)}) custom-call(f32[16,128]{1,0:T(8,128)S(1)} %get-tuple-element.23.tap_ref, f32[16,64,128]{2,1,0:T(8,128)S(1)} %copy-done, f32[16,64,128]{2,1,0:T(8,128)S(1)} %collective-permute-done.lo_ref.hi_ref, ...), custom_call_target="tpu_custom_call" | custom-call | flops 6000000000 | bytes 3104768 | tf_op jit(solution)/shard_map/near/pallas_call | solution.py:528
  18.2 0.0 collective-permute-done.3.refs_3_
  18.2 0.0 copy-start.2
  18.2 0.0 copy-start.4
  18.2 0.0 copy-start.5
  18.2 0.0 copy-start.6
  18.3 0.0 copy-start.7
  18.3 0.0 copy-start.8
  18.3 0.0 copy-start.9
  18.3 0.0 copy-start.11
  18.3 0.0 copy-start.13
  18.3 0.0 copy-start.14
  18.3 0.0 copy-start.15
  18.3 0.0 copy-start.16
  18.4 2.2 %depth.1 = (f32[33,32,128]{2,1,0:T(8,128)S(1)}, f32[4,216,128]{2,1,0:T(8,128)}) custom-call(f32[16,128]{1,0:T(8,128)S(1)} %get-tuple-element.23.tap_ref, f32[6,32,128]{2,1,0:T(8,128)S(1)} %get-tuple-element.25.refs_0_, f32[6,32,128]{2,1,0:T(8,128)S(1)} %collective-permute-done.1.refs_1_, f32[6,32,128]{2,1,0:T(8,128)S(1)} %collective-permute-done.2.refs_2_, ...), custom_call_target="tpu_custom_call" | custom-call | flops 2000000000 | bytes 1977344 | tf_op jit(solution)/shard_map/depth/pallas_call | solution.py:528
  20.6 3.5 %all-to-all-start = ((f32[4,216,128]{2,1,0:T(8,128)}), f32[4,216,128]{2,1,0:T(8,128)S(1)}, u32[]{:S(2)}, u32[]{:S(2)}) async-start(f32[4,216,128]{2,1,0:T(8,128)} %get-tuple-element.32), calls=%async_computation | async-start | bytes 884736 | tf_op jit(solution)/shard_map/all_to_all | solution.py:604
  24.1 2.5 %collective-permute-start.6 = (f32[8,64,128]{2,1,0:T(8,128)S(1)}, f32[8,64,128]{2,1,0:T(8,128)S(1)}, u32[]{:S(2)}, u32[]{:S(2)}) collective-permute-start(f32[8,64,128]{2,1,0:T(8,128)S(1)} %get-tuple-element.39), channel_id=1, source_target_pairs={{3,0},{0,1},{1,2},{2,3},{7,4},{4,5},{5,6},{6,7},{11,8},{8,9},{9,10... | collective-permute-start | bytes 786440 | tf_op jit(solution)/shard_map/ppermute | solution.py:551
  26.6 1.3 %collective-permute-start.7 = (f32[8,64,128]{2,1,0:T(8,128)S(1)}, f32[8,64,128]{2,1,0:T(8,128)S(1)}, u32[]{:S(2)}, u32[]{:S(2)}) collective-permute-start(f32[8,64,128]{2,1,0:T(8,128)S(1)} %get-tuple-element.40), channel_id=1, source_target_pairs={{1,0},{2,1},{3,2},{0,3},{5,4},{6,5},{7,6},{4,7},{9,8},{10,9},{11,1... | collective-permute-start | bytes 786440 | tf_op jit(solution)/shard_map/ppermute | solution.py:551
  28.0 3.0 %matrices.1 = (f32[96,128]{1,0:T(8,128)S(1)}, bf16[128,384]{1,0:T(8,128)(2,1)S(1)}, bf16[128,384]{1,0:T(8,128)(2,1)S(1)}, bf16[128,768]{1,0:T(8,128)(2,1)S(1)}, ...) custom-call(f32[4,3]{1,0:T(4,128)S(1)} %copy-done.2, ...), custom_call_target="tpu_custom_call" | custom-call | flops 3000000000 | bytes 1629280 | tf_op jit(solution)/shard_map/matrices/pallas_call | solution.py:528
  31.0 0.6 %copy-done.17 = bf16[128,384]{1,0:T(8,128)(2,1)} copy-done((bf16[128,384]{1,0:T(8,128)(2,1)}, bf16[128,384]{1,0:T(8,128)(2,1)S(1)}, u32[]{:S(2)}) %copy-start.17) | copy-done | bytes 98328
  31.7 0.6 %copy-done.19 = bf16[128,384]{1,0:T(8,128)(2,1)} copy-done((bf16[128,384]{1,0:T(8,128)(2,1)}, bf16[128,384]{1,0:T(8,128)(2,1)S(1)}, u32[]{:S(2)}) %copy-start.19) | copy-done | bytes 98328
  32.3 0.6 %copy-done.21 = f32[96,128]{1,0:T(8,128)} copy-done((f32[96,128]{1,0:T(8,128)}, f32[96,128]{1,0:T(8,128)S(1)}, u32[]{:S(2)}) %copy-start.21) | copy-done | bytes 49176
  32.9 0.0 all-to-all-done.got_ref
  32.9 0.9 %copy-done.18 = bf16[128,384]{1,0:T(8,128)(2,1)S(1)} copy-done((bf16[128,384]{1,0:T(8,128)(2,1)S(1)}, bf16[128,384]{1,0:T(8,128)(2,1)}, u32[]{:S(2)}) %copy-start.18) | copy-done | bytes 98328
  33.8 0.9 %copy-done.20 = bf16[128,384]{1,0:T(8,128)(2,1)S(1)} copy-done((bf16[128,384]{1,0:T(8,128)(2,1)S(1)}, bf16[128,384]{1,0:T(8,128)(2,1)}, u32[]{:S(2)}) %copy-start.20) | copy-done | bytes 98328
  34.7 0.8 %copy-done.22 = f32[96,128]{1,0:T(8,128)S(1)} copy-done((f32[96,128]{1,0:T(8,128)S(1)}, f32[96,128]{1,0:T(8,128)}, u32[]{:S(2)}) %copy-start.22) | copy-done | bytes 49176
  35.5 3.5 %along.1.d_ref = f32[240,1408]{1,0:T(8,128)S(1)} custom-call(f32[96,128]{1,0:T(8,128)S(1)} %copy-done.22, f32[33,32,128]{2,1,0:T(8,128)S(1)} %get-tuple-element.30._.w_ref, f32[4,216,128]{2,1,0:T(8,128)S(1)} %all-to-all-done.got_ref, bf16[128,384]{1,0:T(8,128)(2,1)S(1)} %copy-done.18, bf16[128,384]{1,0:T(8,128)(2,1)S(1)} %copy-done.20, ...), custom_call_target="tpu_custom_call" | custom-call | flops 3000000000 | bytes 2973696 | tf_op jit(solution)/shard_map/along/pallas_call | solution.py:528
  39.0 0.5 %away.1 = f32[64,1408]{1,0:T(8,128)S(1)} custom-call(f32[240,1408]{1,0:T(8,128)S(1)} %along.1.d_ref, bf16[128,240]{1,0:T(8,128)(2,1)S(1)} %get-tuple-element.37.xh_ref, bf16[128,240]{1,0:T(8,128)(2,1)S(1)} %get-tuple-element.38.xl_ref), custom_call_target="tpu_custom_call" | custom-call | flops 1000000000 | bytes 1835008 | tf_op jit(solution)/shard_map/away/pallas_call | solution.py:528
  39.5 0.1 collective-permute-start.8
  39.6 0.0 collective-permute-done.6.low_ref
  39.6 0.0 collective-permute-done.7.high_ref
  39.6 0.6 %home.1.home_ref = f32[16,64,128]{2,1,0:T(8,128)S(1)} custom-call(f32[240,1408]{1,0:T(8,128)S(1)} %along.1.d_ref, bf16[128,240]{1,0:T(8,128)(2,1)S(1)} %get-tuple-element.37.xh_ref, bf16[128,240]{1,0:T(8,128)(2,1)S(1)} %get-tuple-element.38.xl_ref, f32[16,64,128]{2,1,0:T(8,128)S(1)} %get-tuple-element.29.refs_6_.own_ref, ...), custom_call_target="tpu_custom_call" | custom-call | flops 2000000000 | bytes 3047424 | tf_op jit(solution)/shard_map/home/pallas_call | solution.py:528
  40.2 1.1 %collective-permute-done.8.refs_0_ = f32[64,1408]{1,0:T(8,128)S(1)} collective-permute-done((f32[64,1408]{1,0:T(8,128)S(1)}, f32[64,1408]{1,0:T(8,128)S(1)}, u32[]{:S(2)}, u32[]{:S(2)}) %collective-permute-start.8) | collective-permute-done | bytes 360480 | tf_op jit(solution)/shard_map/ppermute | solution.py:551
  41.2 0.9 %last.1 = f32[16,64,128]{2,1,0:T(8,128)} custom-call(f32[16,64,128]{2,1,0:T(8,128)S(1)} %home.1.home_ref, f32[64,1408]{1,0:T(8,128)S(1)} %collective-permute-done.8.refs_0_), custom_call_target="tpu_custom_call" | custom-call | flops 1000000000 | bytes 1409024 | tf_op jit(solution)/shard_map/last/pallas_call | solution.py:528
  (27 shorter events, 0.1 us)
Async XLA Ops:
  0.0 2.6 %copy-start = (f32[16,64,128]{2,1,0:T(8,128)S(1)}, f32[16,64,128]{2,1,0:T(8,128)}, u32[]{:S(2)}) copy-start(f32[16,64,128]{2,1,0:T(8,128)} %b_ref.3) | copy-start | bytes 1572868
  0.0 2.6 %collective-permute-start = (f32[16,64,128]{2,1,0:T(8,128)}, f32[16,64,128]{2,1,0:T(8,128)S(1)}, u32[]{:S(2)}, u32[]{:S(2)}) collective-permute-start(f32[16,64,128]{2,1,0:T(8,128)} %b_ref.3), channel_id=1, source_target_pairs={{16,0},{0,16},{17,1},{1,17},{18,2},{2,18},{19,3},{3,19},{20,4},{4,... | collective-permute-start | bytes 1572872 | tf_op jit(solution)/shard_map/ppermute | solution.py:551
  0.5 0.7 %copy-start.1 = (f32[4,3]{1,0:T(4,128)S(1)}, f32[4,3]{1,0:T(4,128)}, u32[]{:S(2)}) copy-start(f32[4,3]{1,0:T(4,128)} %w_ref.3) | copy-start | bytes 148
  1.1 0.7 %copy-start.3 = (f32[4,3]{1,0:T(4,128)S(1)}, f32[4,3]{1,0:T(4,128)}, u32[]{:S(2)}) copy-start(f32[4,3]{1,0:T(4,128)} %a_ref.3) | copy-start | bytes 148
  3.3 9.6 %collective-permute-start.4 = (f32[1,80,128]{2,1,0:T(8,128)S(1)}, f32[1,80,128]{2,1,0:T(8,128)S(1)}, u32[]{:S(2)}, u32[]{:S(2)}) collective-permute-start(f32[1,80,128]{2,1,0:T(8,128)S(1)} %get-tuple-element.26), channel_id=1, source_target_pairs={{12,0},{0,4},{4,8},{8,12},{13,1},{1,5},{5,9},{9,13},{14,2},{2,6},{... | collective-permute-start | bytes 122888 | tf_op jit(solution)/shard_map/ppermute | solution.py:551
  5.9 7.0 %collective-permute-start.5 = (f32[1,80,128]{2,1,0:T(8,128)S(1)}, f32[1,80,128]{2,1,0:T(8,128)S(1)}, u32[]{:S(2)}, u32[]{:S(2)}) collective-permute-start(f32[1,80,128]{2,1,0:T(8,128)S(1)} %get-tuple-element.27), channel_id=1, source_target_pairs={{4,0},{8,4},{12,8},{0,12},{5,1},{9,5},{13,9},{1,13},{6,2},{10,6},{... | collective-permute-start | bytes 122888 | tf_op jit(solution)/shard_map/ppermute | solution.py:551
  6.9 11.2 %collective-permute-start.3 = (f32[6,32,128]{2,1,0:T(8,128)S(1)}, f32[6,32,128]{2,1,0:T(8,128)S(1)}, u32[]{:S(2)}, u32[]{:S(2)}) collective-permute-start(f32[6,32,128]{2,1,0:T(8,128)S(1)} %get-tuple-element.25.refs_0_), channel_id=1, source_target_pairs={{3,0},{0,1},{1,2},{2,3},{7,4},{4,5},{5,6},{6,7},{11,8},{8,9},{9,10... | collective-permute-start | bytes 294920 | tf_op jit(solution)/shard_map/ppermute | solution.py:551
  8.9 9.3 %collective-permute-start.2 = (f32[6,32,128]{2,1,0:T(8,128)S(1)}, f32[6,32,128]{2,1,0:T(8,128)S(1)}, u32[]{:S(2)}, u32[]{:S(2)}) collective-permute-start(f32[6,32,128]{2,1,0:T(8,128)S(1)} %get-tuple-element.25.refs_0_), channel_id=1, source_target_pairs={{2,0},{3,1},{0,2},{1,3},{6,4},{7,5},{4,6},{5,7},{10,8},{11,9},{8,1... | collective-permute-start | bytes 294920 | tf_op jit(solution)/shard_map/ppermute | solution.py:551
  11.5 6.7 %collective-permute-start.1 = (f32[6,32,128]{2,1,0:T(8,128)S(1)}, f32[6,32,128]{2,1,0:T(8,128)S(1)}, u32[]{:S(2)}, u32[]{:S(2)}) collective-permute-start(f32[6,32,128]{2,1,0:T(8,128)S(1)} %get-tuple-element.25.refs_0_), channel_id=1, source_target_pairs={{1,0},{2,1},{3,2},{0,3},{5,4},{6,5},{7,6},{4,7},{9,8},{10,9},{11,1... | collective-permute-start | bytes 294920 | tf_op jit(solution)/shard_map/ppermute | solution.py:551
  12.9 5.3 %copy-start.10 = (f32[128,128]{1,0:T(8,128)S(1)}, f32[128,128]{1,0:T(8,128)}, u32[]{:S(2)}) copy-start(f32[128,128]{1,0:T(8,128)} %constant.24.clone.refs_4_) | copy-start | bytes 196612
  12.9 5.3 %copy-start.12 = (f32[24,32]{1,0:T(8,128)S(1)}, f32[24,32]{1,0:T(8,128)}, u32[]{:S(2)}) copy-start(f32[24,32]{1,0:T(8,128)} %constant.25.clone.refs_5_) | copy-start | bytes 9220
  18.2 9.7 %copy-start.2 = (f32[4,3]{1,0:T(4,128)S(1)}, f32[4,3]{1,0:T(4,128)}, u32[]{:S(2)}) copy-start(f32[4,3]{1,0:T(4,128)} %w_ref.3) | copy-start | bytes 148
  18.2 9.7 %copy-start.4 = (f32[4,3]{1,0:T(4,128)S(1)}, f32[4,3]{1,0:T(4,128)}, u32[]{:S(2)}) copy-start(f32[4,3]{1,0:T(4,128)} %a_ref.3) | copy-start | bytes 148
  18.2 9.7 %copy-start.5 = (f32[256,128]{1,0:T(8,128)S(1)}, f32[256,128]{1,0:T(8,128)}, u32[]{:S(2)}) copy-start(f32[256,128]{1,0:T(8,128)} %constant.30.clone.py1) | copy-start | bytes 393220
  18.2 9.7 %copy-start.6 = (f32[128,128]{1,0:T(8,128)S(1)}, f32[128,128]{1,0:T(8,128)}, u32[]{:S(2)}) copy-start(f32[128,128]{1,0:T(8,128)} %constant.31.clone.py2) | copy-start | bytes 196612
  18.3 9.7 %copy-start.7 = (f32[128,16]{1,0:T(8,128)S(1)}, f32[128,16]{1,0:T(8,128)}, u32[]{:S(2)}) copy-start(f32[128,16]{1,0:T(8,128)} %constant.28.clone.px3) | copy-start | bytes 24580
  18.3 9.7 %copy-start.8 = (f32[128,32]{1,0:T(8,128)S(1)}, f32[128,32]{1,0:T(8,128)}, u32[]{:S(2)}) copy-start(f32[128,32]{1,0:T(8,128)} %constant.27.clone.px2) | copy-start | bytes 49156
  18.3 9.7 %copy-start.9 = (f32[128,64]{1,0:T(8,128)S(1)}, f32[128,64]{1,0:T(8,128)}, u32[]{:S(2)}) copy-start(f32[128,64]{1,0:T(8,128)} %constant.26.clone.px1.ry3) | copy-start | bytes 98308
  18.3 9.7 %copy-start.11 = (f32[64,128]{1,0:T(8,128)S(1)}, f32[64,128]{1,0:T(8,128)}, u32[]{:S(2)}) copy-start(f32[64,128]{1,0:T(8,128)} %constant.32.clone.py3) | copy-start | bytes 98308
  18.3 9.7 %copy-start.13 = (f32[16,8]{1,0:T(8,128)S(1)}, f32[16,8]{1,0:T(8,128)}, u32[]{:S(2)}) copy-start(f32[16,8]{1,0:T(8,128)} %constant.34.clone.pz3) | copy-start | bytes 1540
  18.3 9.7 %copy-start.14 = (f32[16,16]{1,0:T(8,128)S(1)}, f32[16,16]{1,0:T(8,128)}, u32[]{:S(2)}) copy-start(f32[16,16]{1,0:T(8,128)} %constant.33.clone.pz2) | copy-start | bytes 3076
  18.3 9.7 %copy-start.15 = (f32[16,24]{1,0:T(8,128)S(1)}, f32[16,24]{1,0:T(8,128)}, u32[]{:S(2)}) copy-start(f32[16,24]{1,0:T(8,128)} %constant.29.clone.rx3) | copy-start | bytes 4612
  18.3 9.7 %copy-start.16 = (f32[8,128]{1,0:T(8,128)S(1)}, f32[8,128]{1,0:T(8,128)}, u32[]{:S(2)}) copy-start(f32[8,128]{1,0:T(8,128)} %constant.35.clone.rz3) | copy-start | bytes 12292
  20.6 12.3 %all-to-all-start = ((f32[4,216,128]{2,1,0:T(8,128)}), f32[4,216,128]{2,1,0:T(8,128)S(1)}, u32[]{:S(2)}, u32[]{:S(2)}) async-start(f32[4,216,128]{2,1,0:T(8,128)} %get-tuple-element.32), calls=%async_computation | async-start | bytes 884736 | tf_op jit(solution)/shard_map/all_to_all | solution.py:604
  24.1 15.5 %collective-permute-start.6 = (f32[8,64,128]{2,1,0:T(8,128)S(1)}, f32[8,64,128]{2,1,0:T(8,128)S(1)}, u32[]{:S(2)}, u32[]{:S(2)}) collective-permute-start(f32[8,64,128]{2,1,0:T(8,128)S(1)} %get-tuple-element.39), channel_id=1, source_target_pairs={{3,0},{0,1},{1,2},{2,3},{7,4},{4,5},{5,6},{6,7},{11,8},{8,9},{9,10... | collective-permute-start | bytes 786440 | tf_op jit(solution)/shard_map/ppermute | solution.py:551
  26.6 13.0 %collective-permute-start.7 = (f32[8,64,128]{2,1,0:T(8,128)S(1)}, f32[8,64,128]{2,1,0:T(8,128)S(1)}, u32[]{:S(2)}, u32[]{:S(2)}) collective-permute-start(f32[8,64,128]{2,1,0:T(8,128)S(1)} %get-tuple-element.40), channel_id=1, source_target_pairs={{1,0},{2,1},{3,2},{0,3},{5,4},{6,5},{7,6},{4,7},{9,8},{10,9},{11,1... | collective-permute-start | bytes 786440 | tf_op jit(solution)/shard_map/ppermute | solution.py:551
  31.0 0.6 %copy-start.17 = (bf16[128,384]{1,0:T(8,128)(2,1)}, bf16[128,384]{1,0:T(8,128)(2,1)S(1)}, u32[]{:S(2)}) copy-start(bf16[128,384]{1,0:T(8,128)(2,1)S(1)} %get-tuple-element.33.y1h_ref) | copy-start | bytes 294916
  31.7 0.6 %copy-start.19 = (bf16[128,384]{1,0:T(8,128)(2,1)}, bf16[128,384]{1,0:T(8,128)(2,1)S(1)}, u32[]{:S(2)}) copy-start(bf16[128,384]{1,0:T(8,128)(2,1)S(1)} %get-tuple-element.34.y1l_ref) | copy-start | bytes 294916
  32.3 0.6 %copy-start.21 = (f32[96,128]{1,0:T(8,128)}, f32[96,128]{1,0:T(8,128)S(1)}, u32[]{:S(2)}) copy-start(f32[96,128]{1,0:T(8,128)S(1)} %get-tuple-element.31.z_ref) | copy-start | bytes 147460
  32.9 0.9 %copy-start.18 = (bf16[128,384]{1,0:T(8,128)(2,1)S(1)}, bf16[128,384]{1,0:T(8,128)(2,1)}, u32[]{:S(2)}) copy-start(bf16[128,384]{1,0:T(8,128)(2,1)} %copy-done.17) | copy-start | bytes 294916
  33.8 0.9 %copy-start.20 = (bf16[128,384]{1,0:T(8,128)(2,1)S(1)}, bf16[128,384]{1,0:T(8,128)(2,1)}, u32[]{:S(2)}) copy-start(bf16[128,384]{1,0:T(8,128)(2,1)} %copy-done.19) | copy-start | bytes 294916
  34.7 0.8 %copy-start.22 = (f32[96,128]{1,0:T(8,128)S(1)}, f32[96,128]{1,0:T(8,128)}, u32[]{:S(2)}) copy-start(f32[96,128]{1,0:T(8,128)} %copy-done.21) | copy-start | bytes 147460
  39.5 1.7 %collective-permute-start.8 = (f32[64,1408]{1,0:T(8,128)S(1)}, f32[64,1408]{1,0:T(8,128)S(1)}, u32[]{:S(2)}, u32[]{:S(2)}) collective-permute-start(f32[64,1408]{1,0:T(8,128)S(1)} %away.1), channel_id=1, source_target_pairs={{16,0},{0,16},{17,1},{1,17},{18,2},{2,18},{19,3},{3,19},{20,4},{4,... | collective-permute-start | bytes 1081352 | tf_op jit(solution)/shard_map/ppermute | solution.py:551

commit v4 on v2

--- a/solution.py
+++ b/solution.py
@@ -2,6 +2,7 @@
 
 import jax
 import jax.numpy as jnp
+import ml_dtypes
 import numpy as np
 from jax import lax
 from jax.experimental import pallas as pl
@@ -15,7 +16,6 @@
 FAR = -1.0 / 16.0
 F32 = jnp.float32
 BF16 = jnp.bfloat16
-HIGHEST = lax.Precision.HIGHEST
 VMEM_LIMIT = 40 * 1024 * 1024
 
 
@@ -45,6 +45,8 @@
         self.tiles_s = -(-TERMS * self.planes // self.per_tile)
         self.fine_tiles = -(-nz // (LANES // R))
         self.ext = nx + 2 * R
+        self.depth = TERMS * (self.rows1 + 2 * self.rows2)
+        self.depth_lanes = -(-self.depth // LANES) * LANES
 
 
 def restrict_circle(n):
@@ -80,6 +82,12 @@
     return out
 
 
+def exact(m):
+    out = m.astype(ml_dtypes.bfloat16)
+    assert np.all(out.astype(np.float64) == m)
+    return out
+
+
 def constants(s):
     c = {}
     c["ry2"] = padded(restrict_open(-1, s.wide1, -2, s.wide2).T, LANES, LANES)
@@ -90,23 +98,32 @@
         p2 = p1 @ prolong_circle(n[2])
         return p1, p2, p2 @ prolong_circle(n[3])
 
+    def parts(name, m):
+        m = m.astype(np.float32)
+        c[name] = m.astype(ml_dtypes.bfloat16)
+        c[name + "l"] = (m - c[name].astype(np.float32)).astype(ml_dtypes.bfloat16)
+
     x1, x2, x3 = chain(s.cx)
-    c["px1"], c["px2"], c["px3"] = (m.astype(np.float32) for m in (x1, x2, x3))
+    c["px1"], c["px2"] = exact(x1), exact(x2)
+    parts("px3", x3)
     place = np.zeros((s.cx[2], s.rows2))
     for r in range(s.x2 + 3):
         place[(r - 1) % s.cx[2], r] += 1.0
-    c["rx3"] = (restrict_circle(s.cx[2]) @ place).astype(np.float32)
-    y1, y2, y3 = chain(s.cy)
-    c["py1"], c["py2"], c["py3"] = (
-        np.ascontiguousarray(m[: s.ny].T).astype(np.float32) for m in (y1, y2, y3)
-    )
-    c["ry3"] = np.ascontiguousarray(restrict_circle(s.cy[2]).T).astype(np.float32)
+    rx3 = np.zeros((TERMS, s.cx[3], s.depth_lanes))
+    for t in range(TERMS):
+        first = TERMS * s.rows1 + (TERMS + t) * s.rows2
+        rx3[t, :, first : first + s.rows2] = restrict_circle(s.cx[2]) @ place
+    c["rx3"] = exact(rx3)
+    _, y2, y3 = chain(s.cy)
+    c["py2"] = exact(y2[: s.ny].T)
+    parts("py3", y3[: s.ny].T)
+    c["ry3"] = exact(restrict_circle(s.cy[2]).T)
     z2 = prolong_circle(s.cz[2])
     z3 = z2 @ prolong_circle(s.cz[3])
     own = [(o - 1) % s.cz[1] for o in range(s.planes)]
-    c["pz2"] = padded(z2[own], s.zrows, s.cz[2])
-    c["pz3"] = padded(z3[own], s.zrows, s.cz[3])
-    c["rz3"] = padded(restrict_circle(s.cz[2]), s.cz[3], LANES)
+    c["pz2"] = exact(padded(z2[own], s.zrows, s.cz[2]))
+    c["pz3"] = exact(padded(z3[own], s.zrows, s.cz[3]))
+    c["rz3"] = exact(padded(restrict_circle(s.cz[2]), s.cz[3], LANES))
     return c
 
 
@@ -119,8 +136,9 @@
     return jnp.dot(a, b, preferred_element_type=F32)
 
 
-def exact_dot(a, b):
-    return jnp.dot(a, b, preferred_element_type=F32, precision=HIGHEST)
+def dot2(a, b):
+    high, low = halves(a)
+    return dot(high, b) + dot(low, b)
 
 
 def dot3(a, b_high, b_low):
@@ -179,7 +197,7 @@
     return jnp.concatenate([lo_ref[z, s.nx - R :], b_ref[z], hi_ref[z, 0:R]], axis=0)
 
 
-def share_kernel(s, b_ref, lo_ref, hi_ref, _, m_ref, first_ref, last_ref):
+def share_kernel(s, b_ref, lo_ref, hi_ref, m_ref, first_ref, last_ref):
     b = [extended(s, b_ref, lo_ref, hi_ref, z) for z in range(s.nz)]
     planes = []
     for k in range(-1, s.z1 + 2):
@@ -217,57 +235,86 @@
     return lax.broadcasted_iota(jnp.int32, shape, 0)
 
 
-def spread(w_ref, level, t):
-    w = jnp.full((8, LANES), w_ref[level, t], F32)
-    return (-0.5 / (w * w))[0:1, 0:1]
-
-
 def bell(c, d):
     d = jnp.abs(d)
     return jnp.where(d <= R, jnp.exp(c * d * d), 0.0)
 
 
-def scale(c, count=None):
-    n = lanes_of((1, LANES)).astype(F32)
-    if count is None:
-        d, valid = n - R, n <= 2 * R
-    else:
-        d, valid = jnp.minimum(n, count - n), n < count
-    return 1.0 / jnp.sqrt(jnp.sum(jnp.where(valid, jnp.exp(2.0 * c * d * d), 0.0), axis=1, keepdims=True))
-
-
-def put(high_ref, low_ref, at, x):
-    high, low = halves(x)
-    high_ref[:, at : at + x.shape[1]] = high
-    low_ref[:, at : at + x.shape[1]] = low
-
-
-def tap_kernel(s, w_ref, a_ref, tap_ref, y0h_ref, y0l_ref):
-    coef = [[spread(w_ref, l, t) for t in range(TERMS)] for l in range(2)]
-    unit = [[scale(coef[l][t]) for t in range(TERMS)] for l in range(2)]
+def one(ref, level, t):
+    return ref[level : level + 1, t : t + 1]
+
+
+def spreads(w_ref, levels):
+    out = []
+    for l in levels:
+        w = [one(w_ref, l, t) for t in range(TERMS)]
+        out.append([-0.5 / (x * x) for x in w])
+    return out
+
+
+def units(coef, distance, valid):
+    shape = (up8(len(coef)), LANES)
+    row = rows_of(shape)
+    column = jnp.zeros(shape, F32)
+    for r, c in enumerate(coef):
+        column = jnp.where(row == r, c, column)
+    lane = lanes_of(shape)
+    d = distance(row, lane).astype(F32)
+    total = jnp.sum(jnp.where(valid(row, lane), jnp.exp(2.0 * column * d * d), 0.0), axis=1, keepdims=True)
+    unit = 1.0 / jnp.sqrt(total)
+    return [unit[r : r + 1] for r in range(len(coef))]
+
+
+def near_units(coef):
+    flat = [c for level in coef for c in level]
+    out = units(flat, lambda row, lane: lane - R, lambda row, lane: lane <= 2 * R)
+    return [out[i : i + TERMS] for i in range(0, len(out), TERMS)]
+
+
+def tap_kernel(s, w_ref, a_ref, _, tap_ref, x0_ref, y0_ref):
+    coef = spreads(w_ref, (0, 1))
+    unit = near_units(coef)
     d = lanes_of((1, LANES)).astype(F32)
     for t in range(TERMS):
-        g0 = bell(coef[0][t], d) * unit[0][t]
-        g1 = bell(coef[1][t], d) * unit[1][t]
-        tap_ref[t : t + 1] = g0
-        tap_ref[TERMS + t : TERMS + t + 1] = g0 * a_ref[0, t]
-        tap_ref[2 * TERMS + t : 2 * TERMS + t + 1] = g1 * (a_ref[1, t] * 0.25)
-    for t in range(TERMS):
-        shape = (2 * LANES, s.ny)
-        i = rows_of(shape)
-        cell = jnp.where(i < s.ny, i, jnp.where(i < s.ny + R, i - s.ny - R, i - R))
-        g = bell(coef[0][t], (cell - lanes_of(shape)).astype(F32)) * unit[0][t]
-        put(y0h_ref, y0l_ref, t * s.ny, jnp.where(i < s.ny + 2 * R, g, 0.0))
-
-
-def matrix_kernel(s, w_ref, a_ref, px1, px2, px3, rx3, py1, py2, py3, ry3, pz2, pz3, rz3, _,
-                  z_ref, y1h_ref, y1l_ref, y2h_ref, y2l_ref, xh_ref, xl_ref):
-    coef = [[spread(w_ref, l, t) for t in range(TERMS)] for l in range(4)]
-    unit = [[scale(coef[l][t]) for t in range(TERMS)] for l in range(3)]
-
-    def circle(n, shape, first_row, first_lane, c, u):
-        d = ((rows_of(shape) + first_row) - (lanes_of(shape) + first_lane)) & (n - 1)
-        d = d.astype(F32)
+        tap_ref[t : t + 1] = bell(coef[0][t], d) * (unit[0][t] * one(a_ref, 0, t))
+        tap_ref[TERMS + t : TERMS + t + 1] = bell(coef[1][t], d) * (unit[1][t] * one(a_ref, 1, t) * 0.25)
+    shape = (s.nx, 3 * s.ext)
+    lane = lanes_of(shape)
+    part = jnp.where(lane < s.ext, 0, jnp.where(lane < 2 * s.ext, 1, 2))
+    d = (lane - part * s.ext - R - rows_of(shape)).astype(F32)
+    for t in range(TERMS):
+        high, low = halves(bell(coef[0][t], d) * unit[0][t])
+        x0_ref[t * s.nx : (t + 1) * s.nx] = jnp.where(part == 1, low.astype(F32), high.astype(F32)).astype(BF16)
+    shape = (s.ny + 2 * R, s.ny)
+    i = rows_of(shape)
+    cell = jnp.where(i < s.ny, i, jnp.where(i < s.ny + R, i - s.ny - R, i - R))
+    d = (cell - lanes_of(shape)).astype(F32)
+    for t in range(TERMS):
+        high, low = halves(bell(coef[0][t], d) * unit[0][t])
+        at = 2 * t * s.ny
+        y0_ref[s.ny + 2 * R :, at : at + 2 * s.ny] = jnp.zeros((2 * LANES - s.ny - 2 * R, 2 * s.ny), BF16)
+        y0_ref[: s.ny + 2 * R, at : at + s.ny] = high
+        y0_ref[: s.ny + 2 * R, at + s.ny : at + 2 * s.ny] = low
+
+
+def matrix_kernel(s, w_ref, a_ref, px1, px2, px3, px3l, rx3, py2, py3, py3l, ry3, pz2, pz3, rz3, _,
+                  z_ref, y1_ref, y2h_ref, y2l_ref, xh_ref, xl_ref):
+    coef = spreads(w_ref, range(4))
+    unit = near_units(coef[:3])
+    sizes = [s.cx[3], s.cy[3], s.cz[3]]
+
+    def per_row(row):
+        return jnp.where(row < TERMS, sizes[0], jnp.where(row < 2 * TERMS, sizes[1], sizes[2]))
+
+    top = units(
+        coef[3] * 3,
+        lambda row, lane: jnp.minimum(lane, per_row(row) - lane),
+        lambda row, lane: lane < per_row(row),
+    )
+    top_x, top_y, top_z = top[:TERMS], top[TERMS : 2 * TERMS], top[2 * TERMS :]
+
+    def circle(n, d, c, u):
+        d = (d & (n - 1)).astype(F32)
         return (bell(c, d) + bell(c, n - d)) * u
 
     def full_circle(n, shape, c, u):
@@ -275,84 +322,105 @@
         d = jnp.minimum(d, n - d)
         return jnp.exp(c * d * d) * u
 
-    def by_term(shape, wide, values):
-        t = lanes_of(shape)
-        return jnp.where(t < wide, values[0], jnp.where(t < 2 * wide, values[1], values[2]))
-
-    for t in range(TERMS):
-        shape = (LANES, s.cy[1])
-        g = circle(s.cy[1], shape, -(R + 1), 0, coef[1][t], unit[1][t])
-        g = jnp.where(rows_of(shape) < s.y1 + 3 + 2 * R, g, 0.0)
-        put(y1h_ref, y1l_ref, t * s.ny, exact_dot(g, py1[...]))
-        g = circle(s.cy[2], (s.cy[2], s.cy[2]), 0, 0, coef[2][t], unit[2][t])
-        put(y2h_ref, y2l_ref, t * s.ny, exact_dot(g, py2[...]))
-        u = scale(coef[3][t], s.cy[3])
-        g = full_circle(s.cy[3], (s.cy[3], s.cy[3]), coef[3][t], u)
-        put(y2h_ref, y2l_ref, (TERMS + t) * s.ny, exact_dot(exact_dot(ry3[...], g), py3[...]))
-    wide = s.rows1
-    shape = (s.cx[1], TERMS * wide)
-    lane = lanes_of(shape)
-    column = lane - jnp.where(lane < wide, 0, jnp.where(lane < 2 * wide, wide, 2 * wide))
-    d = ((rows_of(shape) - column) & (s.cx[1] - 1)).astype(F32)
-    c = by_term(shape, wide, coef[1])
-    g = (bell(c, d) + bell(c, s.cx[1] - d)) * by_term(shape, wide, unit[1])
-    put(xh_ref, xl_ref, 0, exact_dot(px1[...], g))
-    wide = s.rows2
-    shape = (s.cx[2], TERMS * wide)
-    lane = lanes_of(shape)
-    column = lane - jnp.where(lane < wide, 0, jnp.where(lane < 2 * wide, wide, 2 * wide))
-    d = ((rows_of(shape) - column + 1) & (s.cx[2] - 1)).astype(F32)
-    c = by_term(shape, wide, coef[2])
-    g = (bell(c, d) + bell(c, s.cx[2] - d)) * by_term(shape, wide, unit[2])
-    put(xh_ref, xl_ref, TERMS * s.rows1, exact_dot(px2[...], jnp.where(column < s.x2 + 3, g, 0.0)))
-    for t in range(TERMS):
-        u = scale(coef[3][t], s.cx[3])
-        g = full_circle(s.cx[3], (s.cx[3], s.cx[3]), coef[3][t], u)
-        put(xh_ref, xl_ref, TERMS * s.rows1 + (TERMS + t) * wide, exact_dot(px3[...], exact_dot(g, rx3[...])))
-    for t in range(TERMS):
-        g = circle(s.cz[2], (s.cz[2], LANES), 0, 0, coef[2][t], unit[2][t])
-        g = exact_dot(pz2[...], g) * (a_ref[2, t] * 0.0625)
-        z_ref[t * s.zrows : (t + 1) * s.zrows] = g
-        u = scale(coef[3][t], s.cz[3])
-        g = full_circle(s.cz[3], (s.cz[3], s.cz[3]), coef[3][t], u)
-        g = exact_dot(exact_dot(pz3[...], g), rz3[...]) * (a_ref[3, t] * 0.015625)
+    shape = (LANES, s.ny)
+    fine = lanes_of(shape)
+    d = (rows_of(shape) - (R + 1) - (fine >> 1)).astype(F32)
+    even = (fine & 1) == 0
+    known = rows_of(shape) < s.y1 + 3 + 2 * R
+    wide = (s.cy[2], s.cy[2])
+    for t in range(TERMS):
+        c = coef[1][t]
+        here = bell(c, d)
+        between = NEAR * (here + bell(c, d - 1.0)) + FAR * (bell(c, d + 1.0) + bell(c, d - 2.0))
+        high, low = halves(jnp.where(known, jnp.where(even, here, between) * unit[1][t], 0.0))
+        y1_ref[:, 2 * t * s.ny : (2 * t + 1) * s.ny] = high
+        y1_ref[:, (2 * t + 1) * s.ny : (2 * t + 2) * s.ny] = low
+        g = circle(s.cy[2], rows_of(wide) - lanes_of(wide), coef[2][t], unit[2][t])
+        high, low = halves(dot2(g, py2[...]))
+        y2h_ref[:, t * s.ny : (t + 1) * s.ny] = high
+        y2l_ref[:, t * s.ny : (t + 1) * s.ny] = low
+        g = full_circle(s.cy[3], (s.cy[3], s.cy[3]), coef[3][t], top_y[t])
+        high, low = halves(g)
+        g = dot(ry3[...], high) + dot(ry3[...], low)
+        high, low = halves(dot3(g, py3[...], py3l[...]))
+        at = (TERMS + t) * s.ny
+        y2h_ref[:, at : at + s.ny] = high
+        y2l_ref[:, at : at + s.ny] = low
+
+    def terms(level, first, rows, valid, shift):
+        shape = (s.cx[level], s.depth_lanes)
+        lane = lanes_of(shape) - first
+        column = lane - jnp.where(lane < rows, 0, jnp.where(lane < 2 * rows, rows, 2 * rows))
+
+        def by_term(v):
+            return jnp.where(lane < rows, v[0], jnp.where(lane < 2 * rows, v[1], v[2]))
+
+        g = circle(s.cx[level], rows_of(shape) - column + shift, by_term(coef[level]), by_term(unit[level]))
+        high, low = halves(jnp.where((lane >= 0) & (lane < TERMS * rows) & (column < valid), g, 0.0))
+        return high, low
+
+    high, low = terms(1, 0, s.rows1, s.rows1, 0)
+    x = dot(px1[...], high) + dot(px1[...], low)
+    high, low = terms(2, TERMS * s.rows1, s.rows2, s.x2 + 3, 1)
+    x += dot(px2[...], high) + dot(px2[...], low)
+    g = None
+    for t in range(TERMS):
+        part = dot2(full_circle(s.cx[3], (s.cx[3], s.cx[3]), coef[3][t], top_x[t]), rx3[t])
+        g = part if g is None else g + part
+    high, low = halves(g)
+    x += dot(px3[...], high) + dot(px3l[...], high) + dot(px3[...], low)
+    xh_ref[...], xl_ref[...] = halves(x)
+    for t in range(TERMS):
+        shape = (s.cz[2], LANES)
+        g = circle(s.cz[2], rows_of(shape) - lanes_of(shape), coef[2][t], unit[2][t])
+        high, low = halves(g * (one(a_ref, 2, t) * 0.0625))
+        z_ref[t * s.zrows : (t + 1) * s.zrows] = dot(pz2[...], high) + dot(pz2[...], low)
+        g = full_circle(s.cz[3], (s.cz[3], s.cz[3]), coef[3][t], top_z[t])
+        high, low = halves(g * (one(a_ref, 3, t) * 0.015625))
+        g = dot2(dot(pz3[...], high) + dot(pz3[...], low), rz3[...])
         z_ref[(TERMS + t) * s.zrows : (TERMS + t + 1) * s.zrows] = g
 
 
-def near_kernel(s, tap_ref, b_ref, lo_ref, hi_ref, left_ref, right_ref, y0h_ref, y0l_ref,
-                own_ref, down_ref, up_ref, eh_ref, el_ref, u_ref, v_ref):
-    ext = s.ext
+def near_kernel(s, tap_ref, b_ref, lo_ref, hi_ref, left_ref, right_ref, x0_ref, y0_ref,
+                own_ref, down_ref, up_ref, e_ref, u_ref, eh_ref, el_ref, v_ref):
     group = LANES // R
-    lane = lanes_of((ext, LANES))
+    tiles = [extended(s, b_ref, lo_ref, hi_ref, z) for z in range(s.nz)]
+    tiles += [left_ref[t] for t in range(s.fine_tiles)] + [right_ref[t] for t in range(s.fine_tiles)]
+    for i, x in enumerate(tiles):
+        high, low = halves(x)
+        columns = slice(i * LANES, (i + 1) * LANES)
+        e_ref[0 : s.ext, columns] = high
+        e_ref[s.ext : 2 * s.ext, columns] = high
+        e_ref[2 * s.ext :, columns] = low
+    x0 = x0_ref[...]
+    for at in range(0, len(tiles) * LANES, 2 * LANES):
+        columns = slice(at, min(at + 2 * LANES, len(tiles) * LANES))
+        u_ref[:, columns] = dot(x0, e_ref[:, columns])
+    lane = lanes_of((TERMS * s.nx, LANES))
     for z in range(s.nz):
         t, g = divmod(z, group)
-        strips = jnp.where((lane >= R * g) & (lane < R * g + R), left_ref[t], right_ref[t])
-        for at, x in ((0, extended(s, b_ref, lo_ref, hi_ref, z)), (LANES, turn(strips, -R * g))):
+        left = u_ref[:, (s.nz + t) * LANES : (s.nz + t + 1) * LANES]
+        right = u_ref[:, (s.nz + s.fine_tiles + t) * LANES : (s.nz + s.fine_tiles + t + 1) * LANES]
+        strips = turn(jnp.where((lane >= R * g) & (lane < R * g + R), left, right), -R * g)
+        for at, x in ((0, u_ref[:, z * LANES : (z + 1) * LANES]), (LANES, strips)):
             high, low = halves(x)
-            eh_ref[z * ext : (z + 1) * ext, at : at + LANES] = high
-            el_ref[z * ext : (z + 1) * ext, at : at + LANES] = low
-    step = 4 * ext
-    y0h, y0l = y0h_ref[...], y0l_ref[...]
-    for at in range(0, s.nz * ext, step):
-        high, low = eh_ref[at : at + step], el_ref[at : at + step]
-        u = dot(high, y0h) + dot(low, y0h) + dot(high, y0l)
-        for t in range(TERMS):
-            for q in range(4):
-                u_ref[t, at // ext + q] = u[q * ext : (q + 1) * ext, t * s.ny : (t + 1) * s.ny]
-
-    def cross(z, _):
-        for t in range(TERMS):
-            v = u_ref[t, z, R : R + s.nx] * tap_ref[t, 0]
-            for d in range(1, R + 1):
-                v += (u_ref[t, z, R + d : R + d + s.nx] + u_ref[t, z, R - d : R - d + s.nx]) * tap_ref[t, d]
-            v_ref[t, z] = v
-        return 0
-
-    lax.fori_loop(0, s.nz, cross, 0)
+            for t in range(TERMS):
+                rows = slice(t * s.nx, (t + 1) * s.nx)
+                eh_ref[t, z * s.nx : (z + 1) * s.nx, at : at + LANES] = high[rows]
+                el_ref[t, z * s.nx : (z + 1) * s.nx, at : at + LANES] = low[rows]
+    step = 4 * s.nx
+    for t in range(TERMS):
+        at = 2 * t * s.ny
+        y0, y0h = y0_ref[:, at : at + 2 * s.ny], y0_ref[:, at : at + s.ny]
+        for first in range(0, s.nz * s.nx, step):
+            both = dot(eh_ref[t, first : first + step], y0)
+            v = both[:, : s.ny] + both[:, s.ny :] + dot(el_ref[t, first : first + step], y0h)
+            for q in range(step // s.nx):
+                v_ref[t, first // s.nx + q] = v[q * s.nx : (q + 1) * s.nx]
 
     def depth(r, _):
         rows = pl.ds(pl.multiple_of(r * 8, 8), 8)
-        taps = [[tap_ref[TERMS + t, d] for d in range(R + 1)] for t in range(TERMS)]
+        taps = [[tap_ref[t, d] for d in range(R + 1)] for t in range(TERMS)]
         for first in range(-R, s.nz + R, R):
             acc = [None] * R
             for t in range(TERMS):
@@ -396,9 +464,9 @@
         sums = [c_ref[(o - 1) % n]]
         sums += [c_ref[(o - 1 + d) % n] + c_ref[(o - 1 - d) % n] for d in range(1, R + 1)]
         for t in range(TERMS):
-            x = sums[0] * tap_ref[2 * TERMS + t, 0]
+            x = sums[0] * tap_ref[TERMS + t, 0]
             for d in range(1, R + 1):
-                x += sums[d] * tap_ref[2 * TERMS + t, d]
+                x += sums[d] * tap_ref[TERMS + t, d]
             k = t * s.planes + o
             w_ref[k] = x
             tile, slot = divmod(k, s.per_tile)
@@ -431,7 +499,7 @@
 
 def along_kernel(s, z_ref, w_ref, *refs):
     c2_refs = refs[: s.gy]
-    y1h_ref, y1l_ref, y2h_ref, y2l_ref, d_ref, yb_ref = refs[s.gy :]
+    y1_ref, y2h_ref, y2l_ref, d_ref, yb_ref = refs[s.gy :]
     base = s.tiles_s * s.rows1
     lane = lanes_of((s.rows1, LANES))
     above, below = c2_refs[1], c2_refs[-1]
@@ -447,8 +515,10 @@
             x += jnp.where(lane < s.strip, turn(below[rows], -at), 0.0)
             x += jnp.where((lane >= end) & (lane < end + s.strip), turn(above[rows], end - at), 0.0)
             cells.append(x)
-        columns = slice(t * s.ny, (t + 1) * s.ny)
-        out = dot3(jnp.concatenate(cells, axis=0), y1h_ref[:, columns], y1l_ref[:, columns])
+        high, low = halves(jnp.concatenate(cells, axis=0))
+        at = 2 * t * s.ny
+        both = dot(high, y1_ref[:, at : at + 2 * s.ny])
+        out = both[:, : s.ny] + both[:, s.ny :] + dot(low, y1_ref[:, at : at + s.ny])
         for o in range(s.planes):
             d_ref[t * s.rows1 : (t + 1) * s.rows1, o * s.ny : (o + 1) * s.ny] = out[o * s.rows1 : (o + 1) * s.rows1]
     cells = []
@@ -476,7 +546,8 @@
 def across(s, d_ref, xh_ref, xl_ref, shift):
     rows = slice(shift * s.nx, (shift + 1) * s.nx)
     high, low = halves(d_ref[...])
-    return dot(xh_ref[rows], high) + dot(xl_ref[rows], high) + dot(xh_ref[rows], low)
+    xh, xl = xh_ref[rows, : s.depth], xl_ref[rows, : s.depth]
+    return dot(xh, high) + dot(xl, high) + dot(xh, low)
 
 
 def away_kernel(s, d_ref, xh_ref, xl_ref, *g_refs):
@@ -561,46 +632,49 @@
     c = {k: jnp.asarray(v) for k, v in constants(s).items()}
     brick = (s.nz, s.nx, s.ny)
     side = (R, s.nx, s.ny)
-    taps, y0h, y0l = call(
-        functools.partial(tap_kernel, s), "taps", [widths, amplitudes],
-        arrays((16, LANES)) + two(2 * LANES, TERMS * s.ny), scalars=(0, 1), flops=6 * 10**8,
-    )
     high_rows = fetch(charges, gx=1)
     low_rows = high_rows if s.gx == 2 else fetch(charges, gx=-1)
     strips = (s.fine_tiles, s.ext, LANES)
     share, first_cells, last_cells = call(
         functools.partial(share_kernel, s), "share", [charges, low_rows, high_rows],
-        arrays((s.tiles1, s.rows1, LANES), strips, strips), after=[y0h], flops=10**9,
+        arrays((s.tiles1, s.rows1, LANES), strips, strips), flops=10**9,
     )
     shares = [share] + [fetch(share, gz=b) for b in range(1, s.gz)]
     left, right = fetch(last_cells, gy=-1), fetch(first_cells, gy=1)
+    taps, x0, y0 = call(
+        functools.partial(tap_kernel, s), "taps", [widths, amplitudes],
+        arrays((8, LANES))
+        + arrays((TERMS * s.nx, 3 * s.ext), (2 * LANES, 2 * TERMS * s.ny), dtype=BF16),
+        after=[share], flops=6 * 10**8,
+    )
+    tiles = s.nz + 2 * s.fine_tiles
+    halved = pltpu.VMEM((TERMS, s.nz * s.nx, 2 * LANES), BF16)
     near, near_down, near_up = call(
         functools.partial(near_kernel, s), "near",
-        [taps, charges, low_rows, high_rows, left, right, y0h, y0l],
+        [taps, charges, low_rows, high_rows, left, right, x0, y0],
         arrays(brick, side, side), scalars=(0,),
         scratch=[
-            pltpu.VMEM((s.nz * s.ext, 2 * LANES), BF16), pltpu.VMEM((s.nz * s.ext, 2 * LANES), BF16),
-            pltpu.VMEM((TERMS, s.nz, s.ext, s.ny), F32), pltpu.VMEM((TERMS,) + brick, F32),
+            pltpu.VMEM((3 * s.ext, tiles * LANES), BF16), pltpu.VMEM((TERMS * s.nx, tiles * LANES), F32),
+            halved, halved, pltpu.VMEM((TERMS,) + brick, F32),
         ],
-        flops=6 * 10**9,
+        flops=5 * 10**9,
     )
     base = s.tiles_s * s.rows1
     size2 = s.tiles2 * s.rows2
-    depth = TERMS * (s.rows1 + 2 * s.rows2)
     waves, to_low, to_high, coarse = call(
         functools.partial(depth_kernel, s), "depth",
         [taps] + shares + [c["ry2"], c["rx2"]],
         arrays((TERMS * s.planes, s.rows1, LANES), (base + size2, LANES), (base + size2, LANES), (size2, LANES)),
         scalars=(0,), after=[near], scratch=[pltpu.VMEM((s.cz[1], s.rows1, LANES), F32)], flops=2 * 10**9,
     )
-    named = ("px1", "px2", "px3", "rx3", "py1", "py2", "py3", "ry3", "pz2", "pz3", "rz3")
-    z_taps, y1h, y1l, y2h, y2l, xh, xl = call(
+    named = ("px1", "px2", "px3", "px3l", "rx3", "py2", "py3", "py3l", "ry3", "pz2", "pz3", "rz3")
+    z_taps, y1, y2h, y2l, xh, xl = call(
         functools.partial(matrix_kernel, s), "matrices",
         [widths, amplitudes] + [c[k] for k in named],
         arrays((2 * TERMS * s.zrows, LANES))
-        + two(LANES, TERMS * s.ny) + two(s.cy[2], 2 * TERMS * s.ny)
-        + two(s.cx[0], depth),
-        scalars=(0, 1), after=[coarse], flops=3 * 10**9,
+        + arrays((LANES, 2 * TERMS * s.ny), dtype=BF16)
+        + two(s.cy[2], 2 * TERMS * s.ny) + two(s.cx[0], s.depth_lanes),
+        after=[coarse], flops=2 * 10**9,
     )
     coarses = [coarse]
     for b in range(1, s.gy):
@@ -608,8 +682,8 @@
     near_low, near_high = fetch(near_up, gz=-1), fetch(near_down, gz=1)
     (terms,) = call(
         functools.partial(along_kernel, s), "along",
-        [z_taps, waves] + coarses + [y1h, y1l, y2h, y2l],
-        arrays((depth, s.planes * s.ny)), scalars=(0,),
+        [z_taps, waves] + coarses + [y1, y2h, y2l],
+        arrays((s.depth, s.planes * s.ny)), scalars=(0,),
         scratch=[pltpu.VMEM((2 * TERMS, s.cz[2], s.rows2, s.ny), F32)], flops=3 * 10**9,
     )
     parts = call(

time: 38.3 us -> 42.2 us (1.10)
  waiting for transfers between devices: 2.14 us -> 9.25 us
  Pallas kernels: 16.6 us -> 13.2 us
  starting transfers between devices: 17.6 us -> 18.2 us
    ppermute x12, waiting for transfers between devices: 2.14 us -> 9.25 us  [fetch(): return lax.ppermute(x, names if len(names) > 1 else names[0], pairs)]
    pallas_call x9, Pallas kernels: 16.6 us -> 13.2 us  [call(): pl.pallas_call(kernel, name=name, out_shape=out_shapes, in_specs=[spec(i)...]
    ppermute x12, starting transfers between devices: 17.6 us -> 18.2 us  [fetch(): return lax.ppermute(x, names if len(names) > 1 else names[0], pairs)]
  transfers between devices with their start and end apart: 12 -> 12, of which waited for: 2 -> 6; matrix products, arithmetic and copies ran while one was open for 0% -> 0% of each run, Pallas kernels for 40% -> 28%
where the time goes in v4:
time: 42.2 us; the launch traced here: 42.1 us
  starting transfers between devices  18.2 us (43%)
  Pallas kernels  13.2 us (31%)
  waiting for transfers between devices  9.25 us (22%)
  local copies, waits for them, and re-layouts  1.14 us (3%)
    ppermute x12, starting transfers between devices, fetch(): return lax.ppermute(x, names if len(names) > 1 else names[0], pairs)  18.2 us
    pallas_call x9, Pallas kernels, call(): pl.pallas_call(kernel, name=name, out_shape=out_shapes, in_specs=[spec(i)...  13.2 us
    ppermute x12, waiting for transfers between devices, fetch(): return lax.ppermute(x, names if len(names) > 1 else names[0], pairs)  9.25 us
    unnamed x34, local copies, waits for them, and re-layouts  1.14 us
  transfers between devices with their start and end apart: 12, of which 6 were waited for; matrix products, arithmetic and copies ran while one was open for 0% of the time, Pallas kernels for 28%

profile of v4, /device:TPU:0, one launch (start us, length us, event | category | flops | bytes accessed | tf_op | source)
XLA Modules:
  0.0 42.1 jit_solution(16001765021378207978)
XLA Ops:
  0.0 0.5 %collective-permute-start = (f32[16,64,128]{2,1,0:T(8,128)}, f32[16,64,128]{2,1,0:T(8,128)S(1)}, u32[]{:S(2)}, u32[]{:S(2)}) collective-permute-start(f32[16,64,128]{2,1,0:T(8,128)} %b_ref.3), channel_id=1, source_target_pairs={{16,0},{0,16},{17,1},{1,17},{18,2},{2,18},{19,3},{3,19},{20,4},{4,... | collective-permute-start | bytes 1572872 | tf_op jit(solution)/shard_map/ppermute | solution.py:623
  0.5 1.7 %collective-permute-done.lo_ref.hi_ref = f32[16,64,128]{2,1,0:T(8,128)S(1)} collective-permute-done((f32[16,64,128]{2,1,0:T(8,128)}, f32[16,64,128]{2,1,0:T(8,128)S(1)}, u32[]{:S(2)}, u32[]{:S(2)}) %collective-permute-start) | collective-permute-done | bytes 524320 | tf_op jit(solution)/shard_map/ppermute | solution.py:623
  2.2 1.0 %copy-done = f32[16,64,128]{2,1,0:T(8,128)S(1)} copy-done((f32[16,64,128]{2,1,0:T(8,128)S(1)}, f32[16,64,128]{2,1,0:T(8,128)}, u32[]{:S(2)}) %copy-start) | copy-done | bytes 524312
  3.2 0.7 %share.1 = (f32[6,32,128]{2,1,0:T(8,128)S(1)}, f32[1,80,128]{2,1,0:T(8,128)S(1)}, f32[1,80,128]{2,1,0:T(8,128)S(1)}) custom-call(f32[16,64,128]{2,1,0:T(8,128)S(1)} %copy-done, f32[16,64,128]{2,1,0:T(8,128)S(1)} %collective-permute-done.lo_ref.hi_ref, f32[16,64,128]{2,1,0:T(8,128)S(1)} %collective-permute-done.lo_ref.hi_ref), custom_call_target="tpu_custom_call" | custom-call | flops 1000000000 | bytes 1753088 | tf_op jit(solution)/shard_map/share/pallas_call | solution.py:600
  4.0 0.0 copy-start.1
  4.0 3.0 %collective-permute-start.3 = (f32[6,32,128]{2,1,0:T(8,128)S(1)}, f32[6,32,128]{2,1,0:T(8,128)S(1)}, u32[]{:S(2)}, u32[]{:S(2)}) collective-permute-start(f32[6,32,128]{2,1,0:T(8,128)S(1)} %get-tuple-element.24._.refs_0_), channel_id=1, source_target_pairs={{3,0},{0,1},{1,2},{2,3},{7,4},{4,5},{5,6},{6,7},{11,8},{8,9},{9,10... | collective-permute-start | bytes 294920 | tf_op jit(solution)/shard_map/ppermute | solution.py:623
  7.0 2.6 %collective-permute-start.2 = (f32[6,32,128]{2,1,0:T(8,128)S(1)}, f32[6,32,128]{2,1,0:T(8,128)S(1)}, u32[]{:S(2)}, u32[]{:S(2)}) collective-permute-start(f32[6,32,128]{2,1,0:T(8,128)S(1)} %get-tuple-element.24._.refs_0_), channel_id=1, source_target_pairs={{2,0},{3,1},{0,2},{1,3},{6,4},{7,5},{4,6},{5,7},{10,8},{11,9},{8,1... | collective-permute-start | bytes 294920 | tf_op jit(solution)/shard_map/ppermute | solution.py:623
  9.6 1.3 %collective-permute-start.1 = (f32[6,32,128]{2,1,0:T(8,128)S(1)}, f32[6,32,128]{2,1,0:T(8,128)S(1)}, u32[]{:S(2)}, u32[]{:S(2)}) collective-permute-start(f32[6,32,128]{2,1,0:T(8,128)S(1)} %get-tuple-element.24._.refs_0_), channel_id=1, source_target_pairs={{1,0},{2,1},{3,2},{0,3},{5,4},{6,5},{7,6},{4,7},{9,8},{10,9},{11,1... | collective-permute-start | bytes 294920 | tf_op jit(solution)/shard_map/ppermute | solution.py:623
  10.9 1.5 %collective-permute-start.4 = (f32[1,80,128]{2,1,0:T(8,128)S(1)}, f32[1,80,128]{2,1,0:T(8,128)S(1)}, u32[]{:S(2)}, u32[]{:S(2)}) collective-permute-start(f32[1,80,128]{2,1,0:T(8,128)S(1)} %get-tuple-element.26), channel_id=1, source_target_pairs={{12,0},{0,4},{4,8},{8,12},{13,1},{1,5},{5,9},{9,13},{14,2},{2,6},{... | collective-permute-start | bytes 122888 | tf_op jit(solution)/shard_map/ppermute | solution.py:623
  12.4 1.4 %collective-permute-start.5 = (f32[1,80,128]{2,1,0:T(8,128)S(1)}, f32[1,80,128]{2,1,0:T(8,128)S(1)}, u32[]{:S(2)}, u32[]{:S(2)}) collective-permute-start(f32[1,80,128]{2,1,0:T(8,128)S(1)} %get-tuple-element.27), channel_id=1, source_target_pairs={{4,0},{8,4},{12,8},{0,12},{5,1},{9,5},{13,9},{1,13},{6,2},{10,6},{... | collective-permute-start | bytes 122888 | tf_op jit(solution)/shard_map/ppermute | solution.py:623
  13.8 0.0 copy-done.2
  13.8 0.4 taps.1
  14.2 1.6 %collective-permute-done.4.left_ref = f32[1,80,128]{2,1,0:T(8,128)S(1)} collective-permute-done((f32[1,80,128]{2,1,0:T(8,128)S(1)}, f32[1,80,128]{2,1,0:T(8,128)S(1)}, u32[]{:S(2)}, u32[]{:S(2)}) %collective-permute-start.4) | collective-permute-done | bytes 40992 | tf_op jit(solution)/shard_map/ppermute | solution.py:623
  15.8 0.6 %collective-permute-done.5.right_ref = f32[1,80,128]{2,1,0:T(8,128)S(1)} collective-permute-done((f32[1,80,128]{2,1,0:T(8,128)S(1)}, f32[1,80,128]{2,1,0:T(8,128)S(1)}, u32[]{:S(2)}, u32[]{:S(2)}) %collective-permute-start.5) | collective-permute-done | bytes 40992 | tf_op jit(solution)/shard_map/ppermute | solution.py:623
  16.4 0.0 copy-done.1
  16.4 4.0 %near.1 = (f32[16,64,128]{2,1,0:T(8,128)S(1)}, f32[8,64,128]{2,1,0:T(8,128)S(1)}, f32[8,64,128]{2,1,0:T(8,128)S(1)}) custom-call(f32[8,128]{1,0:T(8,128)S(1)} %get-tuple-element.25.tap_ref, f32[16,64,128]{2,1,0:T(8,128)S(1)} %copy-done.1, f32[16,64,128]{2,1,0:T(8,128)S(1)} %collective-permute-done.lo_ref.hi_ref, ...), custom_call_target="tpu_custom_call" | custom-call | flops 5000000000 | bytes 3192832 | tf_op jit(solution)/shard_map/near/pallas_call | solution.py:600
  20.4 0.7 %collective-permute-start.9 = (f32[8,64,128]{2,1,0:T(8,128)S(1)}, f32[8,64,128]{2,1,0:T(8,128)S(1)}, u32[]{:S(2)}, u32[]{:S(2)}) collective-permute-start(f32[8,64,128]{2,1,0:T(8,128)S(1)} %get-tuple-element.41), channel_id=1, source_target_pairs={{3,0},{0,1},{1,2},{2,3},{7,4},{4,5},{5,6},{6,7},{11,8},{8,9},{9,10... | collective-permute-start | bytes 786440 | tf_op jit(solution)/shard_map/ppermute | solution.py:623
  21.2 3.1 %collective-permute-start.10 = (f32[8,64,128]{2,1,0:T(8,128)S(1)}, f32[8,64,128]{2,1,0:T(8,128)S(1)}, u32[]{:S(2)}, u32[]{:S(2)}) collective-permute-start(f32[8,64,128]{2,1,0:T(8,128)S(1)} %get-tuple-element.42), channel_id=1, source_target_pairs={{1,0},{2,1},{3,2},{0,3},{5,4},{6,5},{7,6},{4,7},{9,8},{10,9},{11,1... | collective-permute-start | bytes 786440 | tf_op jit(solution)/shard_map/ppermute | solution.py:623
  24.3 0.0 collective-permute-done.3.refs_3_
  24.3 0.0 collective-permute-done.2.refs_2_
  24.3 0.0 collective-permute-done.1.refs_1_
  24.3 0.0 copy-start.5
  24.4 0.0 copy-start.6
  24.4 0.0 copy-start.7
  24.4 0.0 copy-start.8
  24.4 0.0 copy-start.9
  24.4 0.0 copy-start.10
  24.4 0.0 copy-start.11
  24.4 0.0 copy-start.12
  24.4 0.0 copy-start.14
  24.5 0.0 copy-start.15
  24.5 0.0 copy-start.16
  24.5 1.4 %depth.1 = (f32[33,32,128]{2,1,0:T(8,128)S(1)}, f32[216,128]{1,0:T(8,128)S(1)}, f32[216,128]{1,0:T(8,128)S(1)}, f32[120,128]{1,0:T(8,128)S(1)}) custom-call(f32[8,128]{1,0:T(8,128)S(1)} %get-tuple-element.25.tap_ref, f32[6,32,128]{2,1,0:T(8,128)S(1)} %get-tuple-element.24._.refs_0_, f32[6,32,128]{2,1,0:T(8,128)S(1)} %collective-permute-done.1.refs_1_, ...), custom_call_target="tpu_custom_call" | custom-call | flops 2000000000 | bytes 1813504 | tf_op jit(solution)/shard_map/depth/pallas_call | solution.py:600
  25.9 1.6 %collective-permute-start.7 = (f32[120,128]{1,0:T(8,128)S(1)}, f32[120,128]{1,0:T(8,128)S(1)}, u32[]{:S(2)}, u32[]{:S(2)}) collective-permute-start(f32[120,128]{1,0:T(8,128)S(1)} %get-tuple-element.31._.refs_0_), channel_id=1, source_target_pairs={{8,0},{12,4},{0,8},{4,12},{9,1},{13,5},{1,9},{5,13},{10,2},{14,6},... | collective-permute-start | bytes 184328 | tf_op jit(solution)/shard_map/ppermute | solution.py:623
  27.5 2.3 %collective-permute-start.6 = (f32[216,128]{1,0:T(8,128)S(1)}, f32[216,128]{1,0:T(8,128)S(1)}, u32[]{:S(2)}, u32[]{:S(2)}) collective-permute-start(f32[216,128]{1,0:T(8,128)S(1)} %get-tuple-element.34), channel_id=1, source_target_pairs={{4,0},{8,4},{12,8},{0,12},{5,1},{9,5},{13,9},{1,13},{6,2},{10,6},{... | collective-permute-start | bytes 331784 | tf_op jit(solution)/shard_map/ppermute | solution.py:623
  29.8 0.0 collective-permute-start.8
  29.9 1.3 %matrices.1 = (f32[96,128]{1,0:T(8,128)S(1)}, bf16[128,768]{1,0:T(8,128)(2,1)S(1)}, bf16[128,768]{1,0:T(8,128)(2,1)S(1)}, bf16[128,768]{1,0:T(8,128)(2,1)S(1)}, ...) custom-call(f32[4,3]{1,0:T(4,128)S(1)} %copy-done.2, f32[4,3]{1,0:T(4,128)S(1)} %copy-done.3, ...), custom_call_target="tpu_custom_call" | custom-call | flops 2000000000 | bytes 973664 | tf_op jit(solution)/shard_map/matrices/pallas_call | solution.py:600
  31.2 0.0 collective-permute-done.7.refs_2_
  31.2 1.0 %collective-permute-done.6.refs_1_ = f32[216,128]{1,0:T(8,128)S(1)} collective-permute-done((f32[216,128]{1,0:T(8,128)S(1)}, f32[216,128]{1,0:T(8,128)S(1)}, u32[]{:S(2)}, u32[]{:S(2)}) %collective-permute-start.6) | collective-permute-done | bytes 110624 | tf_op jit(solution)/shard_map/ppermute | solution.py:623
  32.2 3.2 %collective-permute-done.8.refs_3_ = f32[216,128]{1,0:T(8,128)S(1)} collective-permute-done((f32[216,128]{1,0:T(8,128)S(1)}, f32[216,128]{1,0:T(8,128)S(1)}, u32[]{:S(2)}, u32[]{:S(2)}) %collective-permute-start.8) | collective-permute-done | bytes 110624 | tf_op jit(solution)/shard_map/ppermute | solution.py:623
  35.4 3.5 %along.1.d_ref = f32[240,1408]{1,0:T(8,128)S(1)} custom-call(f32[96,128]{1,0:T(8,128)S(1)} %get-tuple-element.32.z_ref, f32[33,32,128]{2,1,0:T(8,128)S(1)} %get-tuple-element.33.w_ref, f32[120,128]{1,0:T(8,128)S(1)} %get-tuple-element.31._.refs_0_, f32[216,128]{1,0:T(8,128)S(1)} %collective-permute-done.6.refs_1_, ...), custom_call_target="tpu_custom_call" | custom-call | flops 3000000000 | bytes 2875392 | tf_op jit(solution)/shard_map/along/pallas_call | solution.py:600
  38.9 0.5 %away.1 = f32[64,1408]{1,0:T(8,128)S(1)} custom-call(f32[240,1408]{1,0:T(8,128)S(1)} %along.1.d_ref, bf16[128,256]{1,0:T(8,128)(2,1)S(1)} %get-tuple-element.39.xh_ref, bf16[128,256]{1,0:T(8,128)(2,1)S(1)} %get-tuple-element.40.xl_ref), custom_call_target="tpu_custom_call" | custom-call | flops 1000000000 | bytes 1843200 | tf_op jit(solution)/shard_map/away/pallas_call | solution.py:600
  39.5 0.1 collective-permute-start.11
  39.5 0.0 collective-permute-done.9.low_ref
  39.5 0.0 collective-permute-done.10.high_ref
  39.6 0.6 %home.1.home_ref = f32[16,64,128]{2,1,0:T(8,128)S(1)} custom-call(f32[240,1408]{1,0:T(8,128)S(1)} %along.1.d_ref, bf16[128,256]{1,0:T(8,128)(2,1)S(1)} %get-tuple-element.39.xh_ref, bf16[128,256]{1,0:T(8,128)(2,1)S(1)} %get-tuple-element.40.xl_ref, f32[16,64,128]{2,1,0:T(8,128)S(1)} %get-tuple-element.30.refs_6_.own_ref, ...), custom_call_target="tpu_custom_call" | custom-call | flops 2000000000 | bytes 3055616 | tf_op jit(solution)/shard_map/home/pallas_call | solution.py:600
  40.1 1.1 %collective-permute-done.11.refs_0_ = f32[64,1408]{1,0:T(8,128)S(1)} collective-permute-done((f32[64,1408]{1,0:T(8,128)S(1)}, f32[64,1408]{1,0:T(8,128)S(1)}, u32[]{:S(2)}, u32[]{:S(2)}) %collective-permute-start.11) | collective-permute-done | bytes 360480 | tf_op jit(solution)/shard_map/ppermute | solution.py:623
  41.2 0.9 %last.1 = f32[16,64,128]{2,1,0:T(8,128)} custom-call(f32[16,64,128]{2,1,0:T(8,128)S(1)} %home.1.home_ref, f32[64,1408]{1,0:T(8,128)S(1)} %collective-permute-done.11.refs_0_), custom_call_target="tpu_custom_call" | custom-call | flops 1000000000 | bytes 1409024 | tf_op jit(solution)/shard_map/last/pallas_call | solution.py:600
  (19 shorter events, 0.0 us)
Async XLA Ops:
  0.0 2.2 %collective-permute-start = (f32[16,64,128]{2,1,0:T(8,128)}, f32[16,64,128]{2,1,0:T(8,128)S(1)}, u32[]{:S(2)}, u32[]{:S(2)}) collective-permute-start(f32[16,64,128]{2,1,0:T(8,128)} %b_ref.3), channel_id=1, source_target_pairs={{16,0},{0,16},{17,1},{1,17},{18,2},{2,18},{19,3},{3,19},{20,4},{4,... | collective-permute-start | bytes 1572872 | tf_op jit(solution)/shard_map/ppermute | solution.py:623
  2.2 1.0 %copy-start = (f32[16,64,128]{2,1,0:T(8,128)S(1)}, f32[16,64,128]{2,1,0:T(8,128)}, u32[]{:S(2)}) copy-start(f32[16,64,128]{2,1,0:T(8,128)} %b_ref.3) | copy-start | bytes 1572868
  3.2 10.6 %copy-start.2 = (f32[4,3]{1,0:T(4,128)S(1)}, f32[4,3]{1,0:T(4,128)}, u32[]{:S(2)}) copy-start(f32[4,3]{1,0:T(4,128)} %w_ref.3) | copy-start | bytes 148
  3.2 10.6 %copy-start.3 = (f32[4,3]{1,0:T(4,128)S(1)}, f32[4,3]{1,0:T(4,128)}, u32[]{:S(2)}) copy-start(f32[4,3]{1,0:T(4,128)} %a_ref.3) | copy-start | bytes 148
  4.0 12.4 %copy-start.1 = (f32[16,64,128]{2,1,0:T(8,128)S(1)}, f32[16,64,128]{2,1,0:T(8,128)}, u32[]{:S(2)}) copy-start(f32[16,64,128]{2,1,0:T(8,128)} %b_ref.3) | copy-start | bytes 1572868
  4.0 20.4 %collective-permute-start.3 = (f32[6,32,128]{2,1,0:T(8,128)S(1)}, f32[6,32,128]{2,1,0:T(8,128)S(1)}, u32[]{:S(2)}, u32[]{:S(2)}) collective-permute-start(f32[6,32,128]{2,1,0:T(8,128)S(1)} %get-tuple-element.24._.refs_0_), channel_id=1, source_target_pairs={{3,0},{0,1},{1,2},{2,3},{7,4},{4,5},{5,6},{6,7},{11,8},{8,9},{9,10... | collective-permute-start | bytes 294920 | tf_op jit(solution)/shard_map/ppermute | solution.py:623
  7.0 17.4 %collective-permute-start.2 = (f32[6,32,128]{2,1,0:T(8,128)S(1)}, f32[6,32,128]{2,1,0:T(8,128)S(1)}, u32[]{:S(2)}, u32[]{:S(2)}) collective-permute-start(f32[6,32,128]{2,1,0:T(8,128)S(1)} %get-tuple-element.24._.refs_0_), channel_id=1, source_target_pairs={{2,0},{3,1},{0,2},{1,3},{6,4},{7,5},{4,6},{5,7},{10,8},{11,9},{8,1... | collective-permute-start | bytes 294920 | tf_op jit(solution)/shard_map/ppermute | solution.py:623
  9.6 14.8 %collective-permute-start.1 = (f32[6,32,128]{2,1,0:T(8,128)S(1)}, f32[6,32,128]{2,1,0:T(8,128)S(1)}, u32[]{:S(2)}, u32[]{:S(2)}) collective-permute-start(f32[6,32,128]{2,1,0:T(8,128)S(1)} %get-tuple-element.24._.refs_0_), channel_id=1, source_target_pairs={{1,0},{2,1},{3,2},{0,3},{5,4},{6,5},{7,6},{4,7},{9,8},{10,9},{11,1... | collective-permute-start | bytes 294920 | tf_op jit(solution)/shard_map/ppermute | solution.py:623
  10.9 4.9 %collective-permute-start.4 = (f32[1,80,128]{2,1,0:T(8,128)S(1)}, f32[1,80,128]{2,1,0:T(8,128)S(1)}, u32[]{:S(2)}, u32[]{:S(2)}) collective-permute-start(f32[1,80,128]{2,1,0:T(8,128)S(1)} %get-tuple-element.26), channel_id=1, source_target_pairs={{12,0},{0,4},{4,8},{8,12},{13,1},{1,5},{5,9},{9,13},{14,2},{2,6},{... | collective-permute-start | bytes 122888 | tf_op jit(solution)/shard_map/ppermute | solution.py:623
  12.4 4.0 %collective-permute-start.5 = (f32[1,80,128]{2,1,0:T(8,128)S(1)}, f32[1,80,128]{2,1,0:T(8,128)S(1)}, u32[]{:S(2)}, u32[]{:S(2)}) collective-permute-start(f32[1,80,128]{2,1,0:T(8,128)S(1)} %get-tuple-element.27), channel_id=1, source_target_pairs={{4,0},{8,4},{12,8},{0,12},{5,1},{9,5},{13,9},{1,13},{6,2},{10,6},{... | collective-permute-start | bytes 122888 | tf_op jit(solution)/shard_map/ppermute | solution.py:623
  16.4 7.9 %copy-start.4 = (f32[128,128]{1,0:T(8,128)S(1)}, f32[128,128]{1,0:T(8,128)}, u32[]{:S(2)}) copy-start(f32[128,128]{1,0:T(8,128)} %constant.26.clone.refs_4_) | copy-start | bytes 196612
  16.4 7.9 %copy-start.13 = (f32[24,32]{1,0:T(8,128)S(1)}, f32[24,32]{1,0:T(8,128)}, u32[]{:S(2)}) copy-start(f32[24,32]{1,0:T(8,128)} %constant.27.clone.refs_5_) | copy-start | bytes 9220
  20.4 19.1 %collective-permute-start.9 = (f32[8,64,128]{2,1,0:T(8,128)S(1)}, f32[8,64,128]{2,1,0:T(8,128)S(1)}, u32[]{:S(2)}, u32[]{:S(2)}) collective-permute-start(f32[8,64,128]{2,1,0:T(8,128)S(1)} %get-tuple-element.41), channel_id=1, source_target_pairs={{3,0},{0,1},{1,2},{2,3},{7,4},{4,5},{5,6},{6,7},{11,8},{8,9},{9,10... | collective-permute-start | bytes 786440 | tf_op jit(solution)/shard_map/ppermute | solution.py:623
  21.2 18.4 %collective-permute-start.10 = (f32[8,64,128]{2,1,0:T(8,128)S(1)}, f32[8,64,128]{2,1,0:T(8,128)S(1)}, u32[]{:S(2)}, u32[]{:S(2)}) collective-permute-start(f32[8,64,128]{2,1,0:T(8,128)S(1)} %get-tuple-element.42), channel_id=1, source_target_pairs={{1,0},{2,1},{3,2},{0,3},{5,4},{6,5},{7,6},{4,7},{9,8},{10,9},{11,1... | collective-permute-start | bytes 786440 | tf_op jit(solution)/shard_map/ppermute | solution.py:623
  24.3 5.4 %copy-start.5 = (bf16[128,128]{1,0:T(8,128)(2,1)S(1)}, bf16[128,128]{1,0:T(8,128)(2,1)}, u32[]{:S(2)}) copy-start(bf16[128,128]{1,0:T(8,128)(2,1)} %constant.33.clone.py2) | copy-start | bytes 98308
  24.4 5.4 %copy-start.6 = (bf16[128,16]{1,0:T(8,128)(2,1)S(1)}, bf16[128,16]{1,0:T(8,128)(2,1)}, u32[]{:S(2)}) copy-start(bf16[128,16]{1,0:T(8,128)(2,1)} %constant.31.clone.px3l) | copy-start | bytes 12292
  24.4 5.4 %copy-start.7 = (bf16[128,16]{1,0:T(8,128)(2,1)S(1)}, bf16[128,16]{1,0:T(8,128)(2,1)}, u32[]{:S(2)}) copy-start(bf16[128,16]{1,0:T(8,128)(2,1)} %constant.30.clone.px3) | copy-start | bytes 12292
  24.4 5.4 %copy-start.8 = (bf16[128,32]{1,0:T(8,128)(2,1)S(1)}, bf16[128,32]{1,0:T(8,128)(2,1)}, u32[]{:S(2)}) copy-start(bf16[128,32]{1,0:T(8,128)(2,1)} %constant.29.clone.px2) | copy-start | bytes 24580
  24.4 5.4 %copy-start.9 = (bf16[128,64]{1,0:T(8,128)(2,1)S(1)}, bf16[128,64]{1,0:T(8,128)(2,1)}, u32[]{:S(2)}) copy-start(bf16[128,64]{1,0:T(8,128)(2,1)} %constant.28.clone.px1.ry3) | copy-start | bytes 49156
  24.4 5.4 %copy-start.10 = (bf16[3,16,256]{2,1,0:T(8,128)(2,1)S(1)}, bf16[3,16,256]{2,1,0:T(8,128)(2,1)}, u32[]{:S(2)}) copy-start(bf16[3,16,256]{2,1,0:T(8,128)(2,1)} %constant.32.clone.rx3) | copy-start | bytes 73732
  24.4 5.4 %copy-start.11 = (bf16[64,128]{1,0:T(8,128)(2,1)S(1)}, bf16[64,128]{1,0:T(8,128)(2,1)}, u32[]{:S(2)}) copy-start(bf16[64,128]{1,0:T(8,128)(2,1)} %constant.35.clone.py3l) | copy-start | bytes 49156
  24.4 5.4 %copy-start.12 = (bf16[64,128]{1,0:T(8,128)(2,1)S(1)}, bf16[64,128]{1,0:T(8,128)(2,1)}, u32[]{:S(2)}) copy-start(bf16[64,128]{1,0:T(8,128)(2,1)} %constant.34.clone.py3) | copy-start | bytes 49156
  24.4 5.4 %copy-start.14 = (bf16[16,8]{1,0:T(8,128)(2,1)S(1)}, bf16[16,8]{1,0:T(8,128)(2,1)}, u32[]{:S(2)}) copy-start(bf16[16,8]{1,0:T(8,128)(2,1)} %constant.37.clone.pz3) | copy-start | bytes 772
  24.5 5.4 %copy-start.15 = (bf16[16,16]{1,0:T(8,128)(2,1)S(1)}, bf16[16,16]{1,0:T(8,128)(2,1)}, u32[]{:S(2)}) copy-start(bf16[16,16]{1,0:T(8,128)(2,1)} %constant.36.clone.pz2) | copy-start | bytes 1540
  24.5 5.4 %copy-start.16 = (bf16[8,128]{1,0:T(8,128)(2,1)S(1)}, bf16[8,128]{1,0:T(8,128)(2,1)}, u32[]{:S(2)}) copy-start(bf16[8,128]{1,0:T(8,128)(2,1)} %constant.38.clone.rz3) | copy-start | bytes 6148
  25.9 5.3 %collective-permute-start.7 = (f32[120,128]{1,0:T(8,128)S(1)}, f32[120,128]{1,0:T(8,128)S(1)}, u32[]{:S(2)}, u32[]{:S(2)}) collective-permute-start(f32[120,128]{1,0:T(8,128)S(1)} %get-tuple-element.31._.refs_0_), channel_id=1, source_target_pairs={{8,0},{12,4},{0,8},{4,12},{9,1},{13,5},{1,9},{5,13},{10,2},{14,6},... | collective-permute-start | bytes 184328 | tf_op jit(solution)/shard_map/ppermute | solution.py:623
  27.5 4.7 %collective-permute-start.6 = (f32[216,128]{1,0:T(8,128)S(1)}, f32[216,128]{1,0:T(8,128)S(1)}, u32[]{:S(2)}, u32[]{:S(2)}) collective-permute-start(f32[216,128]{1,0:T(8,128)S(1)} %get-tuple-element.34), channel_id=1, source_target_pairs={{4,0},{8,4},{12,8},{0,12},{5,1},{9,5},{13,9},{1,13},{6,2},{10,6},{... | collective-permute-start | bytes 331784 | tf_op jit(solution)/shard_map/ppermute | solution.py:623
  29.8 5.6 %collective-permute-start.8 = (f32[216,128]{1,0:T(8,128)S(1)}, f32[216,128]{1,0:T(8,128)S(1)}, u32[]{:S(2)}, u32[]{:S(2)}) collective-permute-start(f32[216,128]{1,0:T(8,128)S(1)} %get-tuple-element.35), channel_id=1, source_target_pairs={{12,0},{0,4},{4,8},{8,12},{13,1},{1,5},{5,9},{9,13},{14,2},{2,6},{... | collective-permute-start | bytes 331784 | tf_op jit(solution)/shard_map/ppermute | solution.py:623
  39.5 1.7 %collective-permute-start.11 = (f32[64,1408]{1,0:T(8,128)S(1)}, f32[64,1408]{1,0:T(8,128)S(1)}, u32[]{:S(2)}, u32[]{:S(2)}) collective-permute-start(f32[64,1408]{1,0:T(8,128)S(1)} %away.1), channel_id=1, source_target_pairs={{16,0},{0,16},{17,1},{1,17},{18,2},{2,18},{19,3},{3,19},{20,4},{4,... | collective-permute-start | bytes 1081352 | tf_op jit(solution)/shard_map/ppermute | solution.py:623

commit v5 on v4

--- a/solution.py
+++ b/solution.py
@@ -197,7 +197,7 @@
     return jnp.concatenate([lo_ref[z, s.nx - R :], b_ref[z], hi_ref[z, 0:R]], axis=0)
 
 
-def share_kernel(s, b_ref, lo_ref, hi_ref, m_ref, first_ref, last_ref):
+def share_kernel(s, b_ref, lo_ref, hi_ref, _, m_ref, first_ref, last_ref):
     b = [extended(s, b_ref, lo_ref, hi_ref, z) for z in range(s.nz)]
     planes = []
     for k in range(-1, s.z1 + 2):
@@ -271,7 +271,7 @@
     return [out[i : i + TERMS] for i in range(0, len(out), TERMS)]
 
 
-def tap_kernel(s, w_ref, a_ref, _, tap_ref, x0_ref, y0_ref):
+def tap_kernel(s, w_ref, a_ref, tap_ref, x0_ref, y0_ref):
     coef = spreads(w_ref, (0, 1))
     unit = near_units(coef)
     d = lanes_of((1, LANES)).astype(F32)
@@ -632,21 +632,21 @@
     c = {k: jnp.asarray(v) for k, v in constants(s).items()}
     brick = (s.nz, s.nx, s.ny)
     side = (R, s.nx, s.ny)
+    taps, x0, y0 = call(
+        functools.partial(tap_kernel, s), "taps", [widths, amplitudes],
+        arrays((8, LANES))
+        + arrays((TERMS * s.nx, 3 * s.ext), (2 * LANES, 2 * TERMS * s.ny), dtype=BF16),
+        flops=6 * 10**8,
+    )
     high_rows = fetch(charges, gx=1)
     low_rows = high_rows if s.gx == 2 else fetch(charges, gx=-1)
     strips = (s.fine_tiles, s.ext, LANES)
     share, first_cells, last_cells = call(
         functools.partial(share_kernel, s), "share", [charges, low_rows, high_rows],
-        arrays((s.tiles1, s.rows1, LANES), strips, strips), flops=10**9,
+        arrays((s.tiles1, s.rows1, LANES), strips, strips), after=[x0], flops=10**9,
     )
     shares = [share] + [fetch(share, gz=b) for b in range(1, s.gz)]
     left, right = fetch(last_cells, gy=-1), fetch(first_cells, gy=1)
-    taps, x0, y0 = call(
-        functools.partial(tap_kernel, s), "taps", [widths, amplitudes],
-        arrays((8, LANES))
-        + arrays((TERMS * s.nx, 3 * s.ext), (2 * LANES, 2 * TERMS * s.ny), dtype=BF16),
-        after=[share], flops=6 * 10**8,
-    )
     tiles = s.nz + 2 * s.fine_tiles
     halved = pltpu.VMEM((TERMS, s.nz * s.nx, 2 * LANES), BF16)
     near, near_down, near_up = call(

time: 42.2 us -> 36.9 us (0.87)
  waiting for transfers between devices: 9.25 us -> 3.83 us
    ppermute x12, waiting for transfers between devices: 9.25 us -> 3.83 us  [fetch(): return lax.ppermute(x, names if len(names) > 1 else names[0], pairs)]
    unnamed x34 -> x36, local copies, waits for them, and re-layouts: 1.14 us -> 1.46 us
  transfers between devices with their start and end apart: 12 -> 12, of which waited for: 6 -> 3; matrix products, arithmetic and copies ran while one was open for 0% -> 0% of each run, Pallas kernels for 28% -> 32%
where the time goes in v5:
time: 36.9 us; the launch traced here: 36.7 us
  starting transfers between devices  17.9 us (49%)
  Pallas kernels  13.2 us (36%)
  waiting for transfers between devices  3.83 us (10%)
  local copies, waits for them, and re-layouts  1.46 us (4%)
    ppermute x12, starting transfers between devices, fetch(): return lax.ppermute(x, names if len(names) > 1 else names[0], pairs)  17.9 us
    pallas_call x9, Pallas kernels, call(): pl.pallas_call(kernel, name=name, out_shape=out_shapes, in_specs=[spec(i)...  13.2 us
    ppermute x12, waiting for transfers between devices, fetch(): return lax.ppermute(x, names if len(names) > 1 else names[0], pairs)  3.83 us
    unnamed x36, local copies, waits for them, and re-layouts  1.46 us
  transfers between devices with their start and end apart: 12, of which 3 were waited for; matrix products, arithmetic and copies ran while one was open for 0% of the time, Pallas kernels for 32%

profile of v5, /device:TPU:0, one launch (start us, length us, event | category | flops | bytes accessed | tf_op | source)
XLA Modules:
  0.0 36.7 jit_solution(5495167664850550825)
XLA Ops:
  0.0 0.5 %collective-permute-start = (f32[16,64,128]{2,1,0:T(8,128)}, f32[16,64,128]{2,1,0:T(8,128)S(1)}, u32[]{:S(2)}, u32[]{:S(2)}) collective-permute-start(f32[16,64,128]{2,1,0:T(8,128)} %b_ref.3), channel_id=1, source_target_pairs={{16,0},{0,16},{17,1},{1,17},{18,2},{2,18},{19,3},{3,19},{20,4},{4,... | collective-permute-start | bytes 1572872 | tf_op jit(solution)/shard_map/ppermute | solution.py:623
  0.5 0.7 %copy-done.1 = f32[4,3]{1,0:T(4,128)S(1)} copy-done((f32[4,3]{1,0:T(4,128)S(1)}, f32[4,3]{1,0:T(4,128)}, u32[]{:S(2)}) %copy-start.1) | copy-done | bytes 72
  1.1 0.7 %copy-done.3 = f32[4,3]{1,0:T(4,128)S(1)} copy-done((f32[4,3]{1,0:T(4,128)S(1)}, f32[4,3]{1,0:T(4,128)}, u32[]{:S(2)}) %copy-start.3) | copy-done | bytes 72
  1.8 0.4 %taps.1 = (f32[8,128]{1,0:T(8,128)S(1)}, bf16[192,240]{1,0:T(8,128)(2,1)S(1)}, bf16[256,768]{1,0:T(8,128)(2,1)S(1)}) custom-call(f32[4,3]{1,0:T(4,128)S(1)} %copy-done.1, f32[4,3]{1,0:T(4,128)S(1)} %copy-done.3), custom_call_target="tpu_custom_call" | custom-call | flops 600000000 | bytes 489568 | tf_op jit(solution)/shard_map/taps/pallas_call | solution.py:600
  2.2 0.0 collective-permute-done.lo_ref.hi_ref
  2.2 0.7 %share.1 = (f32[6,32,128]{2,1,0:T(8,128)S(1)}, f32[1,80,128]{2,1,0:T(8,128)S(1)}, f32[1,80,128]{2,1,0:T(8,128)S(1)}) custom-call(f32[16,64,128]{2,1,0:T(8,128)S(1)} %copy-done, f32[16,64,128]{2,1,0:T(8,128)S(1)} %collective-permute-done.lo_ref.hi_ref, f32[16,64,128]{2,1,0:T(8,128)S(1)} %collective-permute-done.lo_ref.hi_ref, ...), custom_call_target="tpu_custom_call" | custom-call | flops 1000000000 | bytes 1845248 | tf_op jit(solution)/shard_map/share/pallas_call | solution.py:600
  2.9 2.9 %collective-permute-start.4 = (f32[1,80,128]{2,1,0:T(8,128)S(1)}, f32[1,80,128]{2,1,0:T(8,128)S(1)}, u32[]{:S(2)}, u32[]{:S(2)}) collective-permute-start(f32[1,80,128]{2,1,0:T(8,128)S(1)} %get-tuple-element.27), channel_id=1, source_target_pairs={{12,0},{0,4},{4,8},{8,12},{13,1},{1,5},{5,9},{9,13},{14,2},{2,6},{... | collective-permute-start | bytes 122888 | tf_op jit(solution)/shard_map/ppermute | solution.py:623
  5.8 1.0 %collective-permute-start.5 = (f32[1,80,128]{2,1,0:T(8,128)S(1)}, f32[1,80,128]{2,1,0:T(8,128)S(1)}, u32[]{:S(2)}, u32[]{:S(2)}) collective-permute-start(f32[1,80,128]{2,1,0:T(8,128)S(1)} %get-tuple-element.28), channel_id=1, source_target_pairs={{4,0},{8,4},{12,8},{0,12},{5,1},{9,5},{13,9},{1,13},{6,2},{10,6},{... | collective-permute-start | bytes 122888 | tf_op jit(solution)/shard_map/ppermute | solution.py:623
  6.8 2.0 %collective-permute-start.3 = (f32[6,32,128]{2,1,0:T(8,128)S(1)}, f32[6,32,128]{2,1,0:T(8,128)S(1)}, u32[]{:S(2)}, u32[]{:S(2)}) collective-permute-start(f32[6,32,128]{2,1,0:T(8,128)S(1)} %get-tuple-element.26.refs_0_), channel_id=1, source_target_pairs={{3,0},{0,1},{1,2},{2,3},{7,4},{4,5},{5,6},{6,7},{11,8},{8,9},{9,10... | collective-permute-start | bytes 294920 | tf_op jit(solution)/shard_map/ppermute | solution.py:623
  8.8 2.6 %collective-permute-start.2 = (f32[6,32,128]{2,1,0:T(8,128)S(1)}, f32[6,32,128]{2,1,0:T(8,128)S(1)}, u32[]{:S(2)}, u32[]{:S(2)}) collective-permute-start(f32[6,32,128]{2,1,0:T(8,128)S(1)} %get-tuple-element.26.refs_0_), channel_id=1, source_target_pairs={{2,0},{3,1},{0,2},{1,3},{6,4},{7,5},{4,6},{5,7},{10,8},{11,9},{8,1... | collective-permute-start | bytes 294920 | tf_op jit(solution)/shard_map/ppermute | solution.py:623
  11.4 1.3 %collective-permute-start.1 = (f32[6,32,128]{2,1,0:T(8,128)S(1)}, f32[6,32,128]{2,1,0:T(8,128)S(1)}, u32[]{:S(2)}, u32[]{:S(2)}) collective-permute-start(f32[6,32,128]{2,1,0:T(8,128)S(1)} %get-tuple-element.26.refs_0_), channel_id=1, source_target_pairs={{1,0},{2,1},{3,2},{0,3},{5,4},{6,5},{7,6},{4,7},{9,8},{10,9},{11,1... | collective-permute-start | bytes 294920 | tf_op jit(solution)/shard_map/ppermute | solution.py:623
  12.8 0.0 collective-permute-done.4.left_ref
  12.8 0.0 collective-permute-done.5.right_ref
  12.8 0.0 copy-start.14
  12.8 4.0 %near.1 = (f32[16,64,128]{2,1,0:T(8,128)S(1)}, f32[8,64,128]{2,1,0:T(8,128)S(1)}, f32[8,64,128]{2,1,0:T(8,128)S(1)}) custom-call(f32[8,128]{1,0:T(8,128)S(1)} %get-tuple-element.24.tap_ref, f32[16,64,128]{2,1,0:T(8,128)S(1)} %copy-done, f32[16,64,128]{2,1,0:T(8,128)S(1)} %collective-permute-done.lo_ref.hi_ref, ...), custom_call_target="tpu_custom_call" | custom-call | flops 5000000000 | bytes 3192832 | tf_op jit(solution)/shard_map/near/pallas_call | solution.py:600
  16.8 0.7 %collective-permute-start.9 = (f32[8,64,128]{2,1,0:T(8,128)S(1)}, f32[8,64,128]{2,1,0:T(8,128)S(1)}, u32[]{:S(2)}, u32[]{:S(2)}) collective-permute-start(f32[8,64,128]{2,1,0:T(8,128)S(1)} %get-tuple-element.41), channel_id=1, source_target_pairs={{3,0},{0,1},{1,2},{2,3},{7,4},{4,5},{5,6},{6,7},{11,8},{8,9},{9,10... | collective-permute-start | bytes 786440 | tf_op jit(solution)/shard_map/ppermute | solution.py:623
  17.6 3.1 %collective-permute-start.10 = (f32[8,64,128]{2,1,0:T(8,128)S(1)}, f32[8,64,128]{2,1,0:T(8,128)S(1)}, u32[]{:S(2)}, u32[]{:S(2)}) collective-permute-start(f32[8,64,128]{2,1,0:T(8,128)S(1)} %get-tuple-element.42), channel_id=1, source_target_pairs={{1,0},{2,1},{3,2},{0,3},{5,4},{6,5},{7,6},{4,7},{9,8},{10,9},{11,1... | collective-permute-start | bytes 786440 | tf_op jit(solution)/shard_map/ppermute | solution.py:623
  20.7 0.0 collective-permute-done.3.refs_3_
  20.7 0.0 collective-permute-done.2.refs_2_
  20.7 0.0 copy-start.2
  20.7 0.0 copy-start.4
  20.8 0.0 copy-start.6
  20.8 0.0 copy-start.7
  20.8 0.0 copy-start.8
  20.8 0.0 copy-start.9
  20.8 0.0 copy-start.10
  20.8 0.0 copy-start.11
  20.8 0.0 copy-start.12
  20.8 0.0 copy-start.13
  20.9 0.0 copy-start.15
  20.9 0.0 copy-start.16
  20.9 0.0 copy-start.17
  20.9 1.4 %depth.1 = (f32[33,32,128]{2,1,0:T(8,128)S(1)}, f32[216,128]{1,0:T(8,128)S(1)}, f32[216,128]{1,0:T(8,128)S(1)}, f32[120,128]{1,0:T(8,128)S(1)}) custom-call(f32[8,128]{1,0:T(8,128)S(1)} %get-tuple-element.24.tap_ref, f32[6,32,128]{2,1,0:T(8,128)S(1)} %get-tuple-element.26.refs_0_, f32[6,32,128]{2,1,0:T(8,128)S(1)} %collective-permute-done.1.refs_1_, ...), custom_call_target="tpu_custom_call" | custom-call | flops 2000000000 | bytes 1813504 | tf_op jit(solution)/shard_map/depth/pallas_call | solution.py:600
  22.3 1.6 %collective-permute-start.7 = (f32[120,128]{1,0:T(8,128)S(1)}, f32[120,128]{1,0:T(8,128)S(1)}, u32[]{:S(2)}, u32[]{:S(2)}) collective-permute-start(f32[120,128]{1,0:T(8,128)S(1)} %get-tuple-element.31._.refs_0_), channel_id=1, source_target_pairs={{8,0},{12,4},{0,8},{4,12},{9,1},{13,5},{1,9},{5,13},{10,2},{14,6},... | collective-permute-start | bytes 184328 | tf_op jit(solution)/shard_map/ppermute | solution.py:623
  23.9 0.5 %collective-permute-start.6 = (f32[216,128]{1,0:T(8,128)S(1)}, f32[216,128]{1,0:T(8,128)S(1)}, u32[]{:S(2)}, u32[]{:S(2)}) collective-permute-start(f32[216,128]{1,0:T(8,128)S(1)} %get-tuple-element.34), channel_id=1, source_target_pairs={{4,0},{8,4},{12,8},{0,12},{5,1},{9,5},{13,9},{1,13},{6,2},{10,6},{... | collective-permute-start | bytes 331784 | tf_op jit(solution)/shard_map/ppermute | solution.py:623
  24.4 1.5 %collective-permute-start.8 = (f32[216,128]{1,0:T(8,128)S(1)}, f32[216,128]{1,0:T(8,128)S(1)}, u32[]{:S(2)}, u32[]{:S(2)}) collective-permute-start(f32[216,128]{1,0:T(8,128)S(1)} %get-tuple-element.35), channel_id=1, source_target_pairs={{12,0},{0,4},{4,8},{8,12},{13,1},{1,5},{5,9},{9,13},{14,2},{2,6},{... | collective-permute-start | bytes 331784 | tf_op jit(solution)/shard_map/ppermute | solution.py:623
  26.0 1.3 %matrices.1 = (f32[96,128]{1,0:T(8,128)S(1)}, bf16[128,768]{1,0:T(8,128)(2,1)S(1)}, bf16[128,768]{1,0:T(8,128)(2,1)S(1)}, bf16[128,768]{1,0:T(8,128)(2,1)S(1)}, ...) custom-call(f32[4,3]{1,0:T(4,128)S(1)} %copy-done.2, f32[4,3]{1,0:T(4,128)S(1)} %copy-done.4, ...), custom_call_target="tpu_custom_call" | custom-call | flops 2000000000 | bytes 973664 | tf_op jit(solution)/shard_map/matrices/pallas_call | solution.py:600
  27.3 0.0 collective-permute-done.7.refs_2_
  27.4 1.3 %collective-permute-done.6.refs_1_ = f32[216,128]{1,0:T(8,128)S(1)} collective-permute-done((f32[216,128]{1,0:T(8,128)S(1)}, f32[216,128]{1,0:T(8,128)S(1)}, u32[]{:S(2)}, u32[]{:S(2)}) %collective-permute-start.6) | collective-permute-done | bytes 110624 | tf_op jit(solution)/shard_map/ppermute | solution.py:623
  28.6 1.4 %collective-permute-done.8.refs_3_ = f32[216,128]{1,0:T(8,128)S(1)} collective-permute-done((f32[216,128]{1,0:T(8,128)S(1)}, f32[216,128]{1,0:T(8,128)S(1)}, u32[]{:S(2)}, u32[]{:S(2)}) %collective-permute-start.8) | collective-permute-done | bytes 110624 | tf_op jit(solution)/shard_map/ppermute | solution.py:623
  30.1 3.5 %along.1.d_ref = f32[240,1408]{1,0:T(8,128)S(1)} custom-call(f32[96,128]{1,0:T(8,128)S(1)} %get-tuple-element.32.z_ref, f32[33,32,128]{2,1,0:T(8,128)S(1)} %get-tuple-element.33.w_ref, f32[120,128]{1,0:T(8,128)S(1)} %get-tuple-element.31._.refs_0_, f32[216,128]{1,0:T(8,128)S(1)} %collective-permute-done.6.refs_1_, ...), custom_call_target="tpu_custom_call" | custom-call | flops 3000000000 | bytes 2875392 | tf_op jit(solution)/shard_map/along/pallas_call | solution.py:600
  33.5 0.5 %away.1 = f32[64,1408]{1,0:T(8,128)S(1)} custom-call(f32[240,1408]{1,0:T(8,128)S(1)} %along.1.d_ref, bf16[128,256]{1,0:T(8,128)(2,1)S(1)} %get-tuple-element.39.xh_ref, bf16[128,256]{1,0:T(8,128)(2,1)S(1)} %get-tuple-element.40.xl_ref), custom_call_target="tpu_custom_call" | custom-call | flops 1000000000 | bytes 1843200 | tf_op jit(solution)/shard_map/away/pallas_call | solution.py:600
  34.1 0.1 collective-permute-start.11
  34.2 0.0 collective-permute-done.9.low_ref
  34.2 0.0 collective-permute-done.10.high_ref
  34.2 0.6 %home.1.home_ref = f32[16,64,128]{2,1,0:T(8,128)S(1)} custom-call(f32[240,1408]{1,0:T(8,128)S(1)} %along.1.d_ref, bf16[128,256]{1,0:T(8,128)(2,1)S(1)} %get-tuple-element.39.xh_ref, bf16[128,256]{1,0:T(8,128)(2,1)S(1)} %get-tuple-element.40.xl_ref, f32[16,64,128]{2,1,0:T(8,128)S(1)} %get-tuple-element.30.refs_6_.own_ref, ...), custom_call_target="tpu_custom_call" | custom-call | flops 2000000000 | bytes 3055616 | tf_op jit(solution)/shard_map/home/pallas_call | solution.py:600
  34.8 1.1 %collective-permute-done.11.refs_0_ = f32[64,1408]{1,0:T(8,128)S(1)} collective-permute-done((f32[64,1408]{1,0:T(8,128)S(1)}, f32[64,1408]{1,0:T(8,128)S(1)}, u32[]{:S(2)}, u32[]{:S(2)}) %collective-permute-start.11) | collective-permute-done | bytes 360480 | tf_op jit(solution)/shard_map/ppermute | solution.py:623
  35.8 0.9 %last.1 = f32[16,64,128]{2,1,0:T(8,128)} custom-call(f32[16,64,128]{2,1,0:T(8,128)S(1)} %home.1.home_ref, f32[64,1408]{1,0:T(8,128)S(1)} %collective-permute-done.11.refs_0_), custom_call_target="tpu_custom_call" | custom-call | flops 1000000000 | bytes 1409024 | tf_op jit(solution)/shard_map/last/pallas_call | solution.py:600
  (21 shorter events, 0.0 us)
Async XLA Ops:
  0.0 2.2 %copy-start = (f32[16,64,128]{2,1,0:T(8,128)S(1)}, f32[16,64,128]{2,1,0:T(8,128)}, u32[]{:S(2)}) copy-start(f32[16,64,128]{2,1,0:T(8,128)} %b_ref.3) | copy-start | bytes 1572868
  0.0 2.2 %collective-permute-start = (f32[16,64,128]{2,1,0:T(8,128)}, f32[16,64,128]{2,1,0:T(8,128)S(1)}, u32[]{:S(2)}, u32[]{:S(2)}) collective-permute-start(f32[16,64,128]{2,1,0:T(8,128)} %b_ref.3), channel_id=1, source_target_pairs={{16,0},{0,16},{17,1},{1,17},{18,2},{2,18},{19,3},{3,19},{20,4},{4,... | collective-permute-start | bytes 1572872 | tf_op jit(solution)/shard_map/ppermute | solution.py:623
  0.5 0.7 %copy-start.1 = (f32[4,3]{1,0:T(4,128)S(1)}, f32[4,3]{1,0:T(4,128)}, u32[]{:S(2)}) copy-start(f32[4,3]{1,0:T(4,128)} %w_ref.3) | copy-start | bytes 148
  1.1 0.7 %copy-start.3 = (f32[4,3]{1,0:T(4,128)S(1)}, f32[4,3]{1,0:T(4,128)}, u32[]{:S(2)}) copy-start(f32[4,3]{1,0:T(4,128)} %a_ref.3) | copy-start | bytes 148
  2.9 9.9 %collective-permute-start.4 = (f32[1,80,128]{2,1,0:T(8,128)S(1)}, f32[1,80,128]{2,1,0:T(8,128)S(1)}, u32[]{:S(2)}, u32[]{:S(2)}) collective-permute-start(f32[1,80,128]{2,1,0:T(8,128)S(1)} %get-tuple-element.27), channel_id=1, source_target_pairs={{12,0},{0,4},{4,8},{8,12},{13,1},{1,5},{5,9},{9,13},{14,2},{2,6},{... | collective-permute-start | bytes 122888 | tf_op jit(solution)/shard_map/ppermute | solution.py:623
  5.8 7.0 %collective-permute-start.5 = (f32[1,80,128]{2,1,0:T(8,128)S(1)}, f32[1,80,128]{2,1,0:T(8,128)S(1)}, u32[]{:S(2)}, u32[]{:S(2)}) collective-permute-start(f32[1,80,128]{2,1,0:T(8,128)S(1)} %get-tuple-element.28), channel_id=1, source_target_pairs={{4,0},{8,4},{12,8},{0,12},{5,1},{9,5},{13,9},{1,13},{6,2},{10,6},{... | collective-permute-start | bytes 122888 | tf_op jit(solution)/shard_map/ppermute | solution.py:623
  6.8 13.9 %collective-permute-start.3 = (f32[6,32,128]{2,1,0:T(8,128)S(1)}, f32[6,32,128]{2,1,0:T(8,128)S(1)}, u32[]{:S(2)}, u32[]{:S(2)}) collective-permute-start(f32[6,32,128]{2,1,0:T(8,128)S(1)} %get-tuple-element.26.refs_0_), channel_id=1, source_target_pairs={{3,0},{0,1},{1,2},{2,3},{7,4},{4,5},{5,6},{6,7},{11,8},{8,9},{9,10... | collective-permute-start | bytes 294920 | tf_op jit(solution)/shard_map/ppermute | solution.py:623
  8.8 11.9 %collective-permute-start.2 = (f32[6,32,128]{2,1,0:T(8,128)S(1)}, f32[6,32,128]{2,1,0:T(8,128)S(1)}, u32[]{:S(2)}, u32[]{:S(2)}) collective-permute-start(f32[6,32,128]{2,1,0:T(8,128)S(1)} %get-tuple-element.26.refs_0_), channel_id=1, source_target_pairs={{2,0},{3,1},{0,2},{1,3},{6,4},{7,5},{4,6},{5,7},{10,8},{11,9},{8,1... | collective-permute-start | bytes 294920 | tf_op jit(solution)/shard_map/ppermute | solution.py:623
  11.4 9.3 %collective-permute-start.1 = (f32[6,32,128]{2,1,0:T(8,128)S(1)}, f32[6,32,128]{2,1,0:T(8,128)S(1)}, u32[]{:S(2)}, u32[]{:S(2)}) collective-permute-start(f32[6,32,128]{2,1,0:T(8,128)S(1)} %get-tuple-element.26.refs_0_), channel_id=1, source_target_pairs={{1,0},{2,1},{3,2},{0,3},{5,4},{6,5},{7,6},{4,7},{9,8},{10,9},{11,1... | collective-permute-start | bytes 294920 | tf_op jit(solution)/shard_map/ppermute | solution.py:623
  12.8 7.9 %copy-start.5 = (f32[128,128]{1,0:T(8,128)S(1)}, f32[128,128]{1,0:T(8,128)}, u32[]{:S(2)}) copy-start(f32[128,128]{1,0:T(8,128)} %constant.26.clone.refs_4_) | copy-start | bytes 196612
  12.8 7.9 %copy-start.14 = (f32[24,32]{1,0:T(8,128)S(1)}, f32[24,32]{1,0:T(8,128)}, u32[]{:S(2)}) copy-start(f32[24,32]{1,0:T(8,128)} %constant.27.clone.refs_5_) | copy-start | bytes 9220
  16.8 17.3 %collective-permute-start.9 = (f32[8,64,128]{2,1,0:T(8,128)S(1)}, f32[8,64,128]{2,1,0:T(8,128)S(1)}, u32[]{:S(2)}, u32[]{:S(2)}) collective-permute-start(f32[8,64,128]{2,1,0:T(8,128)S(1)} %get-tuple-element.41), channel_id=1, source_target_pairs={{3,0},{0,1},{1,2},{2,3},{7,4},{4,5},{5,6},{6,7},{11,8},{8,9},{9,10... | collective-permute-start | bytes 786440 | tf_op jit(solution)/shard_map/ppermute | solution.py:623
  17.6 16.6 %collective-permute-start.10 = (f32[8,64,128]{2,1,0:T(8,128)S(1)}, f32[8,64,128]{2,1,0:T(8,128)S(1)}, u32[]{:S(2)}, u32[]{:S(2)}) collective-permute-start(f32[8,64,128]{2,1,0:T(8,128)S(1)} %get-tuple-element.42), channel_id=1, source_target_pairs={{1,0},{2,1},{3,2},{0,3},{5,4},{6,5},{7,6},{4,7},{9,8},{10,9},{11,1... | collective-permute-start | bytes 786440 | tf_op jit(solution)/shard_map/ppermute | solution.py:623
  20.7 5.2 %copy-start.2 = (f32[4,3]{1,0:T(4,128)S(1)}, f32[4,3]{1,0:T(4,128)}, u32[]{:S(2)}) copy-start(f32[4,3]{1,0:T(4,128)} %w_ref.3) | copy-start | bytes 148
  20.7 5.2 %copy-start.4 = (f32[4,3]{1,0:T(4,128)S(1)}, f32[4,3]{1,0:T(4,128)}, u32[]{:S(2)}) copy-start(f32[4,3]{1,0:T(4,128)} %a_ref.3) | copy-start | bytes 148
  20.8 5.1 %copy-start.6 = (bf16[128,128]{1,0:T(8,128)(2,1)S(1)}, bf16[128,128]{1,0:T(8,128)(2,1)}, u32[]{:S(2)}) copy-start(bf16[128,128]{1,0:T(8,128)(2,1)} %constant.33.clone.py2) | copy-start | bytes 98308
  20.8 5.1 %copy-start.7 = (bf16[128,16]{1,0:T(8,128)(2,1)S(1)}, bf16[128,16]{1,0:T(8,128)(2,1)}, u32[]{:S(2)}) copy-start(bf16[128,16]{1,0:T(8,128)(2,1)} %constant.31.clone.px3l) | copy-start | bytes 12292
  20.8 5.1 %copy-start.8 = (bf16[128,16]{1,0:T(8,128)(2,1)S(1)}, bf16[128,16]{1,0:T(8,128)(2,1)}, u32[]{:S(2)}) copy-start(bf16[128,16]{1,0:T(8,128)(2,1)} %constant.30.clone.px3) | copy-start | bytes 12292
  20.8 5.1 %copy-start.9 = (bf16[128,32]{1,0:T(8,128)(2,1)S(1)}, bf16[128,32]{1,0:T(8,128)(2,1)}, u32[]{:S(2)}) copy-start(bf16[128,32]{1,0:T(8,128)(2,1)} %constant.29.clone.px2) | copy-start | bytes 24580
  20.8 5.1 %copy-start.10 = (bf16[128,64]{1,0:T(8,128)(2,1)S(1)}, bf16[128,64]{1,0:T(8,128)(2,1)}, u32[]{:S(2)}) copy-start(bf16[128,64]{1,0:T(8,128)(2,1)} %constant.28.clone.px1.ry3) | copy-start | bytes 49156
  20.8 5.1 %copy-start.11 = (bf16[3,16,256]{2,1,0:T(8,128)(2,1)S(1)}, bf16[3,16,256]{2,1,0:T(8,128)(2,1)}, u32[]{:S(2)}) copy-start(bf16[3,16,256]{2,1,0:T(8,128)(2,1)} %constant.32.clone.rx3) | copy-start | bytes 73732
  20.8 5.1 %copy-start.12 = (bf16[64,128]{1,0:T(8,128)(2,1)S(1)}, bf16[64,128]{1,0:T(8,128)(2,1)}, u32[]{:S(2)}) copy-start(bf16[64,128]{1,0:T(8,128)(2,1)} %constant.35.clone.py3l) | copy-start | bytes 49156
  20.8 5.1 %copy-start.13 = (bf16[64,128]{1,0:T(8,128)(2,1)S(1)}, bf16[64,128]{1,0:T(8,128)(2,1)}, u32[]{:S(2)}) copy-start(bf16[64,128]{1,0:T(8,128)(2,1)} %constant.34.clone.py3) | copy-start | bytes 49156
  20.9 5.1 %copy-start.15 = (bf16[16,8]{1,0:T(8,128)(2,1)S(1)}, bf16[16,8]{1,0:T(8,128)(2,1)}, u32[]{:S(2)}) copy-start(bf16[16,8]{1,0:T(8,128)(2,1)} %constant.37.clone.pz3) | copy-start | bytes 772
  20.9 5.1 %copy-start.16 = (bf16[16,16]{1,0:T(8,128)(2,1)S(1)}, bf16[16,16]{1,0:T(8,128)(2,1)}, u32[]{:S(2)}) copy-start(bf16[16,16]{1,0:T(8,128)(2,1)} %constant.36.clone.pz2) | copy-start | bytes 1540
  20.9 5.1 %copy-start.17 = (bf16[8,128]{1,0:T(8,128)(2,1)S(1)}, bf16[8,128]{1,0:T(8,128)(2,1)}, u32[]{:S(2)}) copy-start(bf16[8,128]{1,0:T(8,128)(2,1)} %constant.38.clone.rz3) | copy-start | bytes 6148
  22.3 5.1 %collective-permute-start.7 = (f32[120,128]{1,0:T(8,128)S(1)}, f32[120,128]{1,0:T(8,128)S(1)}, u32[]{:S(2)}, u32[]{:S(2)}) collective-permute-start(f32[120,128]{1,0:T(8,128)S(1)} %get-tuple-element.31._.refs_0_), channel_id=1, source_target_pairs={{8,0},{12,4},{0,8},{4,12},{9,1},{13,5},{1,9},{5,13},{10,2},{14,6},... | collective-permute-start | bytes 184328 | tf_op jit(solution)/shard_map/ppermute | solution.py:623
  23.9 4.7 %collective-permute-start.6 = (f32[216,128]{1,0:T(8,128)S(1)}, f32[216,128]{1,0:T(8,128)S(1)}, u32[]{:S(2)}, u32[]{:S(2)}) collective-permute-start(f32[216,128]{1,0:T(8,128)S(1)} %get-tuple-element.34), channel_id=1, source_target_pairs={{4,0},{8,4},{12,8},{0,12},{5,1},{9,5},{13,9},{1,13},{6,2},{10,6},{... | collective-permute-start | bytes 331784 | tf_op jit(solution)/shard_map/ppermute | solution.py:623
  24.4 5.6 %collective-permute-start.8 = (f32[216,128]{1,0:T(8,128)S(1)}, f32[216,128]{1,0:T(8,128)S(1)}, u32[]{:S(2)}, u32[]{:S(2)}) collective-permute-start(f32[216,128]{1,0:T(8,128)S(1)} %get-tuple-element.35), channel_id=1, source_target_pairs={{12,0},{0,4},{4,8},{8,12},{13,1},{1,5},{5,9},{9,13},{14,2},{2,6},{... | collective-permute-start | bytes 331784 | tf_op jit(solution)/shard_map/ppermute | solution.py:623
  34.1 1.7 %collective-permute-start.11 = (f32[64,1408]{1,0:T(8,128)S(1)}, f32[64,1408]{1,0:T(8,128)S(1)}, u32[]{:S(2)}, u32[]{:S(2)}) collective-permute-start(f32[64,1408]{1,0:T(8,128)S(1)} %away.1), channel_id=1, source_target_pairs={{16,0},{0,16},{17,1},{1,17},{18,2},{2,18},{19,3},{3,19},{20,4},{4,... | collective-permute-start | bytes 1081352 | tf_op jit(solution)/shard_map/ppermute | solution.py:623

commit v6 on v5

--- a/solution.py
+++ b/solution.py
@@ -271,7 +271,7 @@
     return [out[i : i + TERMS] for i in range(0, len(out), TERMS)]
 
 
-def tap_kernel(s, w_ref, a_ref, tap_ref, x0_ref, y0_ref):
+def tap_kernel(s, w_ref, a_ref, tap_ref, x0_ref):
     coef = spreads(w_ref, (0, 1))
     unit = near_units(coef)
     d = lanes_of((1, LANES)).astype(F32)
@@ -285,6 +285,11 @@
     for t in range(TERMS):
         high, low = halves(bell(coef[0][t], d) * unit[0][t])
         x0_ref[t * s.nx : (t + 1) * s.nx] = jnp.where(part == 1, low.astype(F32), high.astype(F32)).astype(BF16)
+
+
+def along_matrix_kernel(s, w_ref, _, y0_ref):
+    coef = spreads(w_ref, (0,))
+    unit = near_units(coef)
     shape = (s.ny + 2 * R, s.ny)
     i = rows_of(shape)
     cell = jnp.where(i < s.ny, i, jnp.where(i < s.ny + R, i - s.ny - R, i - R))
@@ -445,7 +450,7 @@
 
 def depth_kernel(s, tap_ref, *refs):
     m_refs = refs[: s.gz]
-    ry2_ref, rx2_ref, _, w_ref, down_ref, up_ref, c2_ref, c_ref = refs[s.gz :]
+    ry2_ref, rx2_ref, _, _, w_ref, down_ref, up_ref, c2_ref, _, _, c_ref = refs[s.gz :]
     n = s.cz[1]
     parts = [[] for _ in range(n)]
     for b in range(s.gz):
@@ -587,11 +592,14 @@
         out_ref[z] = home_ref[z] + prolonged(s, level, z)
 
 
-def call(kernel, name, operands, out_shapes, scalars=(), after=(), scratch=(), flops=0):
-    operands = list(operands) + list(after)
+def call(kernel, name, operands, out_shapes, scalars=(), after=(), through=(), scratch=(), flops=0):
+    read, given = len(operands), len(out_shapes)
+    operands = list(operands) + list(after) + list(through)
+    first = len(operands) - len(through)
+    out_shapes = list(out_shapes) + [jax.ShapeDtypeStruct(x.shape, x.dtype) for x in through]
 
     def spec(i):
-        if i >= len(operands) - len(after):
+        if i >= read:
             return pl.BlockSpec(memory_space=pl.ANY)
         return pl.BlockSpec(memory_space=pltpu.SMEM if i in scalars else pltpu.VMEM)
 
@@ -602,7 +610,9 @@
         name=name,
         out_shape=out_shapes,
         in_specs=[spec(i) for i in range(len(operands))],
-        out_specs=[pl.BlockSpec(memory_space=pltpu.VMEM)] * len(out_shapes),
+        out_specs=[pl.BlockSpec(memory_space=pltpu.VMEM)] * given
+        + [pl.BlockSpec(memory_space=pl.ANY)] * len(through),
+        input_output_aliases={first + i: given + i for i in range(len(through))},
         scratch_shapes=list(scratch),
         compiler_params=pltpu.CompilerParams(vmem_limit_bytes=VMEM_LIMIT),
         cost_estimate=pl.CostEstimate(flops=flops, bytes_accessed=moved, transcendentals=0),
@@ -632,11 +642,9 @@
     c = {k: jnp.asarray(v) for k, v in constants(s).items()}
     brick = (s.nz, s.nx, s.ny)
     side = (R, s.nx, s.ny)
-    taps, x0, y0 = call(
+    taps, x0 = call(
         functools.partial(tap_kernel, s), "taps", [widths, amplitudes],
-        arrays((8, LANES))
-        + arrays((TERMS * s.nx, 3 * s.ext), (2 * LANES, 2 * TERMS * s.ny), dtype=BF16),
-        flops=6 * 10**8,
+        arrays((8, LANES)) + arrays((TERMS * s.nx, 3 * s.ext), dtype=BF16), flops=6 * 10**8,
     )
     high_rows = fetch(charges, gx=1)
     low_rows = high_rows if s.gx == 2 else fetch(charges, gx=-1)
@@ -647,6 +655,10 @@
     )
     shares = [share] + [fetch(share, gz=b) for b in range(1, s.gz)]
     left, right = fetch(last_cells, gy=-1), fetch(first_cells, gy=1)
+    (y0,) = call(
+        functools.partial(along_matrix_kernel, s), "taps_y", [widths],
+        arrays((2 * LANES, 2 * TERMS * s.ny), dtype=BF16), after=[share], flops=6 * 10**8,
+    )
     tiles = s.nz + 2 * s.fine_tiles
     halved = pltpu.VMEM((TERMS, s.nz * s.nx, 2 * LANES), BF16)
     near, near_down, near_up = call(
@@ -661,11 +673,11 @@
     )
     base = s.tiles_s * s.rows1
     size2 = s.tiles2 * s.rows2
-    waves, to_low, to_high, coarse = call(
+    waves, to_low, to_high, coarse, near_down, near_up = call(
         functools.partial(depth_kernel, s), "depth",
         [taps] + shares + [c["ry2"], c["rx2"]],
         arrays((TERMS * s.planes, s.rows1, LANES), (base + size2, LANES), (base + size2, LANES), (size2, LANES)),
-        scalars=(0,), after=[near], scratch=[pltpu.VMEM((s.cz[1], s.rows1, LANES), F32)], flops=2 * 10**9,
+        scalars=(0,), through=[near_down, near_up], scratch=[pltpu.VMEM((s.cz[1], s.rows1, LANES), F32)], flops=2 * 10**9,
     )
     named = ("px1", "px2", "px3", "px3l", "rx3", "py2", "py3", "py3l", "ry3", "pz2", "pz3", "rz3")
     z_taps, y1, y2h, y2l, xh, xl = call(

time: 36.9 us -> 38.1 us (1.033)
  waiting for transfers between devices: 3.83 us -> 4.59 us
    ppermute x12, waiting for transfers between devices: 3.83 us -> 4.59 us  [fetch(): return lax.ppermute(x, names if len(names) > 1 else names[0], pairs)]
    pallas_call x9 -> x10, Pallas kernels: 13.2 us -> 13.4 us  [call(): pl.pallas_call(kernel, name=name, out_shape=out_shapes, in_specs=[spec(i)...]
  transfers between devices with their start and end apart: 12 -> 12, of which waited for: 3 -> 6; matrix products, arithmetic and copies ran while one was open for 0% -> 0% of each run, Pallas kernels for 32% -> 28%
where the time goes in v6:
time: 38.1 us; the launch traced here: 37.9 us
  starting transfers between devices  18.1 us (48%)
  Pallas kernels  13.4 us (35%)
  waiting for transfers between devices  4.59 us (12%)
  local copies, waits for them, and re-layouts  1.46 us (4%)
    ppermute x12, starting transfers between devices, fetch(): return lax.ppermute(x, names if len(names) > 1 else names[0], pairs)  18.1 us
    pallas_call x10, Pallas kernels, call(): pl.pallas_call(kernel, name=name, out_shape=out_shapes, in_specs=[spec(i)...  13.4 us
    ppermute x12, waiting for transfers between devices, fetch(): return lax.ppermute(x, names if len(names) > 1 else names[0], pairs)  4.59 us
    unnamed x36, local copies, waits for them, and re-layouts  1.46 us
  transfers between devices with their start and end apart: 12, of which 6 were waited for; matrix products, arithmetic and copies ran while one was open for 0% of the time, Pallas kernels for 28%

profile of v6, /device:TPU:0, one launch (start us, length us, event | category | flops | bytes accessed | tf_op | source)
XLA Modules:
  0.0 37.9 jit_solution(13613697548608923861)
XLA Ops:
  0.0 0.5 %collective-permute-start = (f32[16,64,128]{2,1,0:T(8,128)}, f32[16,64,128]{2,1,0:T(8,128)S(1)}, u32[]{:S(2)}, u32[]{:S(2)}) collective-permute-start(f32[16,64,128]{2,1,0:T(8,128)} %b_ref.3), channel_id=1, source_target_pairs={{16,0},{0,16},{17,1},{1,17},{18,2},{2,18},{19,3},{3,19},{20,4},{4,... | collective-permute-start | bytes 1572872 | tf_op jit(solution)/shard_map/ppermute | solution.py:633
  0.5 0.7 %copy-done.1 = f32[4,3]{1,0:T(4,128)S(1)} copy-done((f32[4,3]{1,0:T(4,128)S(1)}, f32[4,3]{1,0:T(4,128)}, u32[]{:S(2)}) %copy-start.1) | copy-done | bytes 72
  1.1 0.7 %copy-done.3 = f32[4,3]{1,0:T(4,128)S(1)} copy-done((f32[4,3]{1,0:T(4,128)S(1)}, f32[4,3]{1,0:T(4,128)}, u32[]{:S(2)}) %copy-start.3) | copy-done | bytes 72
  1.8 0.3 taps.1
  2.1 0.1 collective-permute-done.lo_ref.hi_ref
  2.2 0.7 %share.1 = (f32[6,32,128]{2,1,0:T(8,128)S(1)}, f32[1,80,128]{2,1,0:T(8,128)S(1)}, f32[1,80,128]{2,1,0:T(8,128)S(1)}) custom-call(f32[16,64,128]{2,1,0:T(8,128)S(1)} %copy-done, f32[16,64,128]{2,1,0:T(8,128)S(1)} %collective-permute-done.lo_ref.hi_ref, f32[16,64,128]{2,1,0:T(8,128)S(1)} %collective-permute-done.lo_ref.hi_ref, ...), custom_call_target="tpu_custom_call" | custom-call | flops 1000000000 | bytes 1845248 | tf_op jit(solution)/shard_map/share/pallas_call | solution.py:608
  2.9 3.0 %collective-permute-start.3 = (f32[6,32,128]{2,1,0:T(8,128)S(1)}, f32[6,32,128]{2,1,0:T(8,128)S(1)}, u32[]{:S(2)}, u32[]{:S(2)}) collective-permute-start(f32[6,32,128]{2,1,0:T(8,128)S(1)} %get-tuple-element.27._.refs_0_), channel_id=1, source_target_pairs={{3,0},{0,1},{1,2},{2,3},{7,4},{4,5},{5,6},{6,7},{11,8},{8,9},{9,10... | collective-permute-start | bytes 294920 | tf_op jit(solution)/shard_map/ppermute | solution.py:633
  5.9 2.6 %collective-permute-start.2 = (f32[6,32,128]{2,1,0:T(8,128)S(1)}, f32[6,32,128]{2,1,0:T(8,128)S(1)}, u32[]{:S(2)}, u32[]{:S(2)}) collective-permute-start(f32[6,32,128]{2,1,0:T(8,128)S(1)} %get-tuple-element.27._.refs_0_), channel_id=1, source_target_pairs={{2,0},{3,1},{0,2},{1,3},{6,4},{7,5},{4,6},{5,7},{10,8},{11,9},{8,1... | collective-permute-start | bytes 294920 | tf_op jit(solution)/shard_map/ppermute | solution.py:633
  8.5 1.3 %collective-permute-start.1 = (f32[6,32,128]{2,1,0:T(8,128)S(1)}, f32[6,32,128]{2,1,0:T(8,128)S(1)}, u32[]{:S(2)}, u32[]{:S(2)}) collective-permute-start(f32[6,32,128]{2,1,0:T(8,128)S(1)} %get-tuple-element.27._.refs_0_), channel_id=1, source_target_pairs={{1,0},{2,1},{3,2},{0,3},{5,4},{6,5},{7,6},{4,7},{9,8},{10,9},{11,1... | collective-permute-start | bytes 294920 | tf_op jit(solution)/shard_map/ppermute | solution.py:633
  9.8 1.5 %collective-permute-start.4 = (f32[1,80,128]{2,1,0:T(8,128)S(1)}, f32[1,80,128]{2,1,0:T(8,128)S(1)}, u32[]{:S(2)}, u32[]{:S(2)}) collective-permute-start(f32[1,80,128]{2,1,0:T(8,128)S(1)} %get-tuple-element.28), channel_id=1, source_target_pairs={{12,0},{0,4},{4,8},{8,12},{13,1},{1,5},{5,9},{9,13},{14,2},{2,6},{... | collective-permute-start | bytes 122888 | tf_op jit(solution)/shard_map/ppermute | solution.py:633
  11.3 1.4 %collective-permute-start.5 = (f32[1,80,128]{2,1,0:T(8,128)S(1)}, f32[1,80,128]{2,1,0:T(8,128)S(1)}, u32[]{:S(2)}, u32[]{:S(2)}) collective-permute-start(f32[1,80,128]{2,1,0:T(8,128)S(1)} %get-tuple-element.29), channel_id=1, source_target_pairs={{4,0},{8,4},{12,8},{0,12},{5,1},{9,5},{13,9},{1,13},{6,2},{10,6},{... | collective-permute-start | bytes 122888 | tf_op jit(solution)/shard_map/ppermute | solution.py:633
  12.8 0.3 taps_y.1.y0_ref
  13.0 1.7 %collective-permute-done.4.left_ref = f32[1,80,128]{2,1,0:T(8,128)S(1)} collective-permute-done((f32[1,80,128]{2,1,0:T(8,128)S(1)}, f32[1,80,128]{2,1,0:T(8,128)S(1)}, u32[]{:S(2)}, u32[]{:S(2)}) %collective-permute-start.4) | collective-permute-done | bytes 40992 | tf_op jit(solution)/shard_map/ppermute | solution.py:633
  14.8 0.6 %collective-permute-done.5.right_ref = f32[1,80,128]{2,1,0:T(8,128)S(1)} collective-permute-done((f32[1,80,128]{2,1,0:T(8,128)S(1)}, f32[1,80,128]{2,1,0:T(8,128)S(1)}, u32[]{:S(2)}, u32[]{:S(2)}) %collective-permute-start.5) | collective-permute-done | bytes 40992 | tf_op jit(solution)/shard_map/ppermute | solution.py:633
  15.3 4.0 %near.1 = (f32[16,64,128]{2,1,0:T(8,128)S(1)}, f32[8,64,128]{2,1,0:T(8,128)S(1)}, f32[8,64,128]{2,1,0:T(8,128)S(1)}) custom-call(f32[8,128]{1,0:T(8,128)S(1)} %get-tuple-element.25.tap_ref, f32[16,64,128]{2,1,0:T(8,128)S(1)} %copy-done, f32[16,64,128]{2,1,0:T(8,128)S(1)} %collective-permute-done.lo_ref.hi_ref, ...), custom_call_target="tpu_custom_call" | custom-call | flops 5000000000 | bytes 3192832 | tf_op jit(solution)/shard_map/near/pallas_call | solution.py:608
  19.4 0.0 collective-permute-done.3.refs_3_
  19.4 0.0 collective-permute-done.2.refs_2_
  19.4 0.0 collective-permute-done.1.refs_1_
  19.4 0.0 copy-start.4
  19.4 0.0 copy-start.6
  19.5 0.0 copy-start.7
  19.5 0.0 copy-start.8
  19.5 0.0 copy-start.9
  19.5 0.0 copy-start.10
  19.5 0.0 copy-start.11
  19.5 0.0 copy-start.12
  19.5 0.0 copy-start.13
  19.6 0.0 copy-start.15
  19.6 0.0 copy-start.16
  19.6 0.0 copy-start.17
  19.6 1.4 %depth.1 = (f32[33,32,128]{2,1,0:T(8,128)S(1)}, f32[216,128]{1,0:T(8,128)S(1)}, f32[216,128]{1,0:T(8,128)S(1)}, f32[120,128]{1,0:T(8,128)S(1)}, f32[8,64,128]{2,1,0:T(8,128)S(1)}, /*index=5*/f32[8,64,128]{2,1,0:T(8,128)S(1)}) custom-call(f32[8,128]{1,0:T(8,128)S(1)} %get-tuple-element.25.tap_ref, ...), custom_call_target="tpu_custom_call", output_to_operand_aliasing={{4}: (7, {}), {5}: (8, {})} | custom-call | flops 2000000000 | bytes 2337792 | tf_op jit(solution)/shard_map/depth/pallas_call | solution.py:608
  21.0 1.6 %collective-permute-start.7 = (f32[120,128]{1,0:T(8,128)S(1)}, f32[120,128]{1,0:T(8,128)S(1)}, u32[]{:S(2)}, u32[]{:S(2)}) collective-permute-start(f32[120,128]{1,0:T(8,128)S(1)} %get-tuple-element.32._.refs_0_), channel_id=1, source_target_pairs={{8,0},{12,4},{0,8},{4,12},{9,1},{13,5},{1,9},{5,13},{10,2},{14,6},... | collective-permute-start | bytes 184328 | tf_op jit(solution)/shard_map/ppermute | solution.py:633
  22.6 2.3 %collective-permute-start.6 = (f32[216,128]{1,0:T(8,128)S(1)}, f32[216,128]{1,0:T(8,128)S(1)}, u32[]{:S(2)}, u32[]{:S(2)}) collective-permute-start(f32[216,128]{1,0:T(8,128)S(1)} %get-tuple-element.35), channel_id=1, source_target_pairs={{4,0},{8,4},{12,8},{0,12},{5,1},{9,5},{13,9},{1,13},{6,2},{10,6},{... | collective-permute-start | bytes 331784 | tf_op jit(solution)/shard_map/ppermute | solution.py:633
  24.9 0.0 collective-permute-start.8
  24.9 0.7 %collective-permute-start.9 = (f32[8,64,128]{2,1,0:T(8,128)S(1)}, f32[8,64,128]{2,1,0:T(8,128)S(1)}, u32[]{:S(2)}, u32[]{:S(2)}) collective-permute-start(f32[8,64,128]{2,1,0:T(8,128)S(1)} %get-tuple-element.43), channel_id=1, source_target_pairs={{3,0},{0,1},{1,2},{2,3},{7,4},{4,5},{5,6},{6,7},{11,8},{8,9},{9,10... | collective-permute-start | bytes 786440 | tf_op jit(solution)/shard_map/ppermute | solution.py:633
  25.6 3.1 %collective-permute-start.10 = (f32[8,64,128]{2,1,0:T(8,128)S(1)}, f32[8,64,128]{2,1,0:T(8,128)S(1)}, u32[]{:S(2)}, u32[]{:S(2)}) collective-permute-start(f32[8,64,128]{2,1,0:T(8,128)S(1)} %get-tuple-element.44), channel_id=1, source_target_pairs={{1,0},{2,1},{3,2},{0,3},{5,4},{6,5},{7,6},{4,7},{9,8},{10,9},{11,1... | collective-permute-start | bytes 786440 | tf_op jit(solution)/shard_map/ppermute | solution.py:633
  28.8 1.3 %matrices.1 = (f32[96,128]{1,0:T(8,128)S(1)}, bf16[128,768]{1,0:T(8,128)(2,1)S(1)}, bf16[128,768]{1,0:T(8,128)(2,1)S(1)}, bf16[128,768]{1,0:T(8,128)(2,1)S(1)}, ...) custom-call(f32[4,3]{1,0:T(4,128)S(1)} %copy-done.2, f32[4,3]{1,0:T(4,128)S(1)} %copy-done.4, ...), custom_call_target="tpu_custom_call" | custom-call | flops 2000000000 | bytes 973664 | tf_op jit(solution)/shard_map/matrices/pallas_call | solution.py:608
  30.1 0.0 collective-permute-done.7.refs_2_
  30.1 0.0 collective-permute-done.6.refs_1_
  30.1 0.4 %collective-permute-done.8.refs_3_ = f32[216,128]{1,0:T(8,128)S(1)} collective-permute-done((f32[216,128]{1,0:T(8,128)S(1)}, f32[216,128]{1,0:T(8,128)S(1)}, u32[]{:S(2)}, u32[]{:S(2)}) %collective-permute-start.8) | collective-permute-done | bytes 110624 | tf_op jit(solution)/shard_map/ppermute | solution.py:633
  30.5 3.5 %along.1.d_ref = f32[240,1408]{1,0:T(8,128)S(1)} custom-call(f32[96,128]{1,0:T(8,128)S(1)} %get-tuple-element.33.z_ref, f32[33,32,128]{2,1,0:T(8,128)S(1)} %get-tuple-element.34.w_ref, f32[120,128]{1,0:T(8,128)S(1)} %get-tuple-element.32._.refs_0_, f32[216,128]{1,0:T(8,128)S(1)} %collective-permute-done.6.refs_1_, ...), custom_call_target="tpu_custom_call" | custom-call | flops 3000000000 | bytes 2875392 | tf_op jit(solution)/shard_map/along/pallas_call | solution.py:608
  34.0 0.5 %away.1 = f32[64,1408]{1,0:T(8,128)S(1)} custom-call(f32[240,1408]{1,0:T(8,128)S(1)} %along.1.d_ref, bf16[128,256]{1,0:T(8,128)(2,1)S(1)} %get-tuple-element.40.xh_ref, bf16[128,256]{1,0:T(8,128)(2,1)S(1)} %get-tuple-element.41.xl_ref), custom_call_target="tpu_custom_call" | custom-call | flops 1000000000 | bytes 1843200 | tf_op jit(solution)/shard_map/away/pallas_call | solution.py:608
  34.6 0.1 collective-permute-start.11
  34.6 0.9 %collective-permute-done.9.low_ref = f32[8,64,128]{2,1,0:T(8,128)S(1)} collective-permute-done((f32[8,64,128]{2,1,0:T(8,128)S(1)}, f32[8,64,128]{2,1,0:T(8,128)S(1)}, u32[]{:S(2)}, u32[]{:S(2)}) %collective-permute-start.9) | collective-permute-done | bytes 262176 | tf_op jit(solution)/shard_map/ppermute | solution.py:633
  35.5 0.9 %collective-permute-done.10.high_ref = f32[8,64,128]{2,1,0:T(8,128)S(1)} collective-permute-done((f32[8,64,128]{2,1,0:T(8,128)S(1)}, f32[8,64,128]{2,1,0:T(8,128)S(1)}, u32[]{:S(2)}, u32[]{:S(2)}) %collective-permute-start.10) | collective-permute-done | bytes 262176 | tf_op jit(solution)/shard_map/ppermute | solution.py:633
  36.4 0.6 %home.1.home_ref = f32[16,64,128]{2,1,0:T(8,128)S(1)} custom-call(f32[240,1408]{1,0:T(8,128)S(1)} %along.1.d_ref, bf16[128,256]{1,0:T(8,128)(2,1)S(1)} %get-tuple-element.40.xh_ref, bf16[128,256]{1,0:T(8,128)(2,1)S(1)} %get-tuple-element.41.xl_ref, f32[16,64,128]{2,1,0:T(8,128)S(1)} %get-tuple-element.42.own_ref, ...), custom_call_target="tpu_custom_call" | custom-call | flops 2000000000 | bytes 3055616 | tf_op jit(solution)/shard_map/home/pallas_call | solution.py:608
  37.0 0.0 collective-permute-done.11.refs_0_
  37.0 0.9 %last.1 = f32[16,64,128]{2,1,0:T(8,128)} custom-call(f32[16,64,128]{2,1,0:T(8,128)S(1)} %home.1.home_ref, f32[64,1408]{1,0:T(8,128)S(1)} %collective-permute-done.11.refs_0_), custom_call_target="tpu_custom_call" | custom-call | flops 1000000000 | bytes 1409024 | tf_op jit(solution)/shard_map/last/pallas_call | solution.py:608
  (22 shorter events, 0.0 us)
Async XLA Ops:
  0.0 2.2 %copy-start = (f32[16,64,128]{2,1,0:T(8,128)S(1)}, f32[16,64,128]{2,1,0:T(8,128)}, u32[]{:S(2)}) copy-start(f32[16,64,128]{2,1,0:T(8,128)} %b_ref.3) | copy-start | bytes 1572868
  0.0 2.2 %collective-permute-start = (f32[16,64,128]{2,1,0:T(8,128)}, f32[16,64,128]{2,1,0:T(8,128)S(1)}, u32[]{:S(2)}, u32[]{:S(2)}) collective-permute-start(f32[16,64,128]{2,1,0:T(8,128)} %b_ref.3), channel_id=1, source_target_pairs={{16,0},{0,16},{17,1},{1,17},{18,2},{2,18},{19,3},{3,19},{20,4},{4,... | collective-permute-start | bytes 1572872 | tf_op jit(solution)/shard_map/ppermute | solution.py:633
  0.5 0.7 %copy-start.1 = (f32[4,3]{1,0:T(4,128)S(1)}, f32[4,3]{1,0:T(4,128)}, u32[]{:S(2)}) copy-start(f32[4,3]{1,0:T(4,128)} %w_ref.5) | copy-start | bytes 148
  1.1 0.7 %copy-start.3 = (f32[4,3]{1,0:T(4,128)S(1)}, f32[4,3]{1,0:T(4,128)}, u32[]{:S(2)}) copy-start(f32[4,3]{1,0:T(4,128)} %a_ref.3) | copy-start | bytes 148
  2.2 10.6 %copy-start.2 = (f32[4,3]{1,0:T(4,128)S(1)}, f32[4,3]{1,0:T(4,128)}, u32[]{:S(2)}) copy-start(f32[4,3]{1,0:T(4,128)} %w_ref.5) | copy-start | bytes 148
  2.9 16.5 %collective-permute-start.3 = (f32[6,32,128]{2,1,0:T(8,128)S(1)}, f32[6,32,128]{2,1,0:T(8,128)S(1)}, u32[]{:S(2)}, u32[]{:S(2)}) collective-permute-start(f32[6,32,128]{2,1,0:T(8,128)S(1)} %get-tuple-element.27._.refs_0_), channel_id=1, source_target_pairs={{3,0},{0,1},{1,2},{2,3},{7,4},{4,5},{5,6},{6,7},{11,8},{8,9},{9,10... | collective-permute-start | bytes 294920 | tf_op jit(solution)/shard_map/ppermute | solution.py:633
  5.9 13.5 %collective-permute-start.2 = (f32[6,32,128]{2,1,0:T(8,128)S(1)}, f32[6,32,128]{2,1,0:T(8,128)S(1)}, u32[]{:S(2)}, u32[]{:S(2)}) collective-permute-start(f32[6,32,128]{2,1,0:T(8,128)S(1)} %get-tuple-element.27._.refs_0_), channel_id=1, source_target_pairs={{2,0},{3,1},{0,2},{1,3},{6,4},{7,5},{4,6},{5,7},{10,8},{11,9},{8,1... | collective-permute-start | bytes 294920 | tf_op jit(solution)/shard_map/ppermute | solution.py:633
  8.5 10.9 %collective-permute-start.1 = (f32[6,32,128]{2,1,0:T(8,128)S(1)}, f32[6,32,128]{2,1,0:T(8,128)S(1)}, u32[]{:S(2)}, u32[]{:S(2)}) collective-permute-start(f32[6,32,128]{2,1,0:T(8,128)S(1)} %get-tuple-element.27._.refs_0_), channel_id=1, source_target_pairs={{1,0},{2,1},{3,2},{0,3},{5,4},{6,5},{7,6},{4,7},{9,8},{10,9},{11,1... | collective-permute-start | bytes 294920 | tf_op jit(solution)/shard_map/ppermute | solution.py:633
  9.8 4.9 %collective-permute-start.4 = (f32[1,80,128]{2,1,0:T(8,128)S(1)}, f32[1,80,128]{2,1,0:T(8,128)S(1)}, u32[]{:S(2)}, u32[]{:S(2)}) collective-permute-start(f32[1,80,128]{2,1,0:T(8,128)S(1)} %get-tuple-element.28), channel_id=1, source_target_pairs={{12,0},{0,4},{4,8},{8,12},{13,1},{1,5},{5,9},{9,13},{14,2},{2,6},{... | collective-permute-start | bytes 122888 | tf_op jit(solution)/shard_map/ppermute | solution.py:633
  11.3 4.0 %collective-permute-start.5 = (f32[1,80,128]{2,1,0:T(8,128)S(1)}, f32[1,80,128]{2,1,0:T(8,128)S(1)}, u32[]{:S(2)}, u32[]{:S(2)}) collective-permute-start(f32[1,80,128]{2,1,0:T(8,128)S(1)} %get-tuple-element.29), channel_id=1, source_target_pairs={{4,0},{8,4},{12,8},{0,12},{5,1},{9,5},{13,9},{1,13},{6,2},{10,6},{... | collective-permute-start | bytes 122888 | tf_op jit(solution)/shard_map/ppermute | solution.py:633
  15.3 4.1 %copy-start.5 = (f32[128,128]{1,0:T(8,128)S(1)}, f32[128,128]{1,0:T(8,128)}, u32[]{:S(2)}) copy-start(f32[128,128]{1,0:T(8,128)} %constant.26.clone.refs_4_) | copy-start | bytes 196612
  15.3 4.1 %copy-start.14 = (f32[24,32]{1,0:T(8,128)S(1)}, f32[24,32]{1,0:T(8,128)}, u32[]{:S(2)}) copy-start(f32[24,32]{1,0:T(8,128)} %constant.27.clone.refs_5_) | copy-start | bytes 9220
  19.4 9.3 %copy-start.4 = (f32[4,3]{1,0:T(4,128)S(1)}, f32[4,3]{1,0:T(4,128)}, u32[]{:S(2)}) copy-start(f32[4,3]{1,0:T(4,128)} %a_ref.3) | copy-start | bytes 148
  19.4 9.3 %copy-start.6 = (bf16[128,128]{1,0:T(8,128)(2,1)S(1)}, bf16[128,128]{1,0:T(8,128)(2,1)}, u32[]{:S(2)}) copy-start(bf16[128,128]{1,0:T(8,128)(2,1)} %constant.33.clone.py2) | copy-start | bytes 98308
  19.5 9.3 %copy-start.7 = (bf16[128,16]{1,0:T(8,128)(2,1)S(1)}, bf16[128,16]{1,0:T(8,128)(2,1)}, u32[]{:S(2)}) copy-start(bf16[128,16]{1,0:T(8,128)(2,1)} %constant.31.clone.px3l) | copy-start | bytes 12292
  19.5 9.3 %copy-start.8 = (bf16[128,16]{1,0:T(8,128)(2,1)S(1)}, bf16[128,16]{1,0:T(8,128)(2,1)}, u32[]{:S(2)}) copy-start(bf16[128,16]{1,0:T(8,128)(2,1)} %constant.30.clone.px3) | copy-start | bytes 12292
  19.5 9.2 %copy-start.9 = (bf16[128,32]{1,0:T(8,128)(2,1)S(1)}, bf16[128,32]{1,0:T(8,128)(2,1)}, u32[]{:S(2)}) copy-start(bf16[128,32]{1,0:T(8,128)(2,1)} %constant.29.clone.px2) | copy-start | bytes 24580
  19.5 9.2 %copy-start.10 = (bf16[128,64]{1,0:T(8,128)(2,1)S(1)}, bf16[128,64]{1,0:T(8,128)(2,1)}, u32[]{:S(2)}) copy-start(bf16[128,64]{1,0:T(8,128)(2,1)} %constant.28.clone.px1.ry3) | copy-start | bytes 49156
  19.5 9.2 %copy-start.11 = (bf16[3,16,256]{2,1,0:T(8,128)(2,1)S(1)}, bf16[3,16,256]{2,1,0:T(8,128)(2,1)}, u32[]{:S(2)}) copy-start(bf16[3,16,256]{2,1,0:T(8,128)(2,1)} %constant.32.clone.rx3) | copy-start | bytes 73732
  19.5 9.2 %copy-start.12 = (bf16[64,128]{1,0:T(8,128)(2,1)S(1)}, bf16[64,128]{1,0:T(8,128)(2,1)}, u32[]{:S(2)}) copy-start(bf16[64,128]{1,0:T(8,128)(2,1)} %constant.35.clone.py3l) | copy-start | bytes 49156
  19.5 9.2 %copy-start.13 = (bf16[64,128]{1,0:T(8,128)(2,1)S(1)}, bf16[64,128]{1,0:T(8,128)(2,1)}, u32[]{:S(2)}) copy-start(bf16[64,128]{1,0:T(8,128)(2,1)} %constant.34.clone.py3) | copy-start | bytes 49156
  19.6 9.2 %copy-start.15 = (bf16[16,8]{1,0:T(8,128)(2,1)S(1)}, bf16[16,8]{1,0:T(8,128)(2,1)}, u32[]{:S(2)}) copy-start(bf16[16,8]{1,0:T(8,128)(2,1)} %constant.37.clone.pz3) | copy-start | bytes 772
  19.6 9.2 %copy-start.16 = (bf16[16,16]{1,0:T(8,128)(2,1)S(1)}, bf16[16,16]{1,0:T(8,128)(2,1)}, u32[]{:S(2)}) copy-start(bf16[16,16]{1,0:T(8,128)(2,1)} %constant.36.clone.pz2) | copy-start | bytes 1540
  19.6 9.2 %copy-start.17 = (bf16[8,128]{1,0:T(8,128)(2,1)S(1)}, bf16[8,128]{1,0:T(8,128)(2,1)}, u32[]{:S(2)}) copy-start(bf16[8,128]{1,0:T(8,128)(2,1)} %constant.38.clone.rz3) | copy-start | bytes 6148
  21.0 9.2 %collective-permute-start.7 = (f32[120,128]{1,0:T(8,128)S(1)}, f32[120,128]{1,0:T(8,128)S(1)}, u32[]{:S(2)}, u32[]{:S(2)}) collective-permute-start(f32[120,128]{1,0:T(8,128)S(1)} %get-tuple-element.32._.refs_0_), channel_id=1, source_target_pairs={{8,0},{12,4},{0,8},{4,12},{9,1},{13,5},{1,9},{5,13},{10,2},{14,6},... | collective-permute-start | bytes 184328 | tf_op jit(solution)/shard_map/ppermute | solution.py:633
  22.6 7.6 %collective-permute-start.6 = (f32[216,128]{1,0:T(8,128)S(1)}, f32[216,128]{1,0:T(8,128)S(1)}, u32[]{:S(2)}, u32[]{:S(2)}) collective-permute-start(f32[216,128]{1,0:T(8,128)S(1)} %get-tuple-element.35), channel_id=1, source_target_pairs={{4,0},{8,4},{12,8},{0,12},{5,1},{9,5},{13,9},{1,13},{6,2},{10,6},{... | collective-permute-start | bytes 331784 | tf_op jit(solution)/shard_map/ppermute | solution.py:633
  24.9 5.6 %collective-permute-start.8 = (f32[216,128]{1,0:T(8,128)S(1)}, f32[216,128]{1,0:T(8,128)S(1)}, u32[]{:S(2)}, u32[]{:S(2)}) collective-permute-start(f32[216,128]{1,0:T(8,128)S(1)} %get-tuple-element.36), channel_id=1, source_target_pairs={{12,0},{0,4},{4,8},{8,12},{13,1},{1,5},{5,9},{9,13},{14,2},{2,6},{... | collective-permute-start | bytes 331784 | tf_op jit(solution)/shard_map/ppermute | solution.py:633
  24.9 10.6 %collective-permute-start.9 = (f32[8,64,128]{2,1,0:T(8,128)S(1)}, f32[8,64,128]{2,1,0:T(8,128)S(1)}, u32[]{:S(2)}, u32[]{:S(2)}) collective-permute-start(f32[8,64,128]{2,1,0:T(8,128)S(1)} %get-tuple-element.43), channel_id=1, source_target_pairs={{3,0},{0,1},{1,2},{2,3},{7,4},{4,5},{5,6},{6,7},{11,8},{8,9},{9,10... | collective-permute-start | bytes 786440 | tf_op jit(solution)/shard_map/ppermute | solution.py:633
  25.6 10.9 %collective-permute-start.10 = (f32[8,64,128]{2,1,0:T(8,128)S(1)}, f32[8,64,128]{2,1,0:T(8,128)S(1)}, u32[]{:S(2)}, u32[]{:S(2)}) collective-permute-start(f32[8,64,128]{2,1,0:T(8,128)S(1)} %get-tuple-element.44), channel_id=1, source_target_pairs={{1,0},{2,1},{3,2},{0,3},{5,4},{6,5},{7,6},{4,7},{9,8},{10,9},{11,1... | collective-permute-start | bytes 786440 | tf_op jit(solution)/shard_map/ppermute | solution.py:633
  34.6 2.5 %collective-permute-start.11 = (f32[64,1408]{1,0:T(8,128)S(1)}, f32[64,1408]{1,0:T(8,128)S(1)}, u32[]{:S(2)}, u32[]{:S(2)}) collective-permute-start(f32[64,1408]{1,0:T(8,128)S(1)} %away.1), channel_id=1, source_target_pairs={{16,0},{0,16},{17,1},{1,17},{18,2},{2,18},{19,3},{3,19},{20,4},{4,... | collective-permute-start | bytes 1081352 | tf_op jit(solution)/shard_map/ppermute | solution.py:633

commit v7 on v5

--- a/solution.py
+++ b/solution.py
@@ -443,9 +443,10 @@
     lax.fori_loop(0, s.nx // 8, depth, 0)
 
 
-def depth_kernel(s, tap_ref, *refs):
-    m_refs = refs[: s.gz]
-    ry2_ref, rx2_ref, _, w_ref, down_ref, up_ref, c2_ref, c_ref = refs[s.gz :]
+def depth_kernel(s, tap_ref, m_ref, all_ref, ry2_ref, rx2_ref, _,
+                 w_ref, down_ref, up_ref, c2_ref, c_ref):
+    me = lax.axis_index("gz")
+    m_refs = [m_ref] + [all_ref.at[lax.rem(me + b, s.gz)] for b in range(1, s.gz)]
     n = s.cz[1]
     parts = [[] for _ in range(n)]
     for b in range(s.gz):
@@ -645,7 +646,7 @@
         functools.partial(share_kernel, s), "share", [charges, low_rows, high_rows],
         arrays((s.tiles1, s.rows1, LANES), strips, strips), after=[x0], flops=10**9,
     )
-    shares = [share] + [fetch(share, gz=b) for b in range(1, s.gz)]
+    shares = lax.all_gather(share, "gz")
     left, right = fetch(last_cells, gy=-1), fetch(first_cells, gy=1)
     tiles = s.nz + 2 * s.fine_tiles
     halved = pltpu.VMEM((TERMS, s.nz * s.nx, 2 * LANES), BF16)
@@ -663,7 +664,7 @@
     size2 = s.tiles2 * s.rows2
     waves, to_low, to_high, coarse = call(
         functools.partial(depth_kernel, s), "depth",
-        [taps] + shares + [c["ry2"], c["rx2"]],
+        [taps, share, shares, c["ry2"], c["rx2"]],
         arrays((TERMS * s.planes, s.rows1, LANES), (base + size2, LANES), (base + size2, LANES), (size2, LANES)),
         scalars=(0,), after=[near], scratch=[pltpu.VMEM((s.cz[1], s.rows1, LANES), F32)], flops=2 * 10**9,
     )

time: 36.9 us -> 46.4 us (1.26)
  blocking collectives: 0 us -> 15.2 us
  starting transfers between devices: 17.9 us -> 12.3 us
    all_gather x0 -> x1, blocking collectives: none -> 15.2 us  [shards(): shares = lax.all_gather(share, 'gz')]
    ppermute x12 -> x9, starting transfers between devices: 17.9 us -> 12.3 us  [fetch(): return lax.ppermute(x, names if len(names) > 1 else names[0], pairs)]
    ppermute x12 -> x9, waiting for transfers between devices: 3.83 us -> 3.83 us  [fetch(): return lax.ppermute(x, names if len(names) > 1 else names[0], pairs)]
  transfers between devices with their start and end apart: 12 -> 9, of which waited for: 3 -> 3; matrix products, arithmetic and copies ran while one was open for 0% -> 0% of each run, Pallas kernels for 32% -> 17%
where the time goes in v7:
time: 46.4 us; the launch traced here: 46.2 us
  blocking collectives  15.2 us (33%)
  Pallas kernels  13.3 us (29%)
  starting transfers between devices  12.3 us (27%)
  waiting for transfers between devices  3.83 us (8%)
  local copies, waits for them, and re-layouts  1.46 us (3%)
    all_gather x1, blocking collectives, shards(): shares = lax.all_gather(share, 'gz')  15.2 us
    pallas_call x9, Pallas kernels, call(): pl.pallas_call(kernel, name=name, out_shape=out_shapes, in_specs=[spec(i)...  13.3 us
    ppermute x9, starting transfers between devices, fetch(): return lax.ppermute(x, names if len(names) > 1 else names[0], pairs)  12.3 us
    ppermute x9, waiting for transfers between devices, fetch(): return lax.ppermute(x, names if len(names) > 1 else names[0], pairs)  3.83 us
    unnamed x36, local copies, waits for them, and re-layouts  1.46 us
  transfers between devices with their start and end apart: 9, of which 3 were waited for; matrix products, arithmetic and copies ran while one was open for 0% of the time, Pallas kernels for 17%

profile of v7, /device:TPU:0, one launch (start us, length us, event | category | flops | bytes accessed | tf_op | source)
XLA Modules:
  0.0 46.2 jit_solution(12543160927029804993)
XLA Ops:
  0.0 0.5 collective-permute-start
  0.5 0.7 %copy-done.1 = f32[4,3]{1,0:T(4,128)S(1)} copy-done((f32[4,3]{1,0:T(4,128)S(1)}, f32[4,3]{1,0:T(4,128)}, u32[]{:S(2)}) %copy-start.1) | copy-done | bytes 72
  1.1 0.7 %copy-done.3 = f32[4,3]{1,0:T(4,128)S(1)} copy-done((f32[4,3]{1,0:T(4,128)S(1)}, f32[4,3]{1,0:T(4,128)}, u32[]{:S(2)}) %copy-start.3) | copy-done | bytes 72
  1.8 0.4 taps.1
  2.2 0.0 collective-permute-done.lo_ref.hi_ref
  2.2 0.0 copy-done
  2.2 0.7 %share.1 = (f32[6,32,128]{2,1,0:T(8,128)S(1)}, f32[1,80,128]{2,1,0:T(8,128)S(1)}, f32[1,80,128]{2,1,0:T(8,128)S(1)}) custom-call(f32[16,64,128]{2,1,0:T(8,128)S(1)} %copy-done, f32[16,64,128]{2,1,0:T(8,128)S(1)} %collective-permute-done.lo_ref.hi_ref, f32[16,64,128]{2,1,0:T(8,128)S(1)} %collective-permute-done.lo_ref.hi_ref, ...), custom_call_target="tpu_custom_call" | custom-call | flops 1000000000 | bytes 1845248 | tf_op jit(solution)/shard_map/share/pallas_call | solution.py:601
  2.9 2.9 %collective-permute-start.1 = (f32[1,80,128]{2,1,0:T(8,128)S(1)}, f32[1,80,128]{2,1,0:T(8,128)S(1)}, u32[]{:S(2)}, u32[]{:S(2)}) collective-permute-start(f32[1,80,128]{2,1,0:T(8,128)S(1)} %get-tuple-element.27), channel_id=1, source_target_pairs={{12,0},{0,4},{4,8},{8,12},{13,1},{1,5},{5,9},{9,13},{14,2},{2,6},{... | collective-permute-start | bytes 122888 | tf_op jit(solution)/shard_map/ppermute | solution.py:624
  5.8 1.0 %collective-permute-start.2 = (f32[1,80,128]{2,1,0:T(8,128)S(1)}, f32[1,80,128]{2,1,0:T(8,128)S(1)}, u32[]{:S(2)}, u32[]{:S(2)}) collective-permute-start(f32[1,80,128]{2,1,0:T(8,128)S(1)} %get-tuple-element.28), channel_id=1, source_target_pairs={{4,0},{8,4},{12,8},{0,12},{5,1},{9,5},{13,9},{1,13},{6,2},{10,6},{... | collective-permute-start | bytes 122888 | tf_op jit(solution)/shard_map/ppermute | solution.py:624
  6.8 15.2 %all-gather = f32[24,32,128]{2,1,0:T(8,128)S(1)} all-gather(f32[6,32,128]{2,1,0:T(8,128)S(1)} %get-tuple-element.26.m_ref), channel_id=2, replica_groups=mesh['gx'=2,'gy'=4,'gz'=4] {'gz'}, dimensions={0}, use_global_device_ids=true | all-gather | bytes 491520 | tf_op jit(solution)/shard_map/all_gather | solution.py:649
  22.0 0.0 collective-permute-done.1.left_ref
  22.0 0.0 collective-permute-done.2.right_ref
  22.0 4.0 %near.1 = (f32[16,64,128]{2,1,0:T(8,128)S(1)}, f32[8,64,128]{2,1,0:T(8,128)S(1)}, f32[8,64,128]{2,1,0:T(8,128)S(1)}) custom-call(f32[8,128]{1,0:T(8,128)S(1)} %get-tuple-element.24.tap_ref, f32[16,64,128]{2,1,0:T(8,128)S(1)} %copy-done, f32[16,64,128]{2,1,0:T(8,128)S(1)} %collective-permute-done.lo_ref.hi_ref, ...), custom_call_target="tpu_custom_call" | custom-call | flops 5000000000 | bytes 3192832 | tf_op jit(solution)/shard_map/near/pallas_call | solution.py:601
  26.1 2.2 %collective-permute-start.6 = (f32[8,64,128]{2,1,0:T(8,128)S(1)}, f32[8,64,128]{2,1,0:T(8,128)S(1)}, u32[]{:S(2)}, u32[]{:S(2)}) collective-permute-start(f32[8,64,128]{2,1,0:T(8,128)S(1)} %get-tuple-element.41), channel_id=1, source_target_pairs={{3,0},{0,1},{1,2},{2,3},{7,4},{4,5},{5,6},{6,7},{11,8},{8,9},{9,10... | collective-permute-start | bytes 786440 | tf_op jit(solution)/shard_map/ppermute | solution.py:624
  28.3 2.0 %collective-permute-start.7 = (f32[8,64,128]{2,1,0:T(8,128)S(1)}, f32[8,64,128]{2,1,0:T(8,128)S(1)}, u32[]{:S(2)}, u32[]{:S(2)}) collective-permute-start(f32[8,64,128]{2,1,0:T(8,128)S(1)} %get-tuple-element.42), channel_id=1, source_target_pairs={{1,0},{2,1},{3,2},{0,3},{5,4},{6,5},{7,6},{4,7},{9,8},{10,9},{11,1... | collective-permute-start | bytes 786440 | tf_op jit(solution)/shard_map/ppermute | solution.py:624
  30.3 0.0 copy-done.14
  30.3 0.0 copy-start.6
  30.3 0.0 copy-start.7
  30.3 0.0 copy-start.8
  30.3 0.0 copy-start.9
  30.4 0.0 copy-start.10
  30.4 0.0 copy-start.11
  30.4 0.0 copy-start.12
  30.4 0.0 copy-start.13
  30.4 0.0 copy-start.15
  30.4 0.0 copy-start.16
  30.4 0.0 copy-start.17
  30.4 1.4 %depth.1 = (f32[33,32,128]{2,1,0:T(8,128)S(1)}, f32[216,128]{1,0:T(8,128)S(1)}, f32[216,128]{1,0:T(8,128)S(1)}, f32[120,128]{1,0:T(8,128)S(1)}) custom-call(f32[8,128]{1,0:T(8,128)S(1)} %get-tuple-element.24.tap_ref, f32[6,32,128]{2,1,0:T(8,128)S(1)} %get-tuple-element.26.m_ref, f32[4,6,32,128]{3,2,1,0:T(8,128)S(1)} %bitcast.1, f32[128,128]{1,0:T(8,128)S(1)} %copy-done.5, ...), custom_call_target="tpu_custom_call" | custom-call | flops 2000000000 | bytes 1911808 | tf_op jit(solution)/shard_map/depth/pallas_call | solution.py:601
  31.8 1.6 %collective-permute-start.4 = (f32[120,128]{1,0:T(8,128)S(1)}, f32[120,128]{1,0:T(8,128)S(1)}, u32[]{:S(2)}, u32[]{:S(2)}) collective-permute-start(f32[120,128]{1,0:T(8,128)S(1)} %get-tuple-element.31._.refs_0_), channel_id=1, source_target_pairs={{8,0},{12,4},{0,8},{4,12},{9,1},{13,5},{1,9},{5,13},{10,2},{14,6},... | collective-permute-start | bytes 184328 | tf_op jit(solution)/shard_map/ppermute | solution.py:624
  33.4 0.5 %collective-permute-start.3 = (f32[216,128]{1,0:T(8,128)S(1)}, f32[216,128]{1,0:T(8,128)S(1)}, u32[]{:S(2)}, u32[]{:S(2)}) collective-permute-start(f32[216,128]{1,0:T(8,128)S(1)} %get-tuple-element.34), channel_id=1, source_target_pairs={{4,0},{8,4},{12,8},{0,12},{5,1},{9,5},{13,9},{1,13},{6,2},{10,6},{... | collective-permute-start | bytes 331784 | tf_op jit(solution)/shard_map/ppermute | solution.py:624
  34.0 1.5 %collective-permute-start.5 = (f32[216,128]{1,0:T(8,128)S(1)}, f32[216,128]{1,0:T(8,128)S(1)}, u32[]{:S(2)}, u32[]{:S(2)}) collective-permute-start(f32[216,128]{1,0:T(8,128)S(1)} %get-tuple-element.35), channel_id=1, source_target_pairs={{12,0},{0,4},{4,8},{8,12},{13,1},{1,5},{5,9},{9,13},{14,2},{2,6},{... | collective-permute-start | bytes 331784 | tf_op jit(solution)/shard_map/ppermute | solution.py:624
  35.4 0.0 copy-done.2
  35.5 0.0 copy-done.8
  35.5 0.0 copy-done.9
  35.5 0.0 copy-done.10
  35.5 0.0 copy-done.11
  35.6 1.3 %matrices.1 = (f32[96,128]{1,0:T(8,128)S(1)}, bf16[128,768]{1,0:T(8,128)(2,1)S(1)}, bf16[128,768]{1,0:T(8,128)(2,1)S(1)}, bf16[128,768]{1,0:T(8,128)(2,1)S(1)}, ...) custom-call(f32[4,3]{1,0:T(4,128)S(1)} %copy-done.2, f32[4,3]{1,0:T(4,128)S(1)} %copy-done.4, ...), custom_call_target="tpu_custom_call" | custom-call | flops 2000000000 | bytes 973664 | tf_op jit(solution)/shard_map/matrices/pallas_call | solution.py:601
  36.9 0.0 collective-permute-done.4.refs_2_
  36.9 1.3 %collective-permute-done.3.refs_1_ = f32[216,128]{1,0:T(8,128)S(1)} collective-permute-done((f32[216,128]{1,0:T(8,128)S(1)}, f32[216,128]{1,0:T(8,128)S(1)}, u32[]{:S(2)}, u32[]{:S(2)}) %collective-permute-start.3) | collective-permute-done | bytes 110624 | tf_op jit(solution)/shard_map/ppermute | solution.py:624
  38.2 1.4 %collective-permute-done.5.refs_3_ = f32[216,128]{1,0:T(8,128)S(1)} collective-permute-done((f32[216,128]{1,0:T(8,128)S(1)}, f32[216,128]{1,0:T(8,128)S(1)}, u32[]{:S(2)}, u32[]{:S(2)}) %collective-permute-start.5) | collective-permute-done | bytes 110624 | tf_op jit(solution)/shard_map/ppermute | solution.py:624
  39.6 3.5 %along.1.d_ref = f32[240,1408]{1,0:T(8,128)S(1)} custom-call(f32[96,128]{1,0:T(8,128)S(1)} %get-tuple-element.32.z_ref, f32[33,32,128]{2,1,0:T(8,128)S(1)} %get-tuple-element.33.w_ref, f32[120,128]{1,0:T(8,128)S(1)} %get-tuple-element.31._.refs_0_, f32[216,128]{1,0:T(8,128)S(1)} %collective-permute-done.3.refs_1_, ...), custom_call_target="tpu_custom_call" | custom-call | flops 3000000000 | bytes 2875392 | tf_op jit(solution)/shard_map/along/pallas_call | solution.py:601
  43.1 0.5 %away.1 = f32[64,1408]{1,0:T(8,128)S(1)} custom-call(f32[240,1408]{1,0:T(8,128)S(1)} %along.1.d_ref, bf16[128,256]{1,0:T(8,128)(2,1)S(1)} %get-tuple-element.39.xh_ref, bf16[128,256]{1,0:T(8,128)(2,1)S(1)} %get-tuple-element.40.xl_ref), custom_call_target="tpu_custom_call" | custom-call | flops 1000000000 | bytes 1843200 | tf_op jit(solution)/shard_map/away/pallas_call | solution.py:601
  43.6 0.1 collective-permute-start.8
  43.7 0.0 collective-permute-done.6.low_ref
  43.7 0.0 collective-permute-done.7.high_ref
  43.7 0.6 %home.1.home_ref = f32[16,64,128]{2,1,0:T(8,128)S(1)} custom-call(f32[240,1408]{1,0:T(8,128)S(1)} %along.1.d_ref, bf16[128,256]{1,0:T(8,128)(2,1)S(1)} %get-tuple-element.39.xh_ref, bf16[128,256]{1,0:T(8,128)(2,1)S(1)} %get-tuple-element.40.xl_ref, f32[16,64,128]{2,1,0:T(8,128)S(1)} %get-tuple-element.30._.own_ref, ...), custom_call_target="tpu_custom_call" | custom-call | flops 2000000000 | bytes 3055616 | tf_op jit(solution)/shard_map/home/pallas_call | solution.py:601
  44.3 1.1 %collective-permute-done.8.refs_0_ = f32[64,1408]{1,0:T(8,128)S(1)} collective-permute-done((f32[64,1408]{1,0:T(8,128)S(1)}, f32[64,1408]{1,0:T(8,128)S(1)}, u32[]{:S(2)}, u32[]{:S(2)}) %collective-permute-start.8) | collective-permute-done | bytes 360480 | tf_op jit(solution)/shard_map/ppermute | solution.py:624
  45.4 0.9 %last.1 = f32[16,64,128]{2,1,0:T(8,128)} custom-call(f32[16,64,128]{2,1,0:T(8,128)S(1)} %home.1.home_ref, f32[64,1408]{1,0:T(8,128)S(1)} %collective-permute-done.8.refs_0_), custom_call_target="tpu_custom_call" | custom-call | flops 1000000000 | bytes 1409024 | tf_op jit(solution)/shard_map/last/pallas_call | solution.py:601
  (16 shorter events, 0.0 us)
Async XLA Ops:
  0.0 2.2 %copy-start = (f32[16,64,128]{2,1,0:T(8,128)S(1)}, f32[16,64,128]{2,1,0:T(8,128)}, u32[]{:S(2)}) copy-start(f32[16,64,128]{2,1,0:T(8,128)} %b_ref.3) | copy-start | bytes 1572868
  0.0 2.2 %collective-permute-start = (f32[16,64,128]{2,1,0:T(8,128)}, f32[16,64,128]{2,1,0:T(8,128)S(1)}, u32[]{:S(2)}, u32[]{:S(2)}) collective-permute-start(f32[16,64,128]{2,1,0:T(8,128)} %b_ref.3), channel_id=1, source_target_pairs={{16,0},{0,16},{17,1},{1,17},{18,2},{2,18},{19,3},{3,19},{20,4},{4,... | collective-permute-start | bytes 1572872 | tf_op jit(solution)/shard_map/ppermute | solution.py:624
  0.5 0.7 %copy-start.1 = (f32[4,3]{1,0:T(4,128)S(1)}, f32[4,3]{1,0:T(4,128)}, u32[]{:S(2)}) copy-start(f32[4,3]{1,0:T(4,128)} %w_ref.3) | copy-start | bytes 148
  1.1 0.7 %copy-start.3 = (f32[4,3]{1,0:T(4,128)S(1)}, f32[4,3]{1,0:T(4,128)}, u32[]{:S(2)}) copy-start(f32[4,3]{1,0:T(4,128)} %a_ref.3) | copy-start | bytes 148
  2.9 19.1 %collective-permute-start.1 = (f32[1,80,128]{2,1,0:T(8,128)S(1)}, f32[1,80,128]{2,1,0:T(8,128)S(1)}, u32[]{:S(2)}, u32[]{:S(2)}) collective-permute-start(f32[1,80,128]{2,1,0:T(8,128)S(1)} %get-tuple-element.27), channel_id=1, source_target_pairs={{12,0},{0,4},{4,8},{8,12},{13,1},{1,5},{5,9},{9,13},{14,2},{2,6},{... | collective-permute-start | bytes 122888 | tf_op jit(solution)/shard_map/ppermute | solution.py:624
  5.8 16.2 %collective-permute-start.2 = (f32[1,80,128]{2,1,0:T(8,128)S(1)}, f32[1,80,128]{2,1,0:T(8,128)S(1)}, u32[]{:S(2)}, u32[]{:S(2)}) collective-permute-start(f32[1,80,128]{2,1,0:T(8,128)S(1)} %get-tuple-element.28), channel_id=1, source_target_pairs={{4,0},{8,4},{12,8},{0,12},{5,1},{9,5},{13,9},{1,13},{6,2},{10,6},{... | collective-permute-start | bytes 122888 | tf_op jit(solution)/shard_map/ppermute | solution.py:624
  22.0 8.3 %copy-start.5 = (f32[128,128]{1,0:T(8,128)S(1)}, f32[128,128]{1,0:T(8,128)}, u32[]{:S(2)}) copy-start(f32[128,128]{1,0:T(8,128)} %constant.26.clone.ry2_ref) | copy-start | bytes 196612
  22.0 8.3 %copy-start.14 = (f32[24,32]{1,0:T(8,128)S(1)}, f32[24,32]{1,0:T(8,128)}, u32[]{:S(2)}) copy-start(f32[24,32]{1,0:T(8,128)} %constant.27.clone.rx2_ref) | copy-start | bytes 9220
  26.1 17.6 %collective-permute-start.6 = (f32[8,64,128]{2,1,0:T(8,128)S(1)}, f32[8,64,128]{2,1,0:T(8,128)S(1)}, u32[]{:S(2)}, u32[]{:S(2)}) collective-permute-start(f32[8,64,128]{2,1,0:T(8,128)S(1)} %get-tuple-element.41), channel_id=1, source_target_pairs={{3,0},{0,1},{1,2},{2,3},{7,4},{4,5},{5,6},{6,7},{11,8},{8,9},{9,10... | collective-permute-start | bytes 786440 | tf_op jit(solution)/shard_map/ppermute | solution.py:624
  28.3 15.4 %collective-permute-start.7 = (f32[8,64,128]{2,1,0:T(8,128)S(1)}, f32[8,64,128]{2,1,0:T(8,128)S(1)}, u32[]{:S(2)}, u32[]{:S(2)}) collective-permute-start(f32[8,64,128]{2,1,0:T(8,128)S(1)} %get-tuple-element.42), channel_id=1, source_target_pairs={{1,0},{2,1},{3,2},{0,3},{5,4},{6,5},{7,6},{4,7},{9,8},{10,9},{11,1... | collective-permute-start | bytes 786440 | tf_op jit(solution)/shard_map/ppermute | solution.py:624
  30.3 5.2 %copy-start.2 = (f32[4,3]{1,0:T(4,128)S(1)}, f32[4,3]{1,0:T(4,128)}, u32[]{:S(2)}) copy-start(f32[4,3]{1,0:T(4,128)} %w_ref.3) | copy-start | bytes 148
  30.3 5.2 %copy-start.4 = (f32[4,3]{1,0:T(4,128)S(1)}, f32[4,3]{1,0:T(4,128)}, u32[]{:S(2)}) copy-start(f32[4,3]{1,0:T(4,128)} %a_ref.3) | copy-start | bytes 148
  30.3 5.2 %copy-start.6 = (bf16[128,128]{1,0:T(8,128)(2,1)S(1)}, bf16[128,128]{1,0:T(8,128)(2,1)}, u32[]{:S(2)}) copy-start(bf16[128,128]{1,0:T(8,128)(2,1)} %constant.33.clone.py2) | copy-start | bytes 98308
  30.3 5.1 %copy-start.7 = (bf16[128,16]{1,0:T(8,128)(2,1)S(1)}, bf16[128,16]{1,0:T(8,128)(2,1)}, u32[]{:S(2)}) copy-start(bf16[128,16]{1,0:T(8,128)(2,1)} %constant.31.clone.px3l) | copy-start | bytes 12292
  30.3 5.1 %copy-start.8 = (bf16[128,16]{1,0:T(8,128)(2,1)S(1)}, bf16[128,16]{1,0:T(8,128)(2,1)}, u32[]{:S(2)}) copy-start(bf16[128,16]{1,0:T(8,128)(2,1)} %constant.30.clone.px3) | copy-start | bytes 12292
  30.3 5.1 %copy-start.9 = (bf16[128,32]{1,0:T(8,128)(2,1)S(1)}, bf16[128,32]{1,0:T(8,128)(2,1)}, u32[]{:S(2)}) copy-start(bf16[128,32]{1,0:T(8,128)(2,1)} %constant.29.clone.px2) | copy-start | bytes 24580
  30.4 5.1 %copy-start.10 = (bf16[128,64]{1,0:T(8,128)(2,1)S(1)}, bf16[128,64]{1,0:T(8,128)(2,1)}, u32[]{:S(2)}) copy-start(bf16[128,64]{1,0:T(8,128)(2,1)} %constant.28.clone.px1.ry3) | copy-start | bytes 49156
  30.4 5.1 %copy-start.11 = (bf16[3,16,256]{2,1,0:T(8,128)(2,1)S(1)}, bf16[3,16,256]{2,1,0:T(8,128)(2,1)}, u32[]{:S(2)}) copy-start(bf16[3,16,256]{2,1,0:T(8,128)(2,1)} %constant.32.clone.rx3) | copy-start | bytes 73732
  30.4 5.1 %copy-start.12 = (bf16[64,128]{1,0:T(8,128)(2,1)S(1)}, bf16[64,128]{1,0:T(8,128)(2,1)}, u32[]{:S(2)}) copy-start(bf16[64,128]{1,0:T(8,128)(2,1)} %constant.35.clone.py3l) | copy-start | bytes 49156
  30.4 5.1 %copy-start.13 = (bf16[64,128]{1,0:T(8,128)(2,1)S(1)}, bf16[64,128]{1,0:T(8,128)(2,1)}, u32[]{:S(2)}) copy-start(bf16[64,128]{1,0:T(8,128)(2,1)} %constant.34.clone.py3) | copy-start | bytes 49156
  30.4 5.1 %copy-start.15 = (bf16[16,8]{1,0:T(8,128)(2,1)S(1)}, bf16[16,8]{1,0:T(8,128)(2,1)}, u32[]{:S(2)}) copy-start(bf16[16,8]{1,0:T(8,128)(2,1)} %constant.37.clone.pz3) | copy-start | bytes 772
  30.4 5.1 %copy-start.16 = (bf16[16,16]{1,0:T(8,128)(2,1)S(1)}, bf16[16,16]{1,0:T(8,128)(2,1)}, u32[]{:S(2)}) copy-start(bf16[16,16]{1,0:T(8,128)(2,1)} %constant.36.clone.pz2) | copy-start | bytes 1540
  30.4 5.1 %copy-start.17 = (bf16[8,128]{1,0:T(8,128)(2,1)S(1)}, bf16[8,128]{1,0:T(8,128)(2,1)}, u32[]{:S(2)}) copy-start(bf16[8,128]{1,0:T(8,128)(2,1)} %constant.38.clone.rz3) | copy-start | bytes 6148
  31.8 5.0 %collective-permute-start.4 = (f32[120,128]{1,0:T(8,128)S(1)}, f32[120,128]{1,0:T(8,128)S(1)}, u32[]{:S(2)}, u32[]{:S(2)}) collective-permute-start(f32[120,128]{1,0:T(8,128)S(1)} %get-tuple-element.31._.refs_0_), channel_id=1, source_target_pairs={{8,0},{12,4},{0,8},{4,12},{9,1},{13,5},{1,9},{5,13},{10,2},{14,6},... | collective-permute-start | bytes 184328 | tf_op jit(solution)/shard_map/ppermute | solution.py:624
  33.4 4.7 %collective-permute-start.3 = (f32[216,128]{1,0:T(8,128)S(1)}, f32[216,128]{1,0:T(8,128)S(1)}, u32[]{:S(2)}, u32[]{:S(2)}) collective-permute-start(f32[216,128]{1,0:T(8,128)S(1)} %get-tuple-element.34), channel_id=1, source_target_pairs={{4,0},{8,4},{12,8},{0,12},{5,1},{9,5},{13,9},{1,13},{6,2},{10,6},{... | collective-permute-start | bytes 331784 | tf_op jit(solution)/shard_map/ppermute | solution.py:624
  34.0 5.6 %collective-permute-start.5 = (f32[216,128]{1,0:T(8,128)S(1)}, f32[216,128]{1,0:T(8,128)S(1)}, u32[]{:S(2)}, u32[]{:S(2)}) collective-permute-start(f32[216,128]{1,0:T(8,128)S(1)} %get-tuple-element.35), channel_id=1, source_target_pairs={{12,0},{0,4},{4,8},{8,12},{13,1},{1,5},{5,9},{9,13},{14,2},{2,6},{... | collective-permute-start | bytes 331784 | tf_op jit(solution)/shard_map/ppermute | solution.py:624
  43.6 1.7 %collective-permute-start.8 = (f32[64,1408]{1,0:T(8,128)S(1)}, f32[64,1408]{1,0:T(8,128)S(1)}, u32[]{:S(2)}, u32[]{:S(2)}) collective-permute-start(f32[64,1408]{1,0:T(8,128)S(1)} %away.1), channel_id=1, source_target_pairs={{16,0},{0,16},{17,1},{1,17},{18,2},{2,18},{19,3},{3,19},{20,4},{4,... | collective-permute-start | bytes 1081352 | tf_op jit(solution)/shard_map/ppermute | solution.py:624

commit v8 on v6

--- a/solution.py
+++ b/solution.py
@@ -197,7 +197,24 @@
     return jnp.concatenate([lo_ref[z, s.nx - R :], b_ref[z], hi_ref[z, 0:R]], axis=0)
 
 
-def share_kernel(s, b_ref, lo_ref, hi_ref, _, m_ref, first_ref, last_ref):
+def strips(s, rows):
+    lane = lanes_of(rows[0].shape)
+    group = LANES // R
+    first, last = [], []
+    for t in range(s.fine_tiles):
+        f = l = jnp.zeros(rows[0].shape, F32)
+        for g in range(min(group, s.nz - t * group)):
+            x = rows[t * group + g]
+            at = R * ((g + 1) % group)
+            f = jnp.where((lane >= at) & (lane < at + R), turn(x, at), f)
+            at = R * g
+            l = jnp.where((lane >= at) & (lane < at + R), turn(x, at + R - s.ny), l)
+        first.append(f)
+        last.append(l)
+    return first, last
+
+
+def share_kernel(s, b_ref, lo_ref, hi_ref, _, m_ref, *strip_refs):
     b = [extended(s, b_ref, lo_ref, hi_ref, z) for z in range(s.nz)]
     planes = []
     for k in range(-1, s.z1 + 2):
@@ -217,18 +234,16 @@
         shares.append(dot(rx1, high) + dot(rx1, low))
     for t, x in enumerate(packed(shares, s.wide1, s.tiles1)):
         m_ref[t] = x
-    lane = lanes_of((s.ext, LANES))
-    group = LANES // R
-    for t in range(s.fine_tiles):
-        first = last = jnp.zeros((s.ext, LANES), F32)
-        for g in range(min(group, s.nz - t * group)):
-            x = b[t * group + g]
-            at = R * ((g + 1) % group)
-            first = jnp.where((lane >= at) & (lane < at + R), turn(x, at), first)
-            at = R * g
-            last = jnp.where((lane >= at) & (lane < at + R), turn(x, at + R - s.ny), last)
-        first_ref[t] = first
-        last_ref[t] = last
+    if s.gx == 2:
+        low_slab = lax.axis_index("gx") == 0
+        own, other = strips(s, [b_ref[z] for z in range(s.nz)]), strips(s, [hi_ref[z] for z in range(s.nz)])
+        for t in range(s.fine_tiles):
+            strip_refs[0][t, : s.nx] = jnp.where(low_slab, own[1][t], other[0][t])
+            strip_refs[0][t, s.nx :] = jnp.where(low_slab, other[1][t], own[0][t])
+        return
+    for ref, x in zip(strip_refs, strips(s, b)):
+        for t in range(s.fine_tiles):
+            ref[t] = x[t]
 
 
 def rows_of(shape):
@@ -287,7 +302,7 @@
         x0_ref[t * s.nx : (t + 1) * s.nx] = jnp.where(part == 1, low.astype(F32), high.astype(F32)).astype(BF16)
 
 
-def along_matrix_kernel(s, w_ref, _, y0_ref):
+def along_matrix_kernel(s, w_ref, _, y0_ref, _out):
     coef = spreads(w_ref, (0,))
     unit = near_units(coef)
     shape = (s.ny + 2 * R, s.ny)
@@ -390,7 +405,20 @@
                 own_ref, down_ref, up_ref, e_ref, u_ref, eh_ref, el_ref, v_ref):
     group = LANES // R
     tiles = [extended(s, b_ref, lo_ref, hi_ref, z) for z in range(s.nz)]
-    tiles += [left_ref[t] for t in range(s.fine_tiles)] + [right_ref[t] for t in range(s.fine_tiles)]
+    if s.gx == 2:
+        low_slab = lax.axis_index("gx") == 0
+
+        def side(x, y):
+            out = []
+            for t in range(s.fine_tiles):
+                x0, x1 = (jnp.where(low_slab, x[t, r], y[t, r]) for r in (slice(0, s.nx), slice(s.nx, 2 * s.nx)))
+                own, other = jnp.where(low_slab, x0, x1), jnp.where(low_slab, x1, x0)
+                out.append(jnp.concatenate([other[s.nx - R :], own, other[0:R]], axis=0))
+            return out
+
+        tiles += side(left_ref, right_ref) + side(right_ref, left_ref)
+    else:
+        tiles += [ref[t] for ref in (left_ref, right_ref) for t in range(s.fine_tiles)]
     for i, x in enumerate(tiles):
         high, low = halves(x)
         columns = slice(i * LANES, (i + 1) * LANES)
@@ -450,7 +478,7 @@
 
 def depth_kernel(s, tap_ref, *refs):
     m_refs = refs[: s.gz]
-    ry2_ref, rx2_ref, _, _, w_ref, down_ref, up_ref, c2_ref, _, _, c_ref = refs[s.gz :]
+    ry2_ref, rx2_ref, _, w_ref, down_ref, up_ref, c2_ref, c_ref = refs[s.gz :]
     n = s.cz[1]
     parts = [[] for _ in range(n)]
     for b in range(s.gz):
@@ -605,6 +633,7 @@
 
     moved = sum(x.size * x.dtype.itemsize for x in operands)
     moved += sum(int(np.prod(x.shape)) * x.dtype.itemsize for x in out_shapes)
+    moved = moved if flops else 0
     return pl.pallas_call(
         kernel,
         name=name,
@@ -648,17 +677,27 @@
     )
     high_rows = fetch(charges, gx=1)
     low_rows = high_rows if s.gx == 2 else fetch(charges, gx=-1)
-    strips = (s.fine_tiles, s.ext, LANES)
-    share, first_cells, last_cells = call(
+    paired = s.gx == 2
+    strip = (s.fine_tiles, 2 * s.nx if paired else s.ext, LANES)
+    share, *cells = call(
         functools.partial(share_kernel, s), "share", [charges, low_rows, high_rows],
-        arrays((s.tiles1, s.rows1, LANES), strips, strips), after=[x0], flops=10**9,
-    )
+        arrays((s.tiles1, s.rows1, LANES), *[strip] * (1 if paired else 2)), after=[x0], flops=10**9,
+    )
+    if paired:
+        pairs = []
+        for y in range(s.gy):
+            pairs.append((y, (y + 1) % s.gy))
+            pairs.append((s.gy + y, s.gy + (y - 1) % s.gy))
+        left = lax.ppermute(cells[0], ("gx", "gy"), pairs)
+    else:
+        left, right = fetch(cells[1], gy=-1), fetch(cells[0], gy=1)
+    y0, left = call(
+        functools.partial(along_matrix_kernel, s), "taps_y", [widths],
+        arrays((2 * LANES, 2 * TERMS * s.ny), dtype=BF16), through=[left], flops=3 * 10**8,
+    )
+    if paired:
+        right = fetch(left, gx=1)
     shares = [share] + [fetch(share, gz=b) for b in range(1, s.gz)]
-    left, right = fetch(last_cells, gy=-1), fetch(first_cells, gy=1)
-    (y0,) = call(
-        functools.partial(along_matrix_kernel, s), "taps_y", [widths],
-        arrays((2 * LANES, 2 * TERMS * s.ny), dtype=BF16), after=[share], flops=6 * 10**8,
-    )
     tiles = s.nz + 2 * s.fine_tiles
     halved = pltpu.VMEM((TERMS, s.nz * s.nx, 2 * LANES), BF16)
     near, near_down, near_up = call(
@@ -669,15 +708,15 @@
             pltpu.VMEM((3 * s.ext, tiles * LANES), BF16), pltpu.VMEM((TERMS * s.nx, tiles * LANES), F32),
             halved, halved, pltpu.VMEM((TERMS,) + brick, F32),
         ],
-        flops=5 * 10**9,
+        flops=0,
     )
     base = s.tiles_s * s.rows1
     size2 = s.tiles2 * s.rows2
-    waves, to_low, to_high, coarse, near_down, near_up = call(
+    waves, to_low, to_high, coarse = call(
         functools.partial(depth_kernel, s), "depth",
         [taps] + shares + [c["ry2"], c["rx2"]],
         arrays((TERMS * s.planes, s.rows1, LANES), (base + size2, LANES), (base + size2, LANES), (size2, LANES)),
-        scalars=(0,), through=[near_down, near_up], scratch=[pltpu.VMEM((s.cz[1], s.rows1, LANES), F32)], flops=2 * 10**9,
+        scalars=(0,), after=[near], scratch=[pltpu.VMEM((s.cz[1], s.rows1, LANES), F32)], flops=2 * 10**9,
     )
     named = ("px1", "px2", "px3", "px3l", "rx3", "py2", "py3", "py3l", "ry3", "pz2", "pz3", "rz3")
     z_taps, y1, y2h, y2l, xh, xl = call(

time: 38.1 us -> 37.9 us (level)
  starting transfers between devices: 18.1 us -> 16.5 us
  waiting for transfers between devices: 4.59 us -> 6.04 us
    ppermute x12 -> x11, starting transfers between devices: 18.1 us -> 13.6 us  [fetch(): return lax.ppermute(x, names if len(names) > 1 else names[0], pairs)]
    ppermute x0 -> x1, starting transfers between devices: none -> 2.91 us  [shards(): left = lax.ppermute(cells[0], ('gx', 'gy'), pairs)]
    ppermute x12 -> x11, waiting for transfers between devices: 4.59 us -> 6.04 us  [fetch(): return lax.ppermute(x, names if len(names) > 1 else names[0], pairs)]
  transfers between devices with their start and end apart: 12 -> 12, of which waited for: 6 -> 5; matrix products, arithmetic and copies ran while one was open for 0% -> 0% of each run, Pallas kernels for 28% -> 31%
where the time goes in v8:
time: 37.9 us; the launch traced here: 37.8 us
  starting transfers between devices  16.5 us (44%)
  Pallas kernels  13.5 us (36%)
  waiting for transfers between devices  6.04 us (16%)
  local copies, waits for them, and re-layouts  1.46 us (4%)
    ppermute x11, starting transfers between devices, fetch(): return lax.ppermute(x, names if len(names) > 1 else names[0], pairs)  13.6 us
    pallas_call x10, Pallas kernels, call(): pl.pallas_call(kernel, name=name, out_shape=out_shapes, in_specs=[spec(i)...  13.5 us
    ppermute x11, waiting for transfers between devices, fetch(): return lax.ppermute(x, names if len(names) > 1 else names[0], pairs)  6.04 us
    ppermute x1, starting transfers between devices, shards(): left = lax.ppermute(cells[0], ('gx', 'gy'), pairs)  2.91 us
    unnamed x36, local copies, waits for them, and re-layouts  1.46 us
  transfers between devices with their start and end apart: 12, of which 5 were waited for; matrix products, arithmetic and copies ran while one was open for 0% of the time, Pallas kernels for 31%

profile of v8, /device:TPU:0, one launch (start us, length us, event | category | flops | bytes accessed | tf_op | source)
XLA Modules:
  0.0 37.8 jit_solution(16873985672109739605)
XLA Ops:
  0.0 0.5 %collective-permute-start = (f32[16,64,128]{2,1,0:T(8,128)}, f32[16,64,128]{2,1,0:T(8,128)S(1)}, u32[]{:S(2)}, u32[]{:S(2)}) collective-permute-start(f32[16,64,128]{2,1,0:T(8,128)} %b_ref.3), channel_id=1, source_target_pairs={{16,0},{0,16},{17,1},{1,17},{18,2},{2,18},{19,3},{3,19},{20,4},{4,... | collective-permute-start | bytes 1572872 | tf_op jit(solution)/shard_map/ppermute | solution.py:662
  0.5 0.7 %copy-done.1 = f32[4,3]{1,0:T(4,128)S(1)} copy-done((f32[4,3]{1,0:T(4,128)S(1)}, f32[4,3]{1,0:T(4,128)}, u32[]{:S(2)}) %copy-start.1) | copy-done | bytes 72
  1.1 0.7 %copy-done.3 = f32[4,3]{1,0:T(4,128)S(1)} copy-done((f32[4,3]{1,0:T(4,128)S(1)}, f32[4,3]{1,0:T(4,128)}, u32[]{:S(2)}) %copy-start.3) | copy-done | bytes 72
  1.8 0.3 taps.1
  2.1 0.1 collective-permute-done.lo_ref.hi_ref
  2.2 0.7 %share.1 = (f32[6,32,128]{2,1,0:T(8,128)S(1)}, f32[1,128,128]{2,1,0:T(8,128)S(1)}) custom-call(f32[16,64,128]{2,1,0:T(8,128)S(1)} %copy-done, f32[16,64,128]{2,1,0:T(8,128)S(1)} %collective-permute-done.lo_ref.hi_ref, f32[16,64,128]{2,1,0:T(8,128)S(1)} %collective-permute-done.lo_ref.hi_ref, bf16[192,240]{1,0:T(8,128)(2,1)S(1)} %get-tuple-element.25._.x0_ref), custom_call_target="tpu_custom_call" | custom-call | flops 1000000000 | bytes 1828864 | tf_op jit(solution)/shard_map/share/pallas_call | solution.py:637
  2.9 2.9 %collective-permute-start.4 = (f32[1,128,128]{2,1,0:T(8,128)S(1)}, f32[1,128,128]{2,1,0:T(8,128)S(1)}, u32[]{:S(2)}, u32[]{:S(2)}) collective-permute-start(f32[1,128,128]{2,1,0:T(8,128)S(1)} %get-tuple-element.27), channel_id=1, source_target_pairs={{0,4},{16,28},{4,8},{20,16},{8,12},{24,20},{12,0},{28,24},{1,5},{1... | collective-permute-start | bytes 196616 | tf_op jit(solution)/shard_map/ppermute | solution.py:691
  5.8 1.6 %collective-permute-start.3 = (f32[6,32,128]{2,1,0:T(8,128)S(1)}, f32[6,32,128]{2,1,0:T(8,128)S(1)}, u32[]{:S(2)}, u32[]{:S(2)}) collective-permute-start(f32[6,32,128]{2,1,0:T(8,128)S(1)} %get-tuple-element.26.refs_0_), channel_id=1, source_target_pairs={{3,0},{0,1},{1,2},{2,3},{7,4},{4,5},{5,6},{6,7},{11,8},{8,9},{9,10... | collective-permute-start | bytes 294920 | tf_op jit(solution)/shard_map/ppermute | solution.py:662
  7.4 2.6 %collective-permute-start.2 = (f32[6,32,128]{2,1,0:T(8,128)S(1)}, f32[6,32,128]{2,1,0:T(8,128)S(1)}, u32[]{:S(2)}, u32[]{:S(2)}) collective-permute-start(f32[6,32,128]{2,1,0:T(8,128)S(1)} %get-tuple-element.26.refs_0_), channel_id=1, source_target_pairs={{2,0},{3,1},{0,2},{1,3},{6,4},{7,5},{4,6},{5,7},{10,8},{11,9},{8,1... | collective-permute-start | bytes 294920 | tf_op jit(solution)/shard_map/ppermute | solution.py:662
  10.0 1.3 %collective-permute-start.1 = (f32[6,32,128]{2,1,0:T(8,128)S(1)}, f32[6,32,128]{2,1,0:T(8,128)S(1)}, u32[]{:S(2)}, u32[]{:S(2)}) collective-permute-start(f32[6,32,128]{2,1,0:T(8,128)S(1)} %get-tuple-element.26.refs_0_), channel_id=1, source_target_pairs={{1,0},{2,1},{3,2},{0,3},{5,4},{6,5},{7,6},{4,7},{9,8},{10,9},{11,1... | collective-permute-start | bytes 294920 | tf_op jit(solution)/shard_map/ppermute | solution.py:662
  11.4 0.0 collective-permute-done.4._
  11.4 0.3 taps_y.1
  11.6 0.0 copy-start.5
  11.6 0.0 copy-start.14
  11.7 0.1 collective-permute-start.5
  11.7 1.2 %collective-permute-done.5.right_ref = f32[1,128,128]{2,1,0:T(8,128)S(1)} collective-permute-done((f32[1,128,128]{2,1,0:T(8,128)S(1)}, f32[1,128,128]{2,1,0:T(8,128)S(1)}, u32[]{:S(2)}, u32[]{:S(2)}) %collective-permute-start.5) | collective-permute-done | bytes 65568 | tf_op jit(solution)/shard_map/ppermute | solution.py:662
  13.0 4.0 %near.1 = (f32[16,64,128]{2,1,0:T(8,128)S(1)}, f32[8,64,128]{2,1,0:T(8,128)S(1)}, f32[8,64,128]{2,1,0:T(8,128)S(1)}) custom-call(f32[8,128]{1,0:T(8,128)S(1)} %get-tuple-element.24.tap_ref, f32[16,64,128]{2,1,0:T(8,128)S(1)} %copy-done, f32[16,64,128]{2,1,0:T(8,128)S(1)} %collective-permute-done.lo_ref.hi_ref, ...), custom_call_target="tpu_custom_call" | custom-call | tf_op jit(solution)/shard_map/near/pallas_call | solution.py:637
  17.0 0.7 %collective-permute-start.9 = (f32[8,64,128]{2,1,0:T(8,128)S(1)}, f32[8,64,128]{2,1,0:T(8,128)S(1)}, u32[]{:S(2)}, u32[]{:S(2)}) collective-permute-start(f32[8,64,128]{2,1,0:T(8,128)S(1)} %get-tuple-element.41), channel_id=1, source_target_pairs={{3,0},{0,1},{1,2},{2,3},{7,4},{4,5},{5,6},{6,7},{11,8},{8,9},{9,10... | collective-permute-start | bytes 786440 | tf_op jit(solution)/shard_map/ppermute | solution.py:662
  17.8 3.1 %collective-permute-start.10 = (f32[8,64,128]{2,1,0:T(8,128)S(1)}, f32[8,64,128]{2,1,0:T(8,128)S(1)}, u32[]{:S(2)}, u32[]{:S(2)}) collective-permute-start(f32[8,64,128]{2,1,0:T(8,128)S(1)} %get-tuple-element.42), channel_id=1, source_target_pairs={{1,0},{2,1},{3,2},{0,3},{5,4},{6,5},{7,6},{4,7},{9,8},{10,9},{11,1... | collective-permute-start | bytes 786440 | tf_op jit(solution)/shard_map/ppermute | solution.py:662
  20.9 0.0 collective-permute-done.3.refs_3_
  20.9 0.0 collective-permute-done.2.refs_2_
  20.9 0.0 collective-permute-done.1.refs_1_
  20.9 0.0 copy-start.4
  20.9 0.0 copy-start.6
  21.0 0.0 copy-start.7
  21.0 0.0 copy-start.8
  21.0 0.0 copy-start.9
  21.0 0.0 copy-start.10
  21.0 0.0 copy-start.11
  21.0 0.0 copy-start.12
  21.0 0.0 copy-start.13
  21.0 0.0 copy-start.15
  21.1 0.0 copy-start.16
  21.1 0.0 copy-start.17
  21.1 1.4 %depth.1 = (f32[33,32,128]{2,1,0:T(8,128)S(1)}, f32[216,128]{1,0:T(8,128)S(1)}, f32[216,128]{1,0:T(8,128)S(1)}, f32[120,128]{1,0:T(8,128)S(1)}) custom-call(f32[8,128]{1,0:T(8,128)S(1)} %get-tuple-element.24.tap_ref, f32[6,32,128]{2,1,0:T(8,128)S(1)} %get-tuple-element.26.refs_0_, f32[6,32,128]{2,1,0:T(8,128)S(1)} %collective-permute-done.1.refs_1_, ...), custom_call_target="tpu_custom_call" | custom-call | flops 2000000000 | bytes 1813504 | tf_op jit(solution)/shard_map/depth/pallas_call | solution.py:637
  22.5 1.6 %collective-permute-start.7 = (f32[120,128]{1,0:T(8,128)S(1)}, f32[120,128]{1,0:T(8,128)S(1)}, u32[]{:S(2)}, u32[]{:S(2)}) collective-permute-start(f32[120,128]{1,0:T(8,128)S(1)} %get-tuple-element.31._.refs_0_), channel_id=1, source_target_pairs={{8,0},{12,4},{0,8},{4,12},{9,1},{13,5},{1,9},{5,13},{10,2},{14,6},... | collective-permute-start | bytes 184328 | tf_op jit(solution)/shard_map/ppermute | solution.py:662
  24.0 1.4 %collective-permute-start.6 = (f32[216,128]{1,0:T(8,128)S(1)}, f32[216,128]{1,0:T(8,128)S(1)}, u32[]{:S(2)}, u32[]{:S(2)}) collective-permute-start(f32[216,128]{1,0:T(8,128)S(1)} %get-tuple-element.34), channel_id=1, source_target_pairs={{4,0},{8,4},{12,8},{0,12},{5,1},{9,5},{13,9},{1,13},{6,2},{10,6},{... | collective-permute-start | bytes 331784 | tf_op jit(solution)/shard_map/ppermute | solution.py:662
  25.5 0.6 %collective-permute-start.8 = (f32[216,128]{1,0:T(8,128)S(1)}, f32[216,128]{1,0:T(8,128)S(1)}, u32[]{:S(2)}, u32[]{:S(2)}) collective-permute-start(f32[216,128]{1,0:T(8,128)S(1)} %get-tuple-element.35), channel_id=1, source_target_pairs={{12,0},{0,4},{4,8},{8,12},{13,1},{1,5},{5,9},{9,13},{14,2},{2,6},{... | collective-permute-start | bytes 331784 | tf_op jit(solution)/shard_map/ppermute | solution.py:662
  26.2 1.3 %matrices.1 = (f32[96,128]{1,0:T(8,128)S(1)}, bf16[128,768]{1,0:T(8,128)(2,1)S(1)}, bf16[128,768]{1,0:T(8,128)(2,1)S(1)}, bf16[128,768]{1,0:T(8,128)(2,1)S(1)}, ...) custom-call(f32[4,3]{1,0:T(4,128)S(1)} %copy-done.2, f32[4,3]{1,0:T(4,128)S(1)} %copy-done.4, ...), custom_call_target="tpu_custom_call" | custom-call | flops 2000000000 | bytes 973664 | tf_op jit(solution)/shard_map/matrices/pallas_call | solution.py:637
  27.5 0.0 collective-permute-done.7.refs_2_
  27.5 2.0 %collective-permute-done.6.refs_1_ = f32[216,128]{1,0:T(8,128)S(1)} collective-permute-done((f32[216,128]{1,0:T(8,128)S(1)}, f32[216,128]{1,0:T(8,128)S(1)}, u32[]{:S(2)}, u32[]{:S(2)}) %collective-permute-start.6) | collective-permute-done | bytes 110624 | tf_op jit(solution)/shard_map/ppermute | solution.py:662
  29.5 1.6 %collective-permute-done.8.refs_3_ = f32[216,128]{1,0:T(8,128)S(1)} collective-permute-done((f32[216,128]{1,0:T(8,128)S(1)}, f32[216,128]{1,0:T(8,128)S(1)}, u32[]{:S(2)}, u32[]{:S(2)}) %collective-permute-start.8) | collective-permute-done | bytes 110624 | tf_op jit(solution)/shard_map/ppermute | solution.py:662
  31.1 3.5 %along.1.d_ref = f32[240,1408]{1,0:T(8,128)S(1)} custom-call(f32[96,128]{1,0:T(8,128)S(1)} %get-tuple-element.32.z_ref, f32[33,32,128]{2,1,0:T(8,128)S(1)} %get-tuple-element.33.w_ref, f32[120,128]{1,0:T(8,128)S(1)} %get-tuple-element.31._.refs_0_, f32[216,128]{1,0:T(8,128)S(1)} %collective-permute-done.6.refs_1_, ...), custom_call_target="tpu_custom_call" | custom-call | flops 3000000000 | bytes 2875392 | tf_op jit(solution)/shard_map/along/pallas_call | solution.py:637
  34.6 0.5 %away.1 = f32[64,1408]{1,0:T(8,128)S(1)} custom-call(f32[240,1408]{1,0:T(8,128)S(1)} %along.1.d_ref, bf16[128,256]{1,0:T(8,128)(2,1)S(1)} %get-tuple-element.39.xh_ref, bf16[128,256]{1,0:T(8,128)(2,1)S(1)} %get-tuple-element.40.xl_ref), custom_call_target="tpu_custom_call" | custom-call | flops 1000000000 | bytes 1843200 | tf_op jit(solution)/shard_map/away/pallas_call | solution.py:637
  35.1 0.1 collective-permute-start.11
  35.2 0.6 %home.1.home_ref = f32[16,64,128]{2,1,0:T(8,128)S(1)} custom-call(f32[240,1408]{1,0:T(8,128)S(1)} %along.1.d_ref, bf16[128,256]{1,0:T(8,128)(2,1)S(1)} %get-tuple-element.39.xh_ref, bf16[128,256]{1,0:T(8,128)(2,1)S(1)} %get-tuple-element.40.xl_ref, f32[16,64,128]{2,1,0:T(8,128)S(1)} %get-tuple-element.30.refs_6_.own_ref, ...), custom_call_target="tpu_custom_call" | custom-call | flops 2000000000 | bytes 3055616 | tf_op jit(solution)/shard_map/home/pallas_call | solution.py:637
  35.8 1.1 %collective-permute-done.11.refs_0_ = f32[64,1408]{1,0:T(8,128)S(1)} collective-permute-done((f32[64,1408]{1,0:T(8,128)S(1)}, f32[64,1408]{1,0:T(8,128)S(1)}, u32[]{:S(2)}, u32[]{:S(2)}) %collective-permute-start.11) | collective-permute-done | bytes 360480 | tf_op jit(solution)/shard_map/ppermute | solution.py:662
  36.9 0.9 %last.1 = f32[16,64,128]{2,1,0:T(8,128)} custom-call(f32[16,64,128]{2,1,0:T(8,128)S(1)} %home.1.home_ref, f32[64,1408]{1,0:T(8,128)S(1)} %collective-permute-done.11.refs_0_), custom_call_target="tpu_custom_call" | custom-call | flops 1000000000 | bytes 1409024 | tf_op jit(solution)/shard_map/last/pallas_call | solution.py:637
  (22 shorter events, 0.0 us)
Async XLA Ops:
  0.0 2.2 %copy-start = (f32[16,64,128]{2,1,0:T(8,128)S(1)}, f32[16,64,128]{2,1,0:T(8,128)}, u32[]{:S(2)}) copy-start(f32[16,64,128]{2,1,0:T(8,128)} %b_ref.3) | copy-start | bytes 1572868
  0.0 2.2 %collective-permute-start = (f32[16,64,128]{2,1,0:T(8,128)}, f32[16,64,128]{2,1,0:T(8,128)S(1)}, u32[]{:S(2)}, u32[]{:S(2)}) collective-permute-start(f32[16,64,128]{2,1,0:T(8,128)} %b_ref.3), channel_id=1, source_target_pairs={{16,0},{0,16},{17,1},{1,17},{18,2},{2,18},{19,3},{3,19},{20,4},{4,... | collective-permute-start | bytes 1572872 | tf_op jit(solution)/shard_map/ppermute | solution.py:662
  0.5 0.7 %copy-start.1 = (f32[4,3]{1,0:T(4,128)S(1)}, f32[4,3]{1,0:T(4,128)}, u32[]{:S(2)}) copy-start(f32[4,3]{1,0:T(4,128)} %w_ref.5) | copy-start | bytes 148
  1.1 0.7 %copy-start.3 = (f32[4,3]{1,0:T(4,128)S(1)}, f32[4,3]{1,0:T(4,128)}, u32[]{:S(2)}) copy-start(f32[4,3]{1,0:T(4,128)} %a_ref.3) | copy-start | bytes 148
  2.2 9.2 %copy-start.2 = (f32[4,3]{1,0:T(4,128)S(1)}, f32[4,3]{1,0:T(4,128)}, u32[]{:S(2)}) copy-start(f32[4,3]{1,0:T(4,128)} %w_ref.5) | copy-start | bytes 148
  2.9 8.4 %collective-permute-start.4 = (f32[1,128,128]{2,1,0:T(8,128)S(1)}, f32[1,128,128]{2,1,0:T(8,128)S(1)}, u32[]{:S(2)}, u32[]{:S(2)}) collective-permute-start(f32[1,128,128]{2,1,0:T(8,128)S(1)} %get-tuple-element.27), channel_id=1, source_target_pairs={{0,4},{16,28},{4,8},{20,16},{8,12},{24,20},{12,0},{28,24},{1,5},{1... | collective-permute-start | bytes 196616 | tf_op jit(solution)/shard_map/ppermute | solution.py:691
  5.8 15.1 %collective-permute-start.3 = (f32[6,32,128]{2,1,0:T(8,128)S(1)}, f32[6,32,128]{2,1,0:T(8,128)S(1)}, u32[]{:S(2)}, u32[]{:S(2)}) collective-permute-start(f32[6,32,128]{2,1,0:T(8,128)S(1)} %get-tuple-element.26.refs_0_), channel_id=1, source_target_pairs={{3,0},{0,1},{1,2},{2,3},{7,4},{4,5},{5,6},{6,7},{11,8},{8,9},{9,10... | collective-permute-start | bytes 294920 | tf_op jit(solution)/shard_map/ppermute | solution.py:662
  7.4 13.5 %collective-permute-start.2 = (f32[6,32,128]{2,1,0:T(8,128)S(1)}, f32[6,32,128]{2,1,0:T(8,128)S(1)}, u32[]{:S(2)}, u32[]{:S(2)}) collective-permute-start(f32[6,32,128]{2,1,0:T(8,128)S(1)} %get-tuple-element.26.refs_0_), channel_id=1, source_target_pairs={{2,0},{3,1},{0,2},{1,3},{6,4},{7,5},{4,6},{5,7},{10,8},{11,9},{8,1... | collective-permute-start | bytes 294920 | tf_op jit(solution)/shard_map/ppermute | solution.py:662
  10.0 10.9 %collective-permute-start.1 = (f32[6,32,128]{2,1,0:T(8,128)S(1)}, f32[6,32,128]{2,1,0:T(8,128)S(1)}, u32[]{:S(2)}, u32[]{:S(2)}) collective-permute-start(f32[6,32,128]{2,1,0:T(8,128)S(1)} %get-tuple-element.26.refs_0_), channel_id=1, source_target_pairs={{1,0},{2,1},{3,2},{0,3},{5,4},{6,5},{7,6},{4,7},{9,8},{10,9},{11,1... | collective-permute-start | bytes 294920 | tf_op jit(solution)/shard_map/ppermute | solution.py:662
  11.6 9.3 %copy-start.5 = (f32[128,128]{1,0:T(8,128)S(1)}, f32[128,128]{1,0:T(8,128)}, u32[]{:S(2)}) copy-start(f32[128,128]{1,0:T(8,128)} %constant.26.clone.refs_4_) | copy-start | bytes 196612
  11.6 9.3 %copy-start.14 = (f32[24,32]{1,0:T(8,128)S(1)}, f32[24,32]{1,0:T(8,128)}, u32[]{:S(2)}) copy-start(f32[24,32]{1,0:T(8,128)} %constant.27.clone.refs_5_) | copy-start | bytes 9220
  11.7 1.3 %collective-permute-start.5 = (f32[1,128,128]{2,1,0:T(8,128)S(1)}, f32[1,128,128]{2,1,0:T(8,128)S(1)}, u32[]{:S(2)}, u32[]{:S(2)}) collective-permute-start(f32[1,128,128]{2,1,0:T(8,128)S(1)} %get-tuple-element.28.left_ref), channel_id=1, source_target_pairs={{16,0},{0,16},{17,1},{1,17},{18,2},{2,18},{19,3},{3,19},{20,4},{4,... | collective-permute-start | bytes 196616 | tf_op jit(solution)/shard_map/ppermute | solution.py:662
  17.0 18.2 %collective-permute-start.9 = (f32[8,64,128]{2,1,0:T(8,128)S(1)}, f32[8,64,128]{2,1,0:T(8,128)S(1)}, u32[]{:S(2)}, u32[]{:S(2)}) collective-permute-start(f32[8,64,128]{2,1,0:T(8,128)S(1)} %get-tuple-element.41), channel_id=1, source_target_pairs={{3,0},{0,1},{1,2},{2,3},{7,4},{4,5},{5,6},{6,7},{11,8},{8,9},{9,10... | collective-permute-start | bytes 786440 | tf_op jit(solution)/shard_map/ppermute | solution.py:662
  17.8 17.5 %collective-permute-start.10 = (f32[8,64,128]{2,1,0:T(8,128)S(1)}, f32[8,64,128]{2,1,0:T(8,128)S(1)}, u32[]{:S(2)}, u32[]{:S(2)}) collective-permute-start(f32[8,64,128]{2,1,0:T(8,128)S(1)} %get-tuple-element.42), channel_id=1, source_target_pairs={{1,0},{2,1},{3,2},{0,3},{5,4},{6,5},{7,6},{4,7},{9,8},{10,9},{11,1... | collective-permute-start | bytes 786440 | tf_op jit(solution)/shard_map/ppermute | solution.py:662
  20.9 5.1 %copy-start.4 = (f32[4,3]{1,0:T(4,128)S(1)}, f32[4,3]{1,0:T(4,128)}, u32[]{:S(2)}) copy-start(f32[4,3]{1,0:T(4,128)} %a_ref.3) | copy-start | bytes 148
  20.9 5.1 %copy-start.6 = (bf16[128,128]{1,0:T(8,128)(2,1)S(1)}, bf16[128,128]{1,0:T(8,128)(2,1)}, u32[]{:S(2)}) copy-start(bf16[128,128]{1,0:T(8,128)(2,1)} %constant.33.clone.py2) | copy-start | bytes 98308
  21.0 5.1 %copy-start.7 = (bf16[128,16]{1,0:T(8,128)(2,1)S(1)}, bf16[128,16]{1,0:T(8,128)(2,1)}, u32[]{:S(2)}) copy-start(bf16[128,16]{1,0:T(8,128)(2,1)} %constant.31.clone.px3l) | copy-start | bytes 12292
  21.0 5.1 %copy-start.8 = (bf16[128,16]{1,0:T(8,128)(2,1)S(1)}, bf16[128,16]{1,0:T(8,128)(2,1)}, u32[]{:S(2)}) copy-start(bf16[128,16]{1,0:T(8,128)(2,1)} %constant.30.clone.px3) | copy-start | bytes 12292
  21.0 5.1 %copy-start.9 = (bf16[128,32]{1,0:T(8,128)(2,1)S(1)}, bf16[128,32]{1,0:T(8,128)(2,1)}, u32[]{:S(2)}) copy-start(bf16[128,32]{1,0:T(8,128)(2,1)} %constant.29.clone.px2) | copy-start | bytes 24580
  21.0 5.1 %copy-start.10 = (bf16[128,64]{1,0:T(8,128)(2,1)S(1)}, bf16[128,64]{1,0:T(8,128)(2,1)}, u32[]{:S(2)}) copy-start(bf16[128,64]{1,0:T(8,128)(2,1)} %constant.28.clone.px1.ry3) | copy-start | bytes 49156
  21.0 5.1 %copy-start.11 = (bf16[3,16,256]{2,1,0:T(8,128)(2,1)S(1)}, bf16[3,16,256]{2,1,0:T(8,128)(2,1)}, u32[]{:S(2)}) copy-start(bf16[3,16,256]{2,1,0:T(8,128)(2,1)} %constant.32.clone.rx3) | copy-start | bytes 73732
  21.0 5.1 %copy-start.12 = (bf16[64,128]{1,0:T(8,128)(2,1)S(1)}, bf16[64,128]{1,0:T(8,128)(2,1)}, u32[]{:S(2)}) copy-start(bf16[64,128]{1,0:T(8,128)(2,1)} %constant.35.clone.py3l) | copy-start | bytes 49156
  21.0 5.1 %copy-start.13 = (bf16[64,128]{1,0:T(8,128)(2,1)S(1)}, bf16[64,128]{1,0:T(8,128)(2,1)}, u32[]{:S(2)}) copy-start(bf16[64,128]{1,0:T(8,128)(2,1)} %constant.34.clone.py3) | copy-start | bytes 49156
  21.0 5.1 %copy-start.15 = (bf16[16,8]{1,0:T(8,128)(2,1)S(1)}, bf16[16,8]{1,0:T(8,128)(2,1)}, u32[]{:S(2)}) copy-start(bf16[16,8]{1,0:T(8,128)(2,1)} %constant.37.clone.pz3) | copy-start | bytes 772
  21.1 5.1 %copy-start.16 = (bf16[16,16]{1,0:T(8,128)(2,1)S(1)}, bf16[16,16]{1,0:T(8,128)(2,1)}, u32[]{:S(2)}) copy-start(bf16[16,16]{1,0:T(8,128)(2,1)} %constant.36.clone.pz2) | copy-start | bytes 1540
  21.1 5.1 %copy-start.17 = (bf16[8,128]{1,0:T(8,128)(2,1)S(1)}, bf16[8,128]{1,0:T(8,128)(2,1)}, u32[]{:S(2)}) copy-start(bf16[8,128]{1,0:T(8,128)(2,1)} %constant.38.clone.rz3) | copy-start | bytes 6148
  22.5 5.0 %collective-permute-start.7 = (f32[120,128]{1,0:T(8,128)S(1)}, f32[120,128]{1,0:T(8,128)S(1)}, u32[]{:S(2)}, u32[]{:S(2)}) collective-permute-start(f32[120,128]{1,0:T(8,128)S(1)} %get-tuple-element.31._.refs_0_), channel_id=1, source_target_pairs={{8,0},{12,4},{0,8},{4,12},{9,1},{13,5},{1,9},{5,13},{10,2},{14,6},... | collective-permute-start | bytes 184328 | tf_op jit(solution)/shard_map/ppermute | solution.py:662
  24.0 5.5 %collective-permute-start.6 = (f32[216,128]{1,0:T(8,128)S(1)}, f32[216,128]{1,0:T(8,128)S(1)}, u32[]{:S(2)}, u32[]{:S(2)}) collective-permute-start(f32[216,128]{1,0:T(8,128)S(1)} %get-tuple-element.34), channel_id=1, source_target_pairs={{4,0},{8,4},{12,8},{0,12},{5,1},{9,5},{13,9},{1,13},{6,2},{10,6},{... | collective-permute-start | bytes 331784 | tf_op jit(solution)/shard_map/ppermute | solution.py:662
  25.5 5.6 %collective-permute-start.8 = (f32[216,128]{1,0:T(8,128)S(1)}, f32[216,128]{1,0:T(8,128)S(1)}, u32[]{:S(2)}, u32[]{:S(2)}) collective-permute-start(f32[216,128]{1,0:T(8,128)S(1)} %get-tuple-element.35), channel_id=1, source_target_pairs={{12,0},{0,4},{4,8},{8,12},{13,1},{1,5},{5,9},{9,13},{14,2},{2,6},{... | collective-permute-start | bytes 331784 | tf_op jit(solution)/shard_map/ppermute | solution.py:662
  35.1 1.7 %collective-permute-start.11 = (f32[64,1408]{1,0:T(8,128)S(1)}, f32[64,1408]{1,0:T(8,128)S(1)}, u32[]{:S(2)}, u32[]{:S(2)}) collective-permute-start(f32[64,1408]{1,0:T(8,128)S(1)} %away.1), channel_id=1, source_target_pairs={{16,0},{0,16},{17,1},{1,17},{18,2},{2,18},{19,3},{3,19},{20,4},{4,... | collective-permute-start | bytes 1081352 | tf_op jit(solution)/shard_map/ppermute | solution.py:662

commit v9 on v5

--- a/solution.py
+++ b/solution.py
@@ -39,13 +39,21 @@
         self.wide1 = self.y1 + 3
         self.wide2 = self.y2 + 5
         self.tiles1 = -(-self.planes * self.wide1 // LANES)
-        self.tiles2 = -(-self.cz[2] * self.wide2 // LANES)
+        self.x3, self.y3 = nx // 8, ny // 8
+        self.rows3 = up8(self.x3 + 5)
+        self.wide3 = self.y3 + 5
+        self.tiles3 = -(-self.cz[3] * self.wide3 // LANES)
+        self.strip2 = R + 5
+        self.per_tile2 = LANES // self.strip2
+        self.tiles_s2 = -(-self.cz[2] // self.per_tile2)
         self.strip = R + 3
         self.per_tile = LANES // self.strip
         self.tiles_s = -(-TERMS * self.planes // self.per_tile)
         self.fine_tiles = -(-nz // (LANES // R))
         self.ext = nx + 2 * R
-        self.depth = TERMS * (self.rows1 + 2 * self.rows2)
+        self.depth = TERMS * (self.rows1 + self.rows2 + self.rows3)
+        self.base2 = self.tiles_s * self.rows1
+        self.base3 = self.base2 + self.tiles_s2 * self.rows2
         self.depth_lanes = -(-self.depth // LANES) * LANES
 
 
@@ -106,24 +114,16 @@
     x1, x2, x3 = chain(s.cx)
     c["px1"], c["px2"] = exact(x1), exact(x2)
     parts("px3", x3)
-    place = np.zeros((s.cx[2], s.rows2))
-    for r in range(s.x2 + 3):
-        place[(r - 1) % s.cx[2], r] += 1.0
-    rx3 = np.zeros((TERMS, s.cx[3], s.depth_lanes))
-    for t in range(TERMS):
-        first = TERMS * s.rows1 + (TERMS + t) * s.rows2
-        rx3[t, :, first : first + s.rows2] = restrict_circle(s.cx[2]) @ place
-    c["rx3"] = exact(rx3)
     _, y2, y3 = chain(s.cy)
     c["py2"] = exact(y2[: s.ny].T)
     parts("py3", y3[: s.ny].T)
-    c["ry3"] = exact(restrict_circle(s.cy[2]).T)
     z2 = prolong_circle(s.cz[2])
     z3 = z2 @ prolong_circle(s.cz[3])
     own = [(o - 1) % s.cz[1] for o in range(s.planes)]
     c["pz2"] = exact(padded(z2[own], s.zrows, s.cz[2]))
     c["pz3"] = exact(padded(z3[own], s.zrows, s.cz[3]))
-    c["rz3"] = exact(padded(restrict_circle(s.cz[2]), s.cz[3], LANES))
+    c["ry3"] = padded(restrict_open(-2, s.wide2, -2, s.wide3).T, LANES, LANES)
+    c["rx3"] = padded(restrict_open(-1, s.x2 + 3, -2, s.x3 + 5), s.rows3, s.rows2)
     return c
 
 
@@ -297,7 +297,7 @@
         y0_ref[: s.ny + 2 * R, at + s.ny : at + 2 * s.ny] = low
 
 
-def matrix_kernel(s, w_ref, a_ref, px1, px2, px3, px3l, rx3, py2, py3, py3l, ry3, pz2, pz3, rz3, _,
+def matrix_kernel(s, w_ref, a_ref, px1, px2, px3, px3l, py2, py3, py3l, pz2, pz3, _,
                   z_ref, y1_ref, y2h_ref, y2l_ref, xh_ref, xl_ref):
     coef = spreads(w_ref, range(4))
     unit = near_units(coef[:3])
@@ -317,8 +317,8 @@
         d = (d & (n - 1)).astype(F32)
         return (bell(c, d) + bell(c, n - d)) * u
 
-    def full_circle(n, shape, c, u):
-        d = ((rows_of(shape) - lanes_of(shape)) & (n - 1)).astype(F32)
+    def full_circle(n, d, c, u):
+        d = (d & (n - 1)).astype(F32)
         d = jnp.minimum(d, n - d)
         return jnp.exp(c * d * d) * u
 
@@ -327,7 +327,9 @@
     d = (rows_of(shape) - (R + 1) - (fine >> 1)).astype(F32)
     even = (fine & 1) == 0
     known = rows_of(shape) < s.y1 + 3 + 2 * R
-    wide = (s.cy[2], s.cy[2])
+    two, three = (LANES, s.cy[2]), (LANES, s.cy[3])
+    known2 = rows_of(two) < s.y2 + 5 + 2 * R
+    known3 = rows_of(three) < (s.gy - 1) * s.y3 + s.wide3
     for t in range(TERMS):
         c = coef[1][t]
         here = bell(c, d)
@@ -335,19 +337,17 @@
         high, low = halves(jnp.where(known, jnp.where(even, here, between) * unit[1][t], 0.0))
         y1_ref[:, 2 * t * s.ny : (2 * t + 1) * s.ny] = high
         y1_ref[:, (2 * t + 1) * s.ny : (2 * t + 2) * s.ny] = low
-        g = circle(s.cy[2], rows_of(wide) - lanes_of(wide), coef[2][t], unit[2][t])
-        high, low = halves(dot2(g, py2[...]))
+        g = circle(s.cy[2], rows_of(two) - (R + 2) - lanes_of(two), coef[2][t], unit[2][t])
+        high, low = halves(dot2(jnp.where(known2, g, 0.0), py2[...]))
         y2h_ref[:, t * s.ny : (t + 1) * s.ny] = high
         y2l_ref[:, t * s.ny : (t + 1) * s.ny] = low
-        g = full_circle(s.cy[3], (s.cy[3], s.cy[3]), coef[3][t], top_y[t])
-        high, low = halves(g)
-        g = dot(ry3[...], high) + dot(ry3[...], low)
-        high, low = halves(dot3(g, py3[...], py3l[...]))
+        g = full_circle(s.cy[3], rows_of(three) - 2 - lanes_of(three), coef[3][t], top_y[t])
+        high, low = halves(dot3(jnp.where(known3, g, 0.0), py3[...], py3l[...]))
         at = (TERMS + t) * s.ny
         y2h_ref[:, at : at + s.ny] = high
         y2l_ref[:, at : at + s.ny] = low
 
-    def terms(level, first, rows, valid, shift):
+    def terms(level, first, rows, valid, shift, around, u):
         shape = (s.cx[level], s.depth_lanes)
         lane = lanes_of(shape) - first
         column = lane - jnp.where(lane < rows, 0, jnp.where(lane < 2 * rows, rows, 2 * rows))
@@ -355,19 +355,15 @@
         def by_term(v):
             return jnp.where(lane < rows, v[0], jnp.where(lane < 2 * rows, v[1], v[2]))
 
-        g = circle(s.cx[level], rows_of(shape) - column + shift, by_term(coef[level]), by_term(unit[level]))
+        g = around(s.cx[level], rows_of(shape) - column + shift, by_term(coef[level]), by_term(u))
         high, low = halves(jnp.where((lane >= 0) & (lane < TERMS * rows) & (column < valid), g, 0.0))
         return high, low
 
-    high, low = terms(1, 0, s.rows1, s.rows1, 0)
+    high, low = terms(1, 0, s.rows1, s.rows1, 0, circle, unit[1])
     x = dot(px1[...], high) + dot(px1[...], low)
-    high, low = terms(2, TERMS * s.rows1, s.rows2, s.x2 + 3, 1)
+    high, low = terms(2, TERMS * s.rows1, s.rows2, s.x2 + 3, 1, circle, unit[2])
     x += dot(px2[...], high) + dot(px2[...], low)
-    g = None
-    for t in range(TERMS):
-        part = dot2(full_circle(s.cx[3], (s.cx[3], s.cx[3]), coef[3][t], top_x[t]), rx3[t])
-        g = part if g is None else g + part
-    high, low = halves(g)
+    high, low = terms(3, TERMS * (s.rows1 + s.rows2), s.rows3, s.x3 + 5, 2, full_circle, top_x)
     x += dot(px3[...], high) + dot(px3l[...], high) + dot(px3[...], low)
     xh_ref[...], xl_ref[...] = halves(x)
     for t in range(TERMS):
@@ -375,10 +371,10 @@
         g = circle(s.cz[2], rows_of(shape) - lanes_of(shape), coef[2][t], unit[2][t])
         high, low = halves(g * (one(a_ref, 2, t) * 0.0625))
         z_ref[t * s.zrows : (t + 1) * s.zrows] = dot(pz2[...], high) + dot(pz2[...], low)
-        g = full_circle(s.cz[3], (s.cz[3], s.cz[3]), coef[3][t], top_z[t])
+        shape = (s.cz[3], LANES)
+        g = full_circle(s.cz[3], rows_of(shape) - lanes_of(shape), coef[3][t], top_z[t])
         high, low = halves(g * (one(a_ref, 3, t) * 0.015625))
-        g = dot2(dot(pz3[...], high) + dot(pz3[...], low), rz3[...])
-        z_ref[(TERMS + t) * s.zrows : (TERMS + t + 1) * s.zrows] = g
+        z_ref[(TERMS + t) * s.zrows : (TERMS + t + 1) * s.zrows] = dot(pz3[...], high) + dot(pz3[...], low)
 
 
 def near_kernel(s, tap_ref, b_ref, lo_ref, hi_ref, left_ref, right_ref, x0_ref, y0_ref,
@@ -445,7 +441,7 @@
 
 def depth_kernel(s, tap_ref, *refs):
     m_refs = refs[: s.gz]
-    ry2_ref, rx2_ref, _, w_ref, down_ref, up_ref, c2_ref, c_ref = refs[s.gz :]
+    ry2_ref, rx2_ref, ry3_ref, rx3_ref, _, w_ref, down_ref, up_ref, c2_ref, c3_ref, c_ref = refs[s.gz :]
     n = s.cz[1]
     parts = [[] for _ in range(n)]
     for b in range(s.gz):
@@ -474,35 +470,51 @@
             here = (lane >= at) & (lane < at + s.strip)
             down[tile] = jnp.where(here, turn(x, at), down[tile])
             up[tile] = jnp.where(here, turn(x, at - (s.wide1 - s.strip)), up[tile])
-    coarse = []
-    for j in range(s.cz[2]):
-        at = lambda d: c_ref[(2 * j + d) % n]
-        coarse.append(at(0) + NEAR * (at(1) + at(-1)) + FAR * (at(3) + at(-3)))
-    high, low = halves(jnp.concatenate(coarse, axis=0))
-    ry2 = ry2_ref[...].astype(BF16)
-    rx2 = rx2_ref[...].astype(BF16)
-    along = dot(high, ry2) + dot(low, ry2)
-    shares = []
-    for j in range(s.cz[2]):
-        high, low = halves(along[j * s.rows1 : (j + 1) * s.rows1])
-        shares.append(dot(rx2, high) + dot(rx2, low))
+
+    def restricted(planes, y_ref, x_ref):
+        n, rows = len(planes), planes[0].shape[0]
+        coarse = []
+        for j in range(n // 2):
+            at = lambda d: planes[(2 * j + d) % n]
+            coarse.append(at(0) + NEAR * (at(1) + at(-1)) + FAR * (at(3) + at(-3)))
+        along = dot2(jnp.concatenate(coarse, axis=0), y_ref[...].astype(BF16))
+        x = x_ref[...].astype(BF16)
+        out = []
+        for j in range(n // 2):
+            high, low = halves(along[j * rows : (j + 1) * rows])
+            out.append(dot(x, high) + dot(x, low))
+        return out
+
+    level2 = restricted([c_ref[z] for z in range(n)], ry2_ref, rx2_ref)
+    level3 = restricted(level2, ry3_ref, rx3_ref)
     for t in range(s.tiles_s):
         down_ref[t * s.rows1 : (t + 1) * s.rows1] = down[t]
         up_ref[t * s.rows1 : (t + 1) * s.rows1] = up[t]
-    base = s.tiles_s * s.rows1
-    for t, x in enumerate(packed(shares, s.wide2, s.tiles2)):
-        rows = slice(t * s.rows2, (t + 1) * s.rows2)
-        c2_ref[rows] = x
+    lane = lanes_of((s.rows2, LANES))
+    down = [jnp.zeros((s.rows2, LANES), F32)] * s.tiles_s2
+    up = list(down)
+    for j, x in enumerate(level2):
+        c2_ref[j] = x
+        tile, slot = divmod(j, s.per_tile2)
+        at = slot * s.strip2
+        here = (lane >= at) & (lane < at + s.strip2)
+        down[tile] = jnp.where(here, turn(x, at), down[tile])
+        up[tile] = jnp.where(here, turn(x, at - (s.wide2 - s.strip2)), up[tile])
+    for t in range(s.tiles_s2):
+        rows = slice(s.base2 + t * s.rows2, s.base2 + (t + 1) * s.rows2)
+        down_ref[rows] = down[t]
+        up_ref[rows] = up[t]
+    for t, x in enumerate(packed(level3, s.wide3, s.tiles3)):
+        c3_ref[t * s.rows3 : (t + 1) * s.rows3] = x
         for ref in (down_ref, up_ref):
-            ref[base + t * s.rows2 : base + (t + 1) * s.rows2] = x
-
-
-def along_kernel(s, z_ref, w_ref, *refs):
-    c2_refs = refs[: s.gy]
-    y1_ref, y2h_ref, y2l_ref, d_ref, yb_ref = refs[s.gy :]
-    base = s.tiles_s * s.rows1
+            ref[s.base3 + t * s.rows3 : s.base3 + (t + 1) * s.rows3] = x
+
+
+def along_kernel(s, z_ref, w_ref, c2_ref, *refs):
+    c3_refs = refs[: s.gy]
+    y1_ref, y2h_ref, y2l_ref, d_ref, y2_ref, y3_ref = refs[s.gy :]
     lane = lanes_of((s.rows1, LANES))
-    above, below = c2_refs[1], c2_refs[-1]
+    above, below = c3_refs[1], c3_refs[-1]
     end = s.y1 + R
     for t in range(TERMS):
         cells = []
@@ -521,26 +533,41 @@
         out = both[:, : s.ny] + both[:, s.ny :] + dot(low, y1_ref[:, at : at + s.ny])
         for o in range(s.planes):
             d_ref[t * s.rows1 : (t + 1) * s.rows1, o * s.ny : (o + 1) * s.ny] = out[o * s.rows1 : (o + 1) * s.rows1]
+    lane = lanes_of((s.rows2, LANES))
+    end = s.y2 + R
     cells = []
     for j in range(s.cz[2]):
+        tile, slot = divmod(j, s.per_tile2)
+        rows = slice(s.base2 + tile * s.rows2, s.base2 + (tile + 1) * s.rows2)
+        at = slot * s.strip2
+        x = turn(c2_ref[j], R)
+        x += jnp.where(lane < s.strip2, turn(below[rows], -at), 0.0)
+        x += jnp.where((lane >= end) & (lane < end + s.strip2), turn(above[rows], end - at), 0.0)
+        cells.append(x)
+    cells3 = []
+    for j in range(s.cz[3]):
         out = None
         for b in range(s.gy):
-            first = 0 if b == 0 or c2_refs[b].shape[0] == s.tiles2 * s.rows2 else base
-            tile = lambda t, b=b, f=first: c2_refs[b][f + t * s.rows2 : f + (t + 1) * s.rows2]
-            x = unpacked(tile, j, s.wide2, (b * s.y2 - 2) % LANES)
+            first = s.base3 if c3_refs[b].shape[0] > s.tiles3 * s.rows3 else 0
+            tile = lambda t, b=b, f=first: c3_refs[b][f + t * s.rows3 : f + (t + 1) * s.rows3]
+            x = unpacked(tile, j, s.wide3, b * s.y3)
             out = x if out is None else out + x
-        cells.append(out)
-    yb = dot3(jnp.concatenate(cells, axis=0), y2h_ref[...], y2l_ref[...])
-    for j in range(s.cz[2]):
-        for q in range(2 * TERMS):
-            yb_ref[q, j] = yb[j * s.rows2 : (j + 1) * s.rows2, q * s.ny : (q + 1) * s.ny]
-    for o in range(s.planes):
-        for q in range(2 * TERMS):
-            x = yb_ref[q, 0] * z_ref[q * s.zrows + o, 0]
-            for j in range(1, s.cz[2]):
-                x += yb_ref[q, j] * z_ref[q * s.zrows + o, j]
-            at = TERMS * s.rows1 + q * s.rows2
-            d_ref[at : at + s.rows2, o * s.ny : (o + 1) * s.ny] = x
+        cells3.append(out)
+    at = TERMS * s.rows1
+    for q, (x, rows, ref) in enumerate(((cells, s.rows2, y2_ref), (cells3, s.rows3, y3_ref))):
+        columns = slice(q * TERMS * s.ny, (q + 1) * TERMS * s.ny)
+        y = dot3(jnp.concatenate(x, axis=0), y2h_ref[:, columns], y2l_ref[:, columns])
+        for t in range(TERMS):
+            for j in range(len(x)):
+                ref[t, j] = y[j * rows : (j + 1) * rows, t * s.ny : (t + 1) * s.ny]
+        for o in range(s.planes):
+            for t in range(TERMS):
+                scale = [z_ref[(q * TERMS + t) * s.zrows + o, j] for j in range(len(x))]
+                out = ref[t, 0] * scale[0]
+                for j in range(1, len(x)):
+                    out += ref[t, j] * scale[j]
+                d_ref[at + t * rows : at + (t + 1) * rows, o * s.ny : (o + 1) * s.ny] = out
+        at += TERMS * rows
 
 
 def across(s, d_ref, xh_ref, xl_ref, shift):
@@ -659,21 +686,21 @@
         ],
         flops=5 * 10**9,
     )
-    base = s.tiles_s * s.rows1
-    size2 = s.tiles2 * s.rows2
-    waves, to_low, to_high, coarse = call(
+    size3 = s.tiles3 * s.rows3
+    message = (s.base3 + size3, LANES)
+    waves, to_low, to_high, level2, coarse = call(
         functools.partial(depth_kernel, s), "depth",
-        [taps] + shares + [c["ry2"], c["rx2"]],
-        arrays((TERMS * s.planes, s.rows1, LANES), (base + size2, LANES), (base + size2, LANES), (size2, LANES)),
+        [taps] + shares + [c[k] for k in ("ry2", "rx2", "ry3", "rx3")],
+        arrays((TERMS * s.planes, s.rows1, LANES), message, message, (s.cz[2], s.rows2, LANES), (size3, LANES)),
         scalars=(0,), after=[near], scratch=[pltpu.VMEM((s.cz[1], s.rows1, LANES), F32)], flops=2 * 10**9,
     )
-    named = ("px1", "px2", "px3", "px3l", "rx3", "py2", "py3", "py3l", "ry3", "pz2", "pz3", "rz3")
+    named = ("px1", "px2", "px3", "px3l", "py2", "py3", "py3l", "pz2", "pz3")
     z_taps, y1, y2h, y2l, xh, xl = call(
         functools.partial(matrix_kernel, s), "matrices",
         [widths, amplitudes] + [c[k] for k in named],
         arrays((2 * TERMS * s.zrows, LANES))
         + arrays((LANES, 2 * TERMS * s.ny), dtype=BF16)
-        + two(s.cy[2], 2 * TERMS * s.ny) + two(s.cx[0], s.depth_lanes),
+        + two(LANES, 2 * TERMS * s.ny) + two(s.cx[0], s.depth_lanes),
         after=[coarse], flops=2 * 10**9,
     )
     coarses = [coarse]
@@ -682,9 +709,11 @@
     near_low, near_high = fetch(near_up, gz=-1), fetch(near_down, gz=1)
     (terms,) = call(
         functools.partial(along_kernel, s), "along",
-        [z_taps, waves] + coarses + [y1, y2h, y2l],
+        [z_taps, waves, level2] + coarses + [y1, y2h, y2l],
         arrays((s.depth, s.planes * s.ny)), scalars=(0,),
-        scratch=[pltpu.VMEM((2 * TERMS, s.cz[2], s.rows2, s.ny), F32)], flops=3 * 10**9,
+        scratch=[
+            pltpu.VMEM((TERMS, s.cz[2], s.rows2, s.ny), F32), pltpu.VMEM((TERMS, s.cz[3], s.rows3, s.ny), F32)
+        ], flops=3 * 10**9,
     )
     parts = call(
         functools.partial(away_kernel, s), "away", [terms, xh, xl],

time: 36.9 us -> 36.4 us (0.986)
  Pallas kernels: 13.2 us -> 12.3 us
  waiting for transfers between devices: 3.83 us -> 4.24 us
    pallas_call x9, Pallas kernels: 13.2 us -> 12.3 us  [call(): pl.pallas_call(kernel, name=name, out_shape=out_shapes, in_specs=[spec(i)...]
    ppermute x12, waiting for transfers between devices: 3.83 us -> 4.24 us  [fetch(): return lax.ppermute(x, names if len(names) > 1 else names[0], pairs)]
  transfers between devices with their start and end apart: 12 -> 12, of which waited for: 3 -> 3; matrix products, arithmetic and copies ran while one was open for 0% -> 0% of each run, Pallas kernels for 32% -> 30%
where the time goes in v9:
time: 36.4 us; the launch traced here: 36.2 us
  starting transfers between devices  17.9 us (49%)
  Pallas kernels  12.3 us (34%)
  waiting for transfers between devices  4.24 us (12%)
  local copies, waits for them, and re-layouts  1.46 us (4%)
    ppermute x12, starting transfers between devices, fetch(): return lax.ppermute(x, names if len(names) > 1 else names[0], pairs)  17.9 us
    pallas_call x9, Pallas kernels, call(): pl.pallas_call(kernel, name=name, out_shape=out_shapes, in_specs=[spec(i)...  12.3 us
    ppermute x12, waiting for transfers between devices, fetch(): return lax.ppermute(x, names if len(names) > 1 else names[0], pairs)  4.24 us
    unnamed x36, local copies, waits for them, and re-layouts  1.46 us
  transfers between devices with their start and end apart: 12, of which 3 were waited for; matrix products, arithmetic and copies ran while one was open for 0% of the time, Pallas kernels for 30%

profile of v9, /device:TPU:0, one launch (start us, length us, event | category | flops | bytes accessed | tf_op | source)
XLA Modules:
  0.0 36.2 jit_solution(15855019309779934440)
XLA Ops:
  0.0 0.5 %collective-permute-start = (f32[16,64,128]{2,1,0:T(8,128)}, f32[16,64,128]{2,1,0:T(8,128)S(1)}, u32[]{:S(2)}, u32[]{:S(2)}) collective-permute-start(f32[16,64,128]{2,1,0:T(8,128)} %b_ref.3), channel_id=1, source_target_pairs={{16,0},{0,16},{17,1},{1,17},{18,2},{2,18},{19,3},{3,19},{20,4},{4,... | collective-permute-start | bytes 1572872 | tf_op jit(solution)/shard_map/ppermute | solution.py:650
  0.5 0.7 %copy-done.1 = f32[4,3]{1,0:T(4,128)S(1)} copy-done((f32[4,3]{1,0:T(4,128)S(1)}, f32[4,3]{1,0:T(4,128)}, u32[]{:S(2)}) %copy-start.1) | copy-done | bytes 72
  1.1 0.7 %copy-done.3 = f32[4,3]{1,0:T(4,128)S(1)} copy-done((f32[4,3]{1,0:T(4,128)S(1)}, f32[4,3]{1,0:T(4,128)}, u32[]{:S(2)}) %copy-start.3) | copy-done | bytes 72
  1.8 0.4 %taps.1 = (f32[8,128]{1,0:T(8,128)S(1)}, bf16[192,240]{1,0:T(8,128)(2,1)S(1)}, bf16[256,768]{1,0:T(8,128)(2,1)S(1)}) custom-call(f32[4,3]{1,0:T(4,128)S(1)} %copy-done.1, f32[4,3]{1,0:T(4,128)S(1)} %copy-done.3), custom_call_target="tpu_custom_call" | custom-call | flops 600000000 | bytes 489568 | tf_op jit(solution)/shard_map/taps/pallas_call | solution.py:627
  2.2 0.0 collective-permute-done.lo_ref.hi_ref
  2.2 0.7 %share.1 = (f32[6,32,128]{2,1,0:T(8,128)S(1)}, f32[1,80,128]{2,1,0:T(8,128)S(1)}, f32[1,80,128]{2,1,0:T(8,128)S(1)}) custom-call(f32[16,64,128]{2,1,0:T(8,128)S(1)} %copy-done, f32[16,64,128]{2,1,0:T(8,128)S(1)} %collective-permute-done.lo_ref.hi_ref, f32[16,64,128]{2,1,0:T(8,128)S(1)} %collective-permute-done.lo_ref.hi_ref, ...), custom_call_target="tpu_custom_call" | custom-call | flops 1000000000 | bytes 1845248 | tf_op jit(solution)/shard_map/share/pallas_call | solution.py:627
  2.9 2.9 %collective-permute-start.4 = (f32[1,80,128]{2,1,0:T(8,128)S(1)}, f32[1,80,128]{2,1,0:T(8,128)S(1)}, u32[]{:S(2)}, u32[]{:S(2)}) collective-permute-start(f32[1,80,128]{2,1,0:T(8,128)S(1)} %get-tuple-element.28), channel_id=1, source_target_pairs={{12,0},{0,4},{4,8},{8,12},{13,1},{1,5},{5,9},{9,13},{14,2},{2,6},{... | collective-permute-start | bytes 122888 | tf_op jit(solution)/shard_map/ppermute | solution.py:650
  5.8 1.0 %collective-permute-start.5 = (f32[1,80,128]{2,1,0:T(8,128)S(1)}, f32[1,80,128]{2,1,0:T(8,128)S(1)}, u32[]{:S(2)}, u32[]{:S(2)}) collective-permute-start(f32[1,80,128]{2,1,0:T(8,128)S(1)} %get-tuple-element.29), channel_id=1, source_target_pairs={{4,0},{8,4},{12,8},{0,12},{5,1},{9,5},{13,9},{1,13},{6,2},{10,6},{... | collective-permute-start | bytes 122888 | tf_op jit(solution)/shard_map/ppermute | solution.py:650
  6.8 2.0 %collective-permute-start.3 = (f32[6,32,128]{2,1,0:T(8,128)S(1)}, f32[6,32,128]{2,1,0:T(8,128)S(1)}, u32[]{:S(2)}, u32[]{:S(2)}) collective-permute-start(f32[6,32,128]{2,1,0:T(8,128)S(1)} %get-tuple-element.27.refs_0_), channel_id=1, source_target_pairs={{3,0},{0,1},{1,2},{2,3},{7,4},{4,5},{5,6},{6,7},{11,8},{8,9},{9,10... | collective-permute-start | bytes 294920 | tf_op jit(solution)/shard_map/ppermute | solution.py:650
  8.8 2.6 %collective-permute-start.2 = (f32[6,32,128]{2,1,0:T(8,128)S(1)}, f32[6,32,128]{2,1,0:T(8,128)S(1)}, u32[]{:S(2)}, u32[]{:S(2)}) collective-permute-start(f32[6,32,128]{2,1,0:T(8,128)S(1)} %get-tuple-element.27.refs_0_), channel_id=1, source_target_pairs={{2,0},{3,1},{0,2},{1,3},{6,4},{7,5},{4,6},{5,7},{10,8},{11,9},{8,1... | collective-permute-start | bytes 294920 | tf_op jit(solution)/shard_map/ppermute | solution.py:650
  11.4 1.3 %collective-permute-start.1 = (f32[6,32,128]{2,1,0:T(8,128)S(1)}, f32[6,32,128]{2,1,0:T(8,128)S(1)}, u32[]{:S(2)}, u32[]{:S(2)}) collective-permute-start(f32[6,32,128]{2,1,0:T(8,128)S(1)} %get-tuple-element.27.refs_0_), channel_id=1, source_target_pairs={{1,0},{2,1},{3,2},{0,3},{5,4},{6,5},{7,6},{4,7},{9,8},{10,9},{11,1... | collective-permute-start | bytes 294920 | tf_op jit(solution)/shard_map/ppermute | solution.py:650
  12.8 0.0 collective-permute-done.4.left_ref
  12.8 0.0 collective-permute-done.5.right_ref
  12.8 0.0 copy-start.6
  12.8 0.0 copy-start.14
  12.8 0.0 copy-start.15
  12.8 4.1 %near.1 = (f32[16,64,128]{2,1,0:T(8,128)S(1)}, f32[8,64,128]{2,1,0:T(8,128)S(1)}, f32[8,64,128]{2,1,0:T(8,128)S(1)}) custom-call(f32[8,128]{1,0:T(8,128)S(1)} %get-tuple-element.25.tap_ref, f32[16,64,128]{2,1,0:T(8,128)S(1)} %copy-done, f32[16,64,128]{2,1,0:T(8,128)S(1)} %collective-permute-done.lo_ref.hi_ref, ...), custom_call_target="tpu_custom_call" | custom-call | flops 5000000000 | bytes 3192832 | tf_op jit(solution)/shard_map/near/pallas_call | solution.py:627
  16.9 0.7 %collective-permute-start.9 = (f32[8,64,128]{2,1,0:T(8,128)S(1)}, f32[8,64,128]{2,1,0:T(8,128)S(1)}, u32[]{:S(2)}, u32[]{:S(2)}) collective-permute-start(f32[8,64,128]{2,1,0:T(8,128)S(1)} %get-tuple-element.43), channel_id=1, source_target_pairs={{3,0},{0,1},{1,2},{2,3},{7,4},{4,5},{5,6},{6,7},{11,8},{8,9},{9,10... | collective-permute-start | bytes 786440 | tf_op jit(solution)/shard_map/ppermute | solution.py:650
  17.6 3.1 %collective-permute-start.10 = (f32[8,64,128]{2,1,0:T(8,128)S(1)}, f32[8,64,128]{2,1,0:T(8,128)S(1)}, u32[]{:S(2)}, u32[]{:S(2)}) collective-permute-start(f32[8,64,128]{2,1,0:T(8,128)S(1)} %get-tuple-element.44), channel_id=1, source_target_pairs={{1,0},{2,1},{3,2},{0,3},{5,4},{6,5},{7,6},{4,7},{9,8},{10,9},{11,1... | collective-permute-start | bytes 786440 | tf_op jit(solution)/shard_map/ppermute | solution.py:650
  20.8 0.0 collective-permute-done.3.refs_3_
  20.8 0.0 collective-permute-done.2.refs_2_
  20.8 0.0 collective-permute-done.1.refs_1_
  20.8 0.0 copy-start.2
  20.8 0.0 copy-start.4
  20.8 0.0 copy-start.7
  20.8 0.0 copy-start.8
  20.9 0.0 copy-start.9
  20.9 0.0 copy-start.10
  20.9 0.0 copy-start.11
  20.9 0.0 copy-start.12
  20.9 0.0 copy-start.13
  20.9 0.0 copy-start.16
  20.9 0.0 copy-start.17
  20.9 1.7 %depth.1 = (f32[33,32,128]{2,1,0:T(8,128)S(1)}, f32[176,128]{1,0:T(8,128)S(1)}, f32[176,128]{1,0:T(8,128)S(1)}, f32[16,24,128]{2,1,0:T(8,128)S(1)}, f32[32,128]{1,0:T(8,128)S(1)}) custom-call(f32[8,128]{1,0:T(8,128)S(1)} %get-tuple-element.25.tap_ref, f32[6,32,128]{2,1,0:T(8,128)S(1)} %get-tuple-element.27.refs_0_, ...), custom_call_target="tpu_custom_call" | custom-call | flops 2000000000 | bytes 1991168 | tf_op jit(solution)/shard_map/depth/pallas_call | solution.py:627
  22.7 1.6 %collective-permute-start.7 = (f32[32,128]{1,0:T(8,128)S(1)}, f32[32,128]{1,0:T(8,128)S(1)}, u32[]{:S(2)}, u32[]{:S(2)}) collective-permute-start(f32[32,128]{1,0:T(8,128)S(1)} %get-tuple-element.32._.refs_0_), channel_id=1, source_target_pairs={{8,0},{12,4},{0,8},{4,12},{9,1},{13,5},{1,9},{5,13},{10,2},{14,6},... | collective-permute-start | bytes 49160 | tf_op jit(solution)/shard_map/ppermute | solution.py:650
  24.3 0.5 %collective-permute-start.6 = (f32[176,128]{1,0:T(8,128)S(1)}, f32[176,128]{1,0:T(8,128)S(1)}, u32[]{:S(2)}, u32[]{:S(2)}) collective-permute-start(f32[176,128]{1,0:T(8,128)S(1)} %get-tuple-element.36), channel_id=1, source_target_pairs={{4,0},{8,4},{12,8},{0,12},{5,1},{9,5},{13,9},{1,13},{6,2},{10,6},{... | collective-permute-start | bytes 270344 | tf_op jit(solution)/shard_map/ppermute | solution.py:650
  24.8 1.5 %collective-permute-start.8 = (f32[176,128]{1,0:T(8,128)S(1)}, f32[176,128]{1,0:T(8,128)S(1)}, u32[]{:S(2)}, u32[]{:S(2)}) collective-permute-start(f32[176,128]{1,0:T(8,128)S(1)} %get-tuple-element.37), channel_id=1, source_target_pairs={{12,0},{0,4},{4,8},{8,12},{13,1},{1,5},{5,9},{9,13},{14,2},{2,6},{... | collective-permute-start | bytes 270344 | tf_op jit(solution)/shard_map/ppermute | solution.py:650
  26.4 0.7 %matrices.1 = (f32[96,128]{1,0:T(8,128)S(1)}, bf16[128,768]{1,0:T(8,128)(2,1)S(1)}, bf16[128,768]{1,0:T(8,128)(2,1)S(1)}, bf16[128,768]{1,0:T(8,128)(2,1)S(1)}, ...) custom-call(f32[4,3]{1,0:T(4,128)S(1)} %copy-done.2, f32[4,3]{1,0:T(4,128)S(1)} %copy-done.4, ...), custom_call_target="tpu_custom_call" | custom-call | flops 2000000000 | bytes 885600 | tf_op jit(solution)/shard_map/matrices/pallas_call | solution.py:627
  27.1 0.0 collective-permute-done.7.refs_2_
  27.1 1.7 %collective-permute-done.6.refs_1_ = f32[176,128]{1,0:T(8,128)S(1)} collective-permute-done((f32[176,128]{1,0:T(8,128)S(1)}, f32[176,128]{1,0:T(8,128)S(1)}, u32[]{:S(2)}, u32[]{:S(2)}) %collective-permute-start.6) | collective-permute-done | bytes 90144 | tf_op jit(solution)/shard_map/ppermute | solution.py:650
  28.8 1.4 %collective-permute-done.8.refs_3_ = f32[176,128]{1,0:T(8,128)S(1)} collective-permute-done((f32[176,128]{1,0:T(8,128)S(1)}, f32[176,128]{1,0:T(8,128)S(1)}, u32[]{:S(2)}, u32[]{:S(2)}) %collective-permute-start.8) | collective-permute-done | bytes 90144 | tf_op jit(solution)/shard_map/ppermute | solution.py:650
  30.3 2.8 %along.1.d_ref = f32[216,1408]{1,0:T(8,128)S(1)} custom-call(f32[96,128]{1,0:T(8,128)S(1)} %get-tuple-element.33.z_ref, f32[33,32,128]{2,1,0:T(8,128)S(1)} %get-tuple-element.34.w_ref, f32[16,24,128]{2,1,0:T(8,128)S(1)} %get-tuple-element.35.c2_ref, f32[32,128]{1,0:T(8,128)S(1)} %get-tuple-element.32._.refs_0_, ...), custom_call_target="tpu_custom_call" | custom-call | flops 3000000000 | bytes 2805760 | tf_op jit(solution)/shard_map/along/pallas_call | solution.py:627
  33.1 0.5 %away.1 = f32[64,1408]{1,0:T(8,128)S(1)} custom-call(f32[216,1408]{1,0:T(8,128)S(1)} %along.1.d_ref, bf16[128,256]{1,0:T(8,128)(2,1)S(1)} %get-tuple-element.41.xh_ref, bf16[128,256]{1,0:T(8,128)(2,1)S(1)} %get-tuple-element.42.xl_ref), custom_call_target="tpu_custom_call" | custom-call | flops 1000000000 | bytes 1708032 | tf_op jit(solution)/shard_map/away/pallas_call | solution.py:627
  33.6 0.1 collective-permute-start.11
  33.7 0.0 collective-permute-done.9.low_ref
  33.7 0.5 %home.1.home_ref = f32[16,64,128]{2,1,0:T(8,128)S(1)} custom-call(f32[216,1408]{1,0:T(8,128)S(1)} %along.1.d_ref, bf16[128,256]{1,0:T(8,128)(2,1)S(1)} %get-tuple-element.41.xh_ref, bf16[128,256]{1,0:T(8,128)(2,1)S(1)} %get-tuple-element.42.xl_ref, f32[16,64,128]{2,1,0:T(8,128)S(1)} %get-tuple-element.31.refs_8_.own_ref, ...), custom_call_target="tpu_custom_call" | custom-call | flops 2000000000 | bytes 2920448 | tf_op jit(solution)/shard_map/home/pallas_call | solution.py:627
  34.2 1.1 %collective-permute-done.11.refs_0_ = f32[64,1408]{1,0:T(8,128)S(1)} collective-permute-done((f32[64,1408]{1,0:T(8,128)S(1)}, f32[64,1408]{1,0:T(8,128)S(1)}, u32[]{:S(2)}, u32[]{:S(2)}) %collective-permute-start.11) | collective-permute-done | bytes 360480 | tf_op jit(solution)/shard_map/ppermute | solution.py:650
  35.3 0.9 %last.1 = f32[16,64,128]{2,1,0:T(8,128)} custom-call(f32[16,64,128]{2,1,0:T(8,128)S(1)} %home.1.home_ref, f32[64,1408]{1,0:T(8,128)S(1)} %collective-permute-done.11.refs_0_), custom_call_target="tpu_custom_call" | custom-call | flops 1000000000 | bytes 1409024 | tf_op jit(solution)/shard_map/last/pallas_call | solution.py:627
  (21 shorter events, 0.0 us)
Async XLA Ops:
  0.0 2.2 %copy-start = (f32[16,64,128]{2,1,0:T(8,128)S(1)}, f32[16,64,128]{2,1,0:T(8,128)}, u32[]{:S(2)}) copy-start(f32[16,64,128]{2,1,0:T(8,128)} %b_ref.3) | copy-start | bytes 1572868
  0.0 2.2 %collective-permute-start = (f32[16,64,128]{2,1,0:T(8,128)}, f32[16,64,128]{2,1,0:T(8,128)S(1)}, u32[]{:S(2)}, u32[]{:S(2)}) collective-permute-start(f32[16,64,128]{2,1,0:T(8,128)} %b_ref.3), channel_id=1, source_target_pairs={{16,0},{0,16},{17,1},{1,17},{18,2},{2,18},{19,3},{3,19},{20,4},{4,... | collective-permute-start | bytes 1572872 | tf_op jit(solution)/shard_map/ppermute | solution.py:650
  0.5 0.7 %copy-start.1 = (f32[4,3]{1,0:T(4,128)S(1)}, f32[4,3]{1,0:T(4,128)}, u32[]{:S(2)}) copy-start(f32[4,3]{1,0:T(4,128)} %w_ref.3) | copy-start | bytes 148
  1.1 0.7 %copy-start.3 = (f32[4,3]{1,0:T(4,128)S(1)}, f32[4,3]{1,0:T(4,128)}, u32[]{:S(2)}) copy-start(f32[4,3]{1,0:T(4,128)} %a_ref.3) | copy-start | bytes 148
  2.9 9.9 %collective-permute-start.4 = (f32[1,80,128]{2,1,0:T(8,128)S(1)}, f32[1,80,128]{2,1,0:T(8,128)S(1)}, u32[]{:S(2)}, u32[]{:S(2)}) collective-permute-start(f32[1,80,128]{2,1,0:T(8,128)S(1)} %get-tuple-element.28), channel_id=1, source_target_pairs={{12,0},{0,4},{4,8},{8,12},{13,1},{1,5},{5,9},{9,13},{14,2},{2,6},{... | collective-permute-start | bytes 122888 | tf_op jit(solution)/shard_map/ppermute | solution.py:650
  5.8 7.0 %collective-permute-start.5 = (f32[1,80,128]{2,1,0:T(8,128)S(1)}, f32[1,80,128]{2,1,0:T(8,128)S(1)}, u32[]{:S(2)}, u32[]{:S(2)}) collective-permute-start(f32[1,80,128]{2,1,0:T(8,128)S(1)} %get-tuple-element.29), channel_id=1, source_target_pairs={{4,0},{8,4},{12,8},{0,12},{5,1},{9,5},{13,9},{1,13},{6,2},{10,6},{... | collective-permute-start | bytes 122888 | tf_op jit(solution)/shard_map/ppermute | solution.py:650
  6.8 13.9 %collective-permute-start.3 = (f32[6,32,128]{2,1,0:T(8,128)S(1)}, f32[6,32,128]{2,1,0:T(8,128)S(1)}, u32[]{:S(2)}, u32[]{:S(2)}) collective-permute-start(f32[6,32,128]{2,1,0:T(8,128)S(1)} %get-tuple-element.27.refs_0_), channel_id=1, source_target_pairs={{3,0},{0,1},{1,2},{2,3},{7,4},{4,5},{5,6},{6,7},{11,8},{8,9},{9,10... | collective-permute-start | bytes 294920 | tf_op jit(solution)/shard_map/ppermute | solution.py:650
  8.8 11.9 %collective-permute-start.2 = (f32[6,32,128]{2,1,0:T(8,128)S(1)}, f32[6,32,128]{2,1,0:T(8,128)S(1)}, u32[]{:S(2)}, u32[]{:S(2)}) collective-permute-start(f32[6,32,128]{2,1,0:T(8,128)S(1)} %get-tuple-element.27.refs_0_), channel_id=1, source_target_pairs={{2,0},{3,1},{0,2},{1,3},{6,4},{7,5},{4,6},{5,7},{10,8},{11,9},{8,1... | collective-permute-start | bytes 294920 | tf_op jit(solution)/shard_map/ppermute | solution.py:650
  11.4 9.3 %collective-permute-start.1 = (f32[6,32,128]{2,1,0:T(8,128)S(1)}, f32[6,32,128]{2,1,0:T(8,128)S(1)}, u32[]{:S(2)}, u32[]{:S(2)}) collective-permute-start(f32[6,32,128]{2,1,0:T(8,128)S(1)} %get-tuple-element.27.refs_0_), channel_id=1, source_target_pairs={{1,0},{2,1},{3,2},{0,3},{5,4},{6,5},{7,6},{4,7},{9,8},{10,9},{11,1... | collective-permute-start | bytes 294920 | tf_op jit(solution)/shard_map/ppermute | solution.py:650
  12.8 8.0 %copy-start.5 = (f32[128,128]{1,0:T(8,128)S(1)}, f32[128,128]{1,0:T(8,128)}, u32[]{:S(2)}) copy-start(f32[128,128]{1,0:T(8,128)} %constant.37.clone.refs_6_) | copy-start | bytes 196612
  12.8 8.0 %copy-start.6 = (f32[128,128]{1,0:T(8,128)S(1)}, f32[128,128]{1,0:T(8,128)}, u32[]{:S(2)}) copy-start(f32[128,128]{1,0:T(8,128)} %constant.26.clone.refs_4_) | copy-start | bytes 196612
  12.8 8.0 %copy-start.14 = (f32[24,32]{1,0:T(8,128)S(1)}, f32[24,32]{1,0:T(8,128)}, u32[]{:S(2)}) copy-start(f32[24,32]{1,0:T(8,128)} %constant.27.clone.refs_5_) | copy-start | bytes 9220
  12.8 8.0 %copy-start.15 = (f32[16,24]{1,0:T(8,128)S(1)}, f32[16,24]{1,0:T(8,128)}, u32[]{:S(2)}) copy-start(f32[16,24]{1,0:T(8,128)} %constant.38.clone.refs_7_) | copy-start | bytes 4612
  16.9 16.8 %collective-permute-start.9 = (f32[8,64,128]{2,1,0:T(8,128)S(1)}, f32[8,64,128]{2,1,0:T(8,128)S(1)}, u32[]{:S(2)}, u32[]{:S(2)}) collective-permute-start(f32[8,64,128]{2,1,0:T(8,128)S(1)} %get-tuple-element.43), channel_id=1, source_target_pairs={{3,0},{0,1},{1,2},{2,3},{7,4},{4,5},{5,6},{6,7},{11,8},{8,9},{9,10... | collective-permute-start | bytes 786440 | tf_op jit(solution)/shard_map/ppermute | solution.py:650
  17.6 16.1 %collective-permute-start.10 = (f32[8,64,128]{2,1,0:T(8,128)S(1)}, f32[8,64,128]{2,1,0:T(8,128)S(1)}, u32[]{:S(2)}, u32[]{:S(2)}) collective-permute-start(f32[8,64,128]{2,1,0:T(8,128)S(1)} %get-tuple-element.44), channel_id=1, source_target_pairs={{1,0},{2,1},{3,2},{0,3},{5,4},{6,5},{7,6},{4,7},{9,8},{10,9},{11,1... | collective-permute-start | bytes 786440 | tf_op jit(solution)/shard_map/ppermute | solution.py:650
  20.8 5.5 %copy-start.2 = (f32[4,3]{1,0:T(4,128)S(1)}, f32[4,3]{1,0:T(4,128)}, u32[]{:S(2)}) copy-start(f32[4,3]{1,0:T(4,128)} %w_ref.3) | copy-start | bytes 148
  20.8 5.5 %copy-start.4 = (f32[4,3]{1,0:T(4,128)S(1)}, f32[4,3]{1,0:T(4,128)}, u32[]{:S(2)}) copy-start(f32[4,3]{1,0:T(4,128)} %a_ref.3) | copy-start | bytes 148
  20.8 5.5 %copy-start.7 = (bf16[128,128]{1,0:T(8,128)(2,1)S(1)}, bf16[128,128]{1,0:T(8,128)(2,1)}, u32[]{:S(2)}) copy-start(bf16[128,128]{1,0:T(8,128)(2,1)} %constant.32.clone.py2) | copy-start | bytes 98308
  20.8 5.5 %copy-start.8 = (bf16[128,16]{1,0:T(8,128)(2,1)S(1)}, bf16[128,16]{1,0:T(8,128)(2,1)}, u32[]{:S(2)}) copy-start(bf16[128,16]{1,0:T(8,128)(2,1)} %constant.31.clone.px3l) | copy-start | bytes 12292
  20.9 5.5 %copy-start.9 = (bf16[128,16]{1,0:T(8,128)(2,1)S(1)}, bf16[128,16]{1,0:T(8,128)(2,1)}, u32[]{:S(2)}) copy-start(bf16[128,16]{1,0:T(8,128)(2,1)} %constant.30.clone.px3) | copy-start | bytes 12292
  20.9 5.5 %copy-start.10 = (bf16[128,32]{1,0:T(8,128)(2,1)S(1)}, bf16[128,32]{1,0:T(8,128)(2,1)}, u32[]{:S(2)}) copy-start(bf16[128,32]{1,0:T(8,128)(2,1)} %constant.29.clone.px2) | copy-start | bytes 24580
  20.9 5.5 %copy-start.11 = (bf16[128,64]{1,0:T(8,128)(2,1)S(1)}, bf16[128,64]{1,0:T(8,128)(2,1)}, u32[]{:S(2)}) copy-start(bf16[128,64]{1,0:T(8,128)(2,1)} %constant.28.clone.px1) | copy-start | bytes 49156
  20.9 5.5 %copy-start.12 = (bf16[64,128]{1,0:T(8,128)(2,1)S(1)}, bf16[64,128]{1,0:T(8,128)(2,1)}, u32[]{:S(2)}) copy-start(bf16[64,128]{1,0:T(8,128)(2,1)} %constant.34.clone.py3l) | copy-start | bytes 49156
  20.9 5.5 %copy-start.13 = (bf16[64,128]{1,0:T(8,128)(2,1)S(1)}, bf16[64,128]{1,0:T(8,128)(2,1)}, u32[]{:S(2)}) copy-start(bf16[64,128]{1,0:T(8,128)(2,1)} %constant.33.clone.py3) | copy-start | bytes 49156
  20.9 5.5 %copy-start.16 = (bf16[16,8]{1,0:T(8,128)(2,1)S(1)}, bf16[16,8]{1,0:T(8,128)(2,1)}, u32[]{:S(2)}) copy-start(bf16[16,8]{1,0:T(8,128)(2,1)} %constant.36.clone.pz3) | copy-start | bytes 772
  20.9 5.5 %copy-start.17 = (bf16[16,16]{1,0:T(8,128)(2,1)S(1)}, bf16[16,16]{1,0:T(8,128)(2,1)}, u32[]{:S(2)}) copy-start(bf16[16,16]{1,0:T(8,128)(2,1)} %constant.35.clone.pz2) | copy-start | bytes 1540
  22.7 4.4 %collective-permute-start.7 = (f32[32,128]{1,0:T(8,128)S(1)}, f32[32,128]{1,0:T(8,128)S(1)}, u32[]{:S(2)}, u32[]{:S(2)}) collective-permute-start(f32[32,128]{1,0:T(8,128)S(1)} %get-tuple-element.32._.refs_0_), channel_id=1, source_target_pairs={{8,0},{12,4},{0,8},{4,12},{9,1},{13,5},{1,9},{5,13},{10,2},{14,6},... | collective-permute-start | bytes 49160 | tf_op jit(solution)/shard_map/ppermute | solution.py:650
  24.3 4.5 %collective-permute-start.6 = (f32[176,128]{1,0:T(8,128)S(1)}, f32[176,128]{1,0:T(8,128)S(1)}, u32[]{:S(2)}, u32[]{:S(2)}) collective-permute-start(f32[176,128]{1,0:T(8,128)S(1)} %get-tuple-element.36), channel_id=1, source_target_pairs={{4,0},{8,4},{12,8},{0,12},{5,1},{9,5},{13,9},{1,13},{6,2},{10,6},{... | collective-permute-start | bytes 270344 | tf_op jit(solution)/shard_map/ppermute | solution.py:650
  24.8 5.4 %collective-permute-start.8 = (f32[176,128]{1,0:T(8,128)S(1)}, f32[176,128]{1,0:T(8,128)S(1)}, u32[]{:S(2)}, u32[]{:S(2)}) collective-permute-start(f32[176,128]{1,0:T(8,128)S(1)} %get-tuple-element.37), channel_id=1, source_target_pairs={{12,0},{0,4},{4,8},{8,12},{13,1},{1,5},{5,9},{9,13},{14,2},{2,6},{... | collective-permute-start | bytes 270344 | tf_op jit(solution)/shard_map/ppermute | solution.py:650
  33.6 1.7 %collective-permute-start.11 = (f32[64,1408]{1,0:T(8,128)S(1)}, f32[64,1408]{1,0:T(8,128)S(1)}, u32[]{:S(2)}, u32[]{:S(2)}) collective-permute-start(f32[64,1408]{1,0:T(8,128)S(1)} %away.1), channel_id=1, source_target_pairs={{16,0},{0,16},{17,1},{1,17},{18,2},{2,18},{19,3},{3,19},{20,4},{4,... | collective-permute-start | bytes 1081352 | tf_op jit(solution)/shard_map/ppermute | solution.py:650

commit v10 on v9

--- a/solution.py
+++ b/solution.py
@@ -378,7 +378,7 @@
 
 
 def near_kernel(s, tap_ref, b_ref, lo_ref, hi_ref, left_ref, right_ref, x0_ref, y0_ref,
-                own_ref, down_ref, up_ref, e_ref, u_ref, eh_ref, el_ref, v_ref):
+                v_ref, down_ref, up_ref, e_ref, u_ref, eh_ref, el_ref):
     group = LANES // R
     tiles = [extended(s, b_ref, lo_ref, hi_ref, z) for z in range(s.nz)]
     tiles += [left_ref[t] for t in range(s.fine_tiles)] + [right_ref[t] for t in range(s.fine_tiles)]
@@ -414,10 +414,14 @@
             for q in range(step // s.nx):
                 v_ref[t, first // s.nx + q] = v[q * s.nx : (q + 1) * s.nx]
 
+    near_depth(s, tap_ref, v_ref, {-R: down_ref, s.nz: up_ref})
+
+
+def near_depth(s, tap_ref, v_ref, out_refs):
     def depth(r, _):
         rows = pl.ds(pl.multiple_of(r * 8, 8), 8)
         taps = [[tap_ref[t, d] for d in range(R + 1)] for t in range(TERMS)]
-        for first in range(-R, s.nz + R, R):
+        for first, ref in out_refs.items():
             acc = [None] * R
             for t in range(TERMS):
                 for z in range(max(0, first - R), min(s.nz, first + 2 * R)):
@@ -428,15 +432,14 @@
                             term = v * taps[t][d]
                             acc[o] = term if acc[o] is None else acc[o] + term
             for o in range(R):
-                if first < 0:
-                    down_ref[o, rows] = acc[o]
-                elif first >= s.nz:
-                    up_ref[o, rows] = acc[o]
-                else:
-                    own_ref[first + o, rows] = acc[o]
+                ref[o, rows] = acc[o]
         return 0
 
     lax.fori_loop(0, s.nx // 8, depth, 0)
+
+
+def own_kernel(s, tap_ref, v_ref, _, own_ref):
+    near_depth(s, tap_ref, v_ref, {z: own_ref.at[z : z + R] for z in range(0, s.nz, R)})
 
 
 def depth_kernel(s, tap_ref, *refs):
@@ -512,7 +515,7 @@
 
 def along_kernel(s, z_ref, w_ref, c2_ref, *refs):
     c3_refs = refs[: s.gy]
-    y1_ref, y2h_ref, y2l_ref, d_ref, y2_ref, y3_ref = refs[s.gy :]
+    y1_ref, y2h_ref, y2l_ref, _, d_ref, y2_ref, y3_ref = refs[s.gy :]
     lane = lanes_of((s.rows1, LANES))
     above, below = c3_refs[1], c3_refs[-1]
     end = s.y1 + R
@@ -676,13 +679,13 @@
     left, right = fetch(last_cells, gy=-1), fetch(first_cells, gy=1)
     tiles = s.nz + 2 * s.fine_tiles
     halved = pltpu.VMEM((TERMS, s.nz * s.nx, 2 * LANES), BF16)
-    near, near_down, near_up = call(
+    crossed, near_down, near_up = call(
         functools.partial(near_kernel, s), "near",
         [taps, charges, low_rows, high_rows, left, right, x0, y0],
-        arrays(brick, side, side), scalars=(0,),
+        arrays((TERMS,) + brick, side, side), scalars=(0,),
         scratch=[
             pltpu.VMEM((3 * s.ext, tiles * LANES), BF16), pltpu.VMEM((TERMS * s.nx, tiles * LANES), F32),
-            halved, halved, pltpu.VMEM((TERMS,) + brick, F32),
+            halved, halved,
         ],
         flops=5 * 10**9,
     )
@@ -692,7 +695,7 @@
         functools.partial(depth_kernel, s), "depth",
         [taps] + shares + [c[k] for k in ("ry2", "rx2", "ry3", "rx3")],
         arrays((TERMS * s.planes, s.rows1, LANES), message, message, (s.cz[2], s.rows2, LANES), (size3, LANES)),
-        scalars=(0,), after=[near], scratch=[pltpu.VMEM((s.cz[1], s.rows1, LANES), F32)], flops=2 * 10**9,
+        scalars=(0,), after=[near_up], scratch=[pltpu.VMEM((s.cz[1], s.rows1, LANES), F32)], flops=2 * 10**9,
     )
     named = ("px1", "px2", "px3", "px3l", "py2", "py3", "py3l", "pz2", "pz3")
     z_taps, y1, y2h, y2l, xh, xl = call(
@@ -703,6 +706,10 @@
         + two(LANES, 2 * TERMS * s.ny) + two(s.cx[0], s.depth_lanes),
         after=[coarse], flops=2 * 10**9,
     )
+    (near,) = call(
+        functools.partial(own_kernel, s), "own", [taps, crossed], arrays(brick),
+        scalars=(0,), after=[z_taps], flops=10**8,
+    )
     coarses = [coarse]
     for b in range(1, s.gy):
         coarses.append(fetch({1: to_low, s.gy - 1: to_high}.get(b, coarse), gy=b))
@@ -710,7 +717,7 @@
     (terms,) = call(
         functools.partial(along_kernel, s), "along",
         [z_taps, waves, level2] + coarses + [y1, y2h, y2l],
-        arrays((s.depth, s.planes * s.ny)), scalars=(0,),
+        arrays((s.depth, s.planes * s.ny)), scalars=(0,), after=[near],
         scratch=[
             pltpu.VMEM((TERMS, s.cz[2], s.rows2, s.ny), F32), pltpu.VMEM((TERMS, s.cz[3], s.rows3, s.ny), F32)
         ], flops=3 * 10**9,

time: 36.4 us -> 40.9 us (1.12)
  waiting for transfers between devices: 4.24 us -> 9.05 us
  starting transfers between devices: 17.9 us -> 17 us
  Pallas kernels: 12.3 us -> 13 us
    ppermute x12, waiting for transfers between devices: 4.24 us -> 9.05 us  [fetch(): return lax.ppermute(x, names if len(names) > 1 else names[0], pairs)]
    ppermute x12, starting transfers between devices: 17.9 us -> 17 us  [fetch(): return lax.ppermute(x, names if len(names) > 1 else names[0], pairs)]
    pallas_call x9 -> x10, Pallas kernels: 12.3 us -> 13 us  [call(): pl.pallas_call(kernel, name=name, out_shape=out_shapes, in_specs=[spec(i)...]
  transfers between devices with their start and end apart: 12 -> 12, of which waited for: 3 -> 3; matrix products, arithmetic and copies ran while one was open for 0% -> 0% of each run, Pallas kernels for 30% -> 28%
where the time goes in v10:
time: 40.9 us; the launch traced here: 40.8 us
  starting transfers between devices  17 us (42%)
  Pallas kernels  13 us (32%)
  waiting for transfers between devices  9.05 us (22%)
  local copies, waits for them, and re-layouts  1.45 us (4%)
    ppermute x12, starting transfers between devices, fetch(): return lax.ppermute(x, names if len(names) > 1 else names[0], pairs)  17 us
    pallas_call x10, Pallas kernels, call(): pl.pallas_call(kernel, name=name, out_shape=out_shapes, in_specs=[spec(i)...  13 us
    ppermute x12, waiting for transfers between devices, fetch(): return lax.ppermute(x, names if len(names) > 1 else names[0], pairs)  9.05 us
    unnamed x36, local copies, waits for them, and re-layouts  1.45 us
  transfers between devices with their start and end apart: 12, of which 3 were waited for; matrix products, arithmetic and copies ran while one was open for 0% of the time, Pallas kernels for 28%

profile of v10, /device:TPU:0, one launch (start us, length us, event | category | flops | bytes accessed | tf_op | source)
XLA Modules:
  0.0 40.8 jit_solution(9125519265557000954)
XLA Ops:
  0.0 0.5 %collective-permute-start = (f32[16,64,128]{2,1,0:T(8,128)}, f32[16,64,128]{2,1,0:T(8,128)S(1)}, u32[]{:S(2)}, u32[]{:S(2)}) collective-permute-start(f32[16,64,128]{2,1,0:T(8,128)} %b_ref.3), channel_id=1, source_target_pairs={{16,0},{0,16},{17,1},{1,17},{18,2},{2,18},{19,3},{3,19},{20,4},{4,... | collective-permute-start | bytes 1572872 | tf_op jit(solution)/shard_map/ppermute | solution.py:653
  0.5 0.7 %copy-done.1 = f32[4,3]{1,0:T(4,128)S(1)} copy-done((f32[4,3]{1,0:T(4,128)S(1)}, f32[4,3]{1,0:T(4,128)}, u32[]{:S(2)}) %copy-start.1) | copy-done | bytes 72
  1.1 0.7 %copy-done.3 = f32[4,3]{1,0:T(4,128)S(1)} copy-done((f32[4,3]{1,0:T(4,128)S(1)}, f32[4,3]{1,0:T(4,128)}, u32[]{:S(2)}) %copy-start.3) | copy-done | bytes 72
  1.8 0.4 taps.1
  2.2 0.0 collective-permute-done.lo_ref.hi_ref
  2.2 0.0 copy-done
  2.2 0.7 %share.1 = (f32[6,32,128]{2,1,0:T(8,128)S(1)}, f32[1,80,128]{2,1,0:T(8,128)S(1)}, f32[1,80,128]{2,1,0:T(8,128)S(1)}) custom-call(f32[16,64,128]{2,1,0:T(8,128)S(1)} %copy-done, f32[16,64,128]{2,1,0:T(8,128)S(1)} %collective-permute-done.lo_ref.hi_ref, f32[16,64,128]{2,1,0:T(8,128)S(1)} %collective-permute-done.lo_ref.hi_ref, ...), custom_call_target="tpu_custom_call" | custom-call | flops 1000000000 | bytes 1845248 | tf_op jit(solution)/shard_map/share/pallas_call | solution.py:630
  2.9 2.9 %collective-permute-start.4 = (f32[1,80,128]{2,1,0:T(8,128)S(1)}, f32[1,80,128]{2,1,0:T(8,128)S(1)}, u32[]{:S(2)}, u32[]{:S(2)}) collective-permute-start(f32[1,80,128]{2,1,0:T(8,128)S(1)} %get-tuple-element.28), channel_id=1, source_target_pairs={{12,0},{0,4},{4,8},{8,12},{13,1},{1,5},{5,9},{9,13},{14,2},{2,6},{... | collective-permute-start | bytes 122888 | tf_op jit(solution)/shard_map/ppermute | solution.py:653
  5.8 1.0 %collective-permute-start.5 = (f32[1,80,128]{2,1,0:T(8,128)S(1)}, f32[1,80,128]{2,1,0:T(8,128)S(1)}, u32[]{:S(2)}, u32[]{:S(2)}) collective-permute-start(f32[1,80,128]{2,1,0:T(8,128)S(1)} %get-tuple-element.29), channel_id=1, source_target_pairs={{4,0},{8,4},{12,8},{0,12},{5,1},{9,5},{13,9},{1,13},{6,2},{10,6},{... | collective-permute-start | bytes 122888 | tf_op jit(solution)/shard_map/ppermute | solution.py:653
  6.8 4.0 %collective-permute-start.1 = (f32[6,32,128]{2,1,0:T(8,128)S(1)}, f32[6,32,128]{2,1,0:T(8,128)S(1)}, u32[]{:S(2)}, u32[]{:S(2)}) collective-permute-start(f32[6,32,128]{2,1,0:T(8,128)S(1)} %get-tuple-element.27.refs_0_), channel_id=1, source_target_pairs={{1,0},{2,1},{3,2},{0,3},{5,4},{6,5},{7,6},{4,7},{9,8},{10,9},{11,1... | collective-permute-start | bytes 294920 | tf_op jit(solution)/shard_map/ppermute | solution.py:653
  10.9 0.0 collective-permute-start.2
  10.9 1.0 %collective-permute-start.3 = (f32[6,32,128]{2,1,0:T(8,128)S(1)}, f32[6,32,128]{2,1,0:T(8,128)S(1)}, u32[]{:S(2)}, u32[]{:S(2)}) collective-permute-start(f32[6,32,128]{2,1,0:T(8,128)S(1)} %get-tuple-element.27.refs_0_), channel_id=1, source_target_pairs={{3,0},{0,1},{1,2},{2,3},{7,4},{4,5},{5,6},{6,7},{11,8},{8,9},{9,10... | collective-permute-start | bytes 294920 | tf_op jit(solution)/shard_map/ppermute | solution.py:653
  11.9 0.0 collective-permute-done.4.left_ref
  11.9 0.0 collective-permute-done.5.right_ref
  11.9 0.0 copy-start.6
  11.9 0.0 copy-start.14
  11.9 0.0 copy-start.15
  11.9 2.7 %near.1 = (f32[3,16,64,128]{3,2,1,0:T(8,128)S(1)}, f32[8,64,128]{2,1,0:T(8,128)S(1)}, f32[8,64,128]{2,1,0:T(8,128)S(1)}) custom-call(f32[8,128]{1,0:T(8,128)S(1)} %get-tuple-element.25.tap_ref, f32[16,64,128]{2,1,0:T(8,128)S(1)} %copy-done, f32[16,64,128]{2,1,0:T(8,128)S(1)} %collective-permute-done.lo_ref.hi_ref, ...), custom_call_target="tpu_custom_call" | custom-call | flops 5000000000 | bytes 4241408 | tf_op jit(solution)/shard_map/near/pallas_call | solution.py:630
  14.6 2.5 %collective-permute-start.9 = (f32[8,64,128]{2,1,0:T(8,128)S(1)}, f32[8,64,128]{2,1,0:T(8,128)S(1)}, u32[]{:S(2)}, u32[]{:S(2)}) collective-permute-start(f32[8,64,128]{2,1,0:T(8,128)S(1)} %get-tuple-element.31.refs_8_), channel_id=1, source_target_pairs={{3,0},{0,1},{1,2},{2,3},{7,4},{4,5},{5,6},{6,7},{11,8},{8,9},{9,10... | collective-permute-start | bytes 786440 | tf_op jit(solution)/shard_map/ppermute | solution.py:653
  17.1 0.0 copy-start.9
  17.2 0.0 copy-start.10
  17.2 0.0 copy-start.11
  17.2 0.0 copy-start.12
  17.2 0.0 copy-start.13
  17.2 0.0 copy-start.16
  17.2 0.0 copy-start.17
  17.2 1.4 %collective-permute-start.10 = (f32[8,64,128]{2,1,0:T(8,128)S(1)}, f32[8,64,128]{2,1,0:T(8,128)S(1)}, u32[]{:S(2)}, u32[]{:S(2)}) collective-permute-start(f32[8,64,128]{2,1,0:T(8,128)S(1)} %get-tuple-element.44), channel_id=1, source_target_pairs={{1,0},{2,1},{3,2},{0,3},{5,4},{6,5},{7,6},{4,7},{9,8},{10,9},{11,1... | collective-permute-start | bytes 786440 | tf_op jit(solution)/shard_map/ppermute | solution.py:653
  18.6 0.0 collective-permute-done.1.refs_1_
  18.6 6.9 %collective-permute-done.2.refs_2_ = f32[6,32,128]{2,1,0:T(8,128)S(1)} collective-permute-done((f32[6,32,128]{2,1,0:T(8,128)S(1)}, f32[6,32,128]{2,1,0:T(8,128)S(1)}, u32[]{:S(2)}, u32[]{:S(2)}) %collective-permute-start.2) | collective-permute-done | bytes 98336 | tf_op jit(solution)/shard_map/ppermute | solution.py:653
  25.5 0.0 collective-permute-done.3.refs_3_
  25.5 0.0 copy-done.5
  25.5 1.7 %depth.1 = (f32[33,32,128]{2,1,0:T(8,128)S(1)}, f32[176,128]{1,0:T(8,128)S(1)}, f32[176,128]{1,0:T(8,128)S(1)}, f32[16,24,128]{2,1,0:T(8,128)S(1)}, f32[32,128]{1,0:T(8,128)S(1)}) custom-call(f32[8,128]{1,0:T(8,128)S(1)} %get-tuple-element.25.tap_ref, f32[6,32,128]{2,1,0:T(8,128)S(1)} %get-tuple-element.27.refs_0_, ...), custom_call_target="tpu_custom_call" | custom-call | flops 2000000000 | bytes 1729024 | tf_op jit(solution)/shard_map/depth/pallas_call | solution.py:630
  27.3 1.6 %collective-permute-start.7 = (f32[32,128]{1,0:T(8,128)S(1)}, f32[32,128]{1,0:T(8,128)S(1)}, u32[]{:S(2)}, u32[]{:S(2)}) collective-permute-start(f32[32,128]{1,0:T(8,128)S(1)} %get-tuple-element.32._.refs_0_), channel_id=1, source_target_pairs={{8,0},{12,4},{0,8},{4,12},{9,1},{13,5},{1,9},{5,13},{10,2},{14,6},... | collective-permute-start | bytes 49160 | tf_op jit(solution)/shard_map/ppermute | solution.py:653
  28.9 0.5 %collective-permute-start.6 = (f32[176,128]{1,0:T(8,128)S(1)}, f32[176,128]{1,0:T(8,128)S(1)}, u32[]{:S(2)}, u32[]{:S(2)}) collective-permute-start(f32[176,128]{1,0:T(8,128)S(1)} %get-tuple-element.36), channel_id=1, source_target_pairs={{4,0},{8,4},{12,8},{0,12},{5,1},{9,5},{13,9},{1,13},{6,2},{10,6},{... | collective-permute-start | bytes 270344 | tf_op jit(solution)/shard_map/ppermute | solution.py:653
  29.4 1.5 %collective-permute-start.8 = (f32[176,128]{1,0:T(8,128)S(1)}, f32[176,128]{1,0:T(8,128)S(1)}, u32[]{:S(2)}, u32[]{:S(2)}) collective-permute-start(f32[176,128]{1,0:T(8,128)S(1)} %get-tuple-element.37), channel_id=1, source_target_pairs={{12,0},{0,4},{4,8},{8,12},{13,1},{1,5},{5,9},{9,13},{14,2},{2,6},{... | collective-permute-start | bytes 270344 | tf_op jit(solution)/shard_map/ppermute | solution.py:653
  31.0 0.7 %matrices.1 = (f32[96,128]{1,0:T(8,128)S(1)}, bf16[128,768]{1,0:T(8,128)(2,1)S(1)}, bf16[128,768]{1,0:T(8,128)(2,1)S(1)}, bf16[128,768]{1,0:T(8,128)(2,1)S(1)}, ...) custom-call(f32[4,3]{1,0:T(4,128)S(1)} %copy-done.2, f32[4,3]{1,0:T(4,128)S(1)} %copy-done.4, ...), custom_call_target="tpu_custom_call" | custom-call | flops 2000000000 | bytes 885600 | tf_op jit(solution)/shard_map/matrices/pallas_call | solution.py:630
  31.7 2.0 %own.1.refs_7_.own_ref = f32[16,64,128]{2,1,0:T(8,128)S(1)} custom-call(f32[8,128]{1,0:T(8,128)S(1)} %get-tuple-element.25.tap_ref, f32[3,16,64,128]{3,2,1,0:T(8,128)S(1)} %get-tuple-element.41.v_ref, f32[96,128]{1,0:T(8,128)S(1)} %get-tuple-element.33._.z_ref), custom_call_target="tpu_custom_call" | custom-call | flops 100000000 | bytes 2150400 | tf_op jit(solution)/shard_map/own/pallas_call | solution.py:630
  33.7 0.0 collective-permute-done.7.refs_2_
  33.8 0.0 collective-permute-done.6.refs_1_
  33.8 1.1 %collective-permute-done.8.refs_3_ = f32[176,128]{1,0:T(8,128)S(1)} collective-permute-done((f32[176,128]{1,0:T(8,128)S(1)}, f32[176,128]{1,0:T(8,128)S(1)}, u32[]{:S(2)}, u32[]{:S(2)}) %collective-permute-start.8) | collective-permute-done | bytes 90144 | tf_op jit(solution)/shard_map/ppermute | solution.py:653
  34.8 2.8 %along.1.d_ref = f32[216,1408]{1,0:T(8,128)S(1)} custom-call(f32[96,128]{1,0:T(8,128)S(1)} %get-tuple-element.33._.z_ref, f32[33,32,128]{2,1,0:T(8,128)S(1)} %get-tuple-element.34.w_ref, f32[16,24,128]{2,1,0:T(8,128)S(1)} %get-tuple-element.35.c2_ref, f32[32,128]{1,0:T(8,128)S(1)} %get-tuple-element.32._.refs_0_, ...), custom_call_target="tpu_custom_call" | custom-call | flops 3000000000 | bytes 3330048 | tf_op jit(solution)/shard_map/along/pallas_call | solution.py:630
  37.6 0.5 %away.1 = f32[64,1408]{1,0:T(8,128)S(1)} custom-call(f32[216,1408]{1,0:T(8,128)S(1)} %along.1.d_ref, bf16[128,256]{1,0:T(8,128)(2,1)S(1)} %get-tuple-element.42.xh_ref, bf16[128,256]{1,0:T(8,128)(2,1)S(1)} %get-tuple-element.43.xl_ref), custom_call_target="tpu_custom_call" | custom-call | flops 1000000000 | bytes 1708032 | tf_op jit(solution)/shard_map/away/pallas_call | solution.py:630
  38.2 0.1 collective-permute-start.11
  38.2 0.0 collective-permute-done.9.low_ref
  38.2 0.0 collective-permute-done.10.high_ref
  38.3 0.5 %home.1.home_ref = f32[16,64,128]{2,1,0:T(8,128)S(1)} custom-call(f32[216,1408]{1,0:T(8,128)S(1)} %along.1.d_ref, bf16[128,256]{1,0:T(8,128)(2,1)S(1)} %get-tuple-element.42.xh_ref, bf16[128,256]{1,0:T(8,128)(2,1)S(1)} %get-tuple-element.43.xl_ref, f32[16,64,128]{2,1,0:T(8,128)S(1)} %own.1.refs_7_.own_ref, f32[8,64,128]{2,1,0:T(8,128)S(1)} %collective-permute-done.9.low_ref, ...), custom_call_target="tpu_custom_call" | custom-call | flops 2000000000 | bytes 2920448 | tf_op jit(solution)/shard_map/home/pallas_call | solution.py:630
  38.8 1.1 %collective-permute-done.11.refs_0_ = f32[64,1408]{1,0:T(8,128)S(1)} collective-permute-done((f32[64,1408]{1,0:T(8,128)S(1)}, f32[64,1408]{1,0:T(8,128)S(1)}, u32[]{:S(2)}, u32[]{:S(2)}) %collective-permute-start.11) | collective-permute-done | bytes 360480 | tf_op jit(solution)/shard_map/ppermute | solution.py:653
  39.9 0.9 %last.1 = f32[16,64,128]{2,1,0:T(8,128)} custom-call(f32[16,64,128]{2,1,0:T(8,128)S(1)} %home.1.home_ref, f32[64,1408]{1,0:T(8,128)S(1)} %collective-permute-done.11.refs_0_), custom_call_target="tpu_custom_call" | custom-call | flops 1000000000 | bytes 1409024 | tf_op jit(solution)/shard_map/last/pallas_call | solution.py:630
  (22 shorter events, 0.0 us)
Async XLA Ops:
  0.0 2.2 %copy-start = (f32[16,64,128]{2,1,0:T(8,128)S(1)}, f32[16,64,128]{2,1,0:T(8,128)}, u32[]{:S(2)}) copy-start(f32[16,64,128]{2,1,0:T(8,128)} %b_ref.3) | copy-start | bytes 1572868
  0.0 2.2 %collective-permute-start = (f32[16,64,128]{2,1,0:T(8,128)}, f32[16,64,128]{2,1,0:T(8,128)S(1)}, u32[]{:S(2)}, u32[]{:S(2)}) collective-permute-start(f32[16,64,128]{2,1,0:T(8,128)} %b_ref.3), channel_id=1, source_target_pairs={{16,0},{0,16},{17,1},{1,17},{18,2},{2,18},{19,3},{3,19},{20,4},{4,... | collective-permute-start | bytes 1572872 | tf_op jit(solution)/shard_map/ppermute | solution.py:653
  0.5 0.7 %copy-start.1 = (f32[4,3]{1,0:T(4,128)S(1)}, f32[4,3]{1,0:T(4,128)}, u32[]{:S(2)}) copy-start(f32[4,3]{1,0:T(4,128)} %w_ref.3) | copy-start | bytes 148
  1.1 0.7 %copy-start.3 = (f32[4,3]{1,0:T(4,128)S(1)}, f32[4,3]{1,0:T(4,128)}, u32[]{:S(2)}) copy-start(f32[4,3]{1,0:T(4,128)} %a_ref.3) | copy-start | bytes 148
  2.9 9.0 %collective-permute-start.4 = (f32[1,80,128]{2,1,0:T(8,128)S(1)}, f32[1,80,128]{2,1,0:T(8,128)S(1)}, u32[]{:S(2)}, u32[]{:S(2)}) collective-permute-start(f32[1,80,128]{2,1,0:T(8,128)S(1)} %get-tuple-element.28), channel_id=1, source_target_pairs={{12,0},{0,4},{4,8},{8,12},{13,1},{1,5},{5,9},{9,13},{14,2},{2,6},{... | collective-permute-start | bytes 122888 | tf_op jit(solution)/shard_map/ppermute | solution.py:653
  5.8 6.1 %collective-permute-start.5 = (f32[1,80,128]{2,1,0:T(8,128)S(1)}, f32[1,80,128]{2,1,0:T(8,128)S(1)}, u32[]{:S(2)}, u32[]{:S(2)}) collective-permute-start(f32[1,80,128]{2,1,0:T(8,128)S(1)} %get-tuple-element.29), channel_id=1, source_target_pairs={{4,0},{8,4},{12,8},{0,12},{5,1},{9,5},{13,9},{1,13},{6,2},{10,6},{... | collective-permute-start | bytes 122888 | tf_op jit(solution)/shard_map/ppermute | solution.py:653
  6.8 11.8 %collective-permute-start.1 = (f32[6,32,128]{2,1,0:T(8,128)S(1)}, f32[6,32,128]{2,1,0:T(8,128)S(1)}, u32[]{:S(2)}, u32[]{:S(2)}) collective-permute-start(f32[6,32,128]{2,1,0:T(8,128)S(1)} %get-tuple-element.27.refs_0_), channel_id=1, source_target_pairs={{1,0},{2,1},{3,2},{0,3},{5,4},{6,5},{7,6},{4,7},{9,8},{10,9},{11,1... | collective-permute-start | bytes 294920 | tf_op jit(solution)/shard_map/ppermute | solution.py:653
  10.9 14.6 %collective-permute-start.2 = (f32[6,32,128]{2,1,0:T(8,128)S(1)}, f32[6,32,128]{2,1,0:T(8,128)S(1)}, u32[]{:S(2)}, u32[]{:S(2)}) collective-permute-start(f32[6,32,128]{2,1,0:T(8,128)S(1)} %get-tuple-element.27.refs_0_), channel_id=1, source_target_pairs={{2,0},{3,1},{0,2},{1,3},{6,4},{7,5},{4,6},{5,7},{10,8},{11,9},{8,1... | collective-permute-start | bytes 294920 | tf_op jit(solution)/shard_map/ppermute | solution.py:653
  10.9 14.6 %collective-permute-start.3 = (f32[6,32,128]{2,1,0:T(8,128)S(1)}, f32[6,32,128]{2,1,0:T(8,128)S(1)}, u32[]{:S(2)}, u32[]{:S(2)}) collective-permute-start(f32[6,32,128]{2,1,0:T(8,128)S(1)} %get-tuple-element.27.refs_0_), channel_id=1, source_target_pairs={{3,0},{0,1},{1,2},{2,3},{7,4},{4,5},{5,6},{6,7},{11,8},{8,9},{9,10... | collective-permute-start | bytes 294920 | tf_op jit(solution)/shard_map/ppermute | solution.py:653
  11.9 13.6 %copy-start.5 = (f32[128,128]{1,0:T(8,128)S(1)}, f32[128,128]{1,0:T(8,128)}, u32[]{:S(2)}) copy-start(f32[128,128]{1,0:T(8,128)} %constant.26.clone.refs_4_) | copy-start | bytes 196612
  11.9 13.6 %copy-start.6 = (f32[128,128]{1,0:T(8,128)S(1)}, f32[128,128]{1,0:T(8,128)}, u32[]{:S(2)}) copy-start(f32[128,128]{1,0:T(8,128)} %constant.37.clone.refs_6_) | copy-start | bytes 196612
  11.9 13.6 %copy-start.14 = (f32[24,32]{1,0:T(8,128)S(1)}, f32[24,32]{1,0:T(8,128)}, u32[]{:S(2)}) copy-start(f32[24,32]{1,0:T(8,128)} %constant.27.clone.refs_5_) | copy-start | bytes 9220
  11.9 13.6 %copy-start.15 = (f32[16,24]{1,0:T(8,128)S(1)}, f32[16,24]{1,0:T(8,128)}, u32[]{:S(2)}) copy-start(f32[16,24]{1,0:T(8,128)} %constant.38.clone.refs_7_) | copy-start | bytes 4612
  14.6 23.6 %collective-permute-start.9 = (f32[8,64,128]{2,1,0:T(8,128)S(1)}, f32[8,64,128]{2,1,0:T(8,128)S(1)}, u32[]{:S(2)}, u32[]{:S(2)}) collective-permute-start(f32[8,64,128]{2,1,0:T(8,128)S(1)} %get-tuple-element.31.refs_8_), channel_id=1, source_target_pairs={{3,0},{0,1},{1,2},{2,3},{7,4},{4,5},{5,6},{6,7},{11,8},{8,9},{9,10... | collective-permute-start | bytes 786440 | tf_op jit(solution)/shard_map/ppermute | solution.py:653
  17.1 13.8 %copy-start.2 = (f32[4,3]{1,0:T(4,128)S(1)}, f32[4,3]{1,0:T(4,128)}, u32[]{:S(2)}) copy-start(f32[4,3]{1,0:T(4,128)} %w_ref.3) | copy-start | bytes 148
  17.1 13.8 %copy-start.4 = (f32[4,3]{1,0:T(4,128)S(1)}, f32[4,3]{1,0:T(4,128)}, u32[]{:S(2)}) copy-start(f32[4,3]{1,0:T(4,128)} %a_ref.3) | copy-start | bytes 148
  17.1 13.8 %copy-start.7 = (bf16[128,64]{1,0:T(8,128)(2,1)S(1)}, bf16[128,64]{1,0:T(8,128)(2,1)}, u32[]{:S(2)}) copy-start(bf16[128,64]{1,0:T(8,128)(2,1)} %constant.28.clone.px1) | copy-start | bytes 49156
  17.1 13.8 %copy-start.8 = (bf16[128,32]{1,0:T(8,128)(2,1)S(1)}, bf16[128,32]{1,0:T(8,128)(2,1)}, u32[]{:S(2)}) copy-start(bf16[128,32]{1,0:T(8,128)(2,1)} %constant.29.clone.px2) | copy-start | bytes 24580
  17.1 13.8 %copy-start.9 = (bf16[128,16]{1,0:T(8,128)(2,1)S(1)}, bf16[128,16]{1,0:T(8,128)(2,1)}, u32[]{:S(2)}) copy-start(bf16[128,16]{1,0:T(8,128)(2,1)} %constant.30.clone.px3) | copy-start | bytes 12292
  17.2 13.8 %copy-start.10 = (bf16[128,16]{1,0:T(8,128)(2,1)S(1)}, bf16[128,16]{1,0:T(8,128)(2,1)}, u32[]{:S(2)}) copy-start(bf16[128,16]{1,0:T(8,128)(2,1)} %constant.31.clone.px3l) | copy-start | bytes 12292
  17.2 13.7 %copy-start.11 = (bf16[128,128]{1,0:T(8,128)(2,1)S(1)}, bf16[128,128]{1,0:T(8,128)(2,1)}, u32[]{:S(2)}) copy-start(bf16[128,128]{1,0:T(8,128)(2,1)} %constant.32.clone.py2) | copy-start | bytes 98308
  17.2 13.7 %copy-start.12 = (bf16[64,128]{1,0:T(8,128)(2,1)S(1)}, bf16[64,128]{1,0:T(8,128)(2,1)}, u32[]{:S(2)}) copy-start(bf16[64,128]{1,0:T(8,128)(2,1)} %constant.33.clone.py3) | copy-start | bytes 49156
  17.2 13.7 %copy-start.13 = (bf16[64,128]{1,0:T(8,128)(2,1)S(1)}, bf16[64,128]{1,0:T(8,128)(2,1)}, u32[]{:S(2)}) copy-start(bf16[64,128]{1,0:T(8,128)(2,1)} %constant.34.clone.py3l) | copy-start | bytes 49156
  17.2 13.7 %copy-start.16 = (bf16[16,16]{1,0:T(8,128)(2,1)S(1)}, bf16[16,16]{1,0:T(8,128)(2,1)}, u32[]{:S(2)}) copy-start(bf16[16,16]{1,0:T(8,128)(2,1)} %constant.35.clone.pz2) | copy-start | bytes 1540
  17.2 13.7 %copy-start.17 = (bf16[16,8]{1,0:T(8,128)(2,1)S(1)}, bf16[16,8]{1,0:T(8,128)(2,1)}, u32[]{:S(2)}) copy-start(bf16[16,8]{1,0:T(8,128)(2,1)} %constant.36.clone.pz3) | copy-start | bytes 772
  17.2 21.0 %collective-permute-start.10 = (f32[8,64,128]{2,1,0:T(8,128)S(1)}, f32[8,64,128]{2,1,0:T(8,128)S(1)}, u32[]{:S(2)}, u32[]{:S(2)}) collective-permute-start(f32[8,64,128]{2,1,0:T(8,128)S(1)} %get-tuple-element.44), channel_id=1, source_target_pairs={{1,0},{2,1},{3,2},{0,3},{5,4},{6,5},{7,6},{4,7},{9,8},{10,9},{11,1... | collective-permute-start | bytes 786440 | tf_op jit(solution)/shard_map/ppermute | solution.py:653
  27.3 6.5 %collective-permute-start.7 = (f32[32,128]{1,0:T(8,128)S(1)}, f32[32,128]{1,0:T(8,128)S(1)}, u32[]{:S(2)}, u32[]{:S(2)}) collective-permute-start(f32[32,128]{1,0:T(8,128)S(1)} %get-tuple-element.32._.refs_0_), channel_id=1, source_target_pairs={{8,0},{12,4},{0,8},{4,12},{9,1},{13,5},{1,9},{5,13},{10,2},{14,6},... | collective-permute-start | bytes 49160 | tf_op jit(solution)/shard_map/ppermute | solution.py:653
  28.9 4.9 %collective-permute-start.6 = (f32[176,128]{1,0:T(8,128)S(1)}, f32[176,128]{1,0:T(8,128)S(1)}, u32[]{:S(2)}, u32[]{:S(2)}) collective-permute-start(f32[176,128]{1,0:T(8,128)S(1)} %get-tuple-element.36), channel_id=1, source_target_pairs={{4,0},{8,4},{12,8},{0,12},{5,1},{9,5},{13,9},{1,13},{6,2},{10,6},{... | collective-permute-start | bytes 270344 | tf_op jit(solution)/shard_map/ppermute | solution.py:653
  29.4 5.4 %collective-permute-start.8 = (f32[176,128]{1,0:T(8,128)S(1)}, f32[176,128]{1,0:T(8,128)S(1)}, u32[]{:S(2)}, u32[]{:S(2)}) collective-permute-start(f32[176,128]{1,0:T(8,128)S(1)} %get-tuple-element.37), channel_id=1, source_target_pairs={{12,0},{0,4},{4,8},{8,12},{13,1},{1,5},{5,9},{9,13},{14,2},{2,6},{... | collective-permute-start | bytes 270344 | tf_op jit(solution)/shard_map/ppermute | solution.py:653
  38.2 1.7 %collective-permute-start.11 = (f32[64,1408]{1,0:T(8,128)S(1)}, f32[64,1408]{1,0:T(8,128)S(1)}, u32[]{:S(2)}, u32[]{:S(2)}) collective-permute-start(f32[64,1408]{1,0:T(8,128)S(1)} %away.1), channel_id=1, source_target_pairs={{16,0},{0,16},{17,1},{1,17},{18,2},{2,18},{19,3},{3,19},{20,4},{4,... | collective-permute-start | bytes 1081352 | tf_op jit(solution)/shard_map/ppermute | solution.py:653

commit v11 on v10

--- a/solution.py
+++ b/solution.py
@@ -436,6 +436,10 @@
         return 0
 
     lax.fori_loop(0, s.nx // 8, depth, 0)
+
+
+def gate_kernel(*refs):
+    pass
 
 
 def own_kernel(s, tap_ref, v_ref, _, own_ref):
@@ -617,11 +621,14 @@
         out_ref[z] = home_ref[z] + prolonged(s, level, z)
 
 
-def call(kernel, name, operands, out_shapes, scalars=(), after=(), scratch=(), flops=0):
-    operands = list(operands) + list(after)
+def call(kernel, name, operands, out_shapes, scalars=(), after=(), through=(), scratch=(), flops=0):
+    read, given = len(operands), len(out_shapes)
+    operands = list(operands) + list(after) + list(through)
+    first = len(operands) - len(through)
+    out_shapes = list(out_shapes) + [jax.ShapeDtypeStruct(x.shape, x.dtype) for x in through]
 
     def spec(i):
-        if i >= len(operands) - len(after):
+        if i >= read:
             return pl.BlockSpec(memory_space=pl.ANY)
         return pl.BlockSpec(memory_space=pltpu.SMEM if i in scalars else pltpu.VMEM)
 
@@ -632,7 +639,9 @@
         name=name,
         out_shape=out_shapes,
         in_specs=[spec(i) for i in range(len(operands))],
-        out_specs=[pl.BlockSpec(memory_space=pltpu.VMEM)] * len(out_shapes),
+        out_specs=[pl.BlockSpec(memory_space=pltpu.VMEM)] * given
+        + [pl.BlockSpec(memory_space=pl.ANY)] * len(through),
+        input_output_aliases={first + i: given + i for i in range(len(through))},
         scratch_shapes=list(scratch),
         compiler_params=pltpu.CompilerParams(vmem_limit_bytes=VMEM_LIMIT),
         cost_estimate=pl.CostEstimate(flops=flops, bytes_accessed=moved, transcendentals=0),
@@ -689,6 +698,9 @@
         ],
         flops=5 * 10**9,
     )
+    near_down, near_up = call(
+        gate_kernel, "gate", [], [], after=shares[1:], through=[near_down, near_up], flops=10**6,
+    )
     size3 = s.tiles3 * s.rows3
     message = (s.base3 + size3, LANES)
     waves, to_low, to_high, level2, coarse = call(

time: 40.9 us -> 37.6 us (0.919)
  waiting for transfers between devices: 9.05 us -> 5.73 us
    ppermute x12, waiting for transfers between devices: 9.05 us -> 5.73 us  [fetch(): return lax.ppermute(x, names if len(names) > 1 else names[0], pairs)]
    pallas_call x10 -> x11, Pallas kernels: 13 us -> 13 us  [call(): pl.pallas_call(kernel, name=name, out_shape=out_shapes, in_specs=[spec(i)...]
  transfers between devices with their start and end apart: 12 -> 12, of which waited for: 3 -> 2; matrix products, arithmetic and copies ran while one was open for 0% -> 0% of each run, Pallas kernels for 28% -> 31%
where the time goes in v11:
time: 37.6 us; the launch traced here: 37.4 us
  starting transfers between devices  17 us (45%)
  Pallas kernels  13 us (35%)
  waiting for transfers between devices  5.73 us (15%)
  local copies, waits for them, and re-layouts  1.46 us (4%)
    ppermute x12, starting transfers between devices, fetch(): return lax.ppermute(x, names if len(names) > 1 else names[0], pairs)  17 us
    pallas_call x11, Pallas kernels, call(): pl.pallas_call(kernel, name=name, out_shape=out_shapes, in_specs=[spec(i)...  13 us
    ppermute x12, waiting for transfers between devices, fetch(): return lax.ppermute(x, names if len(names) > 1 else names[0], pairs)  5.73 us
    unnamed x36, local copies, waits for them, and re-layouts  1.46 us
  transfers between devices with their start and end apart: 12, of which 2 were waited for; matrix products, arithmetic and copies ran while one was open for 0% of the time, Pallas kernels for 31%

profile of v11, /device:TPU:0, one launch (start us, length us, event | category | flops | bytes accessed | tf_op | source)
XLA Modules:
  0.0 37.4 jit_solution(11979761341960506602)
XLA Ops:
  0.0 0.5 %collective-permute-start = (f32[16,64,128]{2,1,0:T(8,128)}, f32[16,64,128]{2,1,0:T(8,128)S(1)}, u32[]{:S(2)}, u32[]{:S(2)}) collective-permute-start(f32[16,64,128]{2,1,0:T(8,128)} %b_ref.3), channel_id=1, source_target_pairs={{16,0},{0,16},{17,1},{1,17},{18,2},{2,18},{19,3},{3,19},{20,4},{4,... | collective-permute-start | bytes 1572872 | tf_op jit(solution)/shard_map/ppermute | solution.py:662
  0.5 0.7 %copy-done.1 = f32[4,3]{1,0:T(4,128)S(1)} copy-done((f32[4,3]{1,0:T(4,128)S(1)}, f32[4,3]{1,0:T(4,128)}, u32[]{:S(2)}) %copy-start.1) | copy-done | bytes 72
  1.1 0.7 %copy-done.3 = f32[4,3]{1,0:T(4,128)S(1)} copy-done((f32[4,3]{1,0:T(4,128)S(1)}, f32[4,3]{1,0:T(4,128)}, u32[]{:S(2)}) %copy-start.3) | copy-done | bytes 72
  1.8 0.4 taps.1
  2.2 0.0 collective-permute-done.lo_ref.hi_ref
  2.2 0.7 %share.1 = (f32[6,32,128]{2,1,0:T(8,128)S(1)}, f32[1,80,128]{2,1,0:T(8,128)S(1)}, f32[1,80,128]{2,1,0:T(8,128)S(1)}) custom-call(f32[16,64,128]{2,1,0:T(8,128)S(1)} %copy-done, f32[16,64,128]{2,1,0:T(8,128)S(1)} %collective-permute-done.lo_ref.hi_ref, f32[16,64,128]{2,1,0:T(8,128)S(1)} %collective-permute-done.lo_ref.hi_ref, ...), custom_call_target="tpu_custom_call" | custom-call | flops 1000000000 | bytes 1845248 | tf_op jit(solution)/shard_map/share/pallas_call | solution.py:637
  2.9 2.9 %collective-permute-start.4 = (f32[1,80,128]{2,1,0:T(8,128)S(1)}, f32[1,80,128]{2,1,0:T(8,128)S(1)}, u32[]{:S(2)}, u32[]{:S(2)}) collective-permute-start(f32[1,80,128]{2,1,0:T(8,128)S(1)} %get-tuple-element.30), channel_id=1, source_target_pairs={{12,0},{0,4},{4,8},{8,12},{13,1},{1,5},{5,9},{9,13},{14,2},{2,6},{... | collective-permute-start | bytes 122888 | tf_op jit(solution)/shard_map/ppermute | solution.py:662
  5.8 1.0 %collective-permute-start.5 = (f32[1,80,128]{2,1,0:T(8,128)S(1)}, f32[1,80,128]{2,1,0:T(8,128)S(1)}, u32[]{:S(2)}, u32[]{:S(2)}) collective-permute-start(f32[1,80,128]{2,1,0:T(8,128)S(1)} %get-tuple-element.31), channel_id=1, source_target_pairs={{4,0},{8,4},{12,8},{0,12},{5,1},{9,5},{13,9},{1,13},{6,2},{10,6},{... | collective-permute-start | bytes 122888 | tf_op jit(solution)/shard_map/ppermute | solution.py:662
  6.8 4.0 %collective-permute-start.1 = (f32[6,32,128]{2,1,0:T(8,128)S(1)}, f32[6,32,128]{2,1,0:T(8,128)S(1)}, u32[]{:S(2)}, u32[]{:S(2)}) collective-permute-start(f32[6,32,128]{2,1,0:T(8,128)S(1)} %get-tuple-element.29.refs_0_), channel_id=1, source_target_pairs={{1,0},{2,1},{3,2},{0,3},{5,4},{6,5},{7,6},{4,7},{9,8},{10,9},{11,1... | collective-permute-start | bytes 294920 | tf_op jit(solution)/shard_map/ppermute | solution.py:662
  10.9 0.0 collective-permute-start.2
  10.9 1.0 %collective-permute-start.3 = (f32[6,32,128]{2,1,0:T(8,128)S(1)}, f32[6,32,128]{2,1,0:T(8,128)S(1)}, u32[]{:S(2)}, u32[]{:S(2)}) collective-permute-start(f32[6,32,128]{2,1,0:T(8,128)S(1)} %get-tuple-element.29.refs_0_), channel_id=1, source_target_pairs={{3,0},{0,1},{1,2},{2,3},{7,4},{4,5},{5,6},{6,7},{11,8},{8,9},{9,10... | collective-permute-start | bytes 294920 | tf_op jit(solution)/shard_map/ppermute | solution.py:662
  11.9 0.0 collective-permute-done.4.left_ref
  11.9 0.0 collective-permute-done.5.right_ref
  11.9 0.0 copy-start.6
  11.9 0.0 copy-start.14
  11.9 0.0 copy-start.15
  11.9 2.7 %near.1 = (f32[3,16,64,128]{3,2,1,0:T(8,128)S(1)}, f32[8,64,128]{2,1,0:T(8,128)S(1)}, f32[8,64,128]{2,1,0:T(8,128)S(1)}) custom-call(f32[8,128]{1,0:T(8,128)S(1)} %get-tuple-element.27.tap_ref, f32[16,64,128]{2,1,0:T(8,128)S(1)} %copy-done, f32[16,64,128]{2,1,0:T(8,128)S(1)} %collective-permute-done.lo_ref.hi_ref, ...), custom_call_target="tpu_custom_call" | custom-call | flops 5000000000 | bytes 4241408 | tf_op jit(solution)/shard_map/near/pallas_call | solution.py:637
  14.6 0.0 collective-permute-done.1.refs_0_.refs_1_
  14.6 4.6 %collective-permute-done.2.refs_1_.refs_2_ = f32[6,32,128]{2,1,0:T(8,128)S(1)} collective-permute-done((f32[6,32,128]{2,1,0:T(8,128)S(1)}, f32[6,32,128]{2,1,0:T(8,128)S(1)}, u32[]{:S(2)}, u32[]{:S(2)}) %collective-permute-start.2) | collective-permute-done | bytes 98336 | tf_op jit(solution)/shard_map/ppermute | solution.py:662
  19.2 0.0 collective-permute-done.3.refs_2_.refs_3_
  19.2 0.0 copy-start.7
  19.2 0.0 copy-start.8
  19.2 0.0 copy-start.9
  19.3 0.0 copy-start.10
  19.3 0.0 copy-start.11
  19.3 0.0 copy-start.12
  19.3 0.0 copy-start.13
  19.3 0.0 copy-start.16
  19.3 0.0 copy-start.17
  19.3 0.5 %collective-permute-start.9 = (f32[8,64,128]{2,1,0:T(8,128)S(1)}, f32[8,64,128]{2,1,0:T(8,128)S(1)}, u32[]{:S(2)}, u32[]{:S(2)}) collective-permute-start(f32[8,64,128]{2,1,0:T(8,128)S(1)} %get-tuple-element.35.refs_8_), channel_id=1, source_target_pairs={{3,0},{0,1},{1,2},{2,3},{7,4},{4,5},{5,6},{6,7},{11,8},{8,9},{9,10... | collective-permute-start | bytes 786440 | tf_op jit(solution)/shard_map/ppermute | solution.py:662
  19.9 1.7 %depth.1 = (f32[33,32,128]{2,1,0:T(8,128)S(1)}, f32[176,128]{1,0:T(8,128)S(1)}, f32[176,128]{1,0:T(8,128)S(1)}, f32[16,24,128]{2,1,0:T(8,128)S(1)}, f32[32,128]{1,0:T(8,128)S(1)}) custom-call(f32[8,128]{1,0:T(8,128)S(1)} %get-tuple-element.27.tap_ref, f32[6,32,128]{2,1,0:T(8,128)S(1)} %get-tuple-element.29.refs_0_, ...), custom_call_target="tpu_custom_call" | custom-call | flops 2000000000 | bytes 1729024 | tf_op jit(solution)/shard_map/depth/pallas_call | solution.py:637
  21.6 1.6 %collective-permute-start.6 = (f32[176,128]{1,0:T(8,128)S(1)}, f32[176,128]{1,0:T(8,128)S(1)}, u32[]{:S(2)}, u32[]{:S(2)}) collective-permute-start(f32[176,128]{1,0:T(8,128)S(1)} %get-tuple-element.40), channel_id=1, source_target_pairs={{4,0},{8,4},{12,8},{0,12},{5,1},{9,5},{13,9},{1,13},{6,2},{10,6},{... | collective-permute-start | bytes 270344 | tf_op jit(solution)/shard_map/ppermute | solution.py:662
  23.2 0.5 %collective-permute-start.8 = (f32[176,128]{1,0:T(8,128)S(1)}, f32[176,128]{1,0:T(8,128)S(1)}, u32[]{:S(2)}, u32[]{:S(2)}) collective-permute-start(f32[176,128]{1,0:T(8,128)S(1)} %get-tuple-element.41), channel_id=1, source_target_pairs={{12,0},{0,4},{4,8},{8,12},{13,1},{1,5},{5,9},{9,13},{14,2},{2,6},{... | collective-permute-start | bytes 270344 | tf_op jit(solution)/shard_map/ppermute | solution.py:662
  23.7 1.5 %collective-permute-start.7 = (f32[32,128]{1,0:T(8,128)S(1)}, f32[32,128]{1,0:T(8,128)S(1)}, u32[]{:S(2)}, u32[]{:S(2)}) collective-permute-start(f32[32,128]{1,0:T(8,128)S(1)} %get-tuple-element.36._.refs_0_), channel_id=1, source_target_pairs={{8,0},{12,4},{0,8},{4,12},{9,1},{13,5},{1,9},{5,13},{10,2},{14,6},... | collective-permute-start | bytes 49160 | tf_op jit(solution)/shard_map/ppermute | solution.py:662
  25.2 3.3 %collective-permute-start.10 = (f32[8,64,128]{2,1,0:T(8,128)S(1)}, f32[8,64,128]{2,1,0:T(8,128)S(1)}, u32[]{:S(2)}, u32[]{:S(2)}) collective-permute-start(f32[8,64,128]{2,1,0:T(8,128)S(1)} %get-tuple-element.48), channel_id=1, source_target_pairs={{1,0},{2,1},{3,2},{0,3},{5,4},{6,5},{7,6},{4,7},{9,8},{10,9},{11,1... | collective-permute-start | bytes 786440 | tf_op jit(solution)/shard_map/ppermute | solution.py:662
  28.7 0.7 %matrices.1 = (f32[96,128]{1,0:T(8,128)S(1)}, bf16[128,768]{1,0:T(8,128)(2,1)S(1)}, bf16[128,768]{1,0:T(8,128)(2,1)S(1)}, bf16[128,768]{1,0:T(8,128)(2,1)S(1)}, ...) custom-call(f32[4,3]{1,0:T(4,128)S(1)} %copy-done.2, f32[4,3]{1,0:T(4,128)S(1)} %copy-done.4, ...), custom_call_target="tpu_custom_call" | custom-call | flops 2000000000 | bytes 885600 | tf_op jit(solution)/shard_map/matrices/pallas_call | solution.py:637
  29.4 2.0 %own.1.refs_7_.own_ref = f32[16,64,128]{2,1,0:T(8,128)S(1)} custom-call(f32[8,128]{1,0:T(8,128)S(1)} %get-tuple-element.27.tap_ref, f32[3,16,64,128]{3,2,1,0:T(8,128)S(1)} %get-tuple-element.45.v_ref, f32[96,128]{1,0:T(8,128)S(1)} %get-tuple-element.37._.z_ref), custom_call_target="tpu_custom_call" | custom-call | flops 100000000 | bytes 2150400 | tf_op jit(solution)/shard_map/own/pallas_call | solution.py:637
  31.4 0.0 collective-permute-done.7.refs_2_
  31.4 0.0 collective-permute-done.6.refs_1_
  31.4 0.0 collective-permute-done.8.refs_3_
  31.5 2.8 %along.1.d_ref = f32[216,1408]{1,0:T(8,128)S(1)} custom-call(f32[96,128]{1,0:T(8,128)S(1)} %get-tuple-element.37._.z_ref, f32[33,32,128]{2,1,0:T(8,128)S(1)} %get-tuple-element.38.w_ref, f32[16,24,128]{2,1,0:T(8,128)S(1)} %get-tuple-element.39.c2_ref, f32[32,128]{1,0:T(8,128)S(1)} %get-tuple-element.36._.refs_0_, ...), custom_call_target="tpu_custom_call" | custom-call | flops 3000000000 | bytes 3330048 | tf_op jit(solution)/shard_map/along/pallas_call | solution.py:637
  34.3 0.5 %away.1 = f32[64,1408]{1,0:T(8,128)S(1)} custom-call(f32[216,1408]{1,0:T(8,128)S(1)} %along.1.d_ref, bf16[128,256]{1,0:T(8,128)(2,1)S(1)} %get-tuple-element.46.xh_ref, bf16[128,256]{1,0:T(8,128)(2,1)S(1)} %get-tuple-element.47.xl_ref), custom_call_target="tpu_custom_call" | custom-call | flops 1000000000 | bytes 1708032 | tf_op jit(solution)/shard_map/away/pallas_call | solution.py:637
  34.8 0.1 collective-permute-start.11
  34.9 0.0 collective-permute-done.10.high_ref
  34.9 0.0 collective-permute-done.9.low_ref
  34.9 0.5 %home.1.home_ref = f32[16,64,128]{2,1,0:T(8,128)S(1)} custom-call(f32[216,1408]{1,0:T(8,128)S(1)} %along.1.d_ref, bf16[128,256]{1,0:T(8,128)(2,1)S(1)} %get-tuple-element.46.xh_ref, bf16[128,256]{1,0:T(8,128)(2,1)S(1)} %get-tuple-element.47.xl_ref, f32[16,64,128]{2,1,0:T(8,128)S(1)} %own.1.refs_7_.own_ref, f32[8,64,128]{2,1,0:T(8,128)S(1)} %collective-permute-done.9.low_ref, ...), custom_call_target="tpu_custom_call" | custom-call | flops 2000000000 | bytes 2920448 | tf_op jit(solution)/shard_map/home/pallas_call | solution.py:637
  35.5 1.1 %collective-permute-done.11.refs_0_ = f32[64,1408]{1,0:T(8,128)S(1)} collective-permute-done((f32[64,1408]{1,0:T(8,128)S(1)}, f32[64,1408]{1,0:T(8,128)S(1)}, u32[]{:S(2)}, u32[]{:S(2)}) %collective-permute-start.11) | collective-permute-done | bytes 360480 | tf_op jit(solution)/shard_map/ppermute | solution.py:662
  36.5 0.9 %last.1 = f32[16,64,128]{2,1,0:T(8,128)} custom-call(f32[16,64,128]{2,1,0:T(8,128)S(1)} %home.1.home_ref, f32[64,1408]{1,0:T(8,128)S(1)} %collective-permute-done.11.refs_0_), custom_call_target="tpu_custom_call" | custom-call | flops 1000000000 | bytes 1409024 | tf_op jit(solution)/shard_map/last/pallas_call | solution.py:637
  (23 shorter events, 0.0 us)
Async XLA Ops:
  0.0 2.2 %copy-start = (f32[16,64,128]{2,1,0:T(8,128)S(1)}, f32[16,64,128]{2,1,0:T(8,128)}, u32[]{:S(2)}) copy-start(f32[16,64,128]{2,1,0:T(8,128)} %b_ref.3) | copy-start | bytes 1572868
  0.0 2.2 %collective-permute-start = (f32[16,64,128]{2,1,0:T(8,128)}, f32[16,64,128]{2,1,0:T(8,128)S(1)}, u32[]{:S(2)}, u32[]{:S(2)}) collective-permute-start(f32[16,64,128]{2,1,0:T(8,128)} %b_ref.3), channel_id=1, source_target_pairs={{16,0},{0,16},{17,1},{1,17},{18,2},{2,18},{19,3},{3,19},{20,4},{4,... | collective-permute-start | bytes 1572872 | tf_op jit(solution)/shard_map/ppermute | solution.py:662
  0.5 0.7 %copy-start.1 = (f32[4,3]{1,0:T(4,128)S(1)}, f32[4,3]{1,0:T(4,128)}, u32[]{:S(2)}) copy-start(f32[4,3]{1,0:T(4,128)} %w_ref.3) | copy-start | bytes 148
  1.1 0.7 %copy-start.3 = (f32[4,3]{1,0:T(4,128)S(1)}, f32[4,3]{1,0:T(4,128)}, u32[]{:S(2)}) copy-start(f32[4,3]{1,0:T(4,128)} %a_ref.3) | copy-start | bytes 148
  2.9 9.0 %collective-permute-start.4 = (f32[1,80,128]{2,1,0:T(8,128)S(1)}, f32[1,80,128]{2,1,0:T(8,128)S(1)}, u32[]{:S(2)}, u32[]{:S(2)}) collective-permute-start(f32[1,80,128]{2,1,0:T(8,128)S(1)} %get-tuple-element.30), channel_id=1, source_target_pairs={{12,0},{0,4},{4,8},{8,12},{13,1},{1,5},{5,9},{9,13},{14,2},{2,6},{... | collective-permute-start | bytes 122888 | tf_op jit(solution)/shard_map/ppermute | solution.py:662
  5.8 6.1 %collective-permute-start.5 = (f32[1,80,128]{2,1,0:T(8,128)S(1)}, f32[1,80,128]{2,1,0:T(8,128)S(1)}, u32[]{:S(2)}, u32[]{:S(2)}) collective-permute-start(f32[1,80,128]{2,1,0:T(8,128)S(1)} %get-tuple-element.31), channel_id=1, source_target_pairs={{4,0},{8,4},{12,8},{0,12},{5,1},{9,5},{13,9},{1,13},{6,2},{10,6},{... | collective-permute-start | bytes 122888 | tf_op jit(solution)/shard_map/ppermute | solution.py:662
  6.8 7.8 %collective-permute-start.1 = (f32[6,32,128]{2,1,0:T(8,128)S(1)}, f32[6,32,128]{2,1,0:T(8,128)S(1)}, u32[]{:S(2)}, u32[]{:S(2)}) collective-permute-start(f32[6,32,128]{2,1,0:T(8,128)S(1)} %get-tuple-element.29.refs_0_), channel_id=1, source_target_pairs={{1,0},{2,1},{3,2},{0,3},{5,4},{6,5},{7,6},{4,7},{9,8},{10,9},{11,1... | collective-permute-start | bytes 294920 | tf_op jit(solution)/shard_map/ppermute | solution.py:662
  10.9 8.3 %collective-permute-start.2 = (f32[6,32,128]{2,1,0:T(8,128)S(1)}, f32[6,32,128]{2,1,0:T(8,128)S(1)}, u32[]{:S(2)}, u32[]{:S(2)}) collective-permute-start(f32[6,32,128]{2,1,0:T(8,128)S(1)} %get-tuple-element.29.refs_0_), channel_id=1, source_target_pairs={{2,0},{3,1},{0,2},{1,3},{6,4},{7,5},{4,6},{5,7},{10,8},{11,9},{8,1... | collective-permute-start | bytes 294920 | tf_op jit(solution)/shard_map/ppermute | solution.py:662
  10.9 8.3 %collective-permute-start.3 = (f32[6,32,128]{2,1,0:T(8,128)S(1)}, f32[6,32,128]{2,1,0:T(8,128)S(1)}, u32[]{:S(2)}, u32[]{:S(2)}) collective-permute-start(f32[6,32,128]{2,1,0:T(8,128)S(1)} %get-tuple-element.29.refs_0_), channel_id=1, source_target_pairs={{3,0},{0,1},{1,2},{2,3},{7,4},{4,5},{5,6},{6,7},{11,8},{8,9},{9,10... | collective-permute-start | bytes 294920 | tf_op jit(solution)/shard_map/ppermute | solution.py:662
  11.9 8.0 %copy-start.5 = (f32[128,128]{1,0:T(8,128)S(1)}, f32[128,128]{1,0:T(8,128)}, u32[]{:S(2)}) copy-start(f32[128,128]{1,0:T(8,128)} %constant.26.clone.refs_4_) | copy-start | bytes 196612
  11.9 8.0 %copy-start.6 = (f32[128,128]{1,0:T(8,128)S(1)}, f32[128,128]{1,0:T(8,128)}, u32[]{:S(2)}) copy-start(f32[128,128]{1,0:T(8,128)} %constant.37.clone.refs_6_) | copy-start | bytes 196612
  11.9 8.0 %copy-start.14 = (f32[24,32]{1,0:T(8,128)S(1)}, f32[24,32]{1,0:T(8,128)}, u32[]{:S(2)}) copy-start(f32[24,32]{1,0:T(8,128)} %constant.27.clone.refs_5_) | copy-start | bytes 9220
  11.9 8.0 %copy-start.15 = (f32[16,24]{1,0:T(8,128)S(1)}, f32[16,24]{1,0:T(8,128)}, u32[]{:S(2)}) copy-start(f32[16,24]{1,0:T(8,128)} %constant.38.clone.refs_7_) | copy-start | bytes 4612
  19.2 9.4 %copy-start.2 = (f32[4,3]{1,0:T(4,128)S(1)}, f32[4,3]{1,0:T(4,128)}, u32[]{:S(2)}) copy-start(f32[4,3]{1,0:T(4,128)} %w_ref.3) | copy-start | bytes 148
  19.2 9.4 %copy-start.4 = (f32[4,3]{1,0:T(4,128)S(1)}, f32[4,3]{1,0:T(4,128)}, u32[]{:S(2)}) copy-start(f32[4,3]{1,0:T(4,128)} %a_ref.3) | copy-start | bytes 148
  19.2 9.4 %copy-start.7 = (bf16[128,64]{1,0:T(8,128)(2,1)S(1)}, bf16[128,64]{1,0:T(8,128)(2,1)}, u32[]{:S(2)}) copy-start(bf16[128,64]{1,0:T(8,128)(2,1)} %constant.28.clone.px1) | copy-start | bytes 49156
  19.2 9.4 %copy-start.8 = (bf16[128,32]{1,0:T(8,128)(2,1)S(1)}, bf16[128,32]{1,0:T(8,128)(2,1)}, u32[]{:S(2)}) copy-start(bf16[128,32]{1,0:T(8,128)(2,1)} %constant.29.clone.px2) | copy-start | bytes 24580
  19.2 9.3 %copy-start.9 = (bf16[128,16]{1,0:T(8,128)(2,1)S(1)}, bf16[128,16]{1,0:T(8,128)(2,1)}, u32[]{:S(2)}) copy-start(bf16[128,16]{1,0:T(8,128)(2,1)} %constant.30.clone.px3) | copy-start | bytes 12292
  19.3 9.3 %copy-start.10 = (bf16[128,16]{1,0:T(8,128)(2,1)S(1)}, bf16[128,16]{1,0:T(8,128)(2,1)}, u32[]{:S(2)}) copy-start(bf16[128,16]{1,0:T(8,128)(2,1)} %constant.31.clone.px3l) | copy-start | bytes 12292
  19.3 9.3 %copy-start.11 = (bf16[128,128]{1,0:T(8,128)(2,1)S(1)}, bf16[128,128]{1,0:T(8,128)(2,1)}, u32[]{:S(2)}) copy-start(bf16[128,128]{1,0:T(8,128)(2,1)} %constant.32.clone.py2) | copy-start | bytes 98308
  19.3 9.3 %copy-start.12 = (bf16[64,128]{1,0:T(8,128)(2,1)S(1)}, bf16[64,128]{1,0:T(8,128)(2,1)}, u32[]{:S(2)}) copy-start(bf16[64,128]{1,0:T(8,128)(2,1)} %constant.33.clone.py3) | copy-start | bytes 49156
  19.3 9.3 %copy-start.13 = (bf16[64,128]{1,0:T(8,128)(2,1)S(1)}, bf16[64,128]{1,0:T(8,128)(2,1)}, u32[]{:S(2)}) copy-start(bf16[64,128]{1,0:T(8,128)(2,1)} %constant.34.clone.py3l) | copy-start | bytes 49156
  19.3 9.3 %copy-start.16 = (bf16[16,16]{1,0:T(8,128)(2,1)S(1)}, bf16[16,16]{1,0:T(8,128)(2,1)}, u32[]{:S(2)}) copy-start(bf16[16,16]{1,0:T(8,128)(2,1)} %constant.35.clone.pz2) | copy-start | bytes 1540
  19.3 9.3 %copy-start.17 = (bf16[16,8]{1,0:T(8,128)(2,1)S(1)}, bf16[16,8]{1,0:T(8,128)(2,1)}, u32[]{:S(2)}) copy-start(bf16[16,8]{1,0:T(8,128)(2,1)} %constant.36.clone.pz3) | copy-start | bytes 772
  19.3 15.6 %collective-permute-start.9 = (f32[8,64,128]{2,1,0:T(8,128)S(1)}, f32[8,64,128]{2,1,0:T(8,128)S(1)}, u32[]{:S(2)}, u32[]{:S(2)}) collective-permute-start(f32[8,64,128]{2,1,0:T(8,128)S(1)} %get-tuple-element.35.refs_8_), channel_id=1, source_target_pairs={{3,0},{0,1},{1,2},{2,3},{7,4},{4,5},{5,6},{6,7},{11,8},{8,9},{9,10... | collective-permute-start | bytes 786440 | tf_op jit(solution)/shard_map/ppermute | solution.py:662
  21.6 9.8 %collective-permute-start.6 = (f32[176,128]{1,0:T(8,128)S(1)}, f32[176,128]{1,0:T(8,128)S(1)}, u32[]{:S(2)}, u32[]{:S(2)}) collective-permute-start(f32[176,128]{1,0:T(8,128)S(1)} %get-tuple-element.40), channel_id=1, source_target_pairs={{4,0},{8,4},{12,8},{0,12},{5,1},{9,5},{13,9},{1,13},{6,2},{10,6},{... | collective-permute-start | bytes 270344 | tf_op jit(solution)/shard_map/ppermute | solution.py:662
  23.2 8.2 %collective-permute-start.8 = (f32[176,128]{1,0:T(8,128)S(1)}, f32[176,128]{1,0:T(8,128)S(1)}, u32[]{:S(2)}, u32[]{:S(2)}) collective-permute-start(f32[176,128]{1,0:T(8,128)S(1)} %get-tuple-element.41), channel_id=1, source_target_pairs={{12,0},{0,4},{4,8},{8,12},{13,1},{1,5},{5,9},{9,13},{14,2},{2,6},{... | collective-permute-start | bytes 270344 | tf_op jit(solution)/shard_map/ppermute | solution.py:662
  23.7 7.7 %collective-permute-start.7 = (f32[32,128]{1,0:T(8,128)S(1)}, f32[32,128]{1,0:T(8,128)S(1)}, u32[]{:S(2)}, u32[]{:S(2)}) collective-permute-start(f32[32,128]{1,0:T(8,128)S(1)} %get-tuple-element.36._.refs_0_), channel_id=1, source_target_pairs={{8,0},{12,4},{0,8},{4,12},{9,1},{13,5},{1,9},{5,13},{10,2},{14,6},... | collective-permute-start | bytes 49160 | tf_op jit(solution)/shard_map/ppermute | solution.py:662
  25.2 9.7 %collective-permute-start.10 = (f32[8,64,128]{2,1,0:T(8,128)S(1)}, f32[8,64,128]{2,1,0:T(8,128)S(1)}, u32[]{:S(2)}, u32[]{:S(2)}) collective-permute-start(f32[8,64,128]{2,1,0:T(8,128)S(1)} %get-tuple-element.48), channel_id=1, source_target_pairs={{1,0},{2,1},{3,2},{0,3},{5,4},{6,5},{7,6},{4,7},{9,8},{10,9},{11,1... | collective-permute-start | bytes 786440 | tf_op jit(solution)/shard_map/ppermute | solution.py:662
  34.8 1.7 %collective-permute-start.11 = (f32[64,1408]{1,0:T(8,128)S(1)}, f32[64,1408]{1,0:T(8,128)S(1)}, u32[]{:S(2)}, u32[]{:S(2)}) collective-permute-start(f32[64,1408]{1,0:T(8,128)S(1)} %away.1), channel_id=1, source_target_pairs={{16,0},{0,16},{17,1},{1,17},{18,2},{2,18},{19,3},{3,19},{20,4},{4,... | collective-permute-start | bytes 1081352 | tf_op jit(solution)/shard_map/ppermute | solution.py:662

commit v12 on v9

--- a/solution.py
+++ b/solution.py
@@ -602,7 +602,7 @@
 
 
 def last_kernel(s, home_ref, *refs):
-    g_refs, out_ref = refs[:-1], refs[-1]
+    *g_refs, out_ref, sum_ref, sems = refs
     level = []
     for o in range(s.planes):
         columns = slice(o * s.ny, (o + 1) * s.ny)
@@ -610,11 +610,18 @@
         for ref in g_refs[1:]:
             x += ref[:, columns]
         level.append(x)
-    for z in range(s.nz):
-        out_ref[z] = home_ref[z] + prolonged(s, level, z)
-
-
-def call(kernel, name, operands, out_shapes, scalars=(), after=(), scratch=(), flops=0):
+    copies = []
+    for first in range(0, s.nz, 4):
+        for z in range(first, first + 4):
+            sum_ref[z] = home_ref[z] + prolonged(s, level, z)
+        planes = slice(first, first + 4)
+        copies.append(pltpu.make_async_copy(sum_ref.at[planes], out_ref.at[planes], sems.at[first // 4]))
+        copies[-1].start()
+    for copy in copies:
+        copy.wait()
+
+
+def call(kernel, name, operands, out_shapes, scalars=(), after=(), scratch=(), flops=0, out_space=pltpu.VMEM):
     operands = list(operands) + list(after)
 
     def spec(i):
@@ -629,7 +636,7 @@
         name=name,
         out_shape=out_shapes,
         in_specs=[spec(i) for i in range(len(operands))],
-        out_specs=[pl.BlockSpec(memory_space=pltpu.VMEM)] * len(out_shapes),
+        out_specs=[pl.BlockSpec(memory_space=out_space)] * len(out_shapes),
         scratch_shapes=list(scratch),
         compiler_params=pltpu.CompilerParams(vmem_limit_bytes=VMEM_LIMIT),
         cost_estimate=pl.CostEstimate(flops=flops, bytes_accessed=moved, transcendentals=0),
@@ -726,6 +733,7 @@
     )
     (out,) = call(
         functools.partial(last_kernel, s), "last", [home] + parts, arrays(brick), flops=10**9,
+        scratch=[pltpu.VMEM(brick, F32), pltpu.SemaphoreType.DMA((s.nz // 4,))], out_space=pl.ANY,
     )
     return out
 

time: 36.4 us -> 36.4 us (level)
  no operation moved by 1% of the time
where the time goes in v12:
time: 36.4 us; the launch traced here: 36.2 us
  starting transfers between devices  17.9 us (49%)
  Pallas kernels  12.3 us (34%)
  waiting for transfers between devices  4.24 us (12%)
  local copies, waits for them, and re-layouts  1.46 us (4%)
    ppermute x12, starting transfers between devices, fetch(): return lax.ppermute(x, names if len(names) > 1 else names[0], pairs)  17.9 us
    pallas_call x9, Pallas kernels, call(): pl.pallas_call(kernel, name=name, out_shape=out_shapes, in_specs=[spec(i)...  12.3 us
    ppermute x12, waiting for transfers between devices, fetch(): return lax.ppermute(x, names if len(names) > 1 else names[0], pairs)  4.24 us
    unnamed x36, local copies, waits for them, and re-layouts  1.46 us
  transfers between devices with their start and end apart: 12, of which 3 were waited for; matrix products, arithmetic and copies ran while one was open for 0% of the time, Pallas kernels for 30%

profile of v12, /device:TPU:0, one launch (start us, length us, event | category | flops | bytes accessed | tf_op | source)
XLA Modules:
  0.0 36.2 jit_solution(1038545082398172075)
XLA Ops:
  0.0 0.5 %collective-permute-start = (f32[16,64,128]{2,1,0:T(8,128)}, f32[16,64,128]{2,1,0:T(8,128)S(1)}, u32[]{:S(2)}, u32[]{:S(2)}) collective-permute-start(f32[16,64,128]{2,1,0:T(8,128)} %b_ref.3), channel_id=1, source_target_pairs={{16,0},{0,16},{17,1},{1,17},{18,2},{2,18},{19,3},{3,19},{20,4},{4,... | collective-permute-start | bytes 1572872 | tf_op jit(solution)/shard_map/ppermute | solution.py:657
  0.5 0.7 %copy-done.1 = f32[4,3]{1,0:T(4,128)S(1)} copy-done((f32[4,3]{1,0:T(4,128)S(1)}, f32[4,3]{1,0:T(4,128)}, u32[]{:S(2)}) %copy-start.1) | copy-done | bytes 72
  1.1 0.7 %copy-done.3 = f32[4,3]{1,0:T(4,128)S(1)} copy-done((f32[4,3]{1,0:T(4,128)S(1)}, f32[4,3]{1,0:T(4,128)}, u32[]{:S(2)}) %copy-start.3) | copy-done | bytes 72
  1.8 0.4 %taps.1 = (f32[8,128]{1,0:T(8,128)S(1)}, bf16[192,240]{1,0:T(8,128)(2,1)S(1)}, bf16[256,768]{1,0:T(8,128)(2,1)S(1)}) custom-call(f32[4,3]{1,0:T(4,128)S(1)} %copy-done.1, f32[4,3]{1,0:T(4,128)S(1)} %copy-done.3), custom_call_target="tpu_custom_call" | custom-call | flops 600000000 | bytes 489568 | tf_op jit(solution)/shard_map/taps/pallas_call | solution.py:634
  2.2 0.0 collective-permute-done.lo_ref.hi_ref
  2.2 0.7 %share.1 = (f32[6,32,128]{2,1,0:T(8,128)S(1)}, f32[1,80,128]{2,1,0:T(8,128)S(1)}, f32[1,80,128]{2,1,0:T(8,128)S(1)}) custom-call(f32[16,64,128]{2,1,0:T(8,128)S(1)} %copy-done, f32[16,64,128]{2,1,0:T(8,128)S(1)} %collective-permute-done.lo_ref.hi_ref, f32[16,64,128]{2,1,0:T(8,128)S(1)} %collective-permute-done.lo_ref.hi_ref, ...), custom_call_target="tpu_custom_call" | custom-call | flops 1000000000 | bytes 1845248 | tf_op jit(solution)/shard_map/share/pallas_call | solution.py:634
  2.9 2.9 %collective-permute-start.4 = (f32[1,80,128]{2,1,0:T(8,128)S(1)}, f32[1,80,128]{2,1,0:T(8,128)S(1)}, u32[]{:S(2)}, u32[]{:S(2)}) collective-permute-start(f32[1,80,128]{2,1,0:T(8,128)S(1)} %get-tuple-element.28), channel_id=1, source_target_pairs={{12,0},{0,4},{4,8},{8,12},{13,1},{1,5},{5,9},{9,13},{14,2},{2,6},{... | collective-permute-start | bytes 122888 | tf_op jit(solution)/shard_map/ppermute | solution.py:657
  5.8 1.0 %collective-permute-start.5 = (f32[1,80,128]{2,1,0:T(8,128)S(1)}, f32[1,80,128]{2,1,0:T(8,128)S(1)}, u32[]{:S(2)}, u32[]{:S(2)}) collective-permute-start(f32[1,80,128]{2,1,0:T(8,128)S(1)} %get-tuple-element.29), channel_id=1, source_target_pairs={{4,0},{8,4},{12,8},{0,12},{5,1},{9,5},{13,9},{1,13},{6,2},{10,6},{... | collective-permute-start | bytes 122888 | tf_op jit(solution)/shard_map/ppermute | solution.py:657
  6.8 2.0 %collective-permute-start.3 = (f32[6,32,128]{2,1,0:T(8,128)S(1)}, f32[6,32,128]{2,1,0:T(8,128)S(1)}, u32[]{:S(2)}, u32[]{:S(2)}) collective-permute-start(f32[6,32,128]{2,1,0:T(8,128)S(1)} %get-tuple-element.27.refs_0_), channel_id=1, source_target_pairs={{3,0},{0,1},{1,2},{2,3},{7,4},{4,5},{5,6},{6,7},{11,8},{8,9},{9,10... | collective-permute-start | bytes 294920 | tf_op jit(solution)/shard_map/ppermute | solution.py:657
  8.8 2.6 %collective-permute-start.2 = (f32[6,32,128]{2,1,0:T(8,128)S(1)}, f32[6,32,128]{2,1,0:T(8,128)S(1)}, u32[]{:S(2)}, u32[]{:S(2)}) collective-permute-start(f32[6,32,128]{2,1,0:T(8,128)S(1)} %get-tuple-element.27.refs_0_), channel_id=1, source_target_pairs={{2,0},{3,1},{0,2},{1,3},{6,4},{7,5},{4,6},{5,7},{10,8},{11,9},{8,1... | collective-permute-start | bytes 294920 | tf_op jit(solution)/shard_map/ppermute | solution.py:657
  11.4 1.3 %collective-permute-start.1 = (f32[6,32,128]{2,1,0:T(8,128)S(1)}, f32[6,32,128]{2,1,0:T(8,128)S(1)}, u32[]{:S(2)}, u32[]{:S(2)}) collective-permute-start(f32[6,32,128]{2,1,0:T(8,128)S(1)} %get-tuple-element.27.refs_0_), channel_id=1, source_target_pairs={{1,0},{2,1},{3,2},{0,3},{5,4},{6,5},{7,6},{4,7},{9,8},{10,9},{11,1... | collective-permute-start | bytes 294920 | tf_op jit(solution)/shard_map/ppermute | solution.py:657
  12.8 0.0 collective-permute-done.4.left_ref
  12.8 0.0 collective-permute-done.5.right_ref
  12.8 0.0 copy-start.6
  12.8 0.0 copy-start.14
  12.8 0.0 copy-start.15
  12.8 4.1 %near.1 = (f32[16,64,128]{2,1,0:T(8,128)S(1)}, f32[8,64,128]{2,1,0:T(8,128)S(1)}, f32[8,64,128]{2,1,0:T(8,128)S(1)}) custom-call(f32[8,128]{1,0:T(8,128)S(1)} %get-tuple-element.25.tap_ref, f32[16,64,128]{2,1,0:T(8,128)S(1)} %copy-done, f32[16,64,128]{2,1,0:T(8,128)S(1)} %collective-permute-done.lo_ref.hi_ref, ...), custom_call_target="tpu_custom_call" | custom-call | flops 5000000000 | bytes 3192832 | tf_op jit(solution)/shard_map/near/pallas_call | solution.py:634
  16.9 0.7 %collective-permute-start.9 = (f32[8,64,128]{2,1,0:T(8,128)S(1)}, f32[8,64,128]{2,1,0:T(8,128)S(1)}, u32[]{:S(2)}, u32[]{:S(2)}) collective-permute-start(f32[8,64,128]{2,1,0:T(8,128)S(1)} %get-tuple-element.43), channel_id=1, source_target_pairs={{3,0},{0,1},{1,2},{2,3},{7,4},{4,5},{5,6},{6,7},{11,8},{8,9},{9,10... | collective-permute-start | bytes 786440 | tf_op jit(solution)/shard_map/ppermute | solution.py:657
  17.6 3.1 %collective-permute-start.10 = (f32[8,64,128]{2,1,0:T(8,128)S(1)}, f32[8,64,128]{2,1,0:T(8,128)S(1)}, u32[]{:S(2)}, u32[]{:S(2)}) collective-permute-start(f32[8,64,128]{2,1,0:T(8,128)S(1)} %get-tuple-element.44), channel_id=1, source_target_pairs={{1,0},{2,1},{3,2},{0,3},{5,4},{6,5},{7,6},{4,7},{9,8},{10,9},{11,1... | collective-permute-start | bytes 786440 | tf_op jit(solution)/shard_map/ppermute | solution.py:657
  20.8 0.0 collective-permute-done.3.refs_3_
  20.8 0.0 collective-permute-done.2.refs_2_
  20.8 0.0 collective-permute-done.1.refs_1_
  20.8 0.0 copy-start.2
  20.8 0.0 copy-start.4
  20.8 0.0 copy-start.7
  20.8 0.0 copy-start.8
  20.9 0.0 copy-start.9
  20.9 0.0 copy-start.10
  20.9 0.0 copy-start.11
  20.9 0.0 copy-start.12
  20.9 0.0 copy-start.13
  20.9 0.0 copy-start.16
  20.9 0.0 copy-start.17
  20.9 1.7 %depth.1 = (f32[33,32,128]{2,1,0:T(8,128)S(1)}, f32[176,128]{1,0:T(8,128)S(1)}, f32[176,128]{1,0:T(8,128)S(1)}, f32[16,24,128]{2,1,0:T(8,128)S(1)}, f32[32,128]{1,0:T(8,128)S(1)}) custom-call(f32[8,128]{1,0:T(8,128)S(1)} %get-tuple-element.25.tap_ref, f32[6,32,128]{2,1,0:T(8,128)S(1)} %get-tuple-element.27.refs_0_, ...), custom_call_target="tpu_custom_call" | custom-call | flops 2000000000 | bytes 1991168 | tf_op jit(solution)/shard_map/depth/pallas_call | solution.py:634
  22.7 1.6 %collective-permute-start.7 = (f32[32,128]{1,0:T(8,128)S(1)}, f32[32,128]{1,0:T(8,128)S(1)}, u32[]{:S(2)}, u32[]{:S(2)}) collective-permute-start(f32[32,128]{1,0:T(8,128)S(1)} %get-tuple-element.32._.refs_0_), channel_id=1, source_target_pairs={{8,0},{12,4},{0,8},{4,12},{9,1},{13,5},{1,9},{5,13},{10,2},{14,6},... | collective-permute-start | bytes 49160 | tf_op jit(solution)/shard_map/ppermute | solution.py:657
  24.3 0.5 %collective-permute-start.6 = (f32[176,128]{1,0:T(8,128)S(1)}, f32[176,128]{1,0:T(8,128)S(1)}, u32[]{:S(2)}, u32[]{:S(2)}) collective-permute-start(f32[176,128]{1,0:T(8,128)S(1)} %get-tuple-element.36), channel_id=1, source_target_pairs={{4,0},{8,4},{12,8},{0,12},{5,1},{9,5},{13,9},{1,13},{6,2},{10,6},{... | collective-permute-start | bytes 270344 | tf_op jit(solution)/shard_map/ppermute | solution.py:657
  24.8 1.5 %collective-permute-start.8 = (f32[176,128]{1,0:T(8,128)S(1)}, f32[176,128]{1,0:T(8,128)S(1)}, u32[]{:S(2)}, u32[]{:S(2)}) collective-permute-start(f32[176,128]{1,0:T(8,128)S(1)} %get-tuple-element.37), channel_id=1, source_target_pairs={{12,0},{0,4},{4,8},{8,12},{13,1},{1,5},{5,9},{9,13},{14,2},{2,6},{... | collective-permute-start | bytes 270344 | tf_op jit(solution)/shard_map/ppermute | solution.py:657
  26.4 0.7 %matrices.1 = (f32[96,128]{1,0:T(8,128)S(1)}, bf16[128,768]{1,0:T(8,128)(2,1)S(1)}, bf16[128,768]{1,0:T(8,128)(2,1)S(1)}, bf16[128,768]{1,0:T(8,128)(2,1)S(1)}, ...) custom-call(f32[4,3]{1,0:T(4,128)S(1)} %copy-done.2, f32[4,3]{1,0:T(4,128)S(1)} %copy-done.4, ...), custom_call_target="tpu_custom_call" | custom-call | flops 2000000000 | bytes 885600 | tf_op jit(solution)/shard_map/matrices/pallas_call | solution.py:634
  27.1 0.0 collective-permute-done.7.refs_2_
  27.1 1.7 %collective-permute-done.6.refs_1_ = f32[176,128]{1,0:T(8,128)S(1)} collective-permute-done((f32[176,128]{1,0:T(8,128)S(1)}, f32[176,128]{1,0:T(8,128)S(1)}, u32[]{:S(2)}, u32[]{:S(2)}) %collective-permute-start.6) | collective-permute-done | bytes 90144 | tf_op jit(solution)/shard_map/ppermute | solution.py:657
  28.8 1.4 %collective-permute-done.8.refs_3_ = f32[176,128]{1,0:T(8,128)S(1)} collective-permute-done((f32[176,128]{1,0:T(8,128)S(1)}, f32[176,128]{1,0:T(8,128)S(1)}, u32[]{:S(2)}, u32[]{:S(2)}) %collective-permute-start.8) | collective-permute-done | bytes 90144 | tf_op jit(solution)/shard_map/ppermute | solution.py:657
  30.3 2.8 %along.1.d_ref = f32[216,1408]{1,0:T(8,128)S(1)} custom-call(f32[96,128]{1,0:T(8,128)S(1)} %get-tuple-element.33.z_ref, f32[33,32,128]{2,1,0:T(8,128)S(1)} %get-tuple-element.34.w_ref, f32[16,24,128]{2,1,0:T(8,128)S(1)} %get-tuple-element.35.c2_ref, f32[32,128]{1,0:T(8,128)S(1)} %get-tuple-element.32._.refs_0_, ...), custom_call_target="tpu_custom_call" | custom-call | flops 3000000000 | bytes 2805760 | tf_op jit(solution)/shard_map/along/pallas_call | solution.py:634
  33.1 0.5 %away.1 = f32[64,1408]{1,0:T(8,128)S(1)} custom-call(f32[216,1408]{1,0:T(8,128)S(1)} %along.1.d_ref, bf16[128,256]{1,0:T(8,128)(2,1)S(1)} %get-tuple-element.41.xh_ref, bf16[128,256]{1,0:T(8,128)(2,1)S(1)} %get-tuple-element.42.xl_ref), custom_call_target="tpu_custom_call" | custom-call | flops 1000000000 | bytes 1708032 | tf_op jit(solution)/shard_map/away/pallas_call | solution.py:634
  33.6 0.1 collective-permute-start.11
  33.7 0.0 collective-permute-done.10.high_ref
  33.7 0.5 %home.1.home_ref = f32[16,64,128]{2,1,0:T(8,128)S(1)} custom-call(f32[216,1408]{1,0:T(8,128)S(1)} %along.1.d_ref, bf16[128,256]{1,0:T(8,128)(2,1)S(1)} %get-tuple-element.41.xh_ref, bf16[128,256]{1,0:T(8,128)(2,1)S(1)} %get-tuple-element.42.xl_ref, f32[16,64,128]{2,1,0:T(8,128)S(1)} %get-tuple-element.31.refs_8_.own_ref, ...), custom_call_target="tpu_custom_call" | custom-call | flops 2000000000 | bytes 2920448 | tf_op jit(solution)/shard_map/home/pallas_call | solution.py:634
  34.2 1.1 %collective-permute-done.11.refs_0_ = f32[64,1408]{1,0:T(8,128)S(1)} collective-permute-done((f32[64,1408]{1,0:T(8,128)S(1)}, f32[64,1408]{1,0:T(8,128)S(1)}, u32[]{:S(2)}, u32[]{:S(2)}) %collective-permute-start.11) | collective-permute-done | bytes 360480 | tf_op jit(solution)/shard_map/ppermute | solution.py:657
  35.3 0.8 %last.1 = f32[16,64,128]{2,1,0:T(8,128)} custom-call(f32[16,64,128]{2,1,0:T(8,128)S(1)} %home.1.home_ref, f32[64,1408]{1,0:T(8,128)S(1)} %collective-permute-done.11.refs_0_), custom_call_target="tpu_custom_call" | custom-call | flops 1000000000 | bytes 1409024 | tf_op jit(solution)/shard_map/last/pallas_call | solution.py:634
  (21 shorter events, 0.0 us)
Async XLA Ops:
  0.0 2.2 %copy-start = (f32[16,64,128]{2,1,0:T(8,128)S(1)}, f32[16,64,128]{2,1,0:T(8,128)}, u32[]{:S(2)}) copy-start(f32[16,64,128]{2,1,0:T(8,128)} %b_ref.3) | copy-start | bytes 1572868
  0.0 2.2 %collective-permute-start = (f32[16,64,128]{2,1,0:T(8,128)}, f32[16,64,128]{2,1,0:T(8,128)S(1)}, u32[]{:S(2)}, u32[]{:S(2)}) collective-permute-start(f32[16,64,128]{2,1,0:T(8,128)} %b_ref.3), channel_id=1, source_target_pairs={{16,0},{0,16},{17,1},{1,17},{18,2},{2,18},{19,3},{3,19},{20,4},{4,... | collective-permute-start | bytes 1572872 | tf_op jit(solution)/shard_map/ppermute | solution.py:657
  0.5 0.7 %copy-start.1 = (f32[4,3]{1,0:T(4,128)S(1)}, f32[4,3]{1,0:T(4,128)}, u32[]{:S(2)}) copy-start(f32[4,3]{1,0:T(4,128)} %w_ref.3) | copy-start | bytes 148
  1.1 0.7 %copy-start.3 = (f32[4,3]{1,0:T(4,128)S(1)}, f32[4,3]{1,0:T(4,128)}, u32[]{:S(2)}) copy-start(f32[4,3]{1,0:T(4,128)} %a_ref.3) | copy-start | bytes 148
  2.9 9.9 %collective-permute-start.4 = (f32[1,80,128]{2,1,0:T(8,128)S(1)}, f32[1,80,128]{2,1,0:T(8,128)S(1)}, u32[]{:S(2)}, u32[]{:S(2)}) collective-permute-start(f32[1,80,128]{2,1,0:T(8,128)S(1)} %get-tuple-element.28), channel_id=1, source_target_pairs={{12,0},{0,4},{4,8},{8,12},{13,1},{1,5},{5,9},{9,13},{14,2},{2,6},{... | collective-permute-start | bytes 122888 | tf_op jit(solution)/shard_map/ppermute | solution.py:657
  5.8 7.0 %collective-permute-start.5 = (f32[1,80,128]{2,1,0:T(8,128)S(1)}, f32[1,80,128]{2,1,0:T(8,128)S(1)}, u32[]{:S(2)}, u32[]{:S(2)}) collective-permute-start(f32[1,80,128]{2,1,0:T(8,128)S(1)} %get-tuple-element.29), channel_id=1, source_target_pairs={{4,0},{8,4},{12,8},{0,12},{5,1},{9,5},{13,9},{1,13},{6,2},{10,6},{... | collective-permute-start | bytes 122888 | tf_op jit(solution)/shard_map/ppermute | solution.py:657
  6.8 13.9 %collective-permute-start.3 = (f32[6,32,128]{2,1,0:T(8,128)S(1)}, f32[6,32,128]{2,1,0:T(8,128)S(1)}, u32[]{:S(2)}, u32[]{:S(2)}) collective-permute-start(f32[6,32,128]{2,1,0:T(8,128)S(1)} %get-tuple-element.27.refs_0_), channel_id=1, source_target_pairs={{3,0},{0,1},{1,2},{2,3},{7,4},{4,5},{5,6},{6,7},{11,8},{8,9},{9,10... | collective-permute-start | bytes 294920 | tf_op jit(solution)/shard_map/ppermute | solution.py:657
  8.8 11.9 %collective-permute-start.2 = (f32[6,32,128]{2,1,0:T(8,128)S(1)}, f32[6,32,128]{2,1,0:T(8,128)S(1)}, u32[]{:S(2)}, u32[]{:S(2)}) collective-permute-start(f32[6,32,128]{2,1,0:T(8,128)S(1)} %get-tuple-element.27.refs_0_), channel_id=1, source_target_pairs={{2,0},{3,1},{0,2},{1,3},{6,4},{7,5},{4,6},{5,7},{10,8},{11,9},{8,1... | collective-permute-start | bytes 294920 | tf_op jit(solution)/shard_map/ppermute | solution.py:657
  11.4 9.3 %collective-permute-start.1 = (f32[6,32,128]{2,1,0:T(8,128)S(1)}, f32[6,32,128]{2,1,0:T(8,128)S(1)}, u32[]{:S(2)}, u32[]{:S(2)}) collective-permute-start(f32[6,32,128]{2,1,0:T(8,128)S(1)} %get-tuple-element.27.refs_0_), channel_id=1, source_target_pairs={{1,0},{2,1},{3,2},{0,3},{5,4},{6,5},{7,6},{4,7},{9,8},{10,9},{11,1... | collective-permute-start | bytes 294920 | tf_op jit(solution)/shard_map/ppermute | solution.py:657
  12.8 8.0 %copy-start.5 = (f32[128,128]{1,0:T(8,128)S(1)}, f32[128,128]{1,0:T(8,128)}, u32[]{:S(2)}) copy-start(f32[128,128]{1,0:T(8,128)} %constant.37.clone.refs_6_) | copy-start | bytes 196612
  12.8 8.0 %copy-start.6 = (f32[128,128]{1,0:T(8,128)S(1)}, f32[128,128]{1,0:T(8,128)}, u32[]{:S(2)}) copy-start(f32[128,128]{1,0:T(8,128)} %constant.26.clone.refs_4_) | copy-start | bytes 196612
  12.8 8.0 %copy-start.14 = (f32[24,32]{1,0:T(8,128)S(1)}, f32[24,32]{1,0:T(8,128)}, u32[]{:S(2)}) copy-start(f32[24,32]{1,0:T(8,128)} %constant.27.clone.refs_5_) | copy-start | bytes 9220
  12.8 8.0 %copy-start.15 = (f32[16,24]{1,0:T(8,128)S(1)}, f32[16,24]{1,0:T(8,128)}, u32[]{:S(2)}) copy-start(f32[16,24]{1,0:T(8,128)} %constant.38.clone.refs_7_) | copy-start | bytes 4612
  16.9 16.8 %collective-permute-start.9 = (f32[8,64,128]{2,1,0:T(8,128)S(1)}, f32[8,64,128]{2,1,0:T(8,128)S(1)}, u32[]{:S(2)}, u32[]{:S(2)}) collective-permute-start(f32[8,64,128]{2,1,0:T(8,128)S(1)} %get-tuple-element.43), channel_id=1, source_target_pairs={{3,0},{0,1},{1,2},{2,3},{7,4},{4,5},{5,6},{6,7},{11,8},{8,9},{9,10... | collective-permute-start | bytes 786440 | tf_op jit(solution)/shard_map/ppermute | solution.py:657
  17.6 16.1 %collective-permute-start.10 = (f32[8,64,128]{2,1,0:T(8,128)S(1)}, f32[8,64,128]{2,1,0:T(8,128)S(1)}, u32[]{:S(2)}, u32[]{:S(2)}) collective-permute-start(f32[8,64,128]{2,1,0:T(8,128)S(1)} %get-tuple-element.44), channel_id=1, source_target_pairs={{1,0},{2,1},{3,2},{0,3},{5,4},{6,5},{7,6},{4,7},{9,8},{10,9},{11,1... | collective-permute-start | bytes 786440 | tf_op jit(solution)/shard_map/ppermute | solution.py:657
  20.8 5.5 %copy-start.2 = (f32[4,3]{1,0:T(4,128)S(1)}, f32[4,3]{1,0:T(4,128)}, u32[]{:S(2)}) copy-start(f32[4,3]{1,0:T(4,128)} %w_ref.3) | copy-start | bytes 148
  20.8 5.5 %copy-start.4 = (f32[4,3]{1,0:T(4,128)S(1)}, f32[4,3]{1,0:T(4,128)}, u32[]{:S(2)}) copy-start(f32[4,3]{1,0:T(4,128)} %a_ref.3) | copy-start | bytes 148
  20.8 5.5 %copy-start.7 = (bf16[128,128]{1,0:T(8,128)(2,1)S(1)}, bf16[128,128]{1,0:T(8,128)(2,1)}, u32[]{:S(2)}) copy-start(bf16[128,128]{1,0:T(8,128)(2,1)} %constant.32.clone.py2) | copy-start | bytes 98308
  20.8 5.5 %copy-start.8 = (bf16[128,16]{1,0:T(8,128)(2,1)S(1)}, bf16[128,16]{1,0:T(8,128)(2,1)}, u32[]{:S(2)}) copy-start(bf16[128,16]{1,0:T(8,128)(2,1)} %constant.31.clone.px3l) | copy-start | bytes 12292
  20.9 5.5 %copy-start.9 = (bf16[128,16]{1,0:T(8,128)(2,1)S(1)}, bf16[128,16]{1,0:T(8,128)(2,1)}, u32[]{:S(2)}) copy-start(bf16[128,16]{1,0:T(8,128)(2,1)} %constant.30.clone.px3) | copy-start | bytes 12292
  20.9 5.5 %copy-start.10 = (bf16[128,32]{1,0:T(8,128)(2,1)S(1)}, bf16[128,32]{1,0:T(8,128)(2,1)}, u32[]{:S(2)}) copy-start(bf16[128,32]{1,0:T(8,128)(2,1)} %constant.29.clone.px2) | copy-start | bytes 24580
  20.9 5.5 %copy-start.11 = (bf16[128,64]{1,0:T(8,128)(2,1)S(1)}, bf16[128,64]{1,0:T(8,128)(2,1)}, u32[]{:S(2)}) copy-start(bf16[128,64]{1,0:T(8,128)(2,1)} %constant.28.clone.px1) | copy-start | bytes 49156
  20.9 5.5 %copy-start.12 = (bf16[64,128]{1,0:T(8,128)(2,1)S(1)}, bf16[64,128]{1,0:T(8,128)(2,1)}, u32[]{:S(2)}) copy-start(bf16[64,128]{1,0:T(8,128)(2,1)} %constant.34.clone.py3l) | copy-start | bytes 49156
  20.9 5.5 %copy-start.13 = (bf16[64,128]{1,0:T(8,128)(2,1)S(1)}, bf16[64,128]{1,0:T(8,128)(2,1)}, u32[]{:S(2)}) copy-start(bf16[64,128]{1,0:T(8,128)(2,1)} %constant.33.clone.py3) | copy-start | bytes 49156
  20.9 5.5 %copy-start.16 = (bf16[16,8]{1,0:T(8,128)(2,1)S(1)}, bf16[16,8]{1,0:T(8,128)(2,1)}, u32[]{:S(2)}) copy-start(bf16[16,8]{1,0:T(8,128)(2,1)} %constant.36.clone.pz3) | copy-start | bytes 772
  20.9 5.5 %copy-start.17 = (bf16[16,16]{1,0:T(8,128)(2,1)S(1)}, bf16[16,16]{1,0:T(8,128)(2,1)}, u32[]{:S(2)}) copy-start(bf16[16,16]{1,0:T(8,128)(2,1)} %constant.35.clone.pz2) | copy-start | bytes 1540
  22.7 4.4 %collective-permute-start.7 = (f32[32,128]{1,0:T(8,128)S(1)}, f32[32,128]{1,0:T(8,128)S(1)}, u32[]{:S(2)}, u32[]{:S(2)}) collective-permute-start(f32[32,128]{1,0:T(8,128)S(1)} %get-tuple-element.32._.refs_0_), channel_id=1, source_target_pairs={{8,0},{12,4},{0,8},{4,12},{9,1},{13,5},{1,9},{5,13},{10,2},{14,6},... | collective-permute-start | bytes 49160 | tf_op jit(solution)/shard_map/ppermute | solution.py:657
  24.3 4.5 %collective-permute-start.6 = (f32[176,128]{1,0:T(8,128)S(1)}, f32[176,128]{1,0:T(8,128)S(1)}, u32[]{:S(2)}, u32[]{:S(2)}) collective-permute-start(f32[176,128]{1,0:T(8,128)S(1)} %get-tuple-element.36), channel_id=1, source_target_pairs={{4,0},{8,4},{12,8},{0,12},{5,1},{9,5},{13,9},{1,13},{6,2},{10,6},{... | collective-permute-start | bytes 270344 | tf_op jit(solution)/shard_map/ppermute | solution.py:657
  24.8 5.4 %collective-permute-start.8 = (f32[176,128]{1,0:T(8,128)S(1)}, f32[176,128]{1,0:T(8,128)S(1)}, u32[]{:S(2)}, u32[]{:S(2)}) collective-permute-start(f32[176,128]{1,0:T(8,128)S(1)} %get-tuple-element.37), channel_id=1, source_target_pairs={{12,0},{0,4},{4,8},{8,12},{13,1},{1,5},{5,9},{9,13},{14,2},{2,6},{... | collective-permute-start | bytes 270344 | tf_op jit(solution)/shard_map/ppermute | solution.py:657
  33.6 1.7 %collective-permute-start.11 = (f32[64,1408]{1,0:T(8,128)S(1)}, f32[64,1408]{1,0:T(8,128)S(1)}, u32[]{:S(2)}, u32[]{:S(2)}) collective-permute-start(f32[64,1408]{1,0:T(8,128)S(1)} %away.1), channel_id=1, source_target_pairs={{16,0},{0,16},{17,1},{1,17},{18,2},{2,18},{19,3},{3,19},{20,4},{4,... | collective-permute-start | bytes 1081352 | tf_op jit(solution)/shard_map/ppermute | solution.py:657

commit v13 on v12

--- a/solution.py
+++ b/solution.py
@@ -512,7 +512,7 @@
 
 def along_kernel(s, z_ref, w_ref, c2_ref, *refs):
     c3_refs = refs[: s.gy]
-    y1_ref, y2h_ref, y2l_ref, d_ref, y2_ref, y3_ref = refs[s.gy :]
+    y1_ref, y2h_ref, y2l_ref, xh_ref, xl_ref, d_ref, *g_refs, y2_ref, y3_ref = refs[s.gy :]
     lane = lanes_of((s.rows1, LANES))
     above, below = c3_refs[1], c3_refs[-1]
     end = s.y1 + R
@@ -568,6 +568,7 @@
                     out += ref[t, j] * scale[j]
                 d_ref[at + t * rows : at + (t + 1) * rows, o * s.ny : (o + 1) * s.ny] = out
         at += TERMS * rows
+    away_kernel(s, d_ref, xh_ref, xl_ref, *g_refs)
 
 
 def across(s, d_ref, xh_ref, xl_ref, shift):
@@ -714,17 +715,13 @@
     for b in range(1, s.gy):
         coarses.append(fetch({1: to_low, s.gy - 1: to_high}.get(b, coarse), gy=b))
     near_low, near_high = fetch(near_up, gz=-1), fetch(near_down, gz=1)
-    (terms,) = call(
+    terms, *parts = call(
         functools.partial(along_kernel, s), "along",
-        [z_taps, waves, level2] + coarses + [y1, y2h, y2l],
-        arrays((s.depth, s.planes * s.ny)), scalars=(0,),
+        [z_taps, waves, level2] + coarses + [y1, y2h, y2l, xh, xl],
+        arrays((s.depth, s.planes * s.ny), *[(s.nx, s.planes * s.ny)] * (s.gx - 1)), scalars=(0,),
         scratch=[
             pltpu.VMEM((TERMS, s.cz[2], s.rows2, s.ny), F32), pltpu.VMEM((TERMS, s.cz[3], s.rows3, s.ny), F32)
         ], flops=3 * 10**9,
-    )
-    parts = call(
-        functools.partial(away_kernel, s), "away", [terms, xh, xl],
-        arrays(*[(s.nx, s.planes * s.ny)] * (s.gx - 1)), flops=10**9,
     )
     parts = [fetch(x, gx=-dx) for dx, x in enumerate(parts, 1)]
     (home,) = call(

time: 36.4 us -> 36.4 us (level)
    pallas_call x9 -> x8, Pallas kernels: 12.3 us -> 12.3 us  [call(): pl.pallas_call(kernel, name=name, out_shape=out_shapes, in_specs=[spec(i)...]
where the time goes in v13:
time: 36.4 us; the launch traced here: 36.2 us
  starting transfers between devices  17.9 us (49%)
  Pallas kernels  12.3 us (34%)
  waiting for transfers between devices  4.24 us (12%)
  local copies, waits for them, and re-layouts  1.46 us (4%)
    ppermute x12, starting transfers between devices, fetch(): return lax.ppermute(x, names if len(names) > 1 else names[0], pairs)  17.9 us
    pallas_call x8, Pallas kernels, call(): pl.pallas_call(kernel, name=name, out_shape=out_shapes, in_specs=[spec(i)...  12.3 us
    ppermute x12, waiting for transfers between devices, fetch(): return lax.ppermute(x, names if len(names) > 1 else names[0], pairs)  4.24 us
    unnamed x36, local copies, waits for them, and re-layouts  1.46 us
  transfers between devices with their start and end apart: 12, of which 3 were waited for; matrix products, arithmetic and copies ran while one was open for 0% of the time, Pallas kernels for 30%

profile of v13, /device:TPU:0, one launch (start us, length us, event | category | flops | bytes accessed | tf_op | source)
XLA Modules:
  0.0 36.2 jit_solution(17099626255891579451)
XLA Ops:
  0.0 0.5 %collective-permute-start = (f32[16,64,128]{2,1,0:T(8,128)}, f32[16,64,128]{2,1,0:T(8,128)S(1)}, u32[]{:S(2)}, u32[]{:S(2)}) collective-permute-start(f32[16,64,128]{2,1,0:T(8,128)} %b_ref.3), channel_id=1, source_target_pairs={{16,0},{0,16},{17,1},{1,17},{18,2},{2,18},{19,3},{3,19},{20,4},{4,... | collective-permute-start | bytes 1572872 | tf_op jit(solution)/shard_map/ppermute | solution.py:658
  0.5 0.7 %copy-done.1 = f32[4,3]{1,0:T(4,128)S(1)} copy-done((f32[4,3]{1,0:T(4,128)S(1)}, f32[4,3]{1,0:T(4,128)}, u32[]{:S(2)}) %copy-start.1) | copy-done | bytes 72
  1.1 0.7 %copy-done.3 = f32[4,3]{1,0:T(4,128)S(1)} copy-done((f32[4,3]{1,0:T(4,128)S(1)}, f32[4,3]{1,0:T(4,128)}, u32[]{:S(2)}) %copy-start.3) | copy-done | bytes 72
  1.8 0.4 %taps.1 = (f32[8,128]{1,0:T(8,128)S(1)}, bf16[192,240]{1,0:T(8,128)(2,1)S(1)}, bf16[256,768]{1,0:T(8,128)(2,1)S(1)}) custom-call(f32[4,3]{1,0:T(4,128)S(1)} %copy-done.1, f32[4,3]{1,0:T(4,128)S(1)} %copy-done.3), custom_call_target="tpu_custom_call" | custom-call | flops 600000000 | bytes 489568 | tf_op jit(solution)/shard_map/taps/pallas_call | solution.py:635
  2.2 0.0 collective-permute-done.lo_ref.hi_ref
  2.2 0.7 %share.1 = (f32[6,32,128]{2,1,0:T(8,128)S(1)}, f32[1,80,128]{2,1,0:T(8,128)S(1)}, f32[1,80,128]{2,1,0:T(8,128)S(1)}) custom-call(f32[16,64,128]{2,1,0:T(8,128)S(1)} %copy-done, f32[16,64,128]{2,1,0:T(8,128)S(1)} %collective-permute-done.lo_ref.hi_ref, f32[16,64,128]{2,1,0:T(8,128)S(1)} %collective-permute-done.lo_ref.hi_ref, ...), custom_call_target="tpu_custom_call" | custom-call | flops 1000000000 | bytes 1845248 | tf_op jit(solution)/shard_map/share/pallas_call | solution.py:635
  2.9 2.9 %collective-permute-start.4 = (f32[1,80,128]{2,1,0:T(8,128)S(1)}, f32[1,80,128]{2,1,0:T(8,128)S(1)}, u32[]{:S(2)}, u32[]{:S(2)}) collective-permute-start(f32[1,80,128]{2,1,0:T(8,128)S(1)} %get-tuple-element.30), channel_id=1, source_target_pairs={{12,0},{0,4},{4,8},{8,12},{13,1},{1,5},{5,9},{9,13},{14,2},{2,6},{... | collective-permute-start | bytes 122888 | tf_op jit(solution)/shard_map/ppermute | solution.py:658
  5.8 1.0 %collective-permute-start.5 = (f32[1,80,128]{2,1,0:T(8,128)S(1)}, f32[1,80,128]{2,1,0:T(8,128)S(1)}, u32[]{:S(2)}, u32[]{:S(2)}) collective-permute-start(f32[1,80,128]{2,1,0:T(8,128)S(1)} %get-tuple-element.31), channel_id=1, source_target_pairs={{4,0},{8,4},{12,8},{0,12},{5,1},{9,5},{13,9},{1,13},{6,2},{10,6},{... | collective-permute-start | bytes 122888 | tf_op jit(solution)/shard_map/ppermute | solution.py:658
  6.8 2.0 %collective-permute-start.3 = (f32[6,32,128]{2,1,0:T(8,128)S(1)}, f32[6,32,128]{2,1,0:T(8,128)S(1)}, u32[]{:S(2)}, u32[]{:S(2)}) collective-permute-start(f32[6,32,128]{2,1,0:T(8,128)S(1)} %get-tuple-element.29.refs_0_), channel_id=1, source_target_pairs={{3,0},{0,1},{1,2},{2,3},{7,4},{4,5},{5,6},{6,7},{11,8},{8,9},{9,10... | collective-permute-start | bytes 294920 | tf_op jit(solution)/shard_map/ppermute | solution.py:658
  8.8 2.6 %collective-permute-start.2 = (f32[6,32,128]{2,1,0:T(8,128)S(1)}, f32[6,32,128]{2,1,0:T(8,128)S(1)}, u32[]{:S(2)}, u32[]{:S(2)}) collective-permute-start(f32[6,32,128]{2,1,0:T(8,128)S(1)} %get-tuple-element.29.refs_0_), channel_id=1, source_target_pairs={{2,0},{3,1},{0,2},{1,3},{6,4},{7,5},{4,6},{5,7},{10,8},{11,9},{8,1... | collective-permute-start | bytes 294920 | tf_op jit(solution)/shard_map/ppermute | solution.py:658
  11.4 1.3 %collective-permute-start.1 = (f32[6,32,128]{2,1,0:T(8,128)S(1)}, f32[6,32,128]{2,1,0:T(8,128)S(1)}, u32[]{:S(2)}, u32[]{:S(2)}) collective-permute-start(f32[6,32,128]{2,1,0:T(8,128)S(1)} %get-tuple-element.29.refs_0_), channel_id=1, source_target_pairs={{1,0},{2,1},{3,2},{0,3},{5,4},{6,5},{7,6},{4,7},{9,8},{10,9},{11,1... | collective-permute-start | bytes 294920 | tf_op jit(solution)/shard_map/ppermute | solution.py:658
  12.8 0.0 collective-permute-done.4.left_ref
  12.8 0.0 collective-permute-done.5.right_ref
  12.8 0.0 copy-start.6
  12.8 0.0 copy-start.14
  12.8 0.0 copy-start.15
  12.8 4.0 %near.1 = (f32[16,64,128]{2,1,0:T(8,128)S(1)}, f32[8,64,128]{2,1,0:T(8,128)S(1)}, f32[8,64,128]{2,1,0:T(8,128)S(1)}) custom-call(f32[8,128]{1,0:T(8,128)S(1)} %get-tuple-element.27.tap_ref, f32[16,64,128]{2,1,0:T(8,128)S(1)} %copy-done, f32[16,64,128]{2,1,0:T(8,128)S(1)} %collective-permute-done.lo_ref.hi_ref, ...), custom_call_target="tpu_custom_call" | custom-call | flops 5000000000 | bytes 3192832 | tf_op jit(solution)/shard_map/near/pallas_call | solution.py:635
  16.9 0.7 %collective-permute-start.9 = (f32[8,64,128]{2,1,0:T(8,128)S(1)}, f32[8,64,128]{2,1,0:T(8,128)S(1)}, u32[]{:S(2)}, u32[]{:S(2)}) collective-permute-start(f32[8,64,128]{2,1,0:T(8,128)S(1)} %get-tuple-element.46), channel_id=1, source_target_pairs={{3,0},{0,1},{1,2},{2,3},{7,4},{4,5},{5,6},{6,7},{11,8},{8,9},{9,10... | collective-permute-start | bytes 786440 | tf_op jit(solution)/shard_map/ppermute | solution.py:658
  17.6 3.1 %collective-permute-start.10 = (f32[8,64,128]{2,1,0:T(8,128)S(1)}, f32[8,64,128]{2,1,0:T(8,128)S(1)}, u32[]{:S(2)}, u32[]{:S(2)}) collective-permute-start(f32[8,64,128]{2,1,0:T(8,128)S(1)} %get-tuple-element.47), channel_id=1, source_target_pairs={{1,0},{2,1},{3,2},{0,3},{5,4},{6,5},{7,6},{4,7},{9,8},{10,9},{11,1... | collective-permute-start | bytes 786440 | tf_op jit(solution)/shard_map/ppermute | solution.py:658
  20.7 0.0 collective-permute-done.3.refs_3_
  20.7 0.0 collective-permute-done.2.refs_2_
  20.7 0.0 collective-permute-done.1.refs_1_
  20.8 0.0 copy-start.2
  20.8 0.0 copy-start.4
  20.8 0.0 copy-start.7
  20.8 0.0 copy-start.8
  20.8 0.0 copy-start.9
  20.9 0.0 copy-start.10
  20.9 0.0 copy-start.11
  20.9 0.0 copy-start.12
  20.9 0.0 copy-start.13
  20.9 0.0 copy-start.16
  20.9 0.0 copy-start.17
  20.9 1.7 %depth.1 = (f32[33,32,128]{2,1,0:T(8,128)S(1)}, f32[176,128]{1,0:T(8,128)S(1)}, f32[176,128]{1,0:T(8,128)S(1)}, f32[16,24,128]{2,1,0:T(8,128)S(1)}, f32[32,128]{1,0:T(8,128)S(1)}) custom-call(f32[8,128]{1,0:T(8,128)S(1)} %get-tuple-element.27.tap_ref, f32[6,32,128]{2,1,0:T(8,128)S(1)} %get-tuple-element.29.refs_0_, ...), custom_call_target="tpu_custom_call" | custom-call | flops 2000000000 | bytes 1991168 | tf_op jit(solution)/shard_map/depth/pallas_call | solution.py:635
  22.7 1.6 %collective-permute-start.7 = (f32[32,128]{1,0:T(8,128)S(1)}, f32[32,128]{1,0:T(8,128)S(1)}, u32[]{:S(2)}, u32[]{:S(2)}) collective-permute-start(f32[32,128]{1,0:T(8,128)S(1)} %get-tuple-element.34._.refs_0_), channel_id=1, source_target_pairs={{8,0},{12,4},{0,8},{4,12},{9,1},{13,5},{1,9},{5,13},{10,2},{14,6},... | collective-permute-start | bytes 49160 | tf_op jit(solution)/shard_map/ppermute | solution.py:658
  24.3 0.5 %collective-permute-start.6 = (f32[176,128]{1,0:T(8,128)S(1)}, f32[176,128]{1,0:T(8,128)S(1)}, u32[]{:S(2)}, u32[]{:S(2)}) collective-permute-start(f32[176,128]{1,0:T(8,128)S(1)} %get-tuple-element.38), channel_id=1, source_target_pairs={{4,0},{8,4},{12,8},{0,12},{5,1},{9,5},{13,9},{1,13},{6,2},{10,6},{... | collective-permute-start | bytes 270344 | tf_op jit(solution)/shard_map/ppermute | solution.py:658
  24.8 1.5 %collective-permute-start.8 = (f32[176,128]{1,0:T(8,128)S(1)}, f32[176,128]{1,0:T(8,128)S(1)}, u32[]{:S(2)}, u32[]{:S(2)}) collective-permute-start(f32[176,128]{1,0:T(8,128)S(1)} %get-tuple-element.39), channel_id=1, source_target_pairs={{12,0},{0,4},{4,8},{8,12},{13,1},{1,5},{5,9},{9,13},{14,2},{2,6},{... | collective-permute-start | bytes 270344 | tf_op jit(solution)/shard_map/ppermute | solution.py:658
  26.4 0.7 %matrices.1 = (f32[96,128]{1,0:T(8,128)S(1)}, bf16[128,768]{1,0:T(8,128)(2,1)S(1)}, bf16[128,768]{1,0:T(8,128)(2,1)S(1)}, bf16[128,768]{1,0:T(8,128)(2,1)S(1)}, ...) custom-call(f32[4,3]{1,0:T(4,128)S(1)} %copy-done.2, f32[4,3]{1,0:T(4,128)S(1)} %copy-done.4, ...), custom_call_target="tpu_custom_call" | custom-call | flops 2000000000 | bytes 885600 | tf_op jit(solution)/shard_map/matrices/pallas_call | solution.py:635
  27.1 0.0 collective-permute-done.7.refs_2_
  27.1 1.7 %collective-permute-done.6.refs_1_ = f32[176,128]{1,0:T(8,128)S(1)} collective-permute-done((f32[176,128]{1,0:T(8,128)S(1)}, f32[176,128]{1,0:T(8,128)S(1)}, u32[]{:S(2)}, u32[]{:S(2)}) %collective-permute-start.6) | collective-permute-done | bytes 90144 | tf_op jit(solution)/shard_map/ppermute | solution.py:658
  28.8 1.4 %collective-permute-done.8.refs_3_ = f32[176,128]{1,0:T(8,128)S(1)} collective-permute-done((f32[176,128]{1,0:T(8,128)S(1)}, f32[176,128]{1,0:T(8,128)S(1)}, u32[]{:S(2)}, u32[]{:S(2)}) %collective-permute-start.8) | collective-permute-done | bytes 90144 | tf_op jit(solution)/shard_map/ppermute | solution.py:658
  30.2 3.4 %along.1 = (f32[216,1408]{1,0:T(8,128)S(1)}, f32[64,1408]{1,0:T(8,128)S(1)}) custom-call(f32[96,128]{1,0:T(8,128)S(1)} %get-tuple-element.35.z_ref, f32[33,32,128]{2,1,0:T(8,128)S(1)} %get-tuple-element.36.w_ref, f32[16,24,128]{2,1,0:T(8,128)S(1)} %get-tuple-element.37.c2_ref, f32[32,128]{1,0:T(8,128)S(1)} %get-tuple-element.34._.refs_0_, ...), custom_call_target="tpu_custom_call" | custom-call | flops 3000000000 | bytes 3297280 | tf_op jit(solution)/shard_map/along/pallas_call | solution.py:635
  33.6 0.1 collective-permute-start.11
  33.7 0.0 collective-permute-done.9.low_ref
  33.7 0.0 collective-permute-done.10.high_ref
  33.7 0.5 %home.1.home_ref = f32[16,64,128]{2,1,0:T(8,128)S(1)} custom-call(f32[216,1408]{1,0:T(8,128)S(1)} %get-tuple-element.45.d_ref, bf16[128,256]{1,0:T(8,128)(2,1)S(1)} %get-tuple-element.43.refs_7_.xh_ref, bf16[128,256]{1,0:T(8,128)(2,1)S(1)} %get-tuple-element.44.refs_8_.xl_ref, f32[16,64,128]{2,1,0:T(8,128)S(1)} %get-tuple-element.33.refs_8_.own_ref, ...), custom_call_target="tpu_custom_call" | custom-call | flops 2000000000 | bytes 2920448 | tf_op jit(solution)/shard_map/home/pallas_call | solution.py:635
  34.3 1.1 %collective-permute-done.11.refs_0_ = f32[64,1408]{1,0:T(8,128)S(1)} collective-permute-done((f32[64,1408]{1,0:T(8,128)S(1)}, f32[64,1408]{1,0:T(8,128)S(1)}, u32[]{:S(2)}, u32[]{:S(2)}) %collective-permute-start.11) | collective-permute-done | bytes 360480 | tf_op jit(solution)/shard_map/ppermute | solution.py:658
  35.4 0.8 %last.1 = f32[16,64,128]{2,1,0:T(8,128)} custom-call(f32[16,64,128]{2,1,0:T(8,128)S(1)} %home.1.home_ref, f32[64,1408]{1,0:T(8,128)S(1)} %collective-permute-done.11.refs_0_), custom_call_target="tpu_custom_call" | custom-call | flops 1000000000 | bytes 1409024 | tf_op jit(solution)/shard_map/last/pallas_call | solution.py:635
  (20 shorter events, 0.0 us)
Async XLA Ops:
  0.0 2.2 %copy-start = (f32[16,64,128]{2,1,0:T(8,128)S(1)}, f32[16,64,128]{2,1,0:T(8,128)}, u32[]{:S(2)}) copy-start(f32[16,64,128]{2,1,0:T(8,128)} %b_ref.3) | copy-start | bytes 1572868
  0.0 2.2 %collective-permute-start = (f32[16,64,128]{2,1,0:T(8,128)}, f32[16,64,128]{2,1,0:T(8,128)S(1)}, u32[]{:S(2)}, u32[]{:S(2)}) collective-permute-start(f32[16,64,128]{2,1,0:T(8,128)} %b_ref.3), channel_id=1, source_target_pairs={{16,0},{0,16},{17,1},{1,17},{18,2},{2,18},{19,3},{3,19},{20,4},{4,... | collective-permute-start | bytes 1572872 | tf_op jit(solution)/shard_map/ppermute | solution.py:658
  0.5 0.7 %copy-start.1 = (f32[4,3]{1,0:T(4,128)S(1)}, f32[4,3]{1,0:T(4,128)}, u32[]{:S(2)}) copy-start(f32[4,3]{1,0:T(4,128)} %w_ref.3) | copy-start | bytes 148
  1.1 0.7 %copy-start.3 = (f32[4,3]{1,0:T(4,128)S(1)}, f32[4,3]{1,0:T(4,128)}, u32[]{:S(2)}) copy-start(f32[4,3]{1,0:T(4,128)} %a_ref.3) | copy-start | bytes 148
  2.9 9.9 %collective-permute-start.4 = (f32[1,80,128]{2,1,0:T(8,128)S(1)}, f32[1,80,128]{2,1,0:T(8,128)S(1)}, u32[]{:S(2)}, u32[]{:S(2)}) collective-permute-start(f32[1,80,128]{2,1,0:T(8,128)S(1)} %get-tuple-element.30), channel_id=1, source_target_pairs={{12,0},{0,4},{4,8},{8,12},{13,1},{1,5},{5,9},{9,13},{14,2},{2,6},{... | collective-permute-start | bytes 122888 | tf_op jit(solution)/shard_map/ppermute | solution.py:658
  5.8 7.0 %collective-permute-start.5 = (f32[1,80,128]{2,1,0:T(8,128)S(1)}, f32[1,80,128]{2,1,0:T(8,128)S(1)}, u32[]{:S(2)}, u32[]{:S(2)}) collective-permute-start(f32[1,80,128]{2,1,0:T(8,128)S(1)} %get-tuple-element.31), channel_id=1, source_target_pairs={{4,0},{8,4},{12,8},{0,12},{5,1},{9,5},{13,9},{1,13},{6,2},{10,6},{... | collective-permute-start | bytes 122888 | tf_op jit(solution)/shard_map/ppermute | solution.py:658
  6.8 13.9 %collective-permute-start.3 = (f32[6,32,128]{2,1,0:T(8,128)S(1)}, f32[6,32,128]{2,1,0:T(8,128)S(1)}, u32[]{:S(2)}, u32[]{:S(2)}) collective-permute-start(f32[6,32,128]{2,1,0:T(8,128)S(1)} %get-tuple-element.29.refs_0_), channel_id=1, source_target_pairs={{3,0},{0,1},{1,2},{2,3},{7,4},{4,5},{5,6},{6,7},{11,8},{8,9},{9,10... | collective-permute-start | bytes 294920 | tf_op jit(solution)/shard_map/ppermute | solution.py:658
  8.8 11.9 %collective-permute-start.2 = (f32[6,32,128]{2,1,0:T(8,128)S(1)}, f32[6,32,128]{2,1,0:T(8,128)S(1)}, u32[]{:S(2)}, u32[]{:S(2)}) collective-permute-start(f32[6,32,128]{2,1,0:T(8,128)S(1)} %get-tuple-element.29.refs_0_), channel_id=1, source_target_pairs={{2,0},{3,1},{0,2},{1,3},{6,4},{7,5},{4,6},{5,7},{10,8},{11,9},{8,1... | collective-permute-start | bytes 294920 | tf_op jit(solution)/shard_map/ppermute | solution.py:658
  11.4 9.3 %collective-permute-start.1 = (f32[6,32,128]{2,1,0:T(8,128)S(1)}, f32[6,32,128]{2,1,0:T(8,128)S(1)}, u32[]{:S(2)}, u32[]{:S(2)}) collective-permute-start(f32[6,32,128]{2,1,0:T(8,128)S(1)} %get-tuple-element.29.refs_0_), channel_id=1, source_target_pairs={{1,0},{2,1},{3,2},{0,3},{5,4},{6,5},{7,6},{4,7},{9,8},{10,9},{11,1... | collective-permute-start | bytes 294920 | tf_op jit(solution)/shard_map/ppermute | solution.py:658
  12.8 8.0 %copy-start.5 = (f32[128,128]{1,0:T(8,128)S(1)}, f32[128,128]{1,0:T(8,128)}, u32[]{:S(2)}) copy-start(f32[128,128]{1,0:T(8,128)} %constant.37.clone.refs_6_) | copy-start | bytes 196612
  12.8 8.0 %copy-start.6 = (f32[128,128]{1,0:T(8,128)S(1)}, f32[128,128]{1,0:T(8,128)}, u32[]{:S(2)}) copy-start(f32[128,128]{1,0:T(8,128)} %constant.26.clone.refs_4_) | copy-start | bytes 196612
  12.8 8.0 %copy-start.14 = (f32[24,32]{1,0:T(8,128)S(1)}, f32[24,32]{1,0:T(8,128)}, u32[]{:S(2)}) copy-start(f32[24,32]{1,0:T(8,128)} %constant.27.clone.refs_5_) | copy-start | bytes 9220
  12.8 8.0 %copy-start.15 = (f32[16,24]{1,0:T(8,128)S(1)}, f32[16,24]{1,0:T(8,128)}, u32[]{:S(2)}) copy-start(f32[16,24]{1,0:T(8,128)} %constant.38.clone.refs_7_) | copy-start | bytes 4612
  16.9 16.8 %collective-permute-start.9 = (f32[8,64,128]{2,1,0:T(8,128)S(1)}, f32[8,64,128]{2,1,0:T(8,128)S(1)}, u32[]{:S(2)}, u32[]{:S(2)}) collective-permute-start(f32[8,64,128]{2,1,0:T(8,128)S(1)} %get-tuple-element.46), channel_id=1, source_target_pairs={{3,0},{0,1},{1,2},{2,3},{7,4},{4,5},{5,6},{6,7},{11,8},{8,9},{9,10... | collective-permute-start | bytes 786440 | tf_op jit(solution)/shard_map/ppermute | solution.py:658
  17.6 16.1 %collective-permute-start.10 = (f32[8,64,128]{2,1,0:T(8,128)S(1)}, f32[8,64,128]{2,1,0:T(8,128)S(1)}, u32[]{:S(2)}, u32[]{:S(2)}) collective-permute-start(f32[8,64,128]{2,1,0:T(8,128)S(1)} %get-tuple-element.47), channel_id=1, source_target_pairs={{1,0},{2,1},{3,2},{0,3},{5,4},{6,5},{7,6},{4,7},{9,8},{10,9},{11,1... | collective-permute-start | bytes 786440 | tf_op jit(solution)/shard_map/ppermute | solution.py:658
  20.8 5.5 %copy-start.2 = (f32[4,3]{1,0:T(4,128)S(1)}, f32[4,3]{1,0:T(4,128)}, u32[]{:S(2)}) copy-start(f32[4,3]{1,0:T(4,128)} %w_ref.3) | copy-start | bytes 148
  20.8 5.5 %copy-start.4 = (f32[4,3]{1,0:T(4,128)S(1)}, f32[4,3]{1,0:T(4,128)}, u32[]{:S(2)}) copy-start(f32[4,3]{1,0:T(4,128)} %a_ref.3) | copy-start | bytes 148
  20.8 5.5 %copy-start.7 = (bf16[128,128]{1,0:T(8,128)(2,1)S(1)}, bf16[128,128]{1,0:T(8,128)(2,1)}, u32[]{:S(2)}) copy-start(bf16[128,128]{1,0:T(8,128)(2,1)} %constant.32.clone.py2) | copy-start | bytes 98308
  20.8 5.5 %copy-start.8 = (bf16[128,16]{1,0:T(8,128)(2,1)S(1)}, bf16[128,16]{1,0:T(8,128)(2,1)}, u32[]{:S(2)}) copy-start(bf16[128,16]{1,0:T(8,128)(2,1)} %constant.31.clone.px3l) | copy-start | bytes 12292
  20.8 5.5 %copy-start.9 = (bf16[128,16]{1,0:T(8,128)(2,1)S(1)}, bf16[128,16]{1,0:T(8,128)(2,1)}, u32[]{:S(2)}) copy-start(bf16[128,16]{1,0:T(8,128)(2,1)} %constant.30.clone.px3) | copy-start | bytes 12292
  20.9 5.5 %copy-start.10 = (bf16[128,32]{1,0:T(8,128)(2,1)S(1)}, bf16[128,32]{1,0:T(8,128)(2,1)}, u32[]{:S(2)}) copy-start(bf16[128,32]{1,0:T(8,128)(2,1)} %constant.29.clone.px2) | copy-start | bytes 24580
  20.9 5.5 %copy-start.11 = (bf16[128,64]{1,0:T(8,128)(2,1)S(1)}, bf16[128,64]{1,0:T(8,128)(2,1)}, u32[]{:S(2)}) copy-start(bf16[128,64]{1,0:T(8,128)(2,1)} %constant.28.clone.px1) | copy-start | bytes 49156
  20.9 5.5 %copy-start.12 = (bf16[64,128]{1,0:T(8,128)(2,1)S(1)}, bf16[64,128]{1,0:T(8,128)(2,1)}, u32[]{:S(2)}) copy-start(bf16[64,128]{1,0:T(8,128)(2,1)} %constant.34.clone.py3l) | copy-start | bytes 49156
  20.9 5.5 %copy-start.13 = (bf16[64,128]{1,0:T(8,128)(2,1)S(1)}, bf16[64,128]{1,0:T(8,128)(2,1)}, u32[]{:S(2)}) copy-start(bf16[64,128]{1,0:T(8,128)(2,1)} %constant.33.clone.py3) | copy-start | bytes 49156
  20.9 5.5 %copy-start.16 = (bf16[16,8]{1,0:T(8,128)(2,1)S(1)}, bf16[16,8]{1,0:T(8,128)(2,1)}, u32[]{:S(2)}) copy-start(bf16[16,8]{1,0:T(8,128)(2,1)} %constant.36.clone.pz3) | copy-start | bytes 772
  20.9 5.5 %copy-start.17 = (bf16[16,16]{1,0:T(8,128)(2,1)S(1)}, bf16[16,16]{1,0:T(8,128)(2,1)}, u32[]{:S(2)}) copy-start(bf16[16,16]{1,0:T(8,128)(2,1)} %constant.35.clone.pz2) | copy-start | bytes 1540
  22.7 4.4 %collective-permute-start.7 = (f32[32,128]{1,0:T(8,128)S(1)}, f32[32,128]{1,0:T(8,128)S(1)}, u32[]{:S(2)}, u32[]{:S(2)}) collective-permute-start(f32[32,128]{1,0:T(8,128)S(1)} %get-tuple-element.34._.refs_0_), channel_id=1, source_target_pairs={{8,0},{12,4},{0,8},{4,12},{9,1},{13,5},{1,9},{5,13},{10,2},{14,6},... | collective-permute-start | bytes 49160 | tf_op jit(solution)/shard_map/ppermute | solution.py:658
  24.3 4.5 %collective-permute-start.6 = (f32[176,128]{1,0:T(8,128)S(1)}, f32[176,128]{1,0:T(8,128)S(1)}, u32[]{:S(2)}, u32[]{:S(2)}) collective-permute-start(f32[176,128]{1,0:T(8,128)S(1)} %get-tuple-element.38), channel_id=1, source_target_pairs={{4,0},{8,4},{12,8},{0,12},{5,1},{9,5},{13,9},{1,13},{6,2},{10,6},{... | collective-permute-start | bytes 270344 | tf_op jit(solution)/shard_map/ppermute | solution.py:658
  24.8 5.4 %collective-permute-start.8 = (f32[176,128]{1,0:T(8,128)S(1)}, f32[176,128]{1,0:T(8,128)S(1)}, u32[]{:S(2)}, u32[]{:S(2)}) collective-permute-start(f32[176,128]{1,0:T(8,128)S(1)} %get-tuple-element.39), channel_id=1, source_target_pairs={{12,0},{0,4},{4,8},{8,12},{13,1},{1,5},{5,9},{9,13},{14,2},{2,6},{... | collective-permute-start | bytes 270344 | tf_op jit(solution)/shard_map/ppermute | solution.py:658
  33.6 1.7 %collective-permute-start.11 = (f32[64,1408]{1,0:T(8,128)S(1)}, f32[64,1408]{1,0:T(8,128)S(1)}, u32[]{:S(2)}, u32[]{:S(2)}) collective-permute-start(f32[64,1408]{1,0:T(8,128)S(1)} %get-tuple-element.48), channel_id=1, source_target_pairs={{16,0},{0,16},{17,1},{1,17},{18,2},{2,18},{19,3},{3,19},{20,4},{4,... | collective-permute-start | bytes 1081352 | tf_op jit(solution)/shard_map/ppermute | solution.py:658
